TPU v7x, 32 devices: a whole 2x2x4 slice. The times are simulated.
32 devices in a mesh: head: 2 (over x), inner: 4 (over y, core), outer: 4 (over z).
Axes of the slice: x: 2, y: 2, z: 4, core: 2. Of those that a mesh axis runs over, the one named last changes fastest.
Arguments:
- query: bfloat16 [2048, 4096], P(('outer', 'inner', 'head')), may hold values from -80 to 80
- key: bfloat16 [2048, 1024], P(('outer', 'inner', 'head')), may hold values from -6 to 6
- value: bfloat16 [2048, 1024], P(('outer', 'inner', 'head')), may hold values from -6 to 6
- doc_lengths: int32 [24], replicated, may hold values from 1 to 512, 2048 in all
- resid: bfloat16 [2048, 4096], P('outer', 'inner'), may hold values from -20 to 20
- norm_gain: float32 [4096], P('inner'), may hold values from 0.1 to 1.9
- w_out: bfloat16 [4096, 4096], P('head', ('inner', 'outer')), may hold values from -0.09375 to 0.09375
- w_gate_up: bfloat16 [2, 4096, 7168], P(None, ('inner', 'outer'), 'head'), may hold values from -0.09375 to 0.09375
- w_down: bfloat16 [7168, 4096], P('head', ('inner', 'outer')), may hold values from -0.0625 to 0.0625
Outputs:
- context: bfloat16 [2048, 4096], P(('outer', 'inner'), 'head')
- layer_out: bfloat16 [2048, 4096], P(('outer', 'head'), 'inner')
Inputs may be any that keep to these rules, and one draw needn't show every extreme that they name: `doc_lengths`: the 24 lengths sum to 2048, and the longest is exactly 512.
All inputs are finite; a program needn't handle non-finite values.
Results may differ from a plain program's by a relative error of at most 0.03.
Values may be sent and summed in bfloat16 or wider, within the bound.
No kernel may reach another device: no remote copies, remote signals or barrier semaphores. Data moves between devices by JAX's collectives and lax.ppermute only.
A program may use at most 128 MiB of HBM per device.

v0:
```python
import jax
import jax.numpy as jnp
from jax import lax
from jax.sharding import PartitionSpec as P

D = 4096
QUERY_HEADS = 32
KEY_VALUE_HEADS = 8
HEAD_WIDTH = 128


def segment_ids(positions, bounds):
    return jnp.sum((bounds[None, :] <= positions[:, None]).astype(jnp.int32), axis=1)


def per_device(query, key, value, doc_lengths, resid, norm_gain, w_out, w_gate_up, w_down):
    inner_count = lax.axis_size("inner")
    outer_count = lax.axis_size("outer")
    head_count = lax.axis_size("head")
    cycle_block = lax.axis_index("outer") * inner_count + lax.axis_index("inner")
    weights_out, weights_gate_up, weights_down = (
        lax.all_gather(w_out, "outer", axis=1, tiled=True),
        lax.all_gather(w_gate_up, "outer", axis=1, tiled=True),
        lax.all_gather(w_down, "outer", axis=1, tiled=True),
    )
    local_query, local_key, local_value = (
        lax.all_to_all(query, "head", split_axis=1, concat_axis=0, tiled=True),
        lax.all_to_all(key, "head", split_axis=1, concat_axis=0, tiled=True),
        lax.all_to_all(value, "head", split_axis=1, concat_axis=0, tiled=True),
    )
    bounds = jnp.cumsum(doc_lengths)
    seq_rows = local_query.shape[0]
    kv_heads = local_key.shape[1] // HEAD_WIDTH
    group_width = QUERY_HEADS // KEY_VALUE_HEADS
    score_scale = HEAD_WIDTH ** (-0.5)
    query_place = cycle_block * seq_rows + jnp.arange(seq_rows, dtype=jnp.int32)
    query_segment = segment_ids(query_place, bounds)
    grouped_query = local_query.reshape(seq_rows, kv_heads, group_width, HEAD_WIDTH)
    portion = (
        lax.all_gather(local_key, ("inner", "outer"), axis=0, tiled=True),
        lax.all_gather(local_value, ("inner", "outer"), axis=0, tiled=True),
    )
    span_rows = portion[0].shape[0]
    gathered_row = jnp.arange(span_rows, dtype=jnp.int32)
    source = gathered_row // seq_rows
    key_place = (
        source % outer_count * inner_count + source // outer_count
    ) * seq_rows + gathered_row % seq_rows
    tile_keys = portion[0]
    tile_values = portion[1]
    count_keys = tile_keys.shape[0]
    key_segment = segment_ids(key_place, bounds)
    allowed = (
        (key_place[None, :] <= query_place[:, None])
        & (key_place[None, :] >= 0)
        & (key_segment[None, :] == query_segment[:, None])
    )
    running_max = jnp.full((kv_heads, group_width, seq_rows), -1e30, jnp.float32)
    scores = (
        jnp.einsum(
            "qkgd,nkd->kgqn",
            grouped_query,
            tile_keys.reshape(count_keys, kv_heads, HEAD_WIDTH),
            preferred_element_type=jnp.float32,
        )
        * score_scale
    )
    masked = jnp.where(allowed, scores, -1e30)
    new_max = jnp.maximum(running_max, jnp.max(masked, axis=-1))
    exp_scores = jnp.where(allowed, jnp.exp(masked - new_max[..., None]), 0.0)
    new_totals = jnp.sum(exp_scores, axis=-1)
    weighted = jnp.einsum(
        "kgqn,nkd->kgqd",
        exp_scores.astype(jnp.bfloat16),
        tile_values.reshape(count_keys, kv_heads, HEAD_WIDTH),
        preferred_element_type=jnp.float32,
    )
    final_state = (new_max, new_totals, weighted)
    running_max, totals, accumulated = final_state
    context = (
        jnp.transpose(accumulated / totals[..., None], (2, 0, 1, 3))
        .reshape(seq_rows, kv_heads * group_width * HEAD_WIDTH)
        .astype(jnp.bfloat16)
    )
    partial_proj = jnp.dot(
        lax.all_gather(context, "inner", axis=0, tiled=True),
        weights_out,
        preferred_element_type=jnp.float32,
    )
    projected = lax.psum(partial_proj.astype(jnp.bfloat16), "head").astype(jnp.float32)
    hidden_state = (resid.astype(jnp.float32) + projected).astype(jnp.bfloat16)
    state_wide = lax.optimization_barrier(hidden_state).astype(jnp.float32)
    square_sums = lax.psum(jnp.sum(state_wide * state_wide, axis=1), "inner")
    inverse = lax.rsqrt(square_sums / D + 1e-05)
    normed = (state_wide * inverse[:, None] * norm_gain[None, :]).astype(jnp.bfloat16)
    gate_up = jnp.einsum("td,kdf->ktf", normed, weights_gate_up, preferred_element_type=jnp.float32)
    gate_up = lax.psum(gate_up.astype(jnp.bfloat16), "inner").astype(jnp.float32)
    activated = (jax.nn.silu(gate_up[0]) * gate_up[1]).astype(jnp.bfloat16)
    share_rows = activated.shape[0] // head_count
    down_part = lax.psum_scatter(
        jnp.dot(activated, weights_down, preferred_element_type=jnp.float32).astype(jnp.bfloat16),
        "head",
        scatter_dimension=0,
        tiled=True,
    ).astype(jnp.float32)
    own_rows_state = lax.dynamic_slice_in_dim(
        state_wide, lax.axis_index("head") * share_rows, share_rows, 0
    )
    layer_out = (own_rows_state + down_part).astype(jnp.bfloat16)
    return (context, layer_out)


def solution(mesh):
    placed = (
        P(("outer", "inner", "head"), None),
        P(("outer", "inner", "head"), None),
        P(("outer", "inner", "head"), None),
        P(),
        P("outer", "inner"),
        P("inner"),
        P("head", ("inner", "outer")),
        P(None, ("inner", "outer"), "head"),
        P("head", ("inner", "outer")),
    )
    return jax.shard_map(
        per_device,
        mesh=mesh,
        in_specs=placed,
        out_specs=(P(("outer", "inner"), "head"), P(("outer", "head"), "inner")),
        check_vma=False,
    )
```

profile of v0, /device:TPU:0, one launch (start us, length us, event | category | flops | bytes accessed | tf_op | source)
XLA Modules:
  0.0 829.3 jit_solution(8555933367819358047)
XLA Ops:
  8.1 8.6 %all_to_all.54 = bf16[64,2,512]{2,0,1:T(8,128)(2,1)} all-to-all(bf16[64,2,512]{2,0,1:T(8,128)(2,1)S(1)} %bitcast.86), channel_id=1, replica_groups=mesh['head'=2,'inner'=4,'outer'=4] {'head'}, dimensions={1} | all-to-all | bytes 262144 | tf_op jit(solution)/shard_map/all_to_all | solution.py:28
  17.7 7.5 all_to_all.55
  27.9 3.5 all-to-all-start.1
  34.3 3.6 all-to-all-done.1
  38.3 20.7 %all-gather.7.cloned.1.call-done = bf16[2048,512]{1,0:T(8,128)(2,1)} async-done(((bf16[128,512]{1,0:T(8,128)(2,1)}), bf16[2048,512]{1,0:T(8,128)(2,1)}) %all-gather.7.cloned.1.call-update) | async-done | bytes 2097168 | tf_op jit(solution)/shard_map/all_gather | solution.py:40
  59.0 2.9 copy.45
  61.9 39.5 %all-gather.9.cloned.1.call-done = bf16[2048,512]{1,0:T(8,128)(2,1)} async-done(((bf16[128,512]{1,0:T(8,128)(2,1)}), bf16[2048,512]{1,0:T(8,128)(2,1)}) %all-gather.9.cloned.1.call-update) | async-done | bytes 2097168 | tf_op jit(solution)/shard_map/all_gather | solution.py:41
  101.4 4.0 copy.50
  105.4 2.8 fusion
  108.2 4.0 fusion.1
  112.2 5.0 divide_convert_fusion
  117.3 65.0 %all-gather.13.cloned.1.call-done = bf16[2048,1024]{1,0:T(8,128)(2,1)} async-done(((bf16[2048,256]{1,0:T(8,128)(2,1)}), bf16[2048,1024]{1,0:T(8,128)(2,1)}) %all-gather.13.cloned.1.call-update) | async-done | bytes 4194320 | tf_op jit(solution)/shard_map/all_gather | solution.py:22
  182.3 23.0 %all-gather.11.cloned.1.call-done = bf16[512,2048]{0,1:T(8,128)(2,1)} async-done(((bf16[128,2048]{0,1:T(8,128)(2,1)}), bf16[512,2048]{0,1:T(8,128)(2,1)}) %all-gather.11.cloned.1.call-update) | async-done | bytes 2097168 | tf_op jit(solution)/shard_map/all_gather | solution.py:86
  205.4 6.2 convolution_convert_fusion.1
  212.2 39.6 %all-reduce.3.cloned.1.call-done = bf16[512,1024]{1,0:T(8,128)(2,1)} async-done(((bf16[512,1024]{1,0:T(8,128)(2,1)}), bf16[512,1024]{1,0:T(8,128)(2,1)}) %all-reduce.3.cloned.1.call-update) | async-done | bytes 1048592 | tf_op jit(solution)/shard_map/psum | solution.py:90
  253.7 7.1 psum.22
  260.7 245.1 %all-gather.15.cloned.1.call-done = bf16[2,1024,3584]{2,1,0:T(8,128)(2,1)} async-done(((bf16[2,256,3584]{2,1,0:T(8,128)(2,1)}), bf16[2,1024,3584]{2,1,0:T(8,128)(2,1)}) %all-gather.15.cloned.1.call-update) | async-done | bytes 14680080 | tf_op jit(solution)/shard_map/all_gather | solution.py:23
  505.8 15.1 %fusion.8 = bf16[2,512,3584]{2,1,0:T(8,128)(2,1)} fusion(bf16[2,1024,3584]{2,1,0:T(8,128)(2,1)} %all-gather.15.cloned.1.call-done, f32[1024]{0:T(1024)S(1)} %copy-done.3, f32[512]{0:T(512)S(1)} %add_rsqrt_fusion, bf16[512,1024]{1,0:T(8,128)(2,1)S(1)} %add_convert_fusion), kind=kOutput, calls=%fused_computation.12 | convolution fusion | flops 7521959936 | bytes 23074816 | tf_op jit(solution)/shard_map/td,kdf->ktf/dot_general | solution.py:96
  521.7 134.2 %all-reduce.5.cloned.1.call-done = bf16[2,512,3584]{2,1,0:T(8,128)(2,1)} async-done(((bf16[2,512,3584]{2,1,0:T(8,128)(2,1)}), bf16[2,512,3584]{2,1,0:T(8,128)(2,1)}) %all-reduce.5.cloned.1.call-update) | async-done | bytes 7340048 | tf_op jit(solution)/shard_map/psum | solution.py:97
  655.9 11.1 %convert_element_type.67 = f32[2,512,3584]{2,1,0:T(8,128)} convert(bf16[2,512,3584]{2,1,0:T(8,128)(2,1)} %all-reduce.5.cloned.1.call-done) | non-fusion elementwise | flops 3670016 | bytes 22020096 | tf_op jit(solution)/shard_map/convert_element_type | solution.py:97
  667.0 122.8 %all-gather.17.cloned.1.call-done = bf16[3584,1024]{1,0:T(8,128)(2,1)} async-done(((bf16[3584,256]{1,0:T(8,128)(2,1)}), bf16[3584,1024]{1,0:T(8,128)(2,1)}) %all-gather.17.cloned.1.call-update) | async-done | bytes 7340048 | tf_op jit(solution)/shard_map/all_gather | solution.py:24
  789.8 12.3 %fusion.11 = bf16[512,1024]{1,0:T(8,128)(2,1)} fusion(bf16[3584,1024]{1,0:T(8,128)(2,1)} %all-gather.17.cloned.1.call-done, f32[2,512,3584]{2,1,0:T(8,128)} %convert_element_type.67), kind=kOutput, calls=%fused_computation.17 | convolution fusion | flops 3769630720 | bytes 23068672 | tf_op jit(solution)/shard_map/dot_general | solution.py:101
  803.4 17.4 %reduce-scatter.2.cloned.1.call-done = bf16[256,1024]{1,0:T(8,128)(2,1)} async-done(((bf16[512,1024]{1,0:T(8,128)(2,1)}), bf16[256,1024]{1,0:T(8,128)(2,1)}) %reduce-scatter.2.cloned.1.call-update) | async-done | bytes 524304 | tf_op jit(solution)/shard_map/reduce_scatter | solution.py:100
  820.8 2.0 add_convert_fusion.1
  (45 shorter events, 12.5 us)
Async XLA Ops:
  7.2 51.8 %all-gather.7.cloned.1.call-start = ((), (), s32[]{:S(2)}) async-start(), calls=%async_computation.4 | async-start | bytes 2228224 | tf_op jit(solution)/shard_map/all_gather | solution.py:40
  16.7 84.7 %all-gather.9.cloned.1.call-start = ((), (), s32[]{:S(2)}) async-start(), calls=%async_computation.5 | async-start | bytes 2228224 | tf_op jit(solution)/shard_map/all_gather | solution.py:41
  25.3 157.1 %all-gather.13.cloned.1.call-start = ((), (), s32[]{:S(2)}) async-start(), calls=%async_computation.7 | async-start | bytes 5242880 | tf_op jit(solution)/shard_map/all_gather | solution.py:22
  27.9 10.1 %all-to-all-start.1 = ((bf16[64,2,2048]{2,0,1:T(8,128)(2,1)}), bf16[64,2,2048]{2,0,1:T(8,128)(2,1)S(1)}, u32[]{:S(2)}, u32[]{:S(2)}) async-start(bf16[64,2,2048]{2,0,1:T(8,128)(2,1)} %bitcast.75), calls=%async_computation.1 | async-start | bytes 1048576 | tf_op jit(solution)/shard_map/all_to_all | solution.py:27
  31.4 174.0 %all-gather.11.cloned.1.call-start = ((), (), s32[]{:S(2)}) async-start(), calls=%async_computation.6 | async-start | bytes 2621440 | tf_op jit(solution)/shard_map/all_gather | solution.py:86
  108.2 4.0 copy-start
  117.3 134.5 %copy-start.2 = (bf16[512,1024]{1,0:T(8,128)(2,1)S(1)}, bf16[512,1024]{1,0:T(8,128)(2,1)}, u32[]{:S(2)}) copy-start(bf16[512,1024]{1,0:T(8,128)(2,1)} %param.13) | copy-start | bytes 3145732
  117.3 134.5 %all-reduce.3.cloned.1.call-start = ((), (), s32[]{:S(2)}) async-start(), calls=%async_computation.8 | async-start | bytes 2097152 | tf_op jit(solution)/shard_map/psum | solution.py:90
  211.5 294.3 %copy-start.3 = (f32[1024]{0:T(1024)S(1)}, f32[1024]{0:T(1024)}, u32[]{:S(2)}) copy-start(f32[1024]{0:T(1024)} %param.14) | copy-start | bytes 12292
  211.6 294.2 %all-gather.15.cloned.1.call-start = ((), (), s32[]{:S(2)}) async-start(), calls=%async_computation.9 | async-start | bytes 18350080 | tf_op jit(solution)/shard_map/all_gather | solution.py:23
  212.1 443.8 %all-reduce.5.cloned.1.call-start = ((), (), s32[]{:S(2)}) async-start(), calls=%async_computation.10 | async-start | bytes 14680064 | tf_op jit(solution)/shard_map/psum | solution.py:97
  520.9 268.9 %all-gather.17.cloned.1.call-start = ((), (), s32[]{:S(2)}) async-start(), calls=%async_computation.11 | async-start | bytes 9175040 | tf_op jit(solution)/shard_map/all_gather | solution.py:24
  521.7 299.1 %reduce-scatter.2.cloned.1.call-start = ((), (), s32[]{:S(2)}) async-start(), calls=%async_computation.12 | async-start | bytes 1572864 | tf_op jit(solution)/shard_map/reduce_scatter | solution.py:100
  667.0 135.1 %copy-start.1 = (bf16[128,4,4,128]{0,3,2,1:T(8,128)(2,1)S(1)}, bf16[128,4,4,128]{0,3,2,1:T(8,128)(2,1)}, u32[]{:S(2)}) copy-start(bf16[128,4,4,128]{0,3,2,1:T(8,128)(2,1)} %divide_convert_fusion) | copy-start | bytes 1572868
Sparse Core Ops, SparseCore 0:
  16.9 42.0 all-gather.6
  61.2 40.1 all-gather.8
  103.0 79.3 all-gather.12
  184.3 21.0 all-gather.10
  211.7 40.0 all-reduce.2
  253.3 252.4 all-gather.14
  521.1 134.7 all-reduce.4
  657.5 132.2 all-gather.16
  802.3 18.4 reduce-scatter.1
where the time goes:
time: 830 us; the launch traced here: 829 us
  waiting for transfers between devices  713 us (86%)
  matrix products  41.4 us (5%)
  blocking collectives  23.2 us (3%)
  other arithmetic  21.3 us (3%)
  between operations  14 us (2%)
  local copies, waits for them, and re-layouts  12.8 us (2%)
    all_gather x1, waiting for transfers between devices, per_device(): lax.all_gather(w_gate_up, 'outer', axis=1, tiled=True)  245 us
    psum x1, waiting for transfers between devices, per_device(): lax.psum(gate_up.astype(jnp.bfloat16), 'inner').astype(jnp.float32)  134 us
    all_gather x1, waiting for transfers between devices, per_device(): lax.all_gather(w_down, 'outer', axis=1, tiled=True)  123 us
    all_gather x1, waiting for transfers between devices, per_device(): lax.all_gather(w_out, 'outer', axis=1, tiled=True)  65 us
    psum x1, waiting for transfers between devices, per_device(): lax.psum(partial_proj.astype(jnp.bfloat16), 'head').astype(jnp.float32)  39.6 us
    all_gather x1, waiting for transfers between devices, per_device(): lax.all_gather(local_value, ('inner', 'outer'), axis=0, tiled=True)  39.5 us
    all_gather x1, waiting for transfers between devices, per_device(): lax.all_gather(context, 'inner', axis=0, tiled=True)  23 us
    all_gather x1, waiting for transfers between devices, per_device(): lax.all_gather(local_key, ('inner', 'outer'), axis=0, tiled=True)  20.7 us
  transfers between devices with their start and end apart: 10, of which 10 were waited for; matrix products, arithmetic and copies ran while one was open for 5% of the time, Pallas kernels for 0%

commit v1 on v0

v1 whole, which is shorter than its diff:
```python
import functools

import jax
import jax.numpy as jnp
from jax import lax
from jax.experimental import pallas as pl
from jax.experimental.pallas import tpu as pltpu
from jax.sharding import PartitionSpec as P

D = 4096
QUERY_HEADS = 32
KEY_VALUE_HEADS = 8
HEAD_WIDTH = 128
GROUP = QUERY_HEADS // KEY_VALUE_HEADS
WINDOW_PER_DOC = 4
QUERY_TILE = 128


def swap(array, axis, distance):
    count = lax.axis_size(axis)
    return lax.ppermute(array, axis, [(s, s ^ distance) for s in range(count)])


def attention_kernel(halo_rows, reach, starts_ref, queries_ref, own_ref, halo_ref, out_ref, keys, values):
    tile = pl.program_id(0)
    rows = queries_ref.shape[0]
    span = reach + rows

    @pl.when(tile == 0)
    def _():
        keys[:halo_rows, :] = halo_ref[:, :HEAD_WIDTH]
        values[:halo_rows, :] = halo_ref[:, HEAD_WIDTH:]
        keys[halo_rows:, :] = own_ref[:, :HEAD_WIDTH]
        values[halo_rows:, :] = own_ref[:, HEAD_WIDTH:]

    first = pl.multiple_of(tile * rows + (halo_rows - reach), rows)
    near_keys = keys[pl.ds(first, span), :]
    near_values = values[pl.ds(first, span), :]
    key_place = lax.broadcasted_iota(jnp.int32, (rows, span), 1)
    query_place = lax.broadcasted_iota(jnp.int32, (rows, span), 0) + reach
    start = starts_ref[...] - (first - halo_rows)
    allowed = (key_place <= query_place) & (key_place >= start)
    for g in range(GROUP):
        cols = slice(g * HEAD_WIDTH, (g + 1) * HEAD_WIDTH)
        scores = lax.dot_general(
            queries_ref[:, cols], near_keys, (((1,), (1,)), ((), ())), preferred_element_type=jnp.float32
        ) * (HEAD_WIDTH ** (-0.5))
        masked = jnp.where(allowed, scores, -1e30)
        row_max = jnp.max(masked, axis=1, keepdims=True)
        weights = jnp.exp(masked - row_max)
        totals = jnp.sum(weights, axis=1, keepdims=True)
        summed = jnp.dot(weights.astype(jnp.bfloat16), near_values, preferred_element_type=jnp.float32)
        out_ref[:, cols] = (summed / totals).astype(jnp.bfloat16)


def attention(packed, halo, starts, reach):
    rows = packed.shape[0]
    halo_rows = halo.shape[0]
    q_cols = GROUP * HEAD_WIDTH
    kv_cols = 2 * HEAD_WIDTH
    return pl.pallas_call(
        functools.partial(attention_kernel, halo_rows, reach),
        grid=(rows // QUERY_TILE,),
        in_specs=[
            pl.BlockSpec((QUERY_TILE, 1), lambda t: (t, 0)),
            pl.BlockSpec((QUERY_TILE, q_cols), lambda t: (t, 0)),
            pl.BlockSpec((rows, kv_cols), lambda t: (0, q_cols // kv_cols)),
            pl.BlockSpec((halo_rows, kv_cols), lambda t: (0, 0)),
        ],
        out_specs=pl.BlockSpec((QUERY_TILE, q_cols), lambda t: (t, 0)),
        out_shape=jax.ShapeDtypeStruct((rows, q_cols), jnp.bfloat16),
        scratch_shapes=[
            pltpu.VMEM((halo_rows + rows, HEAD_WIDTH), jnp.bfloat16),
            pltpu.VMEM((halo_rows + rows, HEAD_WIDTH), jnp.bfloat16),
        ],
        compiler_params=pltpu.CompilerParams(vmem_limit_bytes=32 * 1024 * 1024),
        cost_estimate=pl.CostEstimate(
            flops=4 * rows * (reach + QUERY_TILE) * q_cols,
            bytes_accessed=rows * 4 * q_cols,
            transcendentals=rows * (reach + QUERY_TILE) * GROUP,
        ),
    )(starts, packed, packed, halo)


def earlier_planes(kv, hops):
    count = lax.axis_size("outer")
    moved = [lax.ppermute(kv, "outer", [(s, s + d) for s in range(count - d)]) for d in range(hops, 0, -1)]
    return jnp.concatenate(moved, axis=0)


def document_starts(bounds, first, rows):
    place = first + jnp.arange(rows, dtype=jnp.int32)
    starts = jnp.max(jnp.where(bounds[None, :] <= place[:, None], bounds[None, :], 0), axis=1) - first
    return starts[:, None].astype(jnp.int32)


def per_device(query, key, value, doc_lengths, resid, norm_gain, w_out, w_gate_up, w_down):
    inner_count = lax.axis_size("inner")
    outer_count = lax.axis_size("outer")
    head_count = lax.axis_size("head")
    outer, inner, head = lax.axis_index("outer"), lax.axis_index("inner"), lax.axis_index("head")
    rows = query.shape[0]
    plane_rows = rows * inner_count * head_count
    reach = plane_rows * outer_count // WINDOW_PER_DOC
    feature_rows = w_gate_up.shape[1]
    hidden_cols = w_gate_up.shape[2] // outer_count

    weights_out = lax.all_gather(w_out, "outer", axis=1, tiled=True)
    bounds = jnp.cumsum(doc_lengths)
    hops = reach // plane_rows
    token_rows = plane_rows // inner_count
    packing = (head_count, KEY_VALUE_HEADS // head_count)
    groups = jnp.concatenate(
        [
            query.reshape(rows, *packing, GROUP * HEAD_WIDTH),
            key.reshape(rows, *packing, HEAD_WIDTH),
            value.reshape(rows, *packing, HEAD_WIDTH),
        ],
        axis=3,
    )
    q_cols = GROUP * HEAD_WIDTH
    if packing[1] == inner_count:
        groups = jnp.transpose(groups, (2, 1, 0, 3)).reshape(inner_count * head_count, rows, -1)
        packed = lax.all_to_all(groups, ("inner", "head"), split_axis=0, concat_axis=0, tiled=True)
        packed = packed.reshape(plane_rows, -1)
        halo = earlier_planes(packed[:, q_cols:], hops)
        starts = document_starts(bounds, outer * plane_rows, plane_rows)
        own_context = attention(packed, halo, starts, reach)
        across = swap(own_context, "inner", 2)
        parts = [own_context, swap(own_context, "inner", 1), across, swap(across, "inner", 1)]
        plane_context = jnp.zeros((plane_rows, inner_count * q_cols), jnp.bfloat16)
        for d, part in enumerate(parts):
            plane_context = lax.dynamic_update_slice(plane_context, part, (0, (inner ^ d) * q_cols))
        context = lax.dynamic_slice_in_dim(plane_context, inner * token_rows, token_rows, 0)
    else:
        groups = jnp.transpose(groups[:, :, 0], (1, 0, 2))
        packed = lax.all_to_all(groups, "head", split_axis=0, concat_axis=0, tiled=True).reshape(token_rows, -1)
        plane_kv = lax.all_gather(packed[:, q_cols:], "inner", axis=0, tiled=True)
        every_kv = jnp.concatenate([earlier_planes(plane_kv, hops), plane_kv], axis=0)
        halo = lax.dynamic_slice_in_dim(every_kv, inner * token_rows, reach, 0)
        starts = document_starts(bounds, outer * plane_rows + inner * token_rows, token_rows)
        context = attention(packed, halo, starts, reach)
        plane_context = lax.all_gather(context, "inner", axis=0, tiled=True)

    half = plane_rows // head_count
    partial_proj = jnp.dot(plane_context, weights_out, preferred_element_type=jnp.float32).astype(jnp.bfloat16)
    projected = lax.dynamic_slice_in_dim(partial_proj, head * half, half, 0).astype(jnp.float32)
    for e in range(1, head_count):
        sent = lax.dynamic_slice_in_dim(partial_proj, (head ^ e) * half, half, 0)
        projected = projected + swap(sent, "head", e).astype(jnp.float32)
    own_resid = lax.dynamic_slice_in_dim(resid, head * half, half, 0)
    hidden_part = (own_resid.astype(jnp.float32) + projected).astype(jnp.bfloat16)
    hidden_state = lax.all_to_all(hidden_part, "inner", split_axis=0, concat_axis=1, tiled=True)
    gain = lax.all_gather(norm_gain, "inner", axis=0, tiled=True)
    state_wide = hidden_state.astype(jnp.float32)
    mean_square = jnp.mean(state_wide * state_wide, axis=1, keepdims=True)
    normed = (state_wide * lax.rsqrt(mean_square + 1e-05) * gain[None, :]).astype(jnp.bfloat16)

    tokens = []
    for d in range(outer_count):
        block = swap(normed, "outer", d) if d else normed
        tokens += [block] + [swap(block, "head", e) for e in range(1, head_count)]
    tokens = jnp.concatenate(tokens, axis=0)

    gate_up_weights = jnp.zeros((2, D, hidden_cols), jnp.bfloat16)
    down_weights = jnp.zeros((hidden_cols, D), jnp.bfloat16)
    for d in range(outer_count):
        piece = lax.dynamic_slice_in_dim(w_gate_up, (outer ^ d) * hidden_cols, hidden_cols, 2)
        piece = swap(piece, "outer", d) if d else piece
        across = swap(piece, "inner", 2)
        for e, part in enumerate([piece, swap(piece, "inner", 1), across, swap(across, "inner", 1)]):
            at = ((inner ^ e) * outer_count + (outer ^ d)) * feature_rows
            gate_up_weights = lax.dynamic_update_slice(gate_up_weights, part, (0, at, 0))
    for d in range(outer_count):
        piece = lax.dynamic_slice_in_dim(w_down, (outer ^ d) * hidden_cols, hidden_cols, 0)
        piece = swap(piece, "outer", d) if d else piece
        across = swap(piece, "inner", 2)
        for e, part in enumerate([piece, swap(piece, "inner", 1), across, swap(across, "inner", 1)]):
            at = ((inner ^ e) * outer_count + (outer ^ d)) * feature_rows
            down_weights = lax.dynamic_update_slice(down_weights, part, (0, at))

    gate_up = jnp.einsum("td,kdf->ktf", tokens, gate_up_weights, preferred_element_type=jnp.float32)
    activated = (jax.nn.silu(gate_up[0]) * gate_up[1]).astype(jnp.bfloat16)
    down = jnp.dot(activated, down_weights, preferred_element_type=jnp.float32).astype(jnp.bfloat16)
    down = down.reshape(outer_count, head_count, -1, D)
    paired = down[:, 0].astype(jnp.float32)
    for e in range(1, head_count):
        paired = paired + swap(down[:, e], "head", e).astype(jnp.float32)
    down_sum = paired[0]
    for d in range(1, outer_count):
        down_sum = down_sum + swap(paired[d].astype(jnp.bfloat16), "outer", d).astype(jnp.float32)
    layer_rows = (state_wide + down_sum).astype(jnp.bfloat16)
    layer_out = lax.all_to_all(layer_rows, "inner", split_axis=1, concat_axis=0, tiled=True)
    return (context, layer_out)


def solution(mesh):
    placed = (
        P(("outer", "inner", "head"), None),
        P(("outer", "inner", "head"), None),
        P(("outer", "inner", "head"), None),
        P(),
        P("outer", "inner"),
        P("inner"),
        P("head", ("inner", "outer")),
        P(None, ("inner", "outer"), "head"),
        P("head", ("inner", "outer")),
    )
    return jax.shard_map(
        per_device,
        mesh=mesh,
        in_specs=placed,
        out_specs=(P(("outer", "inner"), "head"), P(("outer", "head"), "inner")),
        check_vma=False,
    )
```

time: 830 us -> 555 us (0.67)
  waiting for transfers between devices: 713 us -> 307 us
  local copies, waits for them, and re-layouts: 12.8 us -> 110 us
  starting transfers between devices: 3.85 us -> 76.7 us
  blocking collectives: 23.2 us -> 5.32 us
  matrix products: 41.4 us -> 24.7 us
  other arithmetic: 21.3 us -> 5.3 us
    all_gather x6 -> x1, waiting for transfers between devices: 516 us -> 0.01 us  [per_device(): weights_out = lax.all_gather(w_out, 'outer', axis=1, tiled=True)]
    ppermute x0 -> x46, waiting for transfers between devices: none -> 298 us  [the longest x45 298 us: swap(): return lax.ppermute(array, axis, [(s, s ^ distance) for s in range(count)])]
    psum x2 -> x0, waiting for transfers between devices: 174 us -> none  [the longest x1 134 us: per_device(): lax.psum(gate_up.astype(jnp.bfloat16), 'inner').astype(jnp.float32)]
    ppermute x0 -> x46, starting transfers between devices: none -> 65.8 us  [the longest x45 44.2 us: swap(): return lax.ppermute(array, axis, [(s, s ^ distance) for s in range(count)])]
    dynamic_update_slice x0 -> x35, local copies, waits for them, and re-layouts: none -> 53.4 us  [the longest x15 26.4 us: per_device(): down_weights = lax.dynamic_update_slice(down_weights, part, (0, at))]
    ppermute x0 -> x15, local copies, waits for them, and re-layouts: none -> 29.6 us  [swap(): return lax.ppermute(array, axis, [(s, s ^ distance) for s in range(count)])]
    reduce_scatter x1 -> x0, waiting for transfers between devices: 17.4 us -> none  [per_device(): lax.psum_scatter(jnp.dot(activated, weights_down, preferred_element_type=...]
    dot_general x5 -> x3, matrix products: 41.4 us -> 24.7 us  [the longest x1 11.3 us: per_device(): jnp.einsum('td,kdf->ktf', tokens, gate_up_weights, preferred_element_type...]
  transfers between devices with their start and end apart: 10 -> 50, of which waited for: 10 -> 19; matrix products, arithmetic and copies ran while one was open for 5% -> 21% of each run, Pallas kernels for 0% -> 1%
where the time goes in v1:
time: 555 us; the launch traced here: 549 us
  waiting for transfers between devices  307 us (55%)
  local copies, waits for them, and re-layouts  110 us (20%)
  starting transfers between devices  76.7 us (14%)
  matrix products  24.7 us (4%)
  between operations  14.7 us (3%)
  Pallas kernels  5.79 us (1%)
    ppermute x45, waiting for transfers between devices, swap(): return lax.ppermute(array, axis, [(s, s ^ distance) for s in range(count)])  298 us
    ppermute x45, starting transfers between devices, swap(): return lax.ppermute(array, axis, [(s, s ^ distance) for s in range(count)])  44.2 us
    ppermute x15, local copies, waits for them, and re-layouts, swap(): return lax.ppermute(array, axis, [(s, s ^ distance) for s in range(count)])  29.6 us
    dynamic_update_slice x15, local copies, waits for them, and re-layouts, per_device(): down_weights = lax.dynamic_update_slice(down_weights, part, (0, at))  26.4 us
    ppermute x1, starting transfers between devices, earlier_planes(): lax.ppermute(kv, 'outer', [(s, s + d) for s in range(count - d)])  21.6 us
    dynamic_update_slice x16, local copies, waits for them, and re-layouts, per_device(): lax.dynamic_update_slice(gate_up_weights, part, (0, at, 0))  21.5 us
    dot_general x1, matrix products, per_device(): jnp.einsum('td,kdf->ktf', tokens, gate_up_weights, preferred_element_type...  11.3 us
  transfers between devices with their start and end apart: 50, of which 19 were waited for; matrix products, arithmetic and copies ran while one was open for 21% of the time, Pallas kernels for 1%

profile of v1, /device:TPU:0, one launch (start us, length us, event | category | flops | bytes accessed | tf_op | source)
XLA Modules:
  0.0 549.3 jit_solution(15960495876926894249)
XLA Ops:
  28.7 17.4 %collective-permute-done.30 = bf16[896,256]{1,0:T(8,128)(2,1)S(1)} collective-permute-done((bf16[896,256]{1,0:T(8,128)(2,1)S(1)}, bf16[896,256]{1,0:T(8,128)(2,1)S(1)}, u32[]{:S(2)}, u32[]{:S(2)}) %collective-permute-start.30) | collective-permute-done | bytes 458784 | tf_op jit(solution)/shard_map/ppermute | solution.py:21
  46.2 17.3 %collective-permute-done.34 = bf16[896,256]{1,0:T(8,128)(2,1)S(1)} collective-permute-done((bf16[896,256]{1,0:T(8,128)(2,1)S(1)}, bf16[896,256]{1,0:T(8,128)(2,1)S(1)}, u32[]{:S(2)}, u32[]{:S(2)}) %collective-permute-start.34) | collective-permute-done | bytes 458784 | tf_op jit(solution)/shard_map/ppermute | solution.py:21
  63.5 13.0 %collective-permute-done.38 = bf16[896,256]{1,0:T(8,128)(2,1)} collective-permute-done((bf16[896,256]{1,0:T(8,128)(2,1)S(1)}, bf16[896,256]{1,0:T(8,128)(2,1)}, u32[]{:S(2)}, u32[]{:S(2)}) %collective-permute-start.38) | collective-permute-done | bytes 458784 | tf_op jit(solution)/shard_map/ppermute | solution.py:21
  90.4 39.4 %collective-permute-done.8 = bf16[2,256,896]{2,1,0:T(8,128)(2,1)S(1)} collective-permute-done((bf16[2,256,896]{2,1,0:T(8,128)(2,1)}, bf16[2,256,896]{2,1,0:T(8,128)(2,1)S(1)}, u32[]{:S(2)}, u32[]{:S(2)}) %collective-permute-start.8) | collective-permute-done | bytes 917536 | tf_op jit(solution)/shard_map/ppermute | solution.py:21
  131.6 5.3 all_gather.7
  136.9 50.3 %collective-permute-done.12 = bf16[2,256,896]{2,1,0:T(8,128)(2,1)} collective-permute-done((bf16[2,256,896]{2,1,0:T(8,128)(2,1)}, bf16[2,256,896]{2,1,0:T(8,128)(2,1)}, u32[]{:S(2)}, u32[]{:S(2)}) %collective-permute-start.12) | collective-permute-done | bytes 917536 | tf_op jit(solution)/shard_map/ppermute | solution.py:21
  187.9 7.0 %broadcast_in_dim.27 = bf16[2,4096,896]{1,2,0:T(8,128)(2,1)} broadcast(bf16[]{:T(256)} %constant.22.clone.1), dimensions={} | broadcast | bytes 14680066 | tf_op jit(solution)/shard_map/broadcast_in_dim | solution.py:165
  202.1 21.6 %collective-permute-start = (bf16[512,256]{1,0:T(8,128)(2,1)}, bf16[512,256]{1,0:T(8,128)(2,1)S(1)}, u32[]{:S(2)}, u32[]{:S(2)}) collective-permute-start(bf16[512,256]{1,0:T(8,128)(2,1)} %slice.39), channel_id=1, source_target_pairs={{0,1},{1,2},{2,3},{4,5},{5,6},{6,7},{8,9},{9,10},{10,11},{12,13},{... | collective-permute-start | bytes 786440 | tf_op jit(solution)/shard_map/ppermute | solution.py:87
  234.4 5.8 %shard_map.104 = bf16[512,512]{1,0:T(8,128)(2,1)S(1)} custom-call(s32[512,1]{1,0:T(8,128)S(1)} %copy.79.starts_ref, bf16[512,768]{1,0:T(8,128)(2,1)S(1)} %bitcast.74, bf16[512,768]{1,0:T(8,128)(2,1)S(1)} %bitcast.75, bf16[512,256]{1,0:T(8,128)(2,1)S(1)} %collective-permute-done.halo_ref), custom_call_target="tpu_custom_call" | custom-call | flops 671088640 | bytes 1048576 | tf_op jit(solution)/shard_map/pallas_call | solution.py:61
  268.5 6.7 %collective-permute-done.10 = bf16[2,256,896]{2,1,0:T(8,128)(2,1)S(1)} collective-permute-done((bf16[2,256,896]{2,1,0:T(8,128)(2,1)S(1)}, bf16[2,256,896]{2,1,0:T(8,128)(2,1)S(1)}, u32[]{:S(2)}, u32[]{:S(2)}) %collective-permute-start.10) | collective-permute-done | bytes 917536 | tf_op jit(solution)/shard_map/ppermute | solution.py:21
  288.0 7.0 %collective-permute-done.14 = bf16[2,256,896]{2,1,0:T(8,128)(2,1)} collective-permute-done((bf16[2,256,896]{2,1,0:T(8,128)(2,1)}, bf16[2,256,896]{2,1,0:T(8,128)(2,1)}, u32[]{:S(2)}, u32[]{:S(2)}) %collective-permute-start.14) | collective-permute-done | bytes 917536 | tf_op jit(solution)/shard_map/ppermute | solution.py:21
  297.2 16.6 %collective-permute-done.18 = bf16[2,256,896]{2,1,0:T(8,128)(2,1)} collective-permute-done((bf16[2,256,896]{2,1,0:T(8,128)(2,1)}, bf16[2,256,896]{2,1,0:T(8,128)(2,1)}, u32[]{:S(2)}, u32[]{:S(2)}) %collective-permute-start.18) | collective-permute-done | bytes 917536 | tf_op jit(solution)/shard_map/ppermute | solution.py:21
  325.1 5.3 convolution_convert_fusion.1
  371.0 15.0 %collective-permute-done.21 = bf16[64,4096]{1,0:T(8,128)(2,1)S(1)} collective-permute-done((bf16[64,4096]{1,0:T(8,128)(2,1)S(1)}, bf16[64,4096]{1,0:T(8,128)(2,1)S(1)}, u32[]{:S(2)}, u32[]{:S(2)}) %collective-permute-start.21) | collective-permute-done | bytes 524320 | tf_op jit(solution)/shard_map/ppermute | solution.py:21
  386.5 16.0 %collective-permute-done.23 = bf16[64,4096]{1,0:T(8,128)(2,1)S(1)} collective-permute-done((bf16[64,4096]{1,0:T(8,128)(2,1)S(1)}, bf16[64,4096]{1,0:T(8,128)(2,1)S(1)}, u32[]{:S(2)}, u32[]{:S(2)}) %collective-permute-start.23) | collective-permute-done | bytes 524320 | tf_op jit(solution)/shard_map/ppermute | solution.py:21
  404.8 10.5 %collective-permute-done.24 = bf16[64,4096]{1,0:T(8,128)(2,1)S(1)} collective-permute-done((bf16[64,4096]{1,0:T(8,128)(2,1)S(1)}, bf16[64,4096]{1,0:T(8,128)(2,1)S(1)}, u32[]{:S(2)}, u32[]{:S(2)}) %collective-permute-start.24) | collective-permute-done | bytes 524320 | tf_op jit(solution)/shard_map/ppermute | solution.py:21
  415.4 5.5 %collective-permute-done.26 = bf16[64,4096]{1,0:T(8,128)(2,1)S(1)} collective-permute-done((bf16[64,4096]{1,0:T(8,128)(2,1)S(1)}, bf16[64,4096]{1,0:T(8,128)(2,1)S(1)}, u32[]{:S(2)}, u32[]{:S(2)}) %collective-permute-start.26) | collective-permute-done | bytes 524320 | tf_op jit(solution)/shard_map/ppermute | solution.py:21
  420.9 11.3 %fusion.2 = f32[2,512,896]{1,2,0:T(8,128)S(1)} fusion(bf16[2,4096,896]{1,2,0:T(8,128)(2,1)} %constant_dynamic-update-slice_fusion.24, bf16[512,4096]{1,0:T(8,128)(2,1)S(1)} %constant_dynamic-update-slice_fusion), kind=kOutput, calls=%fused_computation.6 | convolution fusion | flops 7516192768 | bytes 22544384 | tf_op jit(solution)/shard_map/td,kdf->ktf/dot_general | solution.py:182
  432.2 8.1 %convolution_convert_fusion = bf16[512,4096]{1,0:T(8,128)(2,1)S(1)} fusion(bf16[896,4096]{1,0:T(8,128)(2,1)} %constant_dynamic-update-slice_fusion.8, f32[2,512,896]{1,2,0:T(8,128)S(1)} %fusion.2), kind=kOutput, calls=%fused_computation | convolution fusion | flops 3762946048 | bytes 15204352 | tf_op jit(solution)/shard_map/dot_general | solution.py:184
  441.2 39.3 %collective-permute-done.42 = bf16[4,64,4096]{2,1,0:T(8,128)(2,1)S(1)} collective-permute-done((bf16[4,64,4096]{2,1,0:T(8,128)(2,1)S(1)}, bf16[4,64,4096]{2,1,0:T(8,128)(2,1)S(1)}, u32[]{:S(2)}, u32[]{:S(2)}) %collective-permute-start.42) | collective-permute-done | bytes 2097184 | tf_op jit(solution)/shard_map/ppermute | solution.py:21
  481.5 8.5 %collective-permute-start.43 = (bf16[64,4096]{1,0:T(8,128)(2,1)S(1)}, bf16[64,4096]{1,0:T(8,128)(2,1)S(1)}, u32[]{:S(2)}, u32[]{:S(2)}) collective-permute-start(bf16[64,4096]{1,0:T(8,128)(2,1)S(1)} %get-tuple-element.12), channel_id=1, source_target_pairs={{0,1},{1,0},{2,3},{3,2},{4,5},{5,4},{6,7},{7,6},{8,9},{9,8},{10,11... | collective-permute-start | bytes 1572872 | tf_op jit(solution)/shard_map/ppermute | solution.py:21
  492.6 14.7 %collective-permute-done.43 = bf16[64,4096]{1,0:T(8,128)(2,1)S(1)} collective-permute-done((bf16[64,4096]{1,0:T(8,128)(2,1)S(1)}, bf16[64,4096]{1,0:T(8,128)(2,1)S(1)}, u32[]{:S(2)}, u32[]{:S(2)}) %collective-permute-start.43) | collective-permute-done | bytes 524320 | tf_op jit(solution)/shard_map/ppermute | solution.py:21
  507.2 21.1 %collective-permute-done.44 = bf16[64,4096]{1,0:T(8,128)(2,1)S(1)} collective-permute-done((bf16[64,4096]{1,0:T(8,128)(2,1)S(1)}, bf16[64,4096]{1,0:T(8,128)(2,1)S(1)}, u32[]{:S(2)}, u32[]{:S(2)}) %collective-permute-start.44) | collective-permute-done | bytes 524320 | tf_op jit(solution)/shard_map/ppermute | solution.py:21
  534.8 6.9 %all-to-all-done.2 = bf16[64,4,1024]{2,0,1:T(8,128)(2,1)S(1)} async-done(((bf16[64,4,1024]{2,0,1:T(8,128)(2,1)}), bf16[64,4,1024]{2,0,1:T(8,128)(2,1)S(1)}, u32[]{:S(2)}, u32[]{:S(2)}) %all-to-all-start.2) | async-done | bytes 524320 | tf_op jit(solution)/shard_map/all_to_all | solution.py:193
  (216 shorter events, 164.9 us)
Async XLA Ops:
  7.2 317.9 %all-gather.2.cloned.1.call-start = ((), (), s32[]{:S(2)}) async-start(), calls=%async_computation.3 | async-start | bytes 5242880 | tf_op jit(solution)/shard_map/all_gather | solution.py:108
  17.4 46.2 %collective-permute-start.34 = (bf16[896,256]{1,0:T(8,128)(2,1)S(1)}, bf16[896,256]{1,0:T(8,128)(2,1)S(1)}, u32[]{:S(2)}, u32[]{:S(2)}) collective-permute-start(bf16[896,256]{1,0:T(8,128)(2,1)S(1)} %get-tuple-element.19), channel_id=1, source_target_pairs={{0,2},{1,3},{2,0},{3,1},{4,6},{5,7},{6,4},{7,5},{8,10},{9,11},{10,... | collective-permute-start | bytes 1376264 | tf_op jit(solution)/shard_map/ppermute | solution.py:21
  19.9 56.6 %collective-permute-start.38 = (bf16[896,256]{1,0:T(8,128)(2,1)S(1)}, bf16[896,256]{1,0:T(8,128)(2,1)}, u32[]{:S(2)}, u32[]{:S(2)}) collective-permute-start(bf16[896,256]{1,0:T(8,128)(2,1)S(1)} %get-tuple-element.15), channel_id=1, source_target_pairs={{0,3},{1,2},{2,1},{3,0},{4,7},{5,6},{6,5},{7,4},{8,11},{9,10},{10,... | collective-permute-start | bytes 1376264 | tf_op jit(solution)/shard_map/ppermute | solution.py:21
  21.8 66.4 %collective-permute-start.5 = (bf16[2,256,896]{2,1,0:T(8,128)(2,1)S(1)}, bf16[2,256,896]{2,1,0:T(8,128)(2,1)}, u32[]{:S(2)}, u32[]{:S(2)}) collective-permute-start(bf16[2,256,896]{2,1,0:T(8,128)(2,1)S(1)} %get-tuple-element.10), channel_id=1, source_target_pairs={{0,4},{4,0},{8,12},{12,8},{1,5},{5,1},{9,13},{13,9},{2,6},{6,2},{1... | collective-permute-start | bytes 2752520 | tf_op jit(solution)/shard_map/ppermute | solution.py:21
  27.0 61.7 %collective-permute-start.6 = (bf16[2,256,896]{2,1,0:T(8,128)(2,1)S(1)}, bf16[2,256,896]{2,1,0:T(8,128)(2,1)S(1)}, u32[]{:S(2)}, u32[]{:S(2)}) collective-permute-start(bf16[2,256,896]{2,1,0:T(8,128)(2,1)S(1)} %get-tuple-element.10), channel_id=1, source_target_pairs={{0,8},{4,12},{8,0},{12,4},{1,9},{5,13},{9,1},{13,5},{2,10},{6,14},... | collective-permute-start | bytes 2752520 | tf_op jit(solution)/shard_map/ppermute | solution.py:21
  46.2 83.6 %collective-permute-start.8 = (bf16[2,256,896]{2,1,0:T(8,128)(2,1)}, bf16[2,256,896]{2,1,0:T(8,128)(2,1)S(1)}, u32[]{:S(2)}, u32[]{:S(2)}) collective-permute-start(bf16[2,256,896]{2,1,0:T(8,128)(2,1)} %get-tuple-element.9), channel_id=1, source_target_pairs={{0,1},{1,0},{2,3},{3,2},{4,5},{5,4},{6,7},{7,6},{8,9},{9,8},{10,11... | collective-permute-start | bytes 2752520 | tf_op jit(solution)/shard_map/ppermute | solution.py:21
  63.5 123.7 %collective-permute-start.12 = (bf16[2,256,896]{2,1,0:T(8,128)(2,1)}, bf16[2,256,896]{2,1,0:T(8,128)(2,1)}, u32[]{:S(2)}, u32[]{:S(2)}) collective-permute-start(bf16[2,256,896]{2,1,0:T(8,128)(2,1)} %get-tuple-element.11), channel_id=1, source_target_pairs={{0,2},{1,3},{2,0},{3,1},{4,6},{5,7},{6,4},{7,5},{8,10},{9,11},{10,... | collective-permute-start | bytes 2752520 | tf_op jit(solution)/shard_map/ppermute | solution.py:21
  76.5 110.7 %collective-permute-start.16 = (bf16[2,256,896]{2,1,0:T(8,128)(2,1)}, bf16[2,256,896]{2,1,0:T(8,128)(2,1)}, u32[]{:S(2)}, u32[]{:S(2)}) collective-permute-start(bf16[2,256,896]{2,1,0:T(8,128)(2,1)} %get-tuple-element.8), channel_id=1, source_target_pairs={{0,3},{1,2},{2,1},{3,0},{4,7},{5,6},{6,5},{7,4},{8,11},{9,10},{10,... | collective-permute-start | bytes 2752520 | tf_op jit(solution)/shard_map/ppermute | solution.py:21
  83.0 118.3 %all-to-all-start = ((bf16[8,64,768]{2,1,0:T(8,128)(2,1)}), bf16[8,64,768]{2,1,0:T(8,128)(2,1)S(1)}, u32[]{:S(2)}, u32[]{:S(2)}) async-start(bf16[8,64,768]{2,1,0:T(8,128)(2,1)} %bitcast.3), calls=%async_computation | async-start | bytes 1572864 | tf_op jit(solution)/shard_map/all_to_all | solution.py:124
  88.2 109.9 %collective-permute-start.31 = (bf16[896,256]{1,0:T(8,128)(2,1)}, bf16[896,256]{1,0:T(8,128)(2,1)}, u32[]{:S(2)}, u32[]{:S(2)}) collective-permute-start(bf16[896,256]{1,0:T(8,128)(2,1)} %copy-done.14), channel_id=1, source_target_pairs={{0,4},{4,0},{8,12},{12,8},{1,5},{5,1},{9,13},{13,9},{2,6},{6,2},{1... | collective-permute-start | bytes 1376264 | tf_op jit(solution)/shard_map/ppermute | solution.py:21
  88.7 113.4 %collective-permute-start.32 = (bf16[896,256]{1,0:T(8,128)(2,1)}, bf16[896,256]{1,0:T(8,128)(2,1)}, u32[]{:S(2)}, u32[]{:S(2)}) collective-permute-start(bf16[896,256]{1,0:T(8,128)(2,1)} %copy-done.14), channel_id=1, source_target_pairs={{0,8},{4,12},{8,0},{12,4},{1,9},{5,13},{9,1},{13,5},{2,10},{6,14},... | collective-permute-start | bytes 1376264 | tf_op jit(solution)/shard_map/ppermute | solution.py:21
  129.8 68.1 %collective-permute-start.29 = (bf16[896,256]{1,0:T(8,128)(2,1)}, bf16[896,256]{1,0:T(8,128)(2,1)}, u32[]{:S(2)}, u32[]{:S(2)}) collective-permute-start(bf16[896,256]{1,0:T(8,128)(2,1)} %copy-done.16), channel_id=1, source_target_pairs={{0,4},{4,0},{8,12},{12,8},{1,5},{5,1},{9,13},{13,9},{2,6},{6,2},{1... | collective-permute-start | bytes 1376264 | tf_op jit(solution)/shard_map/ppermute | solution.py:21
  187.2 38.3 %collective-permute-start.35 = (bf16[896,256]{1,0:T(8,128)(2,1)}, bf16[896,256]{1,0:T(8,128)(2,1)}, u32[]{:S(2)}, u32[]{:S(2)}) collective-permute-start(bf16[896,256]{1,0:T(8,128)(2,1)} %copy-done.13), channel_id=1, source_target_pairs={{0,4},{4,0},{8,12},{12,8},{1,5},{5,1},{9,13},{13,9},{2,6},{6,2},{1... | collective-permute-start | bytes 1376264 | tf_op jit(solution)/shard_map/ppermute | solution.py:21
  187.2 38.3 %collective-permute-start.36 = (bf16[896,256]{1,0:T(8,128)(2,1)}, bf16[896,256]{1,0:T(8,128)(2,1)}, u32[]{:S(2)}, u32[]{:S(2)}) collective-permute-start(bf16[896,256]{1,0:T(8,128)(2,1)} %copy-done.13), channel_id=1, source_target_pairs={{0,8},{4,12},{8,0},{12,4},{1,9},{5,13},{9,1},{13,5},{2,10},{6,14},... | collective-permute-start | bytes 1376264 | tf_op jit(solution)/shard_map/ppermute | solution.py:21
  257.9 58.1 %collective-permute-start.13 = (bf16[2,256,896]{2,1,0:T(8,128)(2,1)}, bf16[2,256,896]{2,1,0:T(8,128)(2,1)}, u32[]{:S(2)}, u32[]{:S(2)}) collective-permute-start(bf16[2,256,896]{2,1,0:T(8,128)(2,1)} %collective-permute-done.12), channel_id=1, source_target_pairs={{0,4},{4,0},{8,12},{12,8},{1,5},{5,1},{9,13},{13,9},{2,6},{6,2},{1... | collective-permute-start | bytes 2752520 | tf_op jit(solution)/shard_map/ppermute | solution.py:21
  258.5 60.2 %collective-permute-start.17 = (bf16[2,256,896]{2,1,0:T(8,128)(2,1)}, bf16[2,256,896]{2,1,0:T(8,128)(2,1)}, u32[]{:S(2)}, u32[]{:S(2)}) collective-permute-start(bf16[2,256,896]{2,1,0:T(8,128)(2,1)} %collective-permute-done.16), channel_id=1, source_target_pairs={{0,4},{4,0},{8,12},{12,8},{1,5},{5,1},{9,13},{13,9},{2,6},{6,2},{1... | collective-permute-start | bytes 2752520 | tf_op jit(solution)/shard_map/ppermute | solution.py:21
  258.6 55.1 %collective-permute-start.18 = (bf16[2,256,896]{2,1,0:T(8,128)(2,1)}, bf16[2,256,896]{2,1,0:T(8,128)(2,1)}, u32[]{:S(2)}, u32[]{:S(2)}) collective-permute-start(bf16[2,256,896]{2,1,0:T(8,128)(2,1)} %collective-permute-done.16), channel_id=1, source_target_pairs={{0,8},{4,12},{8,0},{12,4},{1,9},{5,13},{9,1},{13,5},{2,10},{6,14},... | collective-permute-start | bytes 2752520 | tf_op jit(solution)/shard_map/ppermute | solution.py:21
  275.2 49.0 %collective-permute-start.3 = (bf16[512,512]{1,0:T(8,128)(2,1)}, bf16[512,512]{1,0:T(8,128)(2,1)S(1)}, u32[]{:S(2)}, u32[]{:S(2)}) collective-permute-start(bf16[512,512]{1,0:T(8,128)(2,1)} %collective-permute-done.2), channel_id=1, source_target_pairs={{0,4},{4,0},{8,12},{12,8},{1,5},{5,1},{9,13},{13,9},{2,6},{6,2},{1... | collective-permute-start | bytes 1572872 | tf_op jit(solution)/shard_map/ppermute | solution.py:21
  295.0 40.0 %collective-permute-start.11 = (bf16[2,256,896]{2,1,0:T(8,128)(2,1)}, bf16[2,256,896]{2,1,0:T(8,128)(2,1)}, u32[]{:S(2)}, u32[]{:S(2)}) collective-permute-start(bf16[2,256,896]{2,1,0:T(8,128)(2,1)} %copy-done.12), channel_id=1, source_target_pairs={{0,4},{4,0},{8,12},{12,8},{1,5},{5,1},{9,13},{13,9},{2,6},{6,2},{1... | collective-permute-start | bytes 2752520 | tf_op jit(solution)/shard_map/ppermute | solution.py:21
  360.8 43.8 %collective-permute-start.20 = (bf16[64,4096]{1,0:T(8,128)(2,1)S(1)}, bf16[64,4096]{1,0:T(8,128)(2,1)S(1)}, u32[]{:S(2)}, u32[]{:S(2)}) collective-permute-start(bf16[64,4096]{1,0:T(8,128)(2,1)S(1)} %get-tuple-element.3), channel_id=1, source_target_pairs={{0,16},{16,0},{1,17},{17,1},{2,18},{18,2},{3,19},{19,3},{4,20},{20... | collective-permute-start | bytes 1572872 | tf_op jit(solution)/shard_map/ppermute | solution.py:21
  364.3 38.2 %collective-permute-start.23 = (bf16[64,4096]{1,0:T(8,128)(2,1)S(1)}, bf16[64,4096]{1,0:T(8,128)(2,1)S(1)}, u32[]{:S(2)}, u32[]{:S(2)}) collective-permute-start(bf16[64,4096]{1,0:T(8,128)(2,1)S(1)} %get-tuple-element.3), channel_id=1, source_target_pairs={{0,2},{1,3},{2,0},{3,1},{4,6},{5,7},{6,4},{7,5},{8,10},{9,11},{10,... | collective-permute-start | bytes 1572872 | tf_op jit(solution)/shard_map/ppermute | solution.py:21
  365.7 37.4 %collective-permute-start.25 = (bf16[64,4096]{1,0:T(8,128)(2,1)S(1)}, bf16[64,4096]{1,0:T(8,128)(2,1)S(1)}, u32[]{:S(2)}, u32[]{:S(2)}) collective-permute-start(bf16[64,4096]{1,0:T(8,128)(2,1)S(1)} %get-tuple-element.3), channel_id=1, source_target_pairs={{0,3},{1,2},{2,1},{3,0},{4,7},{5,6},{6,5},{7,4},{8,11},{9,10},{10,... | collective-permute-start | bytes 1572872 | tf_op jit(solution)/shard_map/ppermute | solution.py:21
  440.6 40.0 %collective-permute-start.42 = (bf16[4,64,4096]{2,1,0:T(8,128)(2,1)S(1)}, bf16[4,64,4096]{2,1,0:T(8,128)(2,1)S(1)}, u32[]{:S(2)}, u32[]{:S(2)}) collective-permute-start(bf16[4,64,4096]{2,1,0:T(8,128)(2,1)S(1)} %slice_bitcast_fusion), channel_id=1, source_target_pairs={{0,16},{16,0},{1,17},{17,1},{2,18},{18,2},{3,19},{19,3},{4,20},{20... | collective-permute-start | bytes 6291464 | tf_op jit(solution)/shard_map/ppermute | solution.py:21
  490.1 38.2 %collective-permute-start.44 = (bf16[64,4096]{1,0:T(8,128)(2,1)S(1)}, bf16[64,4096]{1,0:T(8,128)(2,1)S(1)}, u32[]{:S(2)}, u32[]{:S(2)}) collective-permute-start(bf16[64,4096]{1,0:T(8,128)(2,1)S(1)} %get-tuple-element.14), channel_id=1, source_target_pairs={{0,2},{1,3},{2,0},{3,1},{4,6},{5,7},{6,4},{7,5},{8,10},{9,11},{10,... | collective-permute-start | bytes 1572872 | tf_op jit(solution)/shard_map/ppermute | solution.py:21
  (48 other events, 1264.3 us)
Sparse Core Ops, SparseCore 0:
  9.6 178.6 all-gather.1

commit v2 on v1

--- a/solution.py
+++ b/solution.py
@@ -14,6 +14,7 @@
 GROUP = QUERY_HEADS // KEY_VALUE_HEADS
 WINDOW_PER_DOC = 4
 QUERY_TILE = 128
+PARTS = 2
 
 
 def swap(array, axis, distance):
@@ -82,6 +83,11 @@
     )(starts, packed, packed, halo)
 
 
+def blocks_over_inner(block):
+    across = swap(block, "inner", 2)
+    return [block, swap(block, "inner", 1), across, swap(across, "inner", 1)]
+
+
 def earlier_planes(kv, hops):
     count = lax.axis_size("outer")
     moved = [lax.ppermute(kv, "outer", [(s, s + d) for s in range(count - d)]) for d in range(hops, 0, -1)]
@@ -126,8 +132,7 @@
         halo = earlier_planes(packed[:, q_cols:], hops)
         starts = document_starts(bounds, outer * plane_rows, plane_rows)
         own_context = attention(packed, halo, starts, reach)
-        across = swap(own_context, "inner", 2)
-        parts = [own_context, swap(own_context, "inner", 1), across, swap(across, "inner", 1)]
+        parts = blocks_over_inner(own_context)
         plane_context = jnp.zeros((plane_rows, inner_count * q_cols), jnp.bfloat16)
         for d, part in enumerate(parts):
             plane_context = lax.dynamic_update_slice(plane_context, part, (0, (inner ^ d) * q_cols))
@@ -150,47 +155,72 @@
         projected = projected + swap(sent, "head", e).astype(jnp.float32)
     own_resid = lax.dynamic_slice_in_dim(resid, head * half, half, 0)
     hidden_part = (own_resid.astype(jnp.float32) + projected).astype(jnp.bfloat16)
-    hidden_state = lax.all_to_all(hidden_part, "inner", split_axis=0, concat_axis=1, tiled=True)
-    gain = lax.all_gather(norm_gain, "inner", axis=0, tiled=True)
-    state_wide = hidden_state.astype(jnp.float32)
-    mean_square = jnp.mean(state_wide * state_wide, axis=1, keepdims=True)
-    normed = (state_wide * lax.rsqrt(mean_square + 1e-05) * gain[None, :]).astype(jnp.bfloat16)
-
+
+    own_rows = half // inner_count
+    state = []
+    for a in range(inner_count):
+        block = lax.dynamic_slice_in_dim(hidden_part, (inner ^ a) * own_rows, own_rows, 0)
+        state.append(swap(block, "inner", a) if a else block)
+    state = jnp.concatenate(state, axis=1).astype(jnp.float32)
+    mean_square = jnp.mean(state * state, axis=1, keepdims=True)
+    normed = (state * lax.rsqrt(mean_square + 1e-05)).astype(jnp.bfloat16)
+    part_rows = feature_rows // PARTS
+    normed = normed.reshape(own_rows, inner_count, outer_count, PARTS, part_rows)
+    normed = jnp.transpose(normed, (0, 3, 1, 2, 4)).reshape(own_rows, D)
     tokens = []
     for d in range(outer_count):
         block = swap(normed, "outer", d) if d else normed
         tokens += [block] + [swap(block, "head", e) for e in range(1, head_count)]
     tokens = jnp.concatenate(tokens, axis=0)
 
-    gate_up_weights = jnp.zeros((2, D, hidden_cols), jnp.bfloat16)
-    down_weights = jnp.zeros((hidden_cols, D), jnp.bfloat16)
-    for d in range(outer_count):
-        piece = lax.dynamic_slice_in_dim(w_gate_up, (outer ^ d) * hidden_cols, hidden_cols, 2)
-        piece = swap(piece, "outer", d) if d else piece
-        across = swap(piece, "inner", 2)
-        for e, part in enumerate([piece, swap(piece, "inner", 1), across, swap(across, "inner", 1)]):
-            at = ((inner ^ e) * outer_count + (outer ^ d)) * feature_rows
-            gate_up_weights = lax.dynamic_update_slice(gate_up_weights, part, (0, at, 0))
-    for d in range(outer_count):
-        piece = lax.dynamic_slice_in_dim(w_down, (outer ^ d) * hidden_cols, hidden_cols, 0)
-        piece = swap(piece, "outer", d) if d else piece
-        across = swap(piece, "inner", 2)
-        for e, part in enumerate([piece, swap(piece, "inner", 1), across, swap(across, "inner", 1)]):
-            at = ((inner ^ e) * outer_count + (outer ^ d)) * feature_rows
-            down_weights = lax.dynamic_update_slice(down_weights, part, (0, at))
-
-    gate_up = jnp.einsum("td,kdf->ktf", tokens, gate_up_weights, preferred_element_type=jnp.float32)
-    activated = (jax.nn.silu(gate_up[0]) * gate_up[1]).astype(jnp.bfloat16)
-    down = jnp.dot(activated, down_weights, preferred_element_type=jnp.float32).astype(jnp.bfloat16)
-    down = down.reshape(outer_count, head_count, -1, D)
-    paired = down[:, 0].astype(jnp.float32)
-    for e in range(1, head_count):
-        paired = paired + swap(down[:, e], "head", e).astype(jnp.float32)
-    down_sum = paired[0]
-    for d in range(1, outer_count):
-        down_sum = down_sum + swap(paired[d].astype(jnp.bfloat16), "outer", d).astype(jnp.float32)
-    layer_rows = (state_wide + down_sum).astype(jnp.bfloat16)
-    layer_out = lax.all_to_all(layer_rows, "inner", split_axis=1, concat_axis=0, tiled=True)
+    own_gain = lax.dynamic_slice_in_dim(norm_gain, outer * feature_rows, feature_rows, 0)
+    streams = []
+    latest = context
+    for part in range(PARTS):
+        rows_of = slice(part * part_rows, (part + 1) * part_rows)
+        for which in range(2):
+            piece = (w_gate_up[which, rows_of].astype(jnp.float32) * own_gain[rows_of, None]).astype(jnp.bfloat16)
+            piece = jnp.transpose(piece.reshape(part_rows, outer_count, hidden_cols), (1, 0, 2))
+            piece = lax.optimization_barrier((piece, latest))[0]
+            latest = lax.all_to_all(piece, "outer", split_axis=0, concat_axis=0, tiled=True)
+            streams.append(blocks_over_inner(latest.reshape(outer_count * part_rows, hidden_cols)))
+    down_streams = []
+    for part in range(PARTS):
+        piece = w_down[:, part * part_rows : (part + 1) * part_rows].reshape(outer_count, hidden_cols, part_rows)
+        piece = lax.optimization_barrier((piece, latest))[0]
+        latest = lax.all_to_all(piece, "outer", split_axis=0, concat_axis=0, tiled=True)
+        columns = jnp.transpose(latest, (1, 0, 2)).reshape(hidden_cols, outer_count * part_rows)
+        down_streams.append(blocks_over_inner(columns))
+
+    depth = outer_count * part_rows
+    gate, up = 0.0, 0.0
+    for part in range(PARTS):
+        for a in range(inner_count):
+            at = (part * inner_count + a) * depth
+            near = tokens[:, at : at + depth]
+            gate = gate + jnp.dot(near, streams[2 * part][a], preferred_element_type=jnp.float32)
+            up = up + jnp.dot(near, streams[2 * part + 1][a], preferred_element_type=jnp.float32)
+    activated = (jax.nn.silu(gate) * up).astype(jnp.bfloat16)
+
+    down_sums = []
+    for part in range(PARTS):
+        down = [jnp.dot(activated, block, preferred_element_type=jnp.float32) for block in down_streams[part]]
+        down = jnp.concatenate(down, axis=1).astype(jnp.bfloat16)
+        down = down.reshape(outer_count, head_count, own_rows, D // PARTS)
+        paired = down[:, 0].astype(jnp.float32)
+        for e in range(1, head_count):
+            paired = paired + swap(down[:, e], "head", e).astype(jnp.float32)
+        down_sum = paired[0]
+        for d in range(1, outer_count):
+            down_sum = down_sum + swap(paired[d].astype(jnp.bfloat16), "outer", d).astype(jnp.float32)
+        down_sums.append(down_sum.reshape(own_rows, inner_count, outer_count, 1, part_rows))
+    down_sum = jnp.concatenate(down_sums, axis=3).reshape(own_rows, D)
+    layer_rows = (state + down_sum).astype(jnp.bfloat16)
+    layer_out = jnp.zeros((half, D // inner_count), jnp.bfloat16)
+    for a in range(inner_count):
+        block = layer_rows[:, a * (D // inner_count) : (a + 1) * (D // inner_count)]
+        block = swap(block, "inner", a) if a else block
+        layer_out = lax.dynamic_update_slice(layer_out, block, ((inner ^ a) * own_rows, 0))
     return (context, layer_out)
 
 

time: 555 us -> 495 us (0.89)
  waiting for transfers between devices: 307 us -> 226 us
  local copies, waits for them, and re-layouts: 110 us -> 52.2 us
  matrix products: 24.7 us -> 76.9 us
  starting transfers between devices: 76.7 us -> 103 us
  other arithmetic: 5.3 us -> 12.2 us
    ppermute x45 -> x43, waiting for transfers between devices: 298 us -> 144 us  [swap(): return lax.ppermute(array, axis, [(s, s ^ distance) for s in range(count)])]
    dot_general x2 -> x24, matrix products: 19.4 us -> 71.7 us  [the longest x8 32.6 us: per_device(): jnp.dot(near, streams[2 * part + 1][a], preferred_element_type=jnp.float32)]
    all_to_all x2 -> x6, starting transfers between devices: 7.3 us -> 56.3 us  [per_device(): lax.all_to_all(piece, 'outer', split_axis=0, concat_axis=0, tiled=True)]
    all_to_all x2 -> x6, waiting for transfers between devices: 8.77 us -> 57.8 us  [per_device(): lax.all_to_all(piece, 'outer', split_axis=0, concat_axis=0, tiled=True)]
    dynamic_update_slice x31 -> x3, local copies, waits for them, and re-layouts: 47.9 us -> 0.04 us  [per_device(): lax.dynamic_update_slice(layer_out, block, ((inner ^ a) * own_rows, 0))]
    ppermute x15 -> x0, local copies, waits for them, and re-layouts: 29.6 us -> none  [swap(): return lax.ppermute(array, axis, [(s, s ^ distance) for s in range(count)])]
    ppermute x1, starting transfers between devices: 21.6 us -> 3.5 us  [earlier_planes(): lax.ppermute(kv, 'outer', [(s, s + d) for s in range(count - d)])]
    unnamed x51, local copies, waits for them, and re-layouts: 1.98 us -> 19.7 us
  transfers between devices with their start and end apart: 50 -> 52, of which waited for: 19 -> 22; matrix products, arithmetic and copies ran while one was open for 21% -> 27% of each run, Pallas kernels for 1% -> 1%
where the time goes in v2:
time: 495 us; the launch traced here: 490 us
  waiting for transfers between devices  226 us (46%)
  starting transfers between devices  103 us (21%)
  matrix products  76.9 us (16%)
  local copies, waits for them, and re-layouts  52.2 us (11%)
  between operations  14.7 us (3%)
  other arithmetic  12.2 us (2%)
  Pallas kernels  5.8 us (1%)
    ppermute x43, waiting for transfers between devices, swap(): return lax.ppermute(array, axis, [(s, s ^ distance) for s in range(count)])  144 us
    all_to_all x6, waiting for transfers between devices, per_device(): lax.all_to_all(piece, 'outer', split_axis=0, concat_axis=0, tiled=True)  57.8 us
    all_to_all x6, starting transfers between devices, per_device(): lax.all_to_all(piece, 'outer', split_axis=0, concat_axis=0, tiled=True)  56.3 us
    ppermute x43, starting transfers between devices, swap(): return lax.ppermute(array, axis, [(s, s ^ distance) for s in range(count)])  37.6 us
    dot_general x8, matrix products, per_device(): jnp.dot(near, streams[2 * part + 1][a], preferred_element_type=jnp.float32)  32.6 us
    dot_general x8, matrix products, per_device(): jnp.dot(near, streams[2 * part][a], preferred_element_type=jnp.float32)  24.4 us
    unnamed x51, local copies, waits for them, and re-layouts  19.7 us
    dot_general x8, matrix products, per_device(): jnp.dot(activated, block, preferred_element_type=jnp.float32)  14.7 us
  transfers between devices with their start and end apart: 52, of which 22 were waited for; matrix products, arithmetic and copies ran while one was open for 27% of the time, Pallas kernels for 1%

profile of v2, /device:TPU:0, one launch (start us, length us, event | category | flops | bytes accessed | tf_op | source)
XLA Modules:
  0.0 490.4 jit_solution(4366556620901745653)
XLA Ops:
  11.0 5.2 %all-to-all-start = ((bf16[8,64,768]{2,1,0:T(8,128)(2,1)}), bf16[8,64,768]{2,1,0:T(8,128)(2,1)S(1)}, u32[]{:S(2)}, u32[]{:S(2)}) async-start(bf16[8,64,768]{2,1,0:T(8,128)(2,1)} %bitcast.3), calls=%async_computation | async-start | bytes 1572864 | tf_op jit(solution)/shard_map/all_to_all | solution.py:130
  16.5 11.9 %all-to-all-done = bf16[8,64,768]{2,1,0:T(8,128)(2,1)S(1)} async-done(((bf16[8,64,768]{2,1,0:T(8,128)(2,1)}), bf16[8,64,768]{2,1,0:T(8,128)(2,1)S(1)}, u32[]{:S(2)}, u32[]{:S(2)}) %all-to-all-start) | async-done | bytes 786464 | tf_op jit(solution)/shard_map/all_to_all | solution.py:130
  32.1 11.6 %collective-permute-done.halo_ref = bf16[512,256]{1,0:T(8,128)(2,1)S(1)} collective-permute-done((bf16[512,256]{1,0:T(8,128)(2,1)S(1)}, bf16[512,256]{1,0:T(8,128)(2,1)S(1)}, u32[]{:S(2)}, u32[]{:S(2)}) %collective-permute-start) | collective-permute-done | bytes 262176 | tf_op jit(solution)/shard_map/ppermute | solution.py:93
  43.7 5.8 %shard_map.104 = bf16[512,512]{1,0:T(8,128)(2,1)S(1)} custom-call(s32[512,1]{1,0:T(8,128)S(1)} %copy.69.starts_ref, bf16[512,768]{1,0:T(8,128)(2,1)S(1)} %bitcast.140, bf16[512,768]{1,0:T(8,128)(2,1)S(1)} %bitcast.141, bf16[512,256]{1,0:T(8,128)(2,1)S(1)} %collective-permute-done.halo_ref), custom_call_target="tpu_custom_call" | custom-call | flops 671088640 | bytes 1048576 | tf_op jit(solution)/shard_map/pallas_call | solution.py:62
  70.4 17.1 %all-to-all-start.1 = ((bf16[4,128,896]{1,2,0:T(8,128)(2,1)}), bf16[4,128,896]{1,2,0:T(8,128)(2,1)S(1)}, u32[]{:S(2)}, u32[]{:S(2)}) async-start(bf16[4,128,896]{1,2,0:T(8,128)(2,1)} %get-tuple-element.8), calls=%async_computation.1 | async-start | bytes 1835008 | tf_op jit(solution)/shard_map/all_to_all | solution.py:185
  87.6 21.6 %all-to-all-done.1 = bf16[4,128,896]{1,2,0:T(8,128)(2,1)S(1)} async-done(((bf16[4,128,896]{1,2,0:T(8,128)(2,1)}), bf16[4,128,896]{1,2,0:T(8,128)(2,1)S(1)}, u32[]{:S(2)}, u32[]{:S(2)}) %all-to-all-start.1) | async-done | bytes 917536 | tf_op jit(solution)/shard_map/all_to_all | solution.py:185
  110.1 10.4 %all-to-all-start.2 = ((bf16[4,128,896]{1,2,0:T(8,128)(2,1)}), bf16[4,128,896]{1,2,0:T(8,128)(2,1)S(1)}, u32[]{:S(2)}, u32[]{:S(2)}) async-start(bf16[4,128,896]{1,2,0:T(8,128)(2,1)} %get-tuple-element.9), calls=%async_computation.2 | async-start | bytes 1835008 | tf_op jit(solution)/shard_map/all_to_all | solution.py:185
  120.5 5.2 %convolution_convert_fusion = bf16[512,1024]{1,0:T(8,128)(2,1)S(1)} fusion(bf16[512,2048]{1,0:T(8,128)(2,1)} %copy-done.5, bf16[2048,1024]{1,0:T(8,128)(2,1)} %all-gather.2.cloned.1.call-done), kind=kOutput, calls=%fused_computation.13 | convolution fusion | flops 2148007936 | bytes 7340032 | tf_op jit(solution)/shard_map/dot_general | solution.py:151
  131.7 9.4 %collective-permute-done.4 = bf16[256,1024]{1,0:T(8,128)(2,1)S(1)} collective-permute-done((bf16[256,1024]{1,0:T(8,128)(2,1)}, bf16[256,1024]{1,0:T(8,128)(2,1)S(1)}, u32[]{:S(2)}, u32[]{:S(2)}) %collective-permute-start.4) | collective-permute-done | bytes 524320 | tf_op jit(solution)/shard_map/ppermute | solution.py:22
  149.7 4.8 all-to-all-start.3
  165.4 6.3 %collective-permute-done.16 = bf16[512,896]{1,0:T(8,128)(2,1)} collective-permute-done((bf16[512,896]{1,0:T(8,128)(2,1)}, bf16[512,896]{1,0:T(8,128)(2,1)}, u32[]{:S(2)}, u32[]{:S(2)}) %collective-permute-start.16) | collective-permute-done | bytes 917536 | tf_op jit(solution)/shard_map/ppermute | solution.py:22
  191.6 24.4 %all-to-all-done.4 = bf16[4,128,896]{1,2,0:T(8,128)(2,1)S(1)} async-done(((bf16[4,128,896]{1,2,0:T(8,128)(2,1)}), bf16[4,128,896]{1,2,0:T(8,128)(2,1)S(1)}, u32[]{:S(2)}, u32[]{:S(2)}) %all-to-all-start.4) | async-done | bytes 917536 | tf_op jit(solution)/shard_map/all_to_all | solution.py:185
  220.8 21.9 %collective-permute-done.11 = bf16[64,4096]{1,0:T(8,128)(2,1)S(1)} collective-permute-done((bf16[64,4096]{1,0:T(8,128)(2,1)S(1)}, bf16[64,4096]{1,0:T(8,128)(2,1)S(1)}, u32[]{:S(2)}, u32[]{:S(2)}) %collective-permute-start.11) | collective-permute-done | bytes 524320 | tf_op jit(solution)/shard_map/ppermute | solution.py:22
  249.2 4.6 collective-permute-done.13
  257.4 10.8 %collective-permute-done.14 = bf16[64,4096]{1,0:T(8,128)(2,1)S(1)} collective-permute-done((bf16[64,4096]{1,0:T(8,128)(2,1)S(1)}, bf16[64,4096]{1,0:T(8,128)(2,1)S(1)}, u32[]{:S(2)}, u32[]{:S(2)}) %collective-permute-start.14) | collective-permute-done | bytes 524320 | tf_op jit(solution)/shard_map/ppermute | solution.py:22
  309.5 13.4 %collective-permute-done.25 = bf16[512,896]{1,0:T(8,128)(2,1)} collective-permute-done((bf16[512,896]{1,0:T(8,128)(2,1)S(1)}, bf16[512,896]{1,0:T(8,128)(2,1)}, u32[]{:S(2)}, u32[]{:S(2)}) %collective-permute-start.25) | collective-permute-done | bytes 917536 | tf_op jit(solution)/shard_map/ppermute | solution.py:22
  338.3 16.7 %all-to-all-start.6 = ((bf16[4,896,128]{2,1,0:T(8,128)(2,1)}), bf16[4,896,128]{2,1,0:T(8,128)(2,1)S(1)}, u32[]{:S(2)}, u32[]{:S(2)}) async-start(bf16[4,896,128]{2,1,0:T(8,128)(2,1)} %bitcast.144), calls=%async_computation.6 | async-start | bytes 1835008 | tf_op jit(solution)/shard_map/all_to_all | solution.py:191
  355.0 10.5 %multiply_convert_fusion = bf16[512,896]{1,0:T(8,128)(2,1)S(1)} fusion(f32[512,896]{1,0:T(8,128)} %fusion.22, f32[512,896]{1,0:T(8,128)} %fusion.26, f32[512,896]{1,0:T(8,128)} %fusion.30, f32[512,896]{1,0:T(8,128)} %fusion.34, f32[512,896]{1,0:T(8,128)} %fusion.38, f32[512,896]{1,0:T(8,128)} %fusion.46, f32[512,896]{1,0:T(8,128)} %fusion.42, ...), kind=kOutput, calls=%fused_computation.12 | convolution fusion | flops 478937088 | bytes 29884416 | tf_op jit(solution)/shard_map/dot_general | solution.py:202
  369.2 8.7 %all-to-all-done.6 = bf16[4,896,128]{2,1,0:T(8,128)(2,1)S(1)} async-done(((bf16[4,896,128]{2,1,0:T(8,128)(2,1)}), bf16[4,896,128]{2,1,0:T(8,128)(2,1)S(1)}, u32[]{:S(2)}, u32[]{:S(2)}) %all-to-all-start.6) | async-done | bytes 917536 | tf_op jit(solution)/shard_map/all_to_all | solution.py:191
  388.0 11.5 %collective-permute-done.35 = bf16[896,512]{1,0:T(8,128)(2,1)} collective-permute-done((bf16[896,512]{1,0:T(8,128)(2,1)S(1)}, bf16[896,512]{1,0:T(8,128)(2,1)}, u32[]{:S(2)}, u32[]{:S(2)}) %collective-permute-start.35) | collective-permute-done | bytes 917536 | tf_op jit(solution)/shard_map/ppermute | solution.py:22
  406.7 19.0 %collective-permute-done.30 = bf16[4,64,2048]{2,1,0:T(8,128)(2,1)S(1)} collective-permute-done((bf16[4,64,2048]{2,1,0:T(8,128)(2,1)S(1)}, bf16[4,64,2048]{2,1,0:T(8,128)(2,1)S(1)}, u32[]{:S(2)}, u32[]{:S(2)}) %collective-permute-start.30) | collective-permute-done | bytes 1048608 | tf_op jit(solution)/shard_map/ppermute | solution.py:22
  430.6 17.1 %collective-permute-done.37 = bf16[4,64,2048]{2,1,0:T(8,128)(2,1)S(1)} collective-permute-done((bf16[4,64,2048]{2,1,0:T(8,128)(2,1)S(1)}, bf16[4,64,2048]{2,1,0:T(8,128)(2,1)S(1)}, u32[]{:S(2)}, u32[]{:S(2)}) %collective-permute-start.37) | collective-permute-done | bytes 1048608 | tf_op jit(solution)/shard_map/ppermute | solution.py:22
  453.9 8.3 %collective-permute-done.38 = bf16[64,2048]{1,0:T(8,128)(2,1)} collective-permute-done((bf16[64,2048]{1,0:T(8,128)(2,1)}, bf16[64,2048]{1,0:T(8,128)(2,1)}, u32[]{:S(2)}, u32[]{:S(2)}) %collective-permute-start.38) | collective-permute-done | bytes 262176 | tf_op jit(solution)/shard_map/ppermute | solution.py:22
  462.2 8.5 %collective-permute-done.39 = bf16[64,2048]{1,0:T(8,128)(2,1)} collective-permute-done((bf16[64,2048]{1,0:T(8,128)(2,1)}, bf16[64,2048]{1,0:T(8,128)(2,1)}, u32[]{:S(2)}, u32[]{:S(2)}) %collective-permute-start.39) | collective-permute-done | bytes 262176 | tf_op jit(solution)/shard_map/ppermute | solution.py:22
  (226 shorter events, 191.2 us)
Async XLA Ops:
  7.2 113.3 %all-gather.2.cloned.1.call-start = ((), (), s32[]{:S(2)}) async-start(), calls=%async_computation.7 | async-start | bytes 5242880 | tf_op jit(solution)/shard_map/all_gather | solution.py:114
  70.4 38.7 %all-to-all-start.1 = ((bf16[4,128,896]{1,2,0:T(8,128)(2,1)}), bf16[4,128,896]{1,2,0:T(8,128)(2,1)S(1)}, u32[]{:S(2)}, u32[]{:S(2)}) async-start(bf16[4,128,896]{1,2,0:T(8,128)(2,1)} %get-tuple-element.8), calls=%async_computation.1 | async-start | bytes 1835008 | tf_op jit(solution)/shard_map/all_to_all | solution.py:185
  110.1 39.6 %all-to-all-start.2 = ((bf16[4,128,896]{1,2,0:T(8,128)(2,1)}), bf16[4,128,896]{1,2,0:T(8,128)(2,1)S(1)}, u32[]{:S(2)}, u32[]{:S(2)}) async-start(bf16[4,128,896]{1,2,0:T(8,128)(2,1)} %get-tuple-element.9), calls=%async_computation.2 | async-start | bytes 1835008 | tf_op jit(solution)/shard_map/all_to_all | solution.py:185
  149.7 28.0 %all-to-all-start.3 = ((bf16[4,128,896]{1,2,0:T(8,128)(2,1)}), bf16[4,128,896]{1,2,0:T(8,128)(2,1)S(1)}, u32[]{:S(2)}, u32[]{:S(2)}) async-start(bf16[4,128,896]{1,2,0:T(8,128)(2,1)} %get-tuple-element.10), calls=%async_computation.3 | async-start | bytes 1835008 | tf_op jit(solution)/shard_map/all_to_all | solution.py:185
  159.1 24.5 %collective-permute-start.8 = (bf16[64,4096]{1,0:T(8,128)(2,1)S(1)}, bf16[64,4096]{1,0:T(8,128)(2,1)}, u32[]{:S(2)}, u32[]{:S(2)}) collective-permute-start(bf16[64,4096]{1,0:T(8,128)(2,1)S(1)} %reshape.181), channel_id=1, source_target_pairs={{0,16},{16,0},{1,17},{17,1},{2,18},{18,2},{3,19},{19,3},{4,20},{20... | collective-permute-start | bytes 1572872 | tf_op jit(solution)/shard_map/ppermute | solution.py:22
  160.6 25.7 %collective-permute-start.9 = (bf16[64,4096]{1,0:T(8,128)(2,1)S(1)}, bf16[64,4096]{1,0:T(8,128)(2,1)}, u32[]{:S(2)}, u32[]{:S(2)}) collective-permute-start(bf16[64,4096]{1,0:T(8,128)(2,1)S(1)} %reshape.181), channel_id=1, source_target_pairs={{0,1},{1,0},{2,3},{3,2},{4,5},{5,4},{6,7},{7,6},{8,9},{9,8},{10,11... | collective-permute-start | bytes 1572872 | tf_op jit(solution)/shard_map/ppermute | solution.py:22
  165.4 131.3 %collective-permute-start.15 = (bf16[512,896]{1,0:T(8,128)(2,1)}, bf16[512,896]{1,0:T(8,128)(2,1)}, u32[]{:S(2)}, u32[]{:S(2)}) collective-permute-start(bf16[512,896]{1,0:T(8,128)(2,1)} %bitcast.8), channel_id=1, source_target_pairs={{0,4},{4,0},{8,12},{12,8},{1,5},{5,1},{9,13},{13,9},{2,6},{6,2},{1... | collective-permute-start | bytes 2752520 | tf_op jit(solution)/shard_map/ppermute | solution.py:22
  171.7 121.2 %collective-permute-start.17 = (bf16[512,896]{1,0:T(8,128)(2,1)}, bf16[512,896]{1,0:T(8,128)(2,1)}, u32[]{:S(2)}, u32[]{:S(2)}) collective-permute-start(bf16[512,896]{1,0:T(8,128)(2,1)} %collective-permute-done.16), channel_id=1, source_target_pairs={{0,4},{4,0},{8,12},{12,8},{1,5},{5,1},{9,13},{13,9},{2,6},{6,2},{1... | collective-permute-start | bytes 2752520 | tf_op jit(solution)/shard_map/ppermute | solution.py:22
  173.0 76.2 %collective-permute-start.22 = (bf16[512,896]{1,0:T(8,128)(2,1)}, bf16[512,896]{1,0:T(8,128)(2,1)}, u32[]{:S(2)}, u32[]{:S(2)}) collective-permute-start(bf16[512,896]{1,0:T(8,128)(2,1)} %bitcast.14), channel_id=1, source_target_pairs={{0,8},{4,12},{8,0},{12,4},{1,9},{5,13},{9,1},{13,5},{2,10},{6,14},... | collective-permute-start | bytes 2752520 | tf_op jit(solution)/shard_map/ppermute | solution.py:22
  177.7 38.3 %all-to-all-start.4 = ((bf16[4,128,896]{1,2,0:T(8,128)(2,1)}), bf16[4,128,896]{1,2,0:T(8,128)(2,1)S(1)}, u32[]{:S(2)}, u32[]{:S(2)}) async-start(bf16[4,128,896]{1,2,0:T(8,128)(2,1)} %get-tuple-element.11), calls=%async_computation.4 | async-start | bytes 1835008 | tf_op jit(solution)/shard_map/all_to_all | solution.py:185
  183.6 59.1 %collective-permute-start.11 = (bf16[64,4096]{1,0:T(8,128)(2,1)S(1)}, bf16[64,4096]{1,0:T(8,128)(2,1)S(1)}, u32[]{:S(2)}, u32[]{:S(2)}) collective-permute-start(bf16[64,4096]{1,0:T(8,128)(2,1)S(1)} %reshape.181), channel_id=1, source_target_pairs={{0,2},{1,3},{2,0},{3,1},{4,6},{5,7},{6,4},{7,5},{8,10},{9,11},{10,... | collective-permute-start | bytes 1572872 | tf_op jit(solution)/shard_map/ppermute | solution.py:22
  186.3 58.7 %collective-permute-start.10 = (bf16[64,4096]{1,0:T(8,128)(2,1)}, bf16[64,4096]{1,0:T(8,128)(2,1)}, u32[]{:S(2)}, u32[]{:S(2)}) collective-permute-start(bf16[64,4096]{1,0:T(8,128)(2,1)} %collective-permute-done.9), channel_id=1, source_target_pairs={{0,16},{16,0},{1,17},{17,1},{2,18},{18,2},{3,19},{19,3},{4,20},{20... | collective-permute-start | bytes 1572872 | tf_op jit(solution)/shard_map/ppermute | solution.py:22
  216.0 116.2 %all-to-all-start.5 = ((bf16[4,896,128]{2,1,0:T(8,128)(2,1)}), bf16[4,896,128]{2,1,0:T(8,128)(2,1)S(1)}, u32[]{:S(2)}, u32[]{:S(2)}) async-start(bf16[4,896,128]{2,1,0:T(8,128)(2,1)} %bitcast.19), calls=%async_computation.5 | async-start | bytes 1835008 | tf_op jit(solution)/shard_map/all_to_all | solution.py:191
  249.2 57.2 %collective-permute-start.21 = (bf16[512,896]{1,0:T(8,128)(2,1)}, bf16[512,896]{1,0:T(8,128)(2,1)S(1)}, u32[]{:S(2)}, u32[]{:S(2)}) collective-permute-start(bf16[512,896]{1,0:T(8,128)(2,1)} %bitcast.14), channel_id=1, source_target_pairs={{0,4},{4,0},{8,12},{12,8},{1,5},{5,1},{9,13},{13,9},{2,6},{6,2},{1... | collective-permute-start | bytes 2752520 | tf_op jit(solution)/shard_map/ppermute | solution.py:22
  253.8 69.1 %collective-permute-start.23 = (bf16[512,896]{1,0:T(8,128)(2,1)}, bf16[512,896]{1,0:T(8,128)(2,1)S(1)}, u32[]{:S(2)}, u32[]{:S(2)}) collective-permute-start(bf16[512,896]{1,0:T(8,128)(2,1)} %collective-permute-done.22), channel_id=1, source_target_pairs={{0,4},{4,0},{8,12},{12,8},{1,5},{5,1},{9,13},{13,9},{2,6},{6,2},{1... | collective-permute-start | bytes 2752520 | tf_op jit(solution)/shard_map/ppermute | solution.py:22
  296.7 32.5 %collective-permute-start.24 = (bf16[512,896]{1,0:T(8,128)(2,1)S(1)}, bf16[512,896]{1,0:T(8,128)(2,1)S(1)}, u32[]{:S(2)}, u32[]{:S(2)}) collective-permute-start(bf16[512,896]{1,0:T(8,128)(2,1)S(1)} %bitcast.146), channel_id=1, source_target_pairs={{0,4},{4,0},{8,12},{12,8},{1,5},{5,1},{9,13},{13,9},{2,6},{6,2},{1... | collective-permute-start | bytes 2752520 | tf_op jit(solution)/shard_map/ppermute | solution.py:22
  322.9 32.1 %collective-permute-start.26 = (bf16[512,896]{1,0:T(8,128)(2,1)}, bf16[512,896]{1,0:T(8,128)(2,1)}, u32[]{:S(2)}, u32[]{:S(2)}) collective-permute-start(bf16[512,896]{1,0:T(8,128)(2,1)} %collective-permute-done.25), channel_id=1, source_target_pairs={{0,4},{4,0},{8,12},{12,8},{1,5},{5,1},{9,13},{13,9},{2,6},{6,2},{1... | collective-permute-start | bytes 2752520 | tf_op jit(solution)/shard_map/ppermute | solution.py:22
  333.3 46.4 %collective-permute-start.27 = (bf16[896,512]{1,0:T(8,128)(2,1)}, bf16[896,512]{1,0:T(8,128)(2,1)}, u32[]{:S(2)}, u32[]{:S(2)}) collective-permute-start(bf16[896,512]{1,0:T(8,128)(2,1)} %copy_bitcast_fusion.1), channel_id=1, source_target_pairs={{0,4},{4,0},{8,12},{12,8},{1,5},{5,1},{9,13},{13,9},{2,6},{6,2},{1... | collective-permute-start | bytes 2752520 | tf_op jit(solution)/shard_map/ppermute | solution.py:22
  333.8 32.5 %collective-permute-start.28 = (bf16[896,512]{1,0:T(8,128)(2,1)}, bf16[896,512]{1,0:T(8,128)(2,1)}, u32[]{:S(2)}, u32[]{:S(2)}) collective-permute-start(bf16[896,512]{1,0:T(8,128)(2,1)} %copy_bitcast_fusion.1), channel_id=1, source_target_pairs={{0,8},{4,12},{8,0},{12,4},{1,9},{5,13},{9,1},{13,5},{2,10},{6,14},... | collective-permute-start | bytes 2752520 | tf_op jit(solution)/shard_map/ppermute | solution.py:22
  338.3 39.6 %all-to-all-start.6 = ((bf16[4,896,128]{2,1,0:T(8,128)(2,1)}), bf16[4,896,128]{2,1,0:T(8,128)(2,1)S(1)}, u32[]{:S(2)}, u32[]{:S(2)}) async-start(bf16[4,896,128]{2,1,0:T(8,128)(2,1)} %bitcast.144), calls=%async_computation.6 | async-start | bytes 1835008 | tf_op jit(solution)/shard_map/all_to_all | solution.py:191
  399.6 26.0 %collective-permute-start.30 = (bf16[4,64,2048]{2,1,0:T(8,128)(2,1)S(1)}, bf16[4,64,2048]{2,1,0:T(8,128)(2,1)S(1)}, u32[]{:S(2)}, u32[]{:S(2)}) collective-permute-start(bf16[4,64,2048]{2,1,0:T(8,128)(2,1)S(1)} %slice_bitcast_fusion.2), channel_id=1, source_target_pairs={{0,16},{16,0},{1,17},{17,1},{2,18},{18,2},{3,19},{19,3},{4,20},{20... | collective-permute-start | bytes 3145736 | tf_op jit(solution)/shard_map/ppermute | solution.py:22
  406.2 41.5 %collective-permute-start.37 = (bf16[4,64,2048]{2,1,0:T(8,128)(2,1)S(1)}, bf16[4,64,2048]{2,1,0:T(8,128)(2,1)S(1)}, u32[]{:S(2)}, u32[]{:S(2)}) collective-permute-start(bf16[4,64,2048]{2,1,0:T(8,128)(2,1)S(1)} %slice_bitcast_fusion), channel_id=1, source_target_pairs={{0,16},{16,0},{1,17},{17,1},{2,18},{18,2},{3,19},{19,3},{4,20},{20... | collective-permute-start | bytes 3145736 | tf_op jit(solution)/shard_map/ppermute | solution.py:22
  426.2 25.8 %collective-permute-start.31 = (bf16[64,2048]{1,0:T(8,128)(2,1)S(1)}, bf16[64,2048]{1,0:T(8,128)(2,1)S(1)}, u32[]{:S(2)}, u32[]{:S(2)}) collective-permute-start(bf16[64,2048]{1,0:T(8,128)(2,1)S(1)} %get-tuple-element.24), channel_id=1, source_target_pairs={{0,1},{1,0},{2,3},{3,2},{4,5},{5,4},{6,7},{7,6},{8,9},{9,8},{10,11... | collective-permute-start | bytes 786440 | tf_op jit(solution)/shard_map/ppermute | solution.py:22
  426.3 27.2 %collective-permute-start.32 = (bf16[64,2048]{1,0:T(8,128)(2,1)S(1)}, bf16[64,2048]{1,0:T(8,128)(2,1)S(1)}, u32[]{:S(2)}, u32[]{:S(2)}) collective-permute-start(bf16[64,2048]{1,0:T(8,128)(2,1)S(1)} %get-tuple-element.26), channel_id=1, source_target_pairs={{0,2},{1,3},{2,0},{3,1},{4,6},{5,7},{6,4},{7,5},{8,10},{9,11},{10,... | collective-permute-start | bytes 786440 | tf_op jit(solution)/shard_map/ppermute | solution.py:22
  (48 other events, 464.8 us)
Sparse Core Ops, SparseCore 0:
  9.6 92.9 all-gather.1

commit v3 on v1

v3 whole, which is shorter than its diff:
```python
import functools

import jax
import jax.numpy as jnp
from jax import lax
from jax.experimental import pallas as pl
from jax.experimental.pallas import tpu as pltpu
from jax.sharding import PartitionSpec as P

D = 4096
QUERY_HEADS = 32
KEY_VALUE_HEADS = 8
HEAD_WIDTH = 128
GROUP = QUERY_HEADS // KEY_VALUE_HEADS
Q_COLS = GROUP * HEAD_WIDTH
KV_COLS = 2 * HEAD_WIDTH
WINDOW_PER_DOC = 4
QUERY_TILE = 128
ROW_TILE = 256
VMEM_LIMIT = 48 * 1024 * 1024
ANY = pl.BlockSpec(memory_space=pl.ANY)
VMEM = pl.BlockSpec(memory_space=pltpu.VMEM)
SMEM = pl.BlockSpec(memory_space=pltpu.SMEM)


def swap(array, axis, distance):
    if distance == 0:
        return array
    count = lax.axis_size(axis)
    return lax.ppermute(array, axis, [(s, s ^ distance) for s in range(count)])


def after(array, earlier):
    return lax.optimization_barrier((array, earlier))[0]


def blocks_over_inner(block):
    across = swap(block, "inner", 2)
    return [block, swap(block, "inner", 1), across, swap(across, "inner", 1)]


def earlier_planes(kv, hops):
    count = lax.axis_size("outer")
    moved = [lax.ppermute(kv, "outer", [(s, s + d) for s in range(count - d)]) for d in range(hops, 0, -1)]
    return jnp.concatenate(moved, axis=0)


def document_starts(bounds, first, rows):
    place = first + jnp.arange(rows, dtype=jnp.int32)
    starts = jnp.max(jnp.where(bounds[None, :] <= place[:, None], bounds[None, :], 0), axis=1) - first
    return starts[:, None].astype(jnp.int32)


def row_tiles(rows):
    step = ROW_TILE if rows % ROW_TILE == 0 else rows
    return [slice(at, at + step) for at in range(0, rows, step)]


def attention_kernel(halo_rows, reach, starts_ref, queries_ref, own_ref, halo_ref, out_ref, keys, values):
    tile = pl.program_id(0)
    rows = queries_ref.shape[0]
    span = reach + rows

    @pl.when(tile == 0)
    def _():
        keys[:halo_rows, :] = halo_ref[:, :HEAD_WIDTH]
        values[:halo_rows, :] = halo_ref[:, HEAD_WIDTH:]
        keys[halo_rows:, :] = own_ref[:, :HEAD_WIDTH]
        values[halo_rows:, :] = own_ref[:, HEAD_WIDTH:]

    first = pl.multiple_of(tile * rows + (halo_rows - reach), rows)
    near_keys = keys[pl.ds(first, span), :]
    near_values = values[pl.ds(first, span), :]
    key_place = lax.broadcasted_iota(jnp.int32, (rows, span), 1)
    query_place = lax.broadcasted_iota(jnp.int32, (rows, span), 0) + reach
    start = starts_ref[...] - (first - halo_rows)
    allowed = (key_place <= query_place) & (key_place >= start)
    for g in range(GROUP):
        cols = slice(g * HEAD_WIDTH, (g + 1) * HEAD_WIDTH)
        scores = lax.dot_general(
            queries_ref[:, cols], near_keys, (((1,), (1,)), ((), ())), preferred_element_type=jnp.float32
        ) * (HEAD_WIDTH ** (-0.5))
        masked = jnp.where(allowed, scores, -1e30)
        row_max = jnp.max(masked, axis=1, keepdims=True)
        weights = jnp.exp(masked - row_max)
        totals = jnp.sum(weights, axis=1, keepdims=True)
        summed = jnp.dot(weights.astype(jnp.bfloat16), near_values, preferred_element_type=jnp.float32)
        out_ref[:, cols] = (summed / totals).astype(jnp.bfloat16)


def attention(packed, halo, halo_at, starts, reach):
    rows = packed.shape[0]
    halo_rows = halo.shape[0]
    return pl.pallas_call(
        functools.partial(attention_kernel, halo_rows, reach),
        grid=(rows // QUERY_TILE,),
        in_specs=[
            pl.BlockSpec((QUERY_TILE, 1), lambda t: (t, 0)),
            pl.BlockSpec((QUERY_TILE, Q_COLS), lambda t: (t, 0)),
            pl.BlockSpec((rows, KV_COLS), lambda t: (0, Q_COLS // KV_COLS)),
            pl.BlockSpec((halo_rows, KV_COLS), lambda t: (0, halo_at)),
        ],
        out_specs=pl.BlockSpec((QUERY_TILE, Q_COLS), lambda t: (t, 0)),
        out_shape=jax.ShapeDtypeStruct((rows, Q_COLS), jnp.bfloat16),
        scratch_shapes=[
            pltpu.VMEM((halo_rows + rows, HEAD_WIDTH), jnp.bfloat16),
            pltpu.VMEM((halo_rows + rows, HEAD_WIDTH), jnp.bfloat16),
        ],
        compiler_params=pltpu.CompilerParams(vmem_limit_bytes=VMEM_LIMIT),
        cost_estimate=pl.CostEstimate(
            flops=4 * rows * (reach + QUERY_TILE) * Q_COLS,
            bytes_accessed=rows * 4 * Q_COLS,
            transcendentals=rows * (reach + QUERY_TILE) * GROUP,
        ),
        name="attention",
    )(starts, packed, packed, halo)


def gain_kernel(gain_ref, weights_ref, gate_ref, up_ref):
    for which, out_ref in enumerate((gate_ref, up_ref)):
        out_ref[0] = (weights_ref[which].astype(jnp.float32) * gain_ref[...]).astype(jnp.bfloat16)


def scaled_gate_up(w_gate_up, gain, outer_count):
    _, rows, width = w_gate_up.shape
    cols = width // outer_count
    if cols % HEAD_WIDTH:
        wide = (w_gate_up.astype(jnp.float32) * gain[None]).astype(jnp.bfloat16)
        return jnp.transpose(wide.reshape(2, rows, outer_count, cols), (0, 2, 1, 3))
    return pl.pallas_call(
        gain_kernel,
        grid=(outer_count,),
        in_specs=[
            pl.BlockSpec((rows, 1), lambda p: (0, 0)),
            pl.BlockSpec((2, rows, cols), lambda p: (0, 0, p)),
        ],
        out_specs=[pl.BlockSpec((1, rows, cols), lambda p: (p, 0, 0))] * 2,
        out_shape=[jax.ShapeDtypeStruct((outer_count, rows, cols), jnp.bfloat16)] * 2,
        compiler_params=pltpu.CompilerParams(vmem_limit_bytes=VMEM_LIMIT),
        cost_estimate=pl.CostEstimate(flops=2 * rows * width, bytes_accessed=8 * rows * width, transcendentals=0),
        name="take_gain",
    )(gain, w_gate_up)


def projection_kernel(block_count, place_ref, *refs):
    blocks, weights_ref = refs[:block_count], refs[block_count]
    kept_ref, sent_ref = refs[block_count + 1 : block_count + 3]
    inner, head = place_ref[0], place_ref[1]
    half, depth = kept_ref.shape[0], blocks[0].shape[1]
    for e in range(sent_ref.shape[0] + 1):
        rows = pl.ds(pl.multiple_of((head ^ e) * half, half), half)
        total = jnp.zeros(kept_ref.shape, jnp.float32)
        for a, block in enumerate(blocks):
            at = pl.ds(pl.multiple_of((inner ^ a) * depth, depth), depth) if block_count > 1 else slice(None)
            total = total + jnp.dot(block[rows, :], weights_ref[at, :], preferred_element_type=jnp.float32)
        if e == 0:
            kept_ref[...] = total.astype(jnp.bfloat16)
        else:
            sent_ref[e - 1] = total.astype(jnp.bfloat16)
    if block_count > 1:
        context_ref = refs[block_count + 3]
        tokens = context_ref.shape[0]
        own = pl.ds(pl.multiple_of(inner * tokens, tokens), tokens)
        for a, block in enumerate(blocks):
            context_ref[:, pl.ds(pl.multiple_of((inner ^ a) * depth, depth), depth)] = block[own, :]


def projection(blocks, weights, place, head_count, inner_count):
    rows, depth = blocks[0].shape
    half, width = rows // head_count, weights.shape[1]
    outs = [(half, width), (head_count - 1, half, width)]
    if len(blocks) > 1:
        outs.append((rows // inner_count, len(blocks) * depth))
    return pl.pallas_call(
        functools.partial(projection_kernel, len(blocks)),
        in_specs=[SMEM] + [VMEM] * (len(blocks) + 1),
        out_specs=[VMEM] * len(outs),
        out_shape=[jax.ShapeDtypeStruct(shape, jnp.bfloat16) for shape in outs],
        compiler_params=pltpu.CompilerParams(vmem_limit_bytes=VMEM_LIMIT),
        cost_estimate=pl.CostEstimate(
            flops=2 * rows * weights.size, bytes_accessed=2 * (weights.size + rows * 2 * width), transcendentals=0
        ),
        name="projection",
    )(place, *blocks, weights)


def gate_up_kernel(token_count, block_count, *refs):
    tokens = refs[:token_count]
    weights = refs[token_count : token_count + 2 * block_count]
    out_ref, held, near, gate, up, token_sems, weight_sems = refs[token_count + 2 * block_count :]
    piece = held.shape[0] // token_count
    token_copies = [
        pltpu.make_async_copy(ref, held.at[pl.ds(j * piece, piece)], token_sems.at[j]) for j, ref in enumerate(tokens)
    ]
    weight_copies = [pltpu.make_async_copy(ref, near.at[j], weight_sems.at[j]) for j, ref in enumerate(weights)]
    for copy in token_copies + weight_copies:
        copy.start()
    for copy in token_copies:
        copy.wait()
    depth = near.shape[1]
    for a in range(block_count):
        for which, total in enumerate((gate, up)):
            weight_copies[2 * a + which].wait()
            for rows in row_tiles(held.shape[0]):
                product = jnp.dot(
                    held[rows, a * depth : (a + 1) * depth], near[2 * a + which], preferred_element_type=jnp.float32
                )
                total[rows, :] = product if a == 0 else total[rows, :] + product
    for rows in row_tiles(held.shape[0]):
        out_ref[rows, :] = (gate[rows, :] / (1.0 + jnp.exp(-gate[rows, :])) * up[rows, :]).astype(jnp.bfloat16)


def gate_up(tokens, gates, ups):
    if len(tokens) > 8:
        tokens = [jnp.concatenate(tokens, axis=0)]
    rows = sum(piece.shape[0] for piece in tokens)
    depth, cols = gates[0].shape
    weights = [block for pair in zip(gates, ups) for block in pair]
    return pl.pallas_call(
        functools.partial(gate_up_kernel, len(tokens), len(gates)),
        in_specs=[ANY] * (len(tokens) + len(weights)),
        out_specs=VMEM,
        out_shape=jax.ShapeDtypeStruct((rows, cols), jnp.bfloat16),
        scratch_shapes=[
            pltpu.VMEM((rows, depth * len(gates)), jnp.bfloat16),
            pltpu.VMEM((len(weights), depth, cols), jnp.bfloat16),
            pltpu.VMEM((rows, cols), jnp.float32),
            pltpu.VMEM((rows, cols), jnp.float32),
            pltpu.SemaphoreType.DMA((len(tokens),)),
            pltpu.SemaphoreType.DMA((len(weights),)),
        ],
        compiler_params=pltpu.CompilerParams(vmem_limit_bytes=VMEM_LIMIT),
        cost_estimate=pl.CostEstimate(
            flops=4 * rows * depth * len(gates) * cols,
            bytes_accessed=2 * (rows * depth * len(gates) + len(weights) * depth * cols),
            transcendentals=rows * cols,
        ),
        name="gate_up",
    )(*tokens, *weights)


def down_kernel(activated_ref, weights_ref, kept_ref, sent_ref):
    sources, _, cols = weights_ref.shape
    kept_rows = kept_ref.shape[0]
    for s in range(sources):
        at = slice(s * cols, (s + 1) * cols)
        for e in range(sent_ref.shape[0] + 1):
            rows = slice(e * kept_rows, (e + 1) * kept_rows)
            product = jnp.dot(activated_ref[rows, :], weights_ref[s], preferred_element_type=jnp.float32)
            if e == 0:
                kept_ref[:, at] = product.astype(jnp.bfloat16)
            else:
                sent_ref[e - 1, :, at] = product.astype(jnp.bfloat16)


def down_product(activated, weights, head_count):
    rows = activated.shape[0] // head_count
    sources, depth, cols = weights.shape
    return pl.pallas_call(
        down_kernel,
        in_specs=[VMEM, VMEM],
        out_specs=[VMEM, VMEM],
        out_shape=[
            jax.ShapeDtypeStruct((rows, sources * cols), jnp.bfloat16),
            jax.ShapeDtypeStruct((head_count - 1, rows, sources * cols), jnp.bfloat16),
        ],
        compiler_params=pltpu.CompilerParams(vmem_limit_bytes=VMEM_LIMIT),
        cost_estimate=pl.CostEstimate(
            flops=2 * activated.size * sources * cols,
            bytes_accessed=2 * (activated.size + weights.size + head_count * rows * sources * cols),
            transcendentals=0,
        ),
        name="down",
    )(activated, weights)


def per_device(query, key, value, doc_lengths, resid, norm_gain, w_out, w_gate_up, w_down):
    inner_count = lax.axis_size("inner")
    outer_count = lax.axis_size("outer")
    head_count = lax.axis_size("head")
    outer, inner, head = lax.axis_index("outer"), lax.axis_index("inner"), lax.axis_index("head")
    rows = query.shape[0]
    plane_rows = rows * inner_count * head_count
    reach = plane_rows * outer_count // WINDOW_PER_DOC
    feature_rows = w_gate_up.shape[1]
    hidden_cols = w_gate_up.shape[2] // outer_count
    bounds = jnp.cumsum(doc_lengths)
    hops = reach // plane_rows
    token_rows = plane_rows // inner_count
    half = plane_rows // head_count
    packing = (rows, head_count, KEY_VALUE_HEADS // head_count, -1)

    weights_out = lax.all_gather(w_out, "outer", axis=1, tiled=True)
    own_gain = lax.dynamic_slice_in_dim(norm_gain, outer * feature_rows, feature_rows, 0)
    w_gate, w_up = scaled_gate_up(w_gate_up, own_gain[:, None], outer_count)
    if packing[2] == inner_count and hops == 1:
        earlier = [lax.ppermute(part, "outer", [(s, s + 1) for s in range(outer_count - 1)]) for part in (key, value)]
        groups = jnp.concatenate([part.reshape(packing) for part in (query, key, value, *earlier)], axis=3)
        groups = jnp.transpose(groups, (2, 1, 0, 3)).reshape(inner_count * head_count, rows, -1)
        packed = lax.all_to_all(groups, ("inner", "head"), split_axis=0, concat_axis=0, tiled=True)
        packed = packed.reshape(plane_rows, -1)
        starts = document_starts(bounds, outer * plane_rows, plane_rows)
        own_context = attention(packed, packed, Q_COLS // KV_COLS + 1, starts, reach)
        blocks = blocks_over_inner(own_context)
    else:
        groups = jnp.concatenate([part.reshape(packing) for part in (query, key, value)], axis=3)
        groups = jnp.transpose(groups[:, :, 0], (1, 0, 2))
        packed = lax.all_to_all(groups, "head", split_axis=0, concat_axis=0, tiled=True).reshape(token_rows, -1)
        plane_kv = lax.all_gather(packed[:, Q_COLS:], "inner", axis=0, tiled=True)
        every_kv = jnp.concatenate([earlier_planes(plane_kv, hops), plane_kv], axis=0)
        halo = lax.dynamic_slice_in_dim(every_kv, inner * token_rows, reach, 0)
        starts = document_starts(bounds, outer * plane_rows + inner * token_rows, token_rows)
        own_context = attention(packed, halo, 0, starts, reach)
        blocks = [lax.all_gather(own_context, "inner", axis=0, tiled=True)]

    spread = functools.partial(lax.all_to_all, axis_name="outer", split_axis=0, concat_axis=0, tiled=True)
    gate_here = spread(after(w_gate, packed))
    up_here = spread(after(w_up, gate_here))
    down_here = spread(after(w_down.reshape(outer_count, hidden_cols, feature_rows), up_here))
    gates = blocks_over_inner(gate_here.reshape(-1, hidden_cols))
    ups = blocks_over_inner(up_here.reshape(-1, hidden_cols))
    downs = blocks_over_inner(down_here)

    place = jnp.stack([inner, head]).astype(jnp.int32)
    kept, sent, *whole = projection(blocks, weights_out, place, head_count, inner_count)
    context = whole[0] if whole else own_context
    projected = kept.astype(jnp.float32)
    for e in range(1, head_count):
        projected = projected + swap(sent[e - 1], "head", e).astype(jnp.float32)
    own_resid = lax.dynamic_slice_in_dim(resid, head * half, half, 0)
    hidden_part = (own_resid.astype(jnp.float32) + projected).astype(jnp.bfloat16)

    own_rows = half // inner_count
    state = []
    for a in range(inner_count):
        block = lax.dynamic_slice_in_dim(hidden_part, (inner ^ a) * own_rows, own_rows, 0)
        state.append(swap(block, "inner", a).astype(jnp.float32))
    squares = sum([jnp.sum(block * block, axis=1, keepdims=True) for block in state])
    inverse = lax.rsqrt(squares / D + 1e-05)
    normed = jnp.concatenate([block * inverse for block in state], axis=1).astype(jnp.bfloat16)
    along_outer = [swap(normed, "outer", d) for d in range(outer_count)]
    tokens = [swap(block, "head", e) for e in range(head_count) for block in along_outer]

    activated = gate_up(tokens, gates, ups)
    layer_out = jnp.zeros((half, D // inner_count), jnp.bfloat16)
    for a in range(inner_count):
        kept, sent = down_product(activated, downs[a], head_count)
        paired = kept.astype(jnp.float32)
        for e in range(1, head_count):
            paired = paired + swap(sent[e - 1], "head", e).astype(jnp.float32)
        paired = paired.reshape(outer_count, own_rows, -1)
        total = state[a] + paired[0]
        for d in range(1, outer_count):
            total = total + swap(paired[d].astype(jnp.bfloat16), "outer", d).astype(jnp.float32)
        block = swap(total.astype(jnp.bfloat16), "inner", a)
        layer_out = lax.dynamic_update_slice(layer_out, block, ((inner ^ a) * own_rows, 0))
    return (context, layer_out)


def solution(mesh):
    placed = (
        P(("outer", "inner", "head"), None),
        P(("outer", "inner", "head"), None),
        P(("outer", "inner", "head"), None),
        P(),
        P("outer", "inner"),
        P("inner"),
        P("head", ("inner", "outer")),
        P(None, ("inner", "outer"), "head"),
        P("head", ("inner", "outer")),
    )
    return jax.shard_map(
        per_device,
        mesh=mesh,
        in_specs=placed,
        out_specs=(P(("outer", "inner"), "head"), P(("outer", "head"), "inner")),
        check_vma=False,
    )
```

time: 555 us -> 420 us (0.76)
  waiting for transfers between devices: 307 us -> 191 us
  local copies, waits for them, and re-layouts: 110 us -> 10.3 us
  blocking collectives: 5.32 us -> 89.2 us
  Pallas kernels: 5.79 us -> 32.8 us
  matrix products: 24.7 us -> 0 us
    ppermute x45 -> x42, waiting for transfers between devices: 298 us -> 168 us  [swap(): return lax.ppermute(array, axis, [(s, s ^ distance) for s in range(count)])]
    all_to_all x0 -> x1, blocking collectives: none -> 89.2 us  [per_device(): gate_here = spread(after(w_gate, packed))]
    dynamic_update_slice x35 -> x3, local copies, waits for them, and re-layouts: 53.4 us -> 0.05 us  [per_device(): lax.dynamic_update_slice(layer_out, block, ((inner ^ a) * own_rows, 0))]
    ppermute x15 -> x0, local copies, waits for them, and re-layouts: 29.6 us -> none  [swap(): return lax.ppermute(array, axis, [(s, s ^ distance) for s in range(count)])]
    pallas_call x0 -> x7, Pallas kernels: none -> 26.9 us  [the longest x1 12.2 us: gate_up(): pl.pallas_call(functools.partial(gate_up_kernel, len(tokens), len(gates))...]
    dot_general x3 -> x0, matrix products: 24.7 us -> none  [the longest x1 11.3 us: per_device(): jnp.einsum('td,kdf->ktf', tokens, gate_up_weights, preferred_element_type...]
    ppermute x1 -> x2, starting transfers between devices: 21.6 us -> 8.42 us  [per_device(): lax.ppermute(part, 'outer', [(s, s + 1) for s in range(outer_count - 1)])]
    broadcast_in_dim x3 -> x2, local copies, waits for them, and re-layouts: 12.5 us -> 0.19 us  [the longest x1 0.13 us: per_device(): w_gate, w_up = scaled_gate_up(w_gate_up, own_gain[:, None], outer_count)]
  transfers between devices with their start and end apart: 50 -> 48, of which waited for: 19 -> 21; matrix products, arithmetic and copies ran while one was open for 21% -> 3% of each run, Pallas kernels for 1% -> 8%
where the time goes in v3:
time: 420 us; the launch traced here: 419 us
  waiting for transfers between devices  191 us (45%)
  blocking collectives  89.2 us (21%)
  starting transfers between devices  76.6 us (18%)
  Pallas kernels  32.8 us (8%)
  between operations  14.5 us (3%)
  local copies, waits for them, and re-layouts  10.3 us (2%)
  other arithmetic  4.44 us (1%)
    ppermute x42, waiting for transfers between devices, swap(): return lax.ppermute(array, axis, [(s, s ^ distance) for s in range(count)])  168 us
    all_to_all x1, blocking collectives, per_device(): gate_here = spread(after(w_gate, packed))  89.2 us
    ppermute x42, starting transfers between devices, swap(): return lax.ppermute(array, axis, [(s, s ^ distance) for s in range(count)])  55.9 us
    all_to_all x1, waiting for transfers between devices, per_device(): up_here = spread(after(w_up, gate_here))  13.2 us
    pallas_call x1, Pallas kernels, gate_up(): pl.pallas_call(functools.partial(gate_up_kernel, len(tokens), len(gates))...  12.2 us
    all_to_all x1, waiting for transfers between devices, per_device(): lax.all_to_all(groups, ('inner', 'head'), split_axis=0, concat_axis=0, ti...  9.57 us
    ppermute x2, starting transfers between devices, per_device(): lax.ppermute(part, 'outer', [(s, s + 1) for s in range(outer_count - 1)])  8.42 us
  transfers between devices with their start and end apart: 48, of which 21 were waited for; matrix products, arithmetic and copies ran while one was open for 3% of the time, Pallas kernels for 8%

profile of v3, /device:TPU:0, one launch (start us, length us, event | category | flops | bytes accessed | tf_op | source)
XLA Modules:
  0.0 419.2 jit_solution(3149030248906187715)
XLA Ops:
  7.9 4.9 %collective-permute-start = (bf16[64,1024]{1,0:T(8,128)(2,1)}, bf16[64,1024]{1,0:T(8,128)(2,1)S(1)}, u32[]{:S(2)}, u32[]{:S(2)}) collective-permute-start(bf16[64,1024]{1,0:T(8,128)(2,1)} %param.10), channel_id=1, source_target_pairs={{0,1},{1,2},{2,3},{4,5},{5,6},{6,7},{8,9},{9,10},{10,11},{12,13},{... | collective-permute-start | bytes 393224 | tf_op jit(solution)/shard_map/ppermute | solution.py:297
  25.9 4.5 %take_gain.1 = (bf16[4,256,896]{2,1,0:T(8,128)(2,1)S(1)}, bf16[4,256,896]{2,1,0:T(8,128)(2,1)}) custom-call(f32[256,1]{1,0:T(8,128)S(1)} %copy.20.gain_ref, bf16[2,256,3584]{2,1,0:T(8,128)(2,1)} %weights_ref.1), custom_call_target="tpu_custom_call" | custom-call | flops 1835008 | bytes 7340032 | tf_op jit(solution)/shard_map/take_gain/pallas_call | solution.py:130
  30.4 9.6 %all-to-all-done = bf16[8,64,1024]{2,1,0:T(8,128)(2,1)S(1)} async-done(((bf16[8,64,1024]{2,1,0:T(8,128)(2,1)}), bf16[8,64,1024]{2,1,0:T(8,128)(2,1)S(1)}, u32[]{:S(2)}, u32[]{:S(2)}) %all-to-all-start) | async-done | bytes 1048608 | tf_op jit(solution)/shard_map/all_to_all | solution.py:300
  40.0 89.2 %all_to_all.20 = bf16[4,256,896]{2,1,0:T(8,128)(2,1)} all-to-all(bf16[4,256,896]{2,1,0:T(8,128)(2,1)S(1)} %get-tuple-element.22), channel_id=1, replica_groups=mesh['head'=2,'inner'=4,'outer'=4] {'outer'}, dimensions={0} | all-to-all | bytes 3670016 | tf_op jit(solution)/shard_map/all_to_all | solution.py:317
  129.2 4.5 %all-to-all-start.2 = ((bf16[4,256,896]{2,1,0:T(8,128)(2,1)}), bf16[4,256,896]{2,1,0:T(8,128)(2,1)}, u32[]{:S(2)}, u32[]{:S(2)}) async-start(bf16[4,256,896]{2,1,0:T(8,128)(2,1)} %get-tuple-element.24), calls=%async_computation.2 | async-start | bytes 3670016 | tf_op jit(solution)/shard_map/all_to_all | solution.py:318
  134.3 5.9 %attention.1.refs_0_ = bf16[512,512]{1,0:T(8,128)(2,1)S(1)} custom-call(s32[512,1]{1,0:T(8,128)S(1)} %copy.19.starts_ref, bf16[512,1024]{1,0:T(8,128)(2,1)S(1)} %bitcast.16, bf16[512,1024]{1,0:T(8,128)(2,1)S(1)} %bitcast.17, bf16[512,1024]{1,0:T(8,128)(2,1)S(1)} %bitcast.18), custom_call_target="tpu_custom_call" | custom-call | flops 671088640 | bytes 1048576 | tf_op jit(solution)/shard_map/attention/pallas_call | solution.py:94
  142.3 12.8 %collective-permute-done.3.refs_2_ = bf16[512,512]{1,0:T(8,128)(2,1)S(1)} collective-permute-done((bf16[512,512]{1,0:T(8,128)(2,1)S(1)}, bf16[512,512]{1,0:T(8,128)(2,1)S(1)}, u32[]{:S(2)}, u32[]{:S(2)}) %collective-permute-start.3) | collective-permute-done | bytes 524320 | tf_op jit(solution)/shard_map/ppermute | solution.py:30
  157.0 5.3 %projection.1 = (bf16[256,1024]{1,0:T(8,128)(2,1)S(1)}, bf16[1,256,1024]{2,1,0:T(8,128)(2,1)S(1)}, bf16[128,2048]{1,0:T(8,128)(2,1)}) custom-call(s32[2]{0:T(128)S(1)} %pad_add_fusion.place_ref, bf16[512,512]{1,0:T(8,128)(2,1)S(1)} %attention.1.refs_0_, bf16[512,512]{1,0:T(8,128)(2,1)S(1)} %collective-permute-done.2.refs_1_, ...), custom_call_target="tpu_custom_call" | custom-call | flops 2147483648 | bytes 6291456 | tf_op jit(solution)/shard_map/projection/pallas_call | solution.py:174
  163.5 13.2 %all-to-all-done.2 = bf16[4,256,896]{2,1,0:T(8,128)(2,1)} async-done(((bf16[4,256,896]{2,1,0:T(8,128)(2,1)}), bf16[4,256,896]{2,1,0:T(8,128)(2,1)}, u32[]{:S(2)}, u32[]{:S(2)}) %all-to-all-start.2) | async-done | bytes 1835040 | tf_op jit(solution)/shard_map/all_to_all | solution.py:318
  184.1 10.3 %collective-permute-done.18.refs_12_ = bf16[1024,896]{1,0:T(8,128)(2,1)} collective-permute-done((bf16[1024,896]{1,0:T(8,128)(2,1)}, bf16[1024,896]{1,0:T(8,128)(2,1)}, u32[]{:S(2)}, u32[]{:S(2)}) %collective-permute-start.18) | collective-permute-done | bytes 1835040 | tf_op jit(solution)/shard_map/ppermute | solution.py:30
  194.6 41.9 %collective-permute-done.7 = bf16[64,1024]{1,0:T(8,128)(2,1)S(1)} collective-permute-done((bf16[64,1024]{1,0:T(8,128)(2,1)S(1)}, bf16[64,1024]{1,0:T(8,128)(2,1)S(1)}, u32[]{:S(2)}, u32[]{:S(2)}) %collective-permute-start.7) | collective-permute-done | bytes 131104 | tf_op jit(solution)/shard_map/ppermute | solution.py:30
  243.4 19.6 %collective-permute-done.9.refs_1_ = bf16[64,4096]{1,0:T(8,128)(2,1)S(1)} collective-permute-done((bf16[64,4096]{1,0:T(8,128)(2,1)S(1)}, bf16[64,4096]{1,0:T(8,128)(2,1)S(1)}, u32[]{:S(2)}, u32[]{:S(2)}) %collective-permute-start.9) | collective-permute-done | bytes 524320 | tf_op jit(solution)/shard_map/ppermute | solution.py:30
  265.7 13.5 %collective-permute-done.10.refs_2_ = bf16[64,4096]{1,0:T(8,128)(2,1)S(1)} collective-permute-done((bf16[64,4096]{1,0:T(8,128)(2,1)S(1)}, bf16[64,4096]{1,0:T(8,128)(2,1)S(1)}, u32[]{:S(2)}, u32[]{:S(2)}) %collective-permute-start.10) | collective-permute-done | bytes 524320 | tf_op jit(solution)/shard_map/ppermute | solution.py:30
  281.3 12.8 %collective-permute-done.12.refs_4_ = bf16[64,4096]{1,0:T(8,128)(2,1)S(1)} collective-permute-done((bf16[64,4096]{1,0:T(8,128)(2,1)S(1)}, bf16[64,4096]{1,0:T(8,128)(2,1)S(1)}, u32[]{:S(2)}, u32[]{:S(2)}) %collective-permute-start.12) | collective-permute-done | bytes 524320 | tf_op jit(solution)/shard_map/ppermute | solution.py:30
  296.7 8.8 %collective-permute-done.13.refs_5_ = bf16[64,4096]{1,0:T(8,128)(2,1)} collective-permute-done((bf16[64,4096]{1,0:T(8,128)(2,1)S(1)}, bf16[64,4096]{1,0:T(8,128)(2,1)}, u32[]{:S(2)}, u32[]{:S(2)}) %collective-permute-start.13) | collective-permute-done | bytes 524320 | tf_op jit(solution)/shard_map/ppermute | solution.py:30
  305.7 7.6 %collective-permute-done.14.refs_6_ = bf16[64,4096]{1,0:T(8,128)(2,1)S(1)} collective-permute-done((bf16[64,4096]{1,0:T(8,128)(2,1)S(1)}, bf16[64,4096]{1,0:T(8,128)(2,1)S(1)}, u32[]{:S(2)}, u32[]{:S(2)}) %collective-permute-start.14) | collective-permute-done | bytes 524320 | tf_op jit(solution)/shard_map/ppermute | solution.py:30
  313.2 5.6 %collective-permute-done.15.refs_7_ = bf16[64,4096]{1,0:T(8,128)(2,1)S(1)} collective-permute-done((bf16[64,4096]{1,0:T(8,128)(2,1)}, bf16[64,4096]{1,0:T(8,128)(2,1)S(1)}, u32[]{:S(2)}, u32[]{:S(2)}) %collective-permute-start.15) | collective-permute-done | bytes 524320 | tf_op jit(solution)/shard_map/ppermute | solution.py:30
  321.0 12.2 %gate_up.1.activated_ref = bf16[512,896]{1,0:T(8,128)(2,1)S(1)} custom-call(bf16[64,4096]{1,0:T(8,128)(2,1)S(1)} %pad_maximum_fusion.refs_0_, bf16[64,4096]{1,0:T(8,128)(2,1)S(1)} %collective-permute-done.9.refs_1_, bf16[64,4096]{1,0:T(8,128)(2,1)S(1)} %collective-permute-done.10.refs_2_, bf16[64,4096]{1,0:T(8,128)(2,1)S(1)} %copy-done.1, ...), custom_call_target="tpu_custom_call" | custom-call | flops 7516192768 | bytes 18874368 | tf_op jit(solution)/shard_map/gate_up/pallas_call | solution.py:219
  334.8 8.9 %collective-permute-done.22 = bf16[256,1024]{1,0:T(8,128)(2,1)S(1)} collective-permute-done((bf16[256,1024]{1,0:T(8,128)(2,1)S(1)}, bf16[256,1024]{1,0:T(8,128)(2,1)S(1)}, u32[]{:S(2)}, u32[]{:S(2)}) %collective-permute-start.22) | collective-permute-done | bytes 524320 | tf_op jit(solution)/shard_map/ppermute | solution.py:30
  343.9 9.9 %collective-permute-start.23 = (bf16[64,1024]{1,0:T(8,128)(2,1)S(1)}, bf16[64,1024]{1,0:T(8,128)(2,1)S(1)}, u32[]{:S(2)}, u32[]{:S(2)}) collective-permute-start(bf16[64,1024]{1,0:T(8,128)(2,1)S(1)} %get-tuple-element.51), channel_id=1, source_target_pairs={{0,1},{1,0},{2,3},{3,2},{4,5},{5,4},{6,7},{7,6},{8,9},{9,8},{10,11... | collective-permute-start | bytes 393224 | tf_op jit(solution)/shard_map/ppermute | solution.py:30
  360.0 5.4 %collective-permute-done.24 = bf16[64,1024]{1,0:T(8,128)(2,1)S(1)} collective-permute-done((bf16[64,1024]{1,0:T(8,128)(2,1)S(1)}, bf16[64,1024]{1,0:T(8,128)(2,1)S(1)}, u32[]{:S(2)}, u32[]{:S(2)}) %collective-permute-start.24) | collective-permute-done | bytes 131104 | tf_op jit(solution)/shard_map/ppermute | solution.py:30
  378.7 6.2 %collective-permute-start.28 = (bf16[64,1024]{1,0:T(8,128)(2,1)S(1)}, bf16[64,1024]{1,0:T(8,128)(2,1)S(1)}, u32[]{:S(2)}, u32[]{:S(2)}) collective-permute-start(bf16[64,1024]{1,0:T(8,128)(2,1)S(1)} %get-tuple-element.48), channel_id=1, source_target_pairs={{0,1},{1,0},{2,3},{3,2},{4,5},{5,4},{6,7},{7,6},{8,9},{9,8},{10,11... | collective-permute-start | bytes 393224 | tf_op jit(solution)/shard_map/ppermute | solution.py:30
  399.1 6.5 %collective-permute-done.41 = bf16[64,1024]{1,0:T(8,128)(2,1)S(1)} collective-permute-done((bf16[64,1024]{1,0:T(8,128)(2,1)S(1)}, bf16[64,1024]{1,0:T(8,128)(2,1)S(1)}, u32[]{:S(2)}, u32[]{:S(2)}) %collective-permute-start.41) | collective-permute-done | bytes 131104 | tf_op jit(solution)/shard_map/ppermute | solution.py:30
  405.8 5.7 %collective-permute-done.43 = bf16[64,1024]{1,0:T(8,128)(2,1)S(1)} collective-permute-done((bf16[64,1024]{1,0:T(8,128)(2,1)S(1)}, bf16[64,1024]{1,0:T(8,128)(2,1)S(1)}, u32[]{:S(2)}, u32[]{:S(2)}) %collective-permute-start.43) | collective-permute-done | bytes 131104 | tf_op jit(solution)/shard_map/ppermute | solution.py:30
  (152 shorter events, 79.9 us)
Async XLA Ops:
  7.2 149.8 %all-gather.2.cloned.1.call-start = ((), (), s32[]{:S(2)}) async-start(), calls=%async_computation.4 | async-start | bytes 5242880 | tf_op jit(solution)/shard_map/all_gather | solution.py:293
  21.3 18.7 %all-to-all-start = ((bf16[8,64,1024]{2,1,0:T(8,128)(2,1)}), bf16[8,64,1024]{2,1,0:T(8,128)(2,1)S(1)}, u32[]{:S(2)}, u32[]{:S(2)}) async-start(bf16[8,64,1024]{2,1,0:T(8,128)(2,1)} %bitcast.5), calls=%async_computation | async-start | bytes 2097152 | tf_op jit(solution)/shard_map/all_to_all | solution.py:300
  129.2 47.5 %all-to-all-start.2 = ((bf16[4,256,896]{2,1,0:T(8,128)(2,1)}), bf16[4,256,896]{2,1,0:T(8,128)(2,1)}, u32[]{:S(2)}, u32[]{:S(2)}) async-start(bf16[4,256,896]{2,1,0:T(8,128)(2,1)} %get-tuple-element.24), calls=%async_computation.2 | async-start | bytes 3670016 | tf_op jit(solution)/shard_map/all_to_all | solution.py:318
  140.2 14.9 %collective-permute-start.3 = (bf16[512,512]{1,0:T(8,128)(2,1)S(1)}, bf16[512,512]{1,0:T(8,128)(2,1)S(1)}, u32[]{:S(2)}, u32[]{:S(2)}) collective-permute-start(bf16[512,512]{1,0:T(8,128)(2,1)S(1)} %attention.1.refs_0_), channel_id=1, source_target_pairs={{0,8},{4,12},{8,0},{12,4},{1,9},{5,13},{9,1},{13,5},{2,10},{6,14},... | collective-permute-start | bytes 1572872 | tf_op jit(solution)/shard_map/ppermute | solution.py:30
  141.7 52.8 %collective-permute-start.18 = (bf16[1024,896]{1,0:T(8,128)(2,1)}, bf16[1024,896]{1,0:T(8,128)(2,1)}, u32[]{:S(2)}, u32[]{:S(2)}) collective-permute-start(bf16[1024,896]{1,0:T(8,128)(2,1)} %bitcast.9.refs_8_), channel_id=1, source_target_pairs={{0,8},{4,12},{8,0},{12,4},{1,9},{5,13},{9,1},{13,5},{2,10},{6,14},... | collective-permute-start | bytes 5505032 | tf_op jit(solution)/shard_map/ppermute | solution.py:30
  162.2 16.0 %collective-permute-start.5 = (bf16[256,1024]{1,0:T(8,128)(2,1)S(1)}, bf16[256,1024]{1,0:T(8,128)(2,1)S(1)}, u32[]{:S(2)}, u32[]{:S(2)}) collective-permute-start(bf16[256,1024]{1,0:T(8,128)(2,1)S(1)} %bitcast.19), channel_id=1, source_target_pairs={{0,16},{16,0},{1,17},{17,1},{2,18},{18,2},{3,19},{19,3},{4,20},{20... | collective-permute-start | bytes 1572872 | tf_op jit(solution)/shard_map/ppermute | solution.py:30
  163.5 77.6 %collective-permute-start.16 = (bf16[1024,896]{1,0:T(8,128)(2,1)}, bf16[1024,896]{1,0:T(8,128)(2,1)}, u32[]{:S(2)}, u32[]{:S(2)}) collective-permute-start(bf16[1024,896]{1,0:T(8,128)(2,1)} %bitcast.9.refs_8_), channel_id=1, source_target_pairs={{0,4},{4,0},{8,12},{12,8},{1,5},{5,1},{9,13},{13,9},{2,6},{6,2},{1... | collective-permute-start | bytes 5505032 | tf_op jit(solution)/shard_map/ppermute | solution.py:30
  176.7 63.9 %collective-permute-start.19 = (bf16[1024,896]{1,0:T(8,128)(2,1)}, bf16[1024,896]{1,0:T(8,128)(2,1)}, u32[]{:S(2)}, u32[]{:S(2)}) collective-permute-start(bf16[1024,896]{1,0:T(8,128)(2,1)} %bitcast.10.refs_9_), channel_id=1, source_target_pairs={{0,8},{4,12},{8,0},{12,4},{1,9},{5,13},{9,1},{13,5},{2,10},{6,14},... | collective-permute-start | bytes 5505032 | tf_op jit(solution)/shard_map/ppermute | solution.py:30
  179.6 56.9 %collective-permute-start.7 = (bf16[64,1024]{1,0:T(8,128)(2,1)S(1)}, bf16[64,1024]{1,0:T(8,128)(2,1)S(1)}, u32[]{:S(2)}, u32[]{:S(2)}) collective-permute-start(bf16[64,1024]{1,0:T(8,128)(2,1)S(1)} %get-tuple-element.56), channel_id=1, source_target_pairs={{0,8},{4,12},{8,0},{12,4},{1,9},{5,13},{9,1},{13,5},{2,10},{6,14},... | collective-permute-start | bytes 393224 | tf_op jit(solution)/shard_map/ppermute | solution.py:30
  180.1 114.8 %all-to-all-start.3 = ((bf16[4,896,256]{2,1,0:T(8,128)(2,1)}), bf16[4,896,256]{2,1,0:T(8,128)(2,1)S(1)}, u32[]{:S(2)}, u32[]{:S(2)}) async-start(bf16[4,896,256]{2,1,0:T(8,128)(2,1)} %bitcast.25), calls=%async_computation.3 | async-start | bytes 3670016 | tf_op jit(solution)/shard_map/all_to_all | solution.py:319
  184.1 53.1 %collective-permute-start.8 = (bf16[64,1024]{1,0:T(8,128)(2,1)S(1)}, bf16[64,1024]{1,0:T(8,128)(2,1)S(1)}, u32[]{:S(2)}, u32[]{:S(2)}) collective-permute-start(bf16[64,1024]{1,0:T(8,128)(2,1)S(1)} %get-tuple-element.55), channel_id=1, source_target_pairs={{0,12},{4,8},{8,4},{12,0},{1,13},{5,9},{9,5},{13,1},{2,14},{6,10},... | collective-permute-start | bytes 393224 | tf_op jit(solution)/shard_map/ppermute | solution.py:30
  194.5 101.9 %collective-permute-start.20 = (bf16[1024,896]{1,0:T(8,128)(2,1)}, bf16[1024,896]{1,0:T(8,128)(2,1)}, u32[]{:S(2)}, u32[]{:S(2)}) collective-permute-start(bf16[1024,896]{1,0:T(8,128)(2,1)} %collective-permute-done.18.refs_12_), channel_id=1, source_target_pairs={{0,4},{4,0},{8,12},{12,8},{1,5},{5,1},{9,13},{13,9},{2,6},{6,2},{1... | collective-permute-start | bytes 5505032 | tf_op jit(solution)/shard_map/ppermute | solution.py:30
  238.5 24.5 %collective-permute-start.9 = (bf16[64,4096]{1,0:T(8,128)(2,1)S(1)}, bf16[64,4096]{1,0:T(8,128)(2,1)S(1)}, u32[]{:S(2)}, u32[]{:S(2)}) collective-permute-start(bf16[64,4096]{1,0:T(8,128)(2,1)S(1)} %pad_maximum_fusion.refs_0_), channel_id=1, source_target_pairs={{0,1},{1,0},{2,3},{3,2},{4,5},{5,4},{6,7},{7,6},{8,9},{9,8},{10,11... | collective-permute-start | bytes 1572872 | tf_op jit(solution)/shard_map/ppermute | solution.py:30
  240.5 78.3 %collective-permute-start.17 = (bf16[1024,896]{1,0:T(8,128)(2,1)}, bf16[1024,896]{1,0:T(8,128)(2,1)}, u32[]{:S(2)}, u32[]{:S(2)}) collective-permute-start(bf16[1024,896]{1,0:T(8,128)(2,1)} %bitcast.10.refs_9_), channel_id=1, source_target_pairs={{0,4},{4,0},{8,12},{12,8},{1,5},{5,1},{9,13},{13,9},{2,6},{6,2},{1... | collective-permute-start | bytes 5505032 | tf_op jit(solution)/shard_map/ppermute | solution.py:30
  240.5 78.3 %collective-permute-start.21 = (bf16[1024,896]{1,0:T(8,128)(2,1)}, bf16[1024,896]{1,0:T(8,128)(2,1)}, u32[]{:S(2)}, u32[]{:S(2)}) collective-permute-start(bf16[1024,896]{1,0:T(8,128)(2,1)} %collective-permute-done.19.refs_13_), channel_id=1, source_target_pairs={{0,4},{4,0},{8,12},{12,8},{1,5},{5,1},{9,13},{13,9},{2,6},{6,2},{1... | collective-permute-start | bytes 5505032 | tf_op jit(solution)/shard_map/ppermute | solution.py:30
  241.1 38.2 %collective-permute-start.10 = (bf16[64,4096]{1,0:T(8,128)(2,1)S(1)}, bf16[64,4096]{1,0:T(8,128)(2,1)S(1)}, u32[]{:S(2)}, u32[]{:S(2)}) collective-permute-start(bf16[64,4096]{1,0:T(8,128)(2,1)S(1)} %pad_maximum_fusion.refs_0_), channel_id=1, source_target_pairs={{0,2},{1,3},{2,0},{3,1},{4,6},{5,7},{6,4},{7,5},{8,10},{9,11},{10,... | collective-permute-start | bytes 1572872 | tf_op jit(solution)/shard_map/ppermute | solution.py:30
  263.1 16.4 %collective-permute-start.11 = (bf16[64,4096]{1,0:T(8,128)(2,1)S(1)}, bf16[64,4096]{1,0:T(8,128)(2,1)S(1)}, u32[]{:S(2)}, u32[]{:S(2)}) collective-permute-start(bf16[64,4096]{1,0:T(8,128)(2,1)S(1)} %pad_maximum_fusion.refs_0_), channel_id=1, source_target_pairs={{0,3},{1,2},{2,1},{3,0},{4,7},{5,6},{6,5},{7,4},{8,11},{9,10},{10,... | collective-permute-start | bytes 1572872 | tf_op jit(solution)/shard_map/ppermute | solution.py:30
  279.5 26.0 %collective-permute-start.13 = (bf16[64,4096]{1,0:T(8,128)(2,1)S(1)}, bf16[64,4096]{1,0:T(8,128)(2,1)}, u32[]{:S(2)}, u32[]{:S(2)}) collective-permute-start(bf16[64,4096]{1,0:T(8,128)(2,1)S(1)} %collective-permute-done.9.refs_1_), channel_id=1, source_target_pairs={{0,16},{16,0},{1,17},{17,1},{2,18},{18,2},{3,19},{19,3},{4,20},{20... | collective-permute-start | bytes 1572872 | tf_op jit(solution)/shard_map/ppermute | solution.py:30
  294.9 39.9 %collective-permute-start.32 = (bf16[4,896,256]{2,1,0:T(8,128)(2,1)S(1)}, bf16[4,896,256]{2,1,0:T(8,128)(2,1)S(1)}, u32[]{:S(2)}, u32[]{:S(2)}) collective-permute-start(bf16[4,896,256]{2,1,0:T(8,128)(2,1)S(1)} %all-to-all-done.3.weights_ref), channel_id=1, source_target_pairs={{0,8},{4,12},{8,0},{12,4},{1,9},{5,13},{9,1},{13,5},{2,10},{6,14},... | collective-permute-start | bytes 5505032 | tf_op jit(solution)/shard_map/ppermute | solution.py:30
  296.4 16.8 %collective-permute-start.14 = (bf16[64,4096]{1,0:T(8,128)(2,1)S(1)}, bf16[64,4096]{1,0:T(8,128)(2,1)S(1)}, u32[]{:S(2)}, u32[]{:S(2)}) collective-permute-start(bf16[64,4096]{1,0:T(8,128)(2,1)S(1)} %collective-permute-done.10.refs_2_), channel_id=1, source_target_pairs={{0,16},{16,0},{1,17},{17,1},{2,18},{18,2},{3,19},{19,3},{4,20},{20... | collective-permute-start | bytes 1572872 | tf_op jit(solution)/shard_map/ppermute | solution.py:30
  313.2 53.2 %collective-permute-start.26 = (bf16[4,896,256]{2,1,0:T(8,128)(2,1)S(1)}, bf16[4,896,256]{2,1,0:T(8,128)(2,1)S(1)}, u32[]{:S(2)}, u32[]{:S(2)}) collective-permute-start(bf16[4,896,256]{2,1,0:T(8,128)(2,1)S(1)} %all-to-all-done.3.weights_ref), channel_id=1, source_target_pairs={{0,4},{4,0},{8,12},{12,8},{1,5},{5,1},{9,13},{13,9},{2,6},{6,2},{1... | collective-permute-start | bytes 5505032 | tf_op jit(solution)/shard_map/ppermute | solution.py:30
  334.8 39.4 %collective-permute-start.38 = (bf16[4,896,256]{2,1,0:T(8,128)(2,1)S(1)}, bf16[4,896,256]{2,1,0:T(8,128)(2,1)S(1)}, u32[]{:S(2)}, u32[]{:S(2)}) collective-permute-start(bf16[4,896,256]{2,1,0:T(8,128)(2,1)S(1)} %collective-permute-done.32.weights_ref), channel_id=1, source_target_pairs={{0,4},{4,0},{8,12},{12,8},{1,5},{5,1},{9,13},{13,9},{2,6},{6,2},{1... | collective-permute-start | bytes 5505032 | tf_op jit(solution)/shard_map/ppermute | solution.py:30
  369.7 15.3 %collective-permute-start.34 = (bf16[64,1024]{1,0:T(8,128)(2,1)S(1)}, bf16[64,1024]{1,0:T(8,128)(2,1)S(1)}, u32[]{:S(2)}, u32[]{:S(2)}) collective-permute-start(bf16[64,1024]{1,0:T(8,128)(2,1)S(1)} %get-tuple-element.45), channel_id=1, source_target_pairs={{0,1},{1,0},{2,3},{3,2},{4,5},{5,4},{6,7},{7,6},{8,9},{9,8},{10,11... | collective-permute-start | bytes 393224 | tf_op jit(solution)/shard_map/ppermute | solution.py:30
  387.5 18.3 %collective-permute-start.37 = (bf16[64,1024]{1,0:T(8,128)(2,1)S(1)}, bf16[64,1024]{1,0:T(8,128)(2,1)S(1)}, u32[]{:S(2)}, u32[]{:S(2)}) collective-permute-start(bf16[64,1024]{1,0:T(8,128)(2,1)S(1)} %fusion.17), channel_id=1, source_target_pairs={{0,8},{4,12},{8,0},{12,4},{1,9},{5,13},{9,1},{13,5},{2,10},{6,14},... | collective-permute-start | bytes 393224 | tf_op jit(solution)/shard_map/ppermute | solution.py:30
  (36 other events, 357.5 us)
Sparse Core Ops, SparseCore 0:
  9.6 122.5 all-gather.1

commit v4 on v3

--- a/solution.py
+++ b/solution.py
@@ -184,23 +184,23 @@
     )(place, *blocks, weights)
 
 
-def gate_up_kernel(token_count, block_count, *refs):
-    tokens = refs[:token_count]
-    weights = refs[token_count : token_count + 2 * block_count]
-    out_ref, held, near, gate, up, token_sems, weight_sems = refs[token_count + 2 * block_count :]
-    piece = held.shape[0] // token_count
-    token_copies = [
-        pltpu.make_async_copy(ref, held.at[pl.ds(j * piece, piece)], token_sems.at[j]) for j, ref in enumerate(tokens)
-    ]
-    weight_copies = [pltpu.make_async_copy(ref, near.at[j], weight_sems.at[j]) for j, ref in enumerate(weights)]
-    for copy in token_copies + weight_copies:
+def gate_up_kernel(block_count, *refs):
+    tokens = refs[0]
+    weights = refs[1 : 1 + 2 * block_count]
+    out_ref, held, near, gate, up, token_sems, weight_sems = refs[1 + 2 * block_count :]
+    depth = near.shape[1]
+    copies = []
+    for a in range(block_count):
+        cols = slice(a * depth, (a + 1) * depth)
+        copies.append(pltpu.make_async_copy(tokens.at[:, cols], held.at[:, cols], token_sems.at[a]))
+        for j in (2 * a, 2 * a + 1):
+            copies.append(pltpu.make_async_copy(weights[j], near.at[j], weight_sems.at[j]))
+    for copy in copies:
         copy.start()
-    for copy in token_copies:
-        copy.wait()
-    depth = near.shape[1]
     for a in range(block_count):
+        copies[3 * a].wait()
         for which, total in enumerate((gate, up)):
-            weight_copies[2 * a + which].wait()
+            copies[3 * a + 1 + which].wait()
             for rows in row_tiles(held.shape[0]):
                 product = jnp.dot(
                     held[rows, a * depth : (a + 1) * depth], near[2 * a + which], preferred_element_type=jnp.float32
@@ -211,14 +211,12 @@
 
 
 def gate_up(tokens, gates, ups):
-    if len(tokens) > 8:
-        tokens = [jnp.concatenate(tokens, axis=0)]
-    rows = sum(piece.shape[0] for piece in tokens)
+    rows = tokens.shape[0]
     depth, cols = gates[0].shape
     weights = [block for pair in zip(gates, ups) for block in pair]
     return pl.pallas_call(
-        functools.partial(gate_up_kernel, len(tokens), len(gates)),
-        in_specs=[ANY] * (len(tokens) + len(weights)),
+        functools.partial(gate_up_kernel, len(gates)),
+        in_specs=[ANY] * (1 + len(weights)),
         out_specs=VMEM,
         out_shape=jax.ShapeDtypeStruct((rows, cols), jnp.bfloat16),
         scratch_shapes=[
@@ -226,7 +224,7 @@
             pltpu.VMEM((len(weights), depth, cols), jnp.bfloat16),
             pltpu.VMEM((rows, cols), jnp.float32),
             pltpu.VMEM((rows, cols), jnp.float32),
-            pltpu.SemaphoreType.DMA((len(tokens),)),
+            pltpu.SemaphoreType.DMA((len(gates),)),
             pltpu.SemaphoreType.DMA((len(weights),)),
         ],
         compiler_params=pltpu.CompilerParams(vmem_limit_bytes=VMEM_LIMIT),
@@ -236,29 +234,35 @@
             transcendentals=rows * cols,
         ),
         name="gate_up",
-    )(*tokens, *weights)
-
-
-def down_kernel(activated_ref, weights_ref, kept_ref, sent_ref):
+    )(tokens, *weights)
+
+
+def down_kernel(place_ref, activated_ref, weights_ref, kept_ref, sent_ref):
     sources, _, cols = weights_ref.shape
-    kept_rows = kept_ref.shape[0]
-    for s in range(sources):
-        at = slice(s * cols, (s + 1) * cols)
-        for e in range(sent_ref.shape[0] + 1):
-            rows = slice(e * kept_rows, (e + 1) * kept_rows)
-            product = jnp.dot(activated_ref[rows, :], weights_ref[s], preferred_element_type=jnp.float32)
+    head_count = sent_ref.shape[0] + 1
+    head = place_ref[1]
+    piece = kept_ref.shape[0] // sources
+    for e in range(head_count):
+        rows = []
+        for o in range(sources):
+            first = pl.multiple_of((o * head_count + (head ^ e)) * piece, piece)
+            rows.append(activated_ref[pl.ds(first, piece), :])
+        rows = jnp.concatenate(rows, axis=0)
+        for s in range(sources):
+            at = slice(s * cols, (s + 1) * cols)
+            product = jnp.dot(rows, weights_ref[s], preferred_element_type=jnp.float32)
             if e == 0:
                 kept_ref[:, at] = product.astype(jnp.bfloat16)
             else:
                 sent_ref[e - 1, :, at] = product.astype(jnp.bfloat16)
 
 
-def down_product(activated, weights, head_count):
+def down_product(activated, weights, place, head_count):
     rows = activated.shape[0] // head_count
     sources, depth, cols = weights.shape
     return pl.pallas_call(
         down_kernel,
-        in_specs=[VMEM, VMEM],
+        in_specs=[SMEM, VMEM, VMEM],
         out_specs=[VMEM, VMEM],
         out_shape=[
             jax.ShapeDtypeStruct((rows, sources * cols), jnp.bfloat16),
@@ -271,7 +275,7 @@
             transcendentals=0,
         ),
         name="down",
-    )(activated, weights)
+    )(place, activated, weights)
 
 
 def per_device(query, key, value, doc_lengths, resid, norm_gain, w_out, w_gate_up, w_down):
@@ -313,14 +317,6 @@
         own_context = attention(packed, halo, 0, starts, reach)
         blocks = [lax.all_gather(own_context, "inner", axis=0, tiled=True)]
 
-    spread = functools.partial(lax.all_to_all, axis_name="outer", split_axis=0, concat_axis=0, tiled=True)
-    gate_here = spread(after(w_gate, packed))
-    up_here = spread(after(w_up, gate_here))
-    down_here = spread(after(w_down.reshape(outer_count, hidden_cols, feature_rows), up_here))
-    gates = blocks_over_inner(gate_here.reshape(-1, hidden_cols))
-    ups = blocks_over_inner(up_here.reshape(-1, hidden_cols))
-    downs = blocks_over_inner(down_here)
-
     place = jnp.stack([inner, head]).astype(jnp.int32)
     kept, sent, *whole = projection(blocks, weights_out, place, head_count, inner_count)
     context = whole[0] if whole else own_context
@@ -338,20 +334,28 @@
     squares = sum([jnp.sum(block * block, axis=1, keepdims=True) for block in state])
     inverse = lax.rsqrt(squares / D + 1e-05)
     normed = jnp.concatenate([block * inverse for block in state], axis=1).astype(jnp.bfloat16)
-    along_outer = [swap(normed, "outer", d) for d in range(outer_count)]
-    tokens = [swap(block, "head", e) for e in range(head_count) for block in along_outer]
+    tokens = lax.all_gather(normed, ("outer", "head"), axis=0, tiled=True)
+
+    spread = functools.partial(lax.all_to_all, axis_name="outer", split_axis=0, concat_axis=0, tiled=True)
+    gate_here = spread(after(w_gate, kept))
+    up_here = spread(after(w_up, hidden_part))
+    down_here = spread(after(w_down.reshape(outer_count, hidden_cols, feature_rows), tokens))
+    gates = blocks_over_inner(after(gate_here, normed).reshape(-1, hidden_cols))
+    ups = blocks_over_inner(after(up_here, normed).reshape(-1, hidden_cols))
+    downs = blocks_over_inner(down_here)
 
     activated = gate_up(tokens, gates, ups)
     layer_out = jnp.zeros((half, D // inner_count), jnp.bfloat16)
     for a in range(inner_count):
-        kept, sent = down_product(activated, downs[a], head_count)
+        kept, sent = down_product(activated, downs[a], place, head_count)
         paired = kept.astype(jnp.float32)
         for e in range(1, head_count):
             paired = paired + swap(sent[e - 1], "head", e).astype(jnp.float32)
         paired = paired.reshape(outer_count, own_rows, -1)
-        total = state[a] + paired[0]
+        total = state[a] + lax.dynamic_index_in_dim(paired, outer, 0, False)
         for d in range(1, outer_count):
-            total = total + swap(paired[d].astype(jnp.bfloat16), "outer", d).astype(jnp.float32)
+            sent = lax.dynamic_index_in_dim(paired, outer ^ d, 0, False).astype(jnp.bfloat16)
+            total = total + swap(sent, "outer", d).astype(jnp.float32)
         block = swap(total.astype(jnp.bfloat16), "inner", a)
         layer_out = lax.dynamic_update_slice(layer_out, block, ((inner ^ a) * own_rows, 0))
     return (context, layer_out)

time: 420 us -> 488 us (1.16)
  waiting for transfers between devices: 191 us -> 346 us
  blocking collectives: 89.2 us -> 0 us
  starting transfers between devices: 76.6 us -> 63.6 us
  local copies, waits for them, and re-layouts: 10.3 us -> 18.9 us
    all_to_all x2 -> x3, waiting for transfers between devices: 13.2 us -> 159 us  [the longest x1 80.8 us: per_device(): gate_here = spread(after(w_gate, kept))]
    all_to_all x1 -> x0, blocking collectives: 89.2 us -> none  [per_device(): gate_here = spread(after(w_gate, packed))]
    ppermute x42 -> x35, waiting for transfers between devices: 168 us -> 136 us  [swap(): return lax.ppermute(array, axis, [(s, s ^ distance) for s in range(count)])]
    all_gather x1, waiting for transfers between devices: 0.01 us -> 31.3 us  [per_device(): weights_out = lax.all_gather(w_out, 'outer', axis=1, tiled=True)]
    ppermute x42 -> x35, starting transfers between devices: 55.9 us -> 39.8 us  [swap(): return lax.ppermute(array, axis, [(s, s ^ distance) for s in range(count)])]
    unnamed x28 -> x44, local copies, waits for them, and re-layouts: 4.59 us -> 12.3 us
    pallas_call x5, Pallas kernels: 17.2 us -> 22.4 us  [the longest x1 11.5 us: gate_up(): pl.pallas_call(functools.partial(gate_up_kernel, len(gates)), in_specs=[A...]
    all_to_all x2 -> x3, starting transfers between devices: 8.54 us -> 11.6 us  [the longest x1 4.4 us: per_device(): up_here = spread(after(w_up, hidden_part))]
  transfers between devices with their start and end apart: 48 -> 43, of which waited for: 21 -> 20; matrix products, arithmetic and copies ran while one was open for 3% -> 2% of each run, Pallas kernels for 8% -> 6%
where the time goes in v4:
time: 488 us; the launch traced here: 487 us
  waiting for transfers between devices  346 us (71%)
  starting transfers between devices  63.6 us (13%)
  Pallas kernels  36.8 us (8%)
  local copies, waits for them, and re-layouts  18.9 us (4%)
  between operations  14.6 us (3%)
  other arithmetic  7.43 us (2%)
    ppermute x35, waiting for transfers between devices, swap(): return lax.ppermute(array, axis, [(s, s ^ distance) for s in range(count)])  136 us
    all_to_all x1, waiting for transfers between devices, per_device(): gate_here = spread(after(w_gate, kept))  80.8 us
    ppermute x35, starting transfers between devices, swap(): return lax.ppermute(array, axis, [(s, s ^ distance) for s in range(count)])  39.8 us
    all_to_all x1, waiting for transfers between devices, per_device(): spread(after(w_down.reshape(outer_count, hidden_cols, feature_rows), toke...  39.6 us
    all_to_all x1, waiting for transfers between devices, per_device(): up_here = spread(after(w_up, hidden_part))  38.8 us
    all_gather x1, waiting for transfers between devices, per_device(): weights_out = lax.all_gather(w_out, 'outer', axis=1, tiled=True)  31.3 us
    all_to_all x1, waiting for transfers between devices, per_device(): lax.all_to_all(groups, ('inner', 'head'), split_axis=0, concat_axis=0, ti...  14.4 us
    unnamed x44, local copies, waits for them, and re-layouts  12.3 us
  transfers between devices with their start and end apart: 43, of which 20 were waited for; matrix products, arithmetic and copies ran while one was open for 2% of the time, Pallas kernels for 6%

profile of v4, /device:TPU:0, one launch (start us, length us, event | category | flops | bytes accessed | tf_op | source)
XLA Modules:
  0.0 487.3 jit_solution(11831614486877397184)
XLA Ops:
  7.9 4.9 %collective-permute-start = (bf16[64,1024]{1,0:T(8,128)(2,1)}, bf16[64,1024]{1,0:T(8,128)(2,1)S(1)}, u32[]{:S(2)}, u32[]{:S(2)}) collective-permute-start(bf16[64,1024]{1,0:T(8,128)(2,1)} %param.10), channel_id=1, source_target_pairs={{0,1},{1,2},{2,3},{4,5},{5,6},{6,7},{8,9},{9,10},{10,11},{12,13},{... | collective-permute-start | bytes 393224 | tf_op jit(solution)/shard_map/ppermute | solution.py:301
  12.9 3.5 collective-permute-start.1
  21.3 3.7 all-to-all-start
  25.6 14.4 %all-to-all-done = bf16[8,64,1024]{2,1,0:T(8,128)(2,1)S(1)} async-done(((bf16[8,64,1024]{2,1,0:T(8,128)(2,1)}), bf16[8,64,1024]{2,1,0:T(8,128)(2,1)S(1)}, u32[]{:S(2)}, u32[]{:S(2)}) %all-to-all-start) | async-done | bytes 1048608 | tf_op jit(solution)/shard_map/all_to_all | solution.py:304
  40.0 5.9 %attention.1.refs_0_ = bf16[512,512]{1,0:T(8,128)(2,1)S(1)} custom-call(s32[512,1]{1,0:T(8,128)S(1)} %copy.19.starts_ref, bf16[512,1024]{1,0:T(8,128)(2,1)S(1)} %bitcast.54, bf16[512,1024]{1,0:T(8,128)(2,1)S(1)} %bitcast.55, bf16[512,1024]{1,0:T(8,128)(2,1)S(1)} %bitcast.56), custom_call_target="tpu_custom_call" | custom-call | flops 671088640 | bytes 1048576 | tf_op jit(solution)/shard_map/attention/pallas_call | solution.py:94
  47.0 12.7 %collective-permute-done.3.refs_2_ = bf16[512,512]{1,0:T(8,128)(2,1)S(1)} collective-permute-done((bf16[512,512]{1,0:T(8,128)(2,1)S(1)}, bf16[512,512]{1,0:T(8,128)(2,1)S(1)}, u32[]{:S(2)}, u32[]{:S(2)}) %collective-permute-start.3) | collective-permute-done | bytes 524320 | tf_op jit(solution)/shard_map/ppermute | solution.py:30
  61.5 31.3 %all-gather.3.cloned.1.call-done.refs_4_ = bf16[2048,1024]{1,0:T(8,128)(2,1)} async-done(((bf16[2048,256]{1,0:T(8,128)(2,1)}), bf16[2048,1024]{1,0:T(8,128)(2,1)}) %all-gather.3.cloned.1.call-update) | async-done | bytes 4194320 | tf_op jit(solution)/shard_map/all_gather | solution.py:297
  92.9 5.3 %projection.1 = (bf16[256,1024]{1,0:T(8,128)(2,1)S(1)}, bf16[1,256,1024]{2,1,0:T(8,128)(2,1)S(1)}, bf16[128,2048]{1,0:T(8,128)(2,1)}) custom-call(s32[2]{0:T(128)S(1)} %pad_add_fusion.place_ref, bf16[512,512]{1,0:T(8,128)(2,1)S(1)} %attention.1.refs_0_, bf16[512,512]{1,0:T(8,128)(2,1)S(1)} %collective-permute-done.2.refs_1_, ...), custom_call_target="tpu_custom_call" | custom-call | flops 2147483648 | bytes 6291456 | tf_op jit(solution)/shard_map/projection/pallas_call | solution.py:174
  99.6 12.3 %collective-permute-done.5 = bf16[256,1024]{1,0:T(8,128)(2,1)S(1)} collective-permute-done((bf16[256,1024]{1,0:T(8,128)(2,1)S(1)}, bf16[256,1024]{1,0:T(8,128)(2,1)S(1)}, u32[]{:S(2)}, u32[]{:S(2)}) %collective-permute-start.5) | collective-permute-done | bytes 524320 | tf_op jit(solution)/shard_map/ppermute | solution.py:30
  128.8 3.6 all-to-all-start.1
  132.4 80.8 %all-to-all-done.1 = bf16[4,256,896]{2,1,0:T(8,128)(2,1)S(1)} async-done(((bf16[4,256,896]{2,1,0:T(8,128)(2,1)}), bf16[4,256,896]{2,1,0:T(8,128)(2,1)S(1)}, u32[]{:S(2)}, u32[]{:S(2)}) %all-to-all-start.1) | async-done | bytes 1835040 | tf_op jit(solution)/shard_map/all_to_all | solution.py:340
  214.4 4.4 all-to-all-start.2
  218.8 4.3 all-gather.5.cloned.1.call-done.refs_0_
  223.1 38.8 %all-to-all-done.2 = bf16[4,256,896]{2,1,0:T(8,128)(2,1)} async-done(((bf16[4,256,896]{2,1,0:T(8,128)(2,1)}), bf16[4,256,896]{2,1,0:T(8,128)(2,1)}, u32[]{:S(2)}, u32[]{:S(2)}) %all-to-all-start.2) | async-done | bytes 1835040 | tf_op jit(solution)/shard_map/all_to_all | solution.py:341
  261.9 3.6 all-to-all-start.3
  268.1 39.6 %all-to-all-done.3.weights_ref = bf16[4,896,256]{2,1,0:T(8,128)(2,1)S(1)} async-done(((bf16[4,896,256]{2,1,0:T(8,128)(2,1)}), bf16[4,896,256]{2,1,0:T(8,128)(2,1)S(1)}, u32[]{:S(2)}, u32[]{:S(2)}) %all-to-all-start.3) | async-done | bytes 1835040 | tf_op jit(solution)/shard_map/all_to_all | solution.py:342
  309.6 38.6 %collective-permute-done.12.refs_6_ = bf16[1024,896]{1,0:T(8,128)(2,1)} collective-permute-done((bf16[1024,896]{1,0:T(8,128)(2,1)}, bf16[1024,896]{1,0:T(8,128)(2,1)}, u32[]{:S(2)}, u32[]{:S(2)}) %collective-permute-start.12) | collective-permute-done | bytes 1835040 | tf_op jit(solution)/shard_map/ppermute | solution.py:30
  348.7 37.1 %collective-permute-done.25.weights_ref = bf16[4,896,256]{2,1,0:T(8,128)(2,1)} collective-permute-done((bf16[4,896,256]{2,1,0:T(8,128)(2,1)S(1)}, bf16[4,896,256]{2,1,0:T(8,128)(2,1)}, u32[]{:S(2)}, u32[]{:S(2)}) %collective-permute-start.25) | collective-permute-done | bytes 1835040 | tf_op jit(solution)/shard_map/ppermute | solution.py:30
  389.8 11.5 %gate_up.1.activated_ref = bf16[512,896]{1,0:T(8,128)(2,1)S(1)} custom-call(bf16[512,4096]{1,0:T(8,128)(2,1)} %all-gather.5.cloned.1.call-done.refs_0_, bf16[1024,896]{1,0:T(8,128)(2,1)S(1)} %bitcast.59, bf16[1024,896]{1,0:T(8,128)(2,1)} %bitcast.10.refs_2_, bf16[1024,896]{1,0:T(8,128)(2,1)} %collective-permute-done.9.refs_3_, ...), custom_call_target="tpu_custom_call" | custom-call | flops 7516192768 | bytes 18874368 | tf_op jit(solution)/shard_map/gate_up/pallas_call | solution.py:217
  410.0 9.0 %collective-permute-done.15 = bf16[256,1024]{1,0:T(8,128)(2,1)} collective-permute-done((bf16[256,1024]{1,0:T(8,128)(2,1)}, bf16[256,1024]{1,0:T(8,128)(2,1)}, u32[]{:S(2)}, u32[]{:S(2)}) %collective-permute-start.15) | collective-permute-done | bytes 524320 | tf_op jit(solution)/shard_map/ppermute | solution.py:30
  430.9 4.2 collective-permute-done.17
  457.4 5.5 %collective-permute-start.33 = (bf16[64,1024]{1,0:T(8,128)(2,1)S(1)}, bf16[64,1024]{1,0:T(8,128)(2,1)S(1)}, u32[]{:S(2)}, u32[]{:S(2)}) collective-permute-start(bf16[64,1024]{1,0:T(8,128)(2,1)S(1)} %get-tuple-element.38), channel_id=1, source_target_pairs={{0,1},{1,0},{2,3},{3,2},{4,5},{5,4},{6,7},{7,6},{8,9},{9,8},{10,11... | collective-permute-start | bytes 393224 | tf_op jit(solution)/shard_map/ppermute | solution.py:30
  467.9 6.1 %collective-permute-done.34 = bf16[64,1024]{1,0:T(8,128)(2,1)S(1)} collective-permute-done((bf16[64,1024]{1,0:T(8,128)(2,1)S(1)}, bf16[64,1024]{1,0:T(8,128)(2,1)S(1)}, u32[]{:S(2)}, u32[]{:S(2)}) %collective-permute-start.34) | collective-permute-done | bytes 131104 | tf_op jit(solution)/shard_map/ppermute | solution.py:30
  474.3 5.4 %collective-permute-done.36 = bf16[64,1024]{1,0:T(8,128)(2,1)S(1)} collective-permute-done((bf16[64,1024]{1,0:T(8,128)(2,1)S(1)}, bf16[64,1024]{1,0:T(8,128)(2,1)S(1)}, u32[]{:S(2)}, u32[]{:S(2)}) %collective-permute-start.36) | collective-permute-done | bytes 131104 | tf_op jit(solution)/shard_map/ppermute | solution.py:30
  (158 shorter events, 86.3 us)
Async XLA Ops:
  7.2 85.7 %all-gather.3.cloned.1.call-start = ((), (), s32[]{:S(2)}) async-start(), calls=%async_computation.4 | async-start | bytes 5242880 | tf_op jit(solution)/shard_map/all_gather | solution.py:297
  21.3 18.7 %all-to-all-start = ((bf16[8,64,1024]{2,1,0:T(8,128)(2,1)}), bf16[8,64,1024]{2,1,0:T(8,128)(2,1)S(1)}, u32[]{:S(2)}, u32[]{:S(2)}) async-start(bf16[8,64,1024]{2,1,0:T(8,128)(2,1)} %bitcast.5), calls=%async_computation | async-start | bytes 2097152 | tf_op jit(solution)/shard_map/all_to_all | solution.py:304
  25.0 198.1 %all-gather.5.cloned.1.call-start = ((), (), s32[]{:S(2)}) async-start(), calls=%async_computation.5 | async-start | bytes 4718592 | tf_op jit(solution)/shard_map/all_gather | solution.py:337
  45.9 13.7 %collective-permute-start.3 = (bf16[512,512]{1,0:T(8,128)(2,1)S(1)}, bf16[512,512]{1,0:T(8,128)(2,1)S(1)}, u32[]{:S(2)}, u32[]{:S(2)}) collective-permute-start(bf16[512,512]{1,0:T(8,128)(2,1)S(1)} %attention.1.refs_0_), channel_id=1, source_target_pairs={{0,8},{4,12},{8,0},{12,4},{1,9},{5,13},{9,1},{13,5},{2,10},{6,14},... | collective-permute-start | bytes 1572872 | tf_op jit(solution)/shard_map/ppermute | solution.py:30
  98.2 13.8 %collective-permute-start.5 = (bf16[256,1024]{1,0:T(8,128)(2,1)S(1)}, bf16[256,1024]{1,0:T(8,128)(2,1)S(1)}, u32[]{:S(2)}, u32[]{:S(2)}) collective-permute-start(bf16[256,1024]{1,0:T(8,128)(2,1)S(1)} %bitcast.63), channel_id=1, source_target_pairs={{0,16},{16,0},{1,17},{17,1},{2,18},{18,2},{3,19},{19,3},{4,20},{20... | collective-permute-start | bytes 1572872 | tf_op jit(solution)/shard_map/ppermute | solution.py:30
  128.8 84.3 %all-to-all-start.1 = ((bf16[4,256,896]{2,1,0:T(8,128)(2,1)}), bf16[4,256,896]{2,1,0:T(8,128)(2,1)S(1)}, u32[]{:S(2)}, u32[]{:S(2)}) async-start(bf16[4,256,896]{2,1,0:T(8,128)(2,1)} %copy-done.3), calls=%async_computation.1 | async-start | bytes 3670016 | tf_op jit(solution)/shard_map/all_to_all | solution.py:340
  214.4 47.5 %all-to-all-start.2 = ((bf16[4,256,896]{2,1,0:T(8,128)(2,1)}), bf16[4,256,896]{2,1,0:T(8,128)(2,1)}, u32[]{:S(2)}, u32[]{:S(2)}) async-start(bf16[4,256,896]{2,1,0:T(8,128)(2,1)} %copy-done.2), calls=%async_computation.2 | async-start | bytes 3670016 | tf_op jit(solution)/shard_map/all_to_all | solution.py:341
  261.9 45.8 %all-to-all-start.3 = ((bf16[4,896,256]{2,1,0:T(8,128)(2,1)}), bf16[4,896,256]{2,1,0:T(8,128)(2,1)S(1)}, u32[]{:S(2)}, u32[]{:S(2)}) async-start(bf16[4,896,256]{2,1,0:T(8,128)(2,1)} %bitcast.73), calls=%async_computation.3 | async-start | bytes 3670016 | tf_op jit(solution)/shard_map/all_to_all | solution.py:342
  265.5 44.0 %collective-permute-start.11 = (bf16[1024,896]{1,0:T(8,128)(2,1)}, bf16[1024,896]{1,0:T(8,128)(2,1)}, u32[]{:S(2)}, u32[]{:S(2)}) collective-permute-start(bf16[1024,896]{1,0:T(8,128)(2,1)} %bitcast.57), channel_id=1, source_target_pairs={{0,8},{4,12},{8,0},{12,4},{1,9},{5,13},{9,1},{13,5},{2,10},{6,14},... | collective-permute-start | bytes 5505032 | tf_op jit(solution)/shard_map/ppermute | solution.py:30
  267.2 81.0 %collective-permute-start.12 = (bf16[1024,896]{1,0:T(8,128)(2,1)}, bf16[1024,896]{1,0:T(8,128)(2,1)}, u32[]{:S(2)}, u32[]{:S(2)}) collective-permute-start(bf16[1024,896]{1,0:T(8,128)(2,1)} %bitcast.10.refs_2_), channel_id=1, source_target_pairs={{0,8},{4,12},{8,0},{12,4},{1,9},{5,13},{9,1},{13,5},{2,10},{6,14},... | collective-permute-start | bytes 5505032 | tf_op jit(solution)/shard_map/ppermute | solution.py:30
  267.6 80.6 %collective-permute-start.9 = (bf16[1024,896]{1,0:T(8,128)(2,1)}, bf16[1024,896]{1,0:T(8,128)(2,1)}, u32[]{:S(2)}, u32[]{:S(2)}) collective-permute-start(bf16[1024,896]{1,0:T(8,128)(2,1)} %bitcast.58), channel_id=1, source_target_pairs={{0,4},{4,0},{8,12},{12,8},{1,5},{5,1},{9,13},{13,9},{2,6},{6,2},{1... | collective-permute-start | bytes 5505032 | tf_op jit(solution)/shard_map/ppermute | solution.py:30
  267.6 118.2 %collective-permute-start.10 = (bf16[1024,896]{1,0:T(8,128)(2,1)}, bf16[1024,896]{1,0:T(8,128)(2,1)}, u32[]{:S(2)}, u32[]{:S(2)}) collective-permute-start(bf16[1024,896]{1,0:T(8,128)(2,1)} %bitcast.10.refs_2_), channel_id=1, source_target_pairs={{0,4},{4,0},{8,12},{12,8},{1,5},{5,1},{9,13},{13,9},{2,6},{6,2},{1... | collective-permute-start | bytes 5505032 | tf_op jit(solution)/shard_map/ppermute | solution.py:30
  307.7 78.1 %collective-permute-start.25 = (bf16[4,896,256]{2,1,0:T(8,128)(2,1)S(1)}, bf16[4,896,256]{2,1,0:T(8,128)(2,1)}, u32[]{:S(2)}, u32[]{:S(2)}) collective-permute-start(bf16[4,896,256]{2,1,0:T(8,128)(2,1)S(1)} %all-to-all-done.3.weights_ref), channel_id=1, source_target_pairs={{0,8},{4,12},{8,0},{12,4},{1,9},{5,13},{9,1},{13,5},{2,10},{6,14},... | collective-permute-start | bytes 5505032 | tf_op jit(solution)/shard_map/ppermute | solution.py:30
  309.5 76.2 %collective-permute-start.13 = (bf16[1024,896]{1,0:T(8,128)(2,1)}, bf16[1024,896]{1,0:T(8,128)(2,1)S(1)}, u32[]{:S(2)}, u32[]{:S(2)}) collective-permute-start(bf16[1024,896]{1,0:T(8,128)(2,1)} %collective-permute-done.11.refs_5_), channel_id=1, source_target_pairs={{0,4},{4,0},{8,12},{12,8},{1,5},{5,1},{9,13},{13,9},{2,6},{6,2},{1... | collective-permute-start | bytes 5505032 | tf_op jit(solution)/shard_map/ppermute | solution.py:30
  348.2 37.6 %collective-permute-start.14 = (bf16[1024,896]{1,0:T(8,128)(2,1)}, bf16[1024,896]{1,0:T(8,128)(2,1)S(1)}, u32[]{:S(2)}, u32[]{:S(2)}) collective-permute-start(bf16[1024,896]{1,0:T(8,128)(2,1)} %collective-permute-done.12.refs_6_), channel_id=1, source_target_pairs={{0,4},{4,0},{8,12},{12,8},{1,5},{5,1},{9,13},{13,9},{2,6},{6,2},{1... | collective-permute-start | bytes 5505032 | tf_op jit(solution)/shard_map/ppermute | solution.py:30
  348.2 76.9 %collective-permute-start.19 = (bf16[4,896,256]{2,1,0:T(8,128)(2,1)S(1)}, bf16[4,896,256]{2,1,0:T(8,128)(2,1)}, u32[]{:S(2)}, u32[]{:S(2)}) collective-permute-start(bf16[4,896,256]{2,1,0:T(8,128)(2,1)S(1)} %all-to-all-done.3.weights_ref), channel_id=1, source_target_pairs={{0,4},{4,0},{8,12},{12,8},{1,5},{5,1},{9,13},{13,9},{2,6},{6,2},{1... | collective-permute-start | bytes 5505032 | tf_op jit(solution)/shard_map/ppermute | solution.py:30
  385.8 57.2 %collective-permute-start.31 = (bf16[4,896,256]{2,1,0:T(8,128)(2,1)}, bf16[4,896,256]{2,1,0:T(8,128)(2,1)}, u32[]{:S(2)}, u32[]{:S(2)}) collective-permute-start(bf16[4,896,256]{2,1,0:T(8,128)(2,1)} %collective-permute-done.25.weights_ref), channel_id=1, source_target_pairs={{0,4},{4,0},{8,12},{12,8},{1,5},{5,1},{9,13},{13,9},{2,6},{6,2},{1... | collective-permute-start | bytes 5505032 | tf_op jit(solution)/shard_map/ppermute | solution.py:30
  403.9 15.0 %collective-permute-start.15 = (bf16[256,1024]{1,0:T(8,128)(2,1)}, bf16[256,1024]{1,0:T(8,128)(2,1)}, u32[]{:S(2)}, u32[]{:S(2)}) collective-permute-start(bf16[256,1024]{1,0:T(8,128)(2,1)} %bitcast.12), channel_id=1, source_target_pairs={{0,16},{16,0},{1,17},{17,1},{2,18},{18,2},{3,19},{19,3},{4,20},{20... | collective-permute-start | bytes 1572872 | tf_op jit(solution)/shard_map/ppermute | solution.py:30
  409.3 27.7 %collective-permute-start.26 = (bf16[256,1024]{1,0:T(8,128)(2,1)S(1)}, bf16[256,1024]{1,0:T(8,128)(2,1)}, u32[]{:S(2)}, u32[]{:S(2)}) collective-permute-start(bf16[256,1024]{1,0:T(8,128)(2,1)S(1)} %bitcast.60), channel_id=1, source_target_pairs={{0,16},{16,0},{1,17},{17,1},{2,18},{18,2},{3,19},{19,3},{4,20},{20... | collective-permute-start | bytes 1572872 | tf_op jit(solution)/shard_map/ppermute | solution.py:30
  429.4 17.9 %collective-permute-start.20 = (bf16[256,1024]{1,0:T(8,128)(2,1)S(1)}, bf16[256,1024]{1,0:T(8,128)(2,1)S(1)}, u32[]{:S(2)}, u32[]{:S(2)}) collective-permute-start(bf16[256,1024]{1,0:T(8,128)(2,1)S(1)} %bitcast.61), channel_id=1, source_target_pairs={{0,16},{16,0},{1,17},{17,1},{2,18},{18,2},{3,19},{19,3},{4,20},{20... | collective-permute-start | bytes 1572872 | tf_op jit(solution)/shard_map/ppermute | solution.py:30
  447.6 15.3 %collective-permute-start.21 = (bf16[64,1024]{1,0:T(8,128)(2,1)S(1)}, bf16[64,1024]{1,0:T(8,128)(2,1)S(1)}, u32[]{:S(2)}, u32[]{:S(2)}) collective-permute-start(bf16[64,1024]{1,0:T(8,128)(2,1)S(1)} %get-tuple-element.44), channel_id=1, source_target_pairs={{0,1},{1,0},{2,3},{3,2},{4,5},{5,4},{6,7},{7,6},{8,9},{9,8},{10,11... | collective-permute-start | bytes 393224 | tf_op jit(solution)/shard_map/ppermute | solution.py:30
  448.0 14.8 %collective-permute-start.22 = (bf16[64,1024]{1,0:T(8,128)(2,1)S(1)}, bf16[64,1024]{1,0:T(8,128)(2,1)S(1)}, u32[]{:S(2)}, u32[]{:S(2)}) collective-permute-start(bf16[64,1024]{1,0:T(8,128)(2,1)S(1)} %get-tuple-element.46), channel_id=1, source_target_pairs={{0,2},{1,3},{2,0},{3,1},{4,6},{5,7},{6,4},{7,5},{8,10},{9,11},{10,... | collective-permute-start | bytes 393224 | tf_op jit(solution)/shard_map/ppermute | solution.py:30
  452.6 13.6 %collective-permute-start.23 = (bf16[64,1024]{1,0:T(8,128)(2,1)S(1)}, bf16[64,1024]{1,0:T(8,128)(2,1)S(1)}, u32[]{:S(2)}, u32[]{:S(2)}) collective-permute-start(bf16[64,1024]{1,0:T(8,128)(2,1)S(1)} %get-tuple-element.45), channel_id=1, source_target_pairs={{0,3},{1,2},{2,1},{3,0},{4,7},{5,6},{6,5},{7,4},{8,11},{9,10},{10,... | collective-permute-start | bytes 393224 | tf_op jit(solution)/shard_map/ppermute | solution.py:30
  455.0 19.2 %collective-permute-start.30 = (bf16[64,1024]{1,0:T(8,128)(2,1)S(1)}, bf16[64,1024]{1,0:T(8,128)(2,1)S(1)}, u32[]{:S(2)}, u32[]{:S(2)}) collective-permute-start(bf16[64,1024]{1,0:T(8,128)(2,1)S(1)} %fusion.17), channel_id=1, source_target_pairs={{0,8},{4,12},{8,0},{12,4},{1,9},{5,13},{9,1},{13,5},{2,10},{6,14},... | collective-permute-start | bytes 393224 | tf_op jit(solution)/shard_map/ppermute | solution.py:30
  (39 other events, 261.7 us)
Sparse Core Ops, SparseCore 0:
  9.6 83.2 all-gather.2
  122.2 100.8 all-gather.4

commit v5 on v4

--- a/solution.py
+++ b/solution.py
@@ -17,6 +17,7 @@
 WINDOW_PER_DOC = 4
 QUERY_TILE = 128
 ROW_TILE = 256
+PARTS = 2
 VMEM_LIMIT = 48 * 1024 * 1024
 ANY = pl.BlockSpec(memory_space=pl.ANY)
 VMEM = pl.BlockSpec(memory_space=pltpu.VMEM)
@@ -116,30 +117,41 @@
     )(starts, packed, packed, halo)
 
 
-def gain_kernel(gain_ref, weights_ref, gate_ref, up_ref):
-    for which, out_ref in enumerate((gate_ref, up_ref)):
-        out_ref[0] = (weights_ref[which].astype(jnp.float32) * gain_ref[...]).astype(jnp.bfloat16)
-
-
-def scaled_gate_up(w_gate_up, gain, outer_count):
-    _, rows, width = w_gate_up.shape
+def cut_kernel(gain_ref, gate_up_ref, down_ref, *out_refs):
+    rows, cols = out_refs[0].shape[1], out_refs[-1].shape[2]
+    for part in range(PARTS):
+        at = slice(part * rows, (part + 1) * rows)
+        for which in range(2):
+            scaled = gate_up_ref[which, at].astype(jnp.float32) * gain_ref[at]
+            out_refs[2 * part + which][0] = scaled.astype(jnp.bfloat16)
+        out_refs[2 * PARTS + part][0] = down_ref[:, part * cols : (part + 1) * cols]
+
+
+def cut_weights(w_gate_up, w_down, gain, outer_count):
+    _, features, width = w_gate_up.shape
     cols = width // outer_count
+    rows = features // PARTS
     if cols % HEAD_WIDTH:
         wide = (w_gate_up.astype(jnp.float32) * gain[None]).astype(jnp.bfloat16)
-        return jnp.transpose(wide.reshape(2, rows, outer_count, cols), (0, 2, 1, 3))
-    return pl.pallas_call(
-        gain_kernel,
+        wide = jnp.transpose(wide.reshape(2, PARTS, rows, outer_count, cols), (1, 0, 3, 2, 4))
+        tall = jnp.transpose(w_down.reshape(outer_count, cols, PARTS, rows), (2, 0, 1, 3))
+        return [wide[part, which] for part in range(PARTS) for which in range(2)] + [tall[part] for part in range(PARTS)]
+    return pl.pallas_call(
+        cut_kernel,
         grid=(outer_count,),
         in_specs=[
-            pl.BlockSpec((rows, 1), lambda p: (0, 0)),
-            pl.BlockSpec((2, rows, cols), lambda p: (0, 0, p)),
+            pl.BlockSpec((features, 1), lambda p: (0, 0)),
+            pl.BlockSpec((2, features, cols), lambda p: (0, 0, p)),
+            pl.BlockSpec((cols, features), lambda p: (p, 0)),
         ],
-        out_specs=[pl.BlockSpec((1, rows, cols), lambda p: (p, 0, 0))] * 2,
-        out_shape=[jax.ShapeDtypeStruct((outer_count, rows, cols), jnp.bfloat16)] * 2,
-        compiler_params=pltpu.CompilerParams(vmem_limit_bytes=VMEM_LIMIT),
-        cost_estimate=pl.CostEstimate(flops=2 * rows * width, bytes_accessed=8 * rows * width, transcendentals=0),
-        name="take_gain",
-    )(gain, w_gate_up)
+        out_specs=[pl.BlockSpec((1, rows, cols), lambda p: (p, 0, 0))] * (2 * PARTS)
+        + [pl.BlockSpec((1, cols, rows), lambda p: (p, 0, 0))] * PARTS,
+        out_shape=[jax.ShapeDtypeStruct((outer_count, rows, cols), jnp.bfloat16)] * (2 * PARTS)
+        + [jax.ShapeDtypeStruct((outer_count, cols, rows), jnp.bfloat16)] * PARTS,
+        compiler_params=pltpu.CompilerParams(vmem_limit_bytes=VMEM_LIMIT),
+        cost_estimate=pl.CostEstimate(flops=2 * features * width, bytes_accessed=12 * features * width, transcendentals=0),
+        name="cut_weights",
+    )(gain, w_gate_up, w_down)
 
 
 def projection_kernel(block_count, place_ref, *refs):
@@ -184,57 +196,81 @@
     )(place, *blocks, weights)
 
 
-def gate_up_kernel(block_count, *refs):
-    tokens = refs[0]
-    weights = refs[1 : 1 + 2 * block_count]
-    out_ref, held, near, gate, up, token_sems, weight_sems = refs[1 + 2 * block_count :]
-    depth = near.shape[1]
+def gate_up_kernel(block_count, tokens, *refs):
+    weights = refs[: 2 * PARTS * block_count]
+    out_ref, held, near, sums, token_sems, weight_sems = refs[2 * PARTS * block_count :]
+    rows, depth = weights[0].shape[0], weights[0].shape[0] * PARTS
     copies = []
     for a in range(block_count):
         cols = slice(a * depth, (a + 1) * depth)
-        copies.append(pltpu.make_async_copy(tokens.at[:, cols], held.at[:, cols], token_sems.at[a]))
-        for j in (2 * a, 2 * a + 1):
-            copies.append(pltpu.make_async_copy(weights[j], near.at[j], weight_sems.at[j]))
-    for copy in copies:
-        copy.start()
-    for a in range(block_count):
-        copies[3 * a].wait()
-        for which, total in enumerate((gate, up)):
-            copies[3 * a + 1 + which].wait()
-            for rows in row_tiles(held.shape[0]):
-                product = jnp.dot(
-                    held[rows, a * depth : (a + 1) * depth], near[2 * a + which], preferred_element_type=jnp.float32
-                )
-                total[rows, :] = product if a == 0 else total[rows, :] + product
-    for rows in row_tiles(held.shape[0]):
-        out_ref[rows, :] = (gate[rows, :] / (1.0 + jnp.exp(-gate[rows, :])) * up[rows, :]).astype(jnp.bfloat16)
-
-
-def gate_up(tokens, gates, ups):
+        copies.append([pltpu.make_async_copy(tokens.at[:, cols], held.at[:, cols], token_sems.at[a])])
+        for j in range(2 * PARTS * a, 2 * PARTS * (a + 1)):
+            part, which = (j // 2) % PARTS, j % 2
+            target = near.at[which, pl.ds(a * depth + part * rows, rows)]
+            copies[a].append(pltpu.make_async_copy(weights[j], target, weight_sems.at[j]))
+    for group in copies:
+        for copy in group:
+            copy.start()
+    for a, group in enumerate(copies):
+        for copy in group:
+            copy.wait()
+        at = slice(a * depth, (a + 1) * depth)
+        for which in range(2):
+            for tile in row_tiles(held.shape[0]):
+                product = jnp.dot(held[tile, at], near[which, at], preferred_element_type=jnp.float32)
+                total = product if a == 0 else sums[which, tile, :] + product
+                if a < block_count - 1:
+                    sums[which, tile, :] = total
+                else:
+                    out_ref[which, tile, :] = total.astype(jnp.bfloat16)
+
+
+def gate_up(tokens, blocks):
     rows = tokens.shape[0]
-    depth, cols = gates[0].shape
-    weights = [block for pair in zip(gates, ups) for block in pair]
-    return pl.pallas_call(
-        functools.partial(gate_up_kernel, len(gates)),
+    weights = [stream for block in blocks for stream in block]
+    depth, cols = weights[0].shape
+    depth = depth * PARTS * len(blocks)
+    return pl.pallas_call(
+        functools.partial(gate_up_kernel, len(blocks)),
         in_specs=[ANY] * (1 + len(weights)),
         out_specs=VMEM,
-        out_shape=jax.ShapeDtypeStruct((rows, cols), jnp.bfloat16),
+        out_shape=jax.ShapeDtypeStruct((2, rows, cols), jnp.bfloat16),
         scratch_shapes=[
-            pltpu.VMEM((rows, depth * len(gates)), jnp.bfloat16),
-            pltpu.VMEM((len(weights), depth, cols), jnp.bfloat16),
-            pltpu.VMEM((rows, cols), jnp.float32),
-            pltpu.VMEM((rows, cols), jnp.float32),
-            pltpu.SemaphoreType.DMA((len(gates),)),
+            pltpu.VMEM((rows, depth), jnp.bfloat16),
+            pltpu.VMEM((2, depth, cols), jnp.bfloat16),
+            pltpu.VMEM((2, rows, cols), jnp.float32),
+            pltpu.SemaphoreType.DMA((len(blocks),)),
             pltpu.SemaphoreType.DMA((len(weights),)),
         ],
         compiler_params=pltpu.CompilerParams(vmem_limit_bytes=VMEM_LIMIT),
         cost_estimate=pl.CostEstimate(
-            flops=4 * rows * depth * len(gates) * cols,
-            bytes_accessed=2 * (rows * depth * len(gates) + len(weights) * depth * cols),
-            transcendentals=rows * cols,
+            flops=4 * rows * depth * cols,
+            bytes_accessed=2 * (rows * depth + 2 * depth * cols + 2 * rows * cols),
+            transcendentals=0,
         ),
         name="gate_up",
     )(tokens, *weights)
+
+
+def activation_kernel(here_ref, there_ref, out_ref):
+    gate = here_ref[0].astype(jnp.float32) + there_ref[0].astype(jnp.float32)
+    up = here_ref[1].astype(jnp.float32) + there_ref[1].astype(jnp.float32)
+    out_ref[...] = (gate / (1.0 + jnp.exp(-gate)) * up).astype(jnp.bfloat16)
+
+
+def activation(here, there):
+    _, rows, cols = here.shape
+    step = min(rows, ROW_TILE)
+    return pl.pallas_call(
+        activation_kernel,
+        grid=(rows // step,),
+        in_specs=[pl.BlockSpec((2, step, cols), lambda t: (0, t, 0))] * 2,
+        out_specs=pl.BlockSpec((step, cols), lambda t: (t, 0)),
+        out_shape=jax.ShapeDtypeStruct((rows, cols), jnp.bfloat16),
+        compiler_params=pltpu.CompilerParams(vmem_limit_bytes=VMEM_LIMIT),
+        cost_estimate=pl.CostEstimate(flops=8 * rows * cols, bytes_accessed=10 * rows * cols, transcendentals=rows * cols),
+        name="activation",
+    )(here, there)
 
 
 def down_kernel(place_ref, activated_ref, weights_ref, kept_ref, sent_ref):
@@ -242,15 +278,19 @@
     head_count = sent_ref.shape[0] + 1
     head = place_ref[1]
     piece = kept_ref.shape[0] // sources
+    if cols % HEAD_WIDTH:
+        blocks = [weights_ref[s] for s in range(sources)]
+    else:
+        blocks = [jnp.concatenate([weights_ref[s] for s in range(sources)], axis=1)]
     for e in range(head_count):
         rows = []
         for o in range(sources):
             first = pl.multiple_of((o * head_count + (head ^ e)) * piece, piece)
             rows.append(activated_ref[pl.ds(first, piece), :])
         rows = jnp.concatenate(rows, axis=0)
-        for s in range(sources):
-            at = slice(s * cols, (s + 1) * cols)
-            product = jnp.dot(rows, weights_ref[s], preferred_element_type=jnp.float32)
+        for s, block in enumerate(blocks):
+            at = slice(s * block.shape[1], (s + 1) * block.shape[1])
+            product = jnp.dot(rows, block, preferred_element_type=jnp.float32)
             if e == 0:
                 kept_ref[:, at] = product.astype(jnp.bfloat16)
             else:
@@ -295,8 +335,6 @@
     packing = (rows, head_count, KEY_VALUE_HEADS // head_count, -1)
 
     weights_out = lax.all_gather(w_out, "outer", axis=1, tiled=True)
-    own_gain = lax.dynamic_slice_in_dim(norm_gain, outer * feature_rows, feature_rows, 0)
-    w_gate, w_up = scaled_gate_up(w_gate_up, own_gain[:, None], outer_count)
     if packing[2] == inner_count and hops == 1:
         earlier = [lax.ppermute(part, "outer", [(s, s + 1) for s in range(outer_count - 1)]) for part in (key, value)]
         groups = jnp.concatenate([part.reshape(packing) for part in (query, key, value, *earlier)], axis=3)
@@ -317,47 +355,69 @@
         own_context = attention(packed, halo, 0, starts, reach)
         blocks = [lax.all_gather(own_context, "inner", axis=0, tiled=True)]
 
+    spread = functools.partial(lax.all_to_all, axis_name="outer", split_axis=0, concat_axis=0, tiled=True)
+    over_y = functools.partial(swap, axis="inner", distance=2)
+    fence = lambda *arrays: lax.optimization_barrier(arrays)
+    own_gain = lax.dynamic_slice_in_dim(norm_gain, outer * feature_rows, feature_rows, 0)
+    cut = cut_weights(w_gate_up, w_down, own_gain[:, None], outer_count)
+
     place = jnp.stack([inner, head]).astype(jnp.int32)
+    first = spread(after(cut[0], weights_out))
     kept, sent, *whole = projection(blocks, weights_out, place, head_count, inner_count)
     context = whole[0] if whole else own_context
     projected = kept.astype(jnp.float32)
     for e in range(1, head_count):
         projected = projected + swap(sent[e - 1], "head", e).astype(jnp.float32)
+    projected, first = fence(projected, first)
     own_resid = lax.dynamic_slice_in_dim(resid, head * half, half, 0)
     hidden_part = (own_resid.astype(jnp.float32) + projected).astype(jnp.bfloat16)
 
-    own_rows = half // inner_count
-    state = []
-    for a in range(inner_count):
-        block = lax.dynamic_slice_in_dim(hidden_part, (inner ^ a) * own_rows, own_rows, 0)
-        state.append(swap(block, "inner", a).astype(jnp.float32))
-    squares = sum([jnp.sum(block * block, axis=1, keepdims=True) for block in state])
-    inverse = lax.rsqrt(squares / D + 1e-05)
-    normed = jnp.concatenate([block * inverse for block in state], axis=1).astype(jnp.bfloat16)
+    second = spread(after(cut[1], first))
+    upper = inner // 2
+    own_rows = half // 2
+    mine = lax.dynamic_slice_in_dim(hidden_part, upper * own_rows, own_rows, 0)
+    others = lax.dynamic_slice_in_dim(hidden_part, (1 - upper) * own_rows, own_rows, 0)
+    state = [mine.astype(jnp.float32), over_y(others).astype(jnp.float32)]
+    squares = sum([jnp.sum(block * block, axis=1) for block in state])
+    squares = squares + swap(squares, "inner", 1)
+    inverse = lax.rsqrt(squares / D + 1e-05)[:, None]
+    part_rows = feature_rows // PARTS
+    normed = jnp.stack([block * inverse for block in state], axis=1).astype(jnp.bfloat16)
+    normed = normed.reshape(own_rows, 2, outer_count, PARTS, part_rows)
+    normed = jnp.transpose(normed, (0, 1, 3, 2, 4)).reshape(own_rows, 2 * feature_rows * outer_count)
+    normed, first, second = fence(normed, first, second)
     tokens = lax.all_gather(normed, ("outer", "head"), axis=0, tiled=True)
 
-    spread = functools.partial(lax.all_to_all, axis_name="outer", split_axis=0, concat_axis=0, tiled=True)
-    gate_here = spread(after(w_gate, kept))
-    up_here = spread(after(w_up, hidden_part))
-    down_here = spread(after(w_down.reshape(outer_count, hidden_cols, feature_rows), tokens))
-    gates = blocks_over_inner(after(gate_here, normed).reshape(-1, hidden_cols))
-    ups = blocks_over_inner(after(up_here, normed).reshape(-1, hidden_cols))
-    downs = blocks_over_inner(down_here)
-
-    activated = gate_up(tokens, gates, ups)
-    layer_out = jnp.zeros((half, D // inner_count), jnp.bfloat16)
-    for a in range(inner_count):
-        kept, sent = down_product(activated, downs[a], place, head_count)
-        paired = kept.astype(jnp.float32)
-        for e in range(1, head_count):
-            paired = paired + swap(sent[e - 1], "head", e).astype(jnp.float32)
-        paired = paired.reshape(outer_count, own_rows, -1)
-        total = state[a] + lax.dynamic_index_in_dim(paired, outer, 0, False)
-        for d in range(1, outer_count):
-            sent = lax.dynamic_index_in_dim(paired, outer ^ d, 0, False).astype(jnp.bfloat16)
-            total = total + swap(sent, "outer", d).astype(jnp.float32)
-        block = swap(total.astype(jnp.bfloat16), "inner", a)
-        layer_out = lax.dynamic_update_slice(layer_out, block, ((inner ^ a) * own_rows, 0))
+    third, first_y, second_y = fence(spread(after(cut[2], normed)), over_y(first), over_y(second))
+    fourth, third_y = fence(spread(after(cut[3], third)), over_y(third))
+    fifth, fourth_y = fence(spread(after(cut[4], fourth)), over_y(fourth))
+    sixth, fifth_y = fence(spread(after(cut[5], fifth)), over_y(fifth))
+    here = [first, second, third, fourth]
+    there = [first_y, second_y, third_y, fourth_y]
+    flat = [[stream.reshape(-1, hidden_cols) for stream in streams] for streams in (here, there)]
+    sums = gate_up(tokens, flat)
+    activated = activation(sums, swap(sums, "inner", 1))
+
+    downs = [[fifth, sixth], [fifth_y, over_y(sixth)]]
+    pieces = [[None] * PARTS, [None] * PARTS]
+    for part in range(PARTS):
+        for a in range(2):
+            kept, sent = down_product(activated, downs[a][part], place, head_count)
+            paired = kept.astype(jnp.float32)
+            for e in range(1, head_count):
+                paired = paired + swap(sent[e - 1], "head", e).astype(jnp.float32)
+            paired = paired.reshape(outer_count, own_rows, -1)
+            total = lax.dynamic_index_in_dim(paired, outer, 0, False)
+            for d in range(1, outer_count):
+                sent = lax.dynamic_index_in_dim(paired, outer ^ d, 0, False).astype(jnp.bfloat16)
+                total = total + swap(sent, "outer", d).astype(jnp.float32)
+            near = state[a].reshape(own_rows, outer_count, PARTS, part_rows)[:, :, part]
+            total = (near.reshape(own_rows, -1) + total).astype(jnp.bfloat16)
+            pieces[a][part] = (over_y(total) if a else total).reshape(own_rows, outer_count, 1, part_rows)
+    halves = [jnp.concatenate(parts, axis=2).reshape(own_rows, -1) for parts in pieces]
+    layer_out = jnp.zeros((half, halves[0].shape[1]), jnp.bfloat16)
+    layer_out = lax.dynamic_update_slice(layer_out, halves[0], (upper * own_rows, 0))
+    layer_out = lax.dynamic_update_slice(layer_out, halves[1], ((1 - upper) * own_rows, 0))
     return (context, layer_out)
 
 

time: 488 us -> 421 us (0.86)
  waiting for transfers between devices: 346 us -> 237 us
  local copies, waits for them, and re-layouts: 18.9 us -> 35.5 us
  starting transfers between devices: 63.6 us -> 78.4 us
  Pallas kernels: 36.8 us -> 43.1 us
    all_to_all x3 -> x6, waiting for transfers between devices: 159 us -> 36.1 us  [the longest x1 26.9 us: per_device(): fourth, third_y = fence(spread(after(cut[3], third)), over_y(third))]
    ppermute x35 -> x31, waiting for transfers between devices: 136 us -> 159 us  [swap(): return lax.ppermute(array, axis, [(s, s ^ distance) for s in range(count)])]
    all_to_all x3 -> x6, starting transfers between devices: 11.6 us -> 24.2 us  [the longest x1 4.71 us: per_device(): fourth, third_y = fence(spread(after(cut[3], third)), over_y(third))]
    pallas_call x2 -> x3, Pallas kernels: 14.7 us -> 22.6 us  [the longest x1 13 us: gate_up(): pl.pallas_call(functools.partial(gate_up_kernel, len(blocks)), in_specs=[...]
    slice x0 -> x2, local copies, waits for them, and re-layouts: none -> 5.7 us  [per_device(): near = state[a].reshape(own_rows, outer_count, PARTS, part_rows)[:, :, part]]
    reshape x0 -> x9, local copies, waits for them, and re-layouts: none -> 5.29 us  [the longest x2 3.5 us: per_device(): near = state[a].reshape(own_rows, outer_count, PARTS, part_rows)[:, :, part]]
    ppermute x35 -> x31, starting transfers between devices: 39.8 us -> 42.1 us  [swap(): return lax.ppermute(array, axis, [(s, s ^ distance) for s in range(count)])]
    unnamed x44 -> x42, local copies, waits for them, and re-layouts: 12.3 us -> 13.5 us
  transfers between devices with their start and end apart: 43 -> 42, of which waited for: 20 -> 23; matrix products, arithmetic and copies ran while one was open for 2% -> 8% of each run, Pallas kernels for 6% -> 7%
where the time goes in v5:
time: 421 us; the launch traced here: 419 us
  waiting for transfers between devices  237 us (56%)
  starting transfers between devices  78.4 us (19%)
  Pallas kernels  43.1 us (10%)
  local copies, waits for them, and re-layouts  35.5 us (8%)
  between operations  14.5 us (3%)
  other arithmetic  10.7 us (3%)
    ppermute x31, waiting for transfers between devices, swap(): return lax.ppermute(array, axis, [(s, s ^ distance) for s in range(count)])  159 us
    ppermute x31, starting transfers between devices, swap(): return lax.ppermute(array, axis, [(s, s ^ distance) for s in range(count)])  42.1 us
    all_gather x1, waiting for transfers between devices, per_device(): weights_out = lax.all_gather(w_out, 'outer', axis=1, tiled=True)  27 us
    all_to_all x1, waiting for transfers between devices, per_device(): fourth, third_y = fence(spread(after(cut[3], third)), over_y(third))  26.9 us
    all_to_all x1, waiting for transfers between devices, per_device(): lax.all_to_all(groups, ('inner', 'head'), split_axis=0, concat_axis=0, ti...  14.4 us
    unnamed x42, local copies, waits for them, and re-layouts  13.5 us
    pallas_call x1, Pallas kernels, gate_up(): pl.pallas_call(functools.partial(gate_up_kernel, len(blocks)), in_specs=[...  13 us
    pallas_call x4, Pallas kernels, down_product(): pl.pallas_call(down_kernel, in_specs=[SMEM, VMEM, VMEM], out_specs=[VMEM,...  9.32 us
  transfers between devices with their start and end apart: 42, of which 23 were waited for; matrix products, arithmetic and copies ran while one was open for 8% of the time, Pallas kernels for 7%

profile of v5, /device:TPU:0, one launch (start us, length us, event | category | flops | bytes accessed | tf_op | source)
XLA Modules:
  0.0 419.3 jit_solution(3266672975789554208)
XLA Ops:
  7.9 4.9 %collective-permute-start = (bf16[64,1024]{1,0:T(8,128)(2,1)}, bf16[64,1024]{1,0:T(8,128)(2,1)S(1)}, u32[]{:S(2)}, u32[]{:S(2)}) collective-permute-start(bf16[64,1024]{1,0:T(8,128)(2,1)} %param.10), channel_id=1, source_target_pairs={{0,1},{1,2},{2,3},{4,5},{5,6},{6,7},{8,9},{9,10},{10,11},{12,13},{... | collective-permute-start | bytes 393224 | tf_op jit(solution)/shard_map/ppermute | solution.py:339
  25.6 14.4 %all-to-all-done = bf16[8,64,1024]{2,1,0:T(8,128)(2,1)S(1)} async-done(((bf16[8,64,1024]{2,1,0:T(8,128)(2,1)}), bf16[8,64,1024]{2,1,0:T(8,128)(2,1)S(1)}, u32[]{:S(2)}, u32[]{:S(2)}) %all-to-all-start) | async-done | bytes 1048608 | tf_op jit(solution)/shard_map/all_to_all | solution.py:342
  40.0 5.9 %attention.1.refs_0_ = bf16[512,512]{1,0:T(8,128)(2,1)S(1)} custom-call(s32[512,1]{1,0:T(8,128)S(1)} %copy.31.starts_ref, bf16[512,1024]{1,0:T(8,128)(2,1)S(1)} %bitcast.103, bf16[512,1024]{1,0:T(8,128)(2,1)S(1)} %bitcast.104, bf16[512,1024]{1,0:T(8,128)(2,1)S(1)} %bitcast.105), custom_call_target="tpu_custom_call" | custom-call | flops 671088640 | bytes 1048576 | tf_op jit(solution)/shard_map/attention/pallas_call | solution.py:95
  46.9 12.6 %collective-permute-done.3.refs_2_ = bf16[512,512]{1,0:T(8,128)(2,1)S(1)} collective-permute-done((bf16[512,512]{1,0:T(8,128)(2,1)S(1)}, bf16[512,512]{1,0:T(8,128)(2,1)S(1)}, u32[]{:S(2)}, u32[]{:S(2)}) %collective-permute-start.3) | collective-permute-done | bytes 524320 | tf_op jit(solution)/shard_map/ppermute | solution.py:31
  60.4 5.4 %cut_weights.1 = (bf16[4,128,896]{2,1,0:T(8,128)(2,1)}, bf16[4,128,896]{2,1,0:T(8,128)(2,1)}, bf16[4,128,896]{2,1,0:T(8,128)(2,1)}, bf16[4,128,896]{2,1,0:T(8,12...) custom-call(f32[256,1]{1,0:T(8,128)S(1)} %copy.32.gain_ref, bf16[2,256,3584]{2,1,0:T(8,128)(2,1)} %gate_up_ref.1, ...), custom_call_target="tpu_custom_call" | custom-call | flops 1835008 | bytes 11010048 | tf_op jit(solution)/shard_map/cut_weights/pallas_call | solution.py:139
  65.9 27.0 %all-gather.3.cloned.1.call-done.refs_4_ = bf16[2048,1024]{1,0:T(8,128)(2,1)} async-done(((bf16[2048,256]{1,0:T(8,128)(2,1)}), bf16[2048,1024]{1,0:T(8,128)(2,1)}) %all-gather.3.cloned.1.call-update) | async-done | bytes 4194320 | tf_op jit(solution)/shard_map/all_gather | solution.py:337
  100.1 5.3 %projection.1 = (bf16[256,1024]{1,0:T(8,128)(2,1)S(1)}, bf16[1,256,1024]{2,1,0:T(8,128)(2,1)S(1)}, bf16[128,2048]{1,0:T(8,128)(2,1)}) custom-call(s32[2]{0:T(128)S(1)} %pad_add_fusion.place_ref, bf16[512,512]{1,0:T(8,128)(2,1)S(1)} %attention.1.refs_0_, bf16[512,512]{1,0:T(8,128)(2,1)S(1)} %copy-done.10, ...), custom_call_target="tpu_custom_call" | custom-call | flops 2147483648 | bytes 6291456 | tf_op jit(solution)/shard_map/projection/pallas_call | solution.py:186
  106.9 12.3 %collective-permute-done.5 = bf16[256,1024]{1,0:T(8,128)(2,1)S(1)} collective-permute-done((bf16[256,1024]{1,0:T(8,128)(2,1)S(1)}, bf16[256,1024]{1,0:T(8,128)(2,1)S(1)}, u32[]{:S(2)}, u32[]{:S(2)}) %collective-permute-start.5) | collective-permute-done | bytes 524320 | tf_op jit(solution)/shard_map/ppermute | solution.py:31
  119.7 4.5 %all-to-all-start.2 = ((bf16[4,128,896]{2,1,0:T(8,128)(2,1)}), bf16[4,128,896]{2,1,0:T(8,128)(2,1)S(1)}, u32[]{:S(2)}, u32[]{:S(2)}) async-start(bf16[4,128,896]{2,1,0:T(8,128)(2,1)} %get-tuple-element.47), calls=%async_computation.2 | async-start | bytes 1835008 | tf_op jit(solution)/shard_map/all_to_all | solution.py:375
  127.2 5.0 %collective-permute-done.6 = bf16[128,1024]{1,0:T(8,128)(2,1)S(1)} collective-permute-done((bf16[128,1024]{1,0:T(8,128)(2,1)S(1)}, bf16[128,1024]{1,0:T(8,128)(2,1)S(1)}, u32[]{:S(2)}, u32[]{:S(2)}) %collective-permute-start.6) | collective-permute-done | bytes 262176 | tf_op jit(solution)/shard_map/ppermute | solution.py:31
  140.1 5.9 %all-to-all-done.2 = bf16[4,128,896]{2,1,0:T(8,128)(2,1)S(1)} async-done(((bf16[4,128,896]{2,1,0:T(8,128)(2,1)}), bf16[4,128,896]{2,1,0:T(8,128)(2,1)S(1)}, u32[]{:S(2)}, u32[]{:S(2)}) %all-to-all-start.2) | async-done | bytes 917536 | tf_op jit(solution)/shard_map/all_to_all | solution.py:375
  151.7 21.3 %collective-permute-done.8 = bf16[4,128,896]{2,1,0:T(8,128)(2,1)S(1)} collective-permute-done((bf16[4,128,896]{2,1,0:T(8,128)(2,1)S(1)}, bf16[4,128,896]{2,1,0:T(8,128)(2,1)S(1)}, u32[]{:S(2)}, u32[]{:S(2)}) %collective-permute-start.8) | collective-permute-done | bytes 917536 | tf_op jit(solution)/shard_map/ppermute | solution.py:31
  174.0 16.6 %collective-permute-done.9 = bf16[4,128,896]{2,1,0:T(8,128)(2,1)S(1)} collective-permute-done((bf16[4,128,896]{2,1,0:T(8,128)(2,1)S(1)}, bf16[4,128,896]{2,1,0:T(8,128)(2,1)S(1)}, u32[]{:S(2)}, u32[]{:S(2)}) %collective-permute-start.9) | collective-permute-done | bytes 917536 | tf_op jit(solution)/shard_map/ppermute | solution.py:31
  191.6 4.7 %all-to-all-start.4 = ((bf16[4,128,896]{2,1,0:T(8,128)(2,1)}), bf16[4,128,896]{2,1,0:T(8,128)(2,1)}, u32[]{:S(2)}, u32[]{:S(2)}) async-start(bf16[4,128,896]{2,1,0:T(8,128)(2,1)} %get-tuple-element.55), calls=%async_computation.4 | async-start | bytes 1835008 | tf_op jit(solution)/shard_map/all_to_all | solution.py:392
  198.0 18.4 %collective-permute-done.10 = bf16[4,128,896]{2,1,0:T(8,128)(2,1)} collective-permute-done((bf16[4,128,896]{2,1,0:T(8,128)(2,1)S(1)}, bf16[4,128,896]{2,1,0:T(8,128)(2,1)}, u32[]{:S(2)}, u32[]{:S(2)}) %collective-permute-start.10) | collective-permute-done | bytes 917536 | tf_op jit(solution)/shard_map/ppermute | solution.py:31
  216.4 26.9 %all-to-all-done.4 = bf16[4,128,896]{2,1,0:T(8,128)(2,1)} async-done(((bf16[4,128,896]{2,1,0:T(8,128)(2,1)}), bf16[4,128,896]{2,1,0:T(8,128)(2,1)}, u32[]{:S(2)}, u32[]{:S(2)}) %all-to-all-start.4) | async-done | bytes 917536 | tf_op jit(solution)/shard_map/all_to_all | solution.py:392
  248.8 18.2 %collective-permute-done.11 = bf16[4,128,896]{2,1,0:T(8,128)(2,1)} collective-permute-done((bf16[4,128,896]{2,1,0:T(8,128)(2,1)}, bf16[4,128,896]{2,1,0:T(8,128)(2,1)}, u32[]{:S(2)}, u32[]{:S(2)}) %collective-permute-start.11) | collective-permute-done | bytes 917536 | tf_op jit(solution)/shard_map/ppermute | solution.py:31
  273.4 13.0 %gate_up.1.here_ref = bf16[2,1024,896]{2,1,0:T(8,128)(2,1)} custom-call(bf16[1024,2048]{1,0:T(8,128)(2,1)} %all-gather.5.cloned.1.call-done.tokens, bf16[512,896]{1,0:T(8,128)(2,1)S(1)} %bitcast.106, bf16[512,896]{1,0:T(8,128)(2,1)S(1)} %bitcast.107, bf16[512,896]{1,0:T(8,128)(2,1)S(1)} %bitcast.108, bf16[512,896]{1,0:T(8,128)(2,1)} %bitcast.13.refs_3_, ...), custom_call_target="tpu_custom_call" | custom-call | flops 7516192768 | bytes 15204352 | tf_op jit(solution)/shard_map/gate_up/pallas_call | solution.py:233
  286.5 4.2 %all-to-all-start.6 = ((bf16[4,896,128]{2,1,0:T(8,128)(2,1)}), bf16[4,896,128]{2,1,0:T(8,128)(2,1)}, u32[]{:S(2)}, u32[]{:S(2)}) async-start(bf16[4,896,128]{2,1,0:T(8,128)(2,1)} %get-tuple-element.67), calls=%async_computation.6 | async-start | bytes 1835008 | tf_op jit(solution)/shard_map/all_to_all | solution.py:394
  292.3 21.3 %collective-permute-done.17.weights_ref = bf16[4,896,128]{2,1,0:T(8,128)(2,1)S(1)} collective-permute-done((bf16[4,896,128]{2,1,0:T(8,128)(2,1)S(1)}, bf16[4,896,128]{2,1,0:T(8,128)(2,1)S(1)}, u32[]{:S(2)}, u32[]{:S(2)}) %collective-permute-start.17) | collective-permute-done | bytes 917536 | tf_op jit(solution)/shard_map/ppermute | solution.py:31
  355.4 8.9 %collective-permute-done.28 = bf16[512,512]{1,0:T(8,128)(2,1)S(1)} collective-permute-done((bf16[512,512]{1,0:T(8,128)(2,1)S(1)}, bf16[512,512]{1,0:T(8,128)(2,1)S(1)}, u32[]{:S(2)}, u32[]{:S(2)}) %collective-permute-start.28) | collective-permute-done | bytes 524320 | tf_op jit(solution)/shard_map/ppermute | solution.py:31
  367.7 6.4 %collective-permute-done.22 = bf16[512,512]{1,0:T(8,128)(2,1)S(1)} collective-permute-done((bf16[512,512]{1,0:T(8,128)(2,1)S(1)}, bf16[512,512]{1,0:T(8,128)(2,1)S(1)}, u32[]{:S(2)}, u32[]{:S(2)}) %collective-permute-start.22) | collective-permute-done | bytes 524320 | tf_op jit(solution)/shard_map/ppermute | solution.py:31
  384.0 5.9 %collective-permute-start.25 = (bf16[128,512]{1,0:T(8,128)(2,1)}, bf16[128,512]{1,0:T(8,128)(2,1)}, u32[]{:S(2)}, u32[]{:S(2)}) collective-permute-start(bf16[128,512]{1,0:T(8,128)(2,1)} %get-tuple-element.81), channel_id=1, source_target_pairs={{0,3},{1,2},{2,1},{3,0},{4,7},{5,6},{6,5},{7,4},{8,11},{9,10},{10,... | collective-permute-start | bytes 393224 | tf_op jit(solution)/shard_map/ppermute | solution.py:31
  393.1 6.9 %collective-permute-done.30 = bf16[128,512]{1,0:T(8,128)(2,1)} collective-permute-done((bf16[128,512]{1,0:T(8,128)(2,1)}, bf16[128,512]{1,0:T(8,128)(2,1)}, u32[]{:S(2)}, u32[]{:S(2)}) %collective-permute-start.30) | collective-permute-done | bytes 131104 | tf_op jit(solution)/shard_map/ppermute | solution.py:31
  (171 shorter events, 128.7 us)
Async XLA Ops:
  7.2 85.7 %all-gather.3.cloned.1.call-start = ((), (), s32[]{:S(2)}) async-start(), calls=%async_computation.7 | async-start | bytes 5242880 | tf_op jit(solution)/shard_map/all_gather | solution.py:337
  21.3 18.7 %all-to-all-start = ((bf16[8,64,1024]{2,1,0:T(8,128)(2,1)}), bf16[8,64,1024]{2,1,0:T(8,128)(2,1)S(1)}, u32[]{:S(2)}, u32[]{:S(2)}) async-start(bf16[8,64,1024]{2,1,0:T(8,128)(2,1)} %bitcast.5), calls=%async_computation | async-start | bytes 2097152 | tf_op jit(solution)/shard_map/all_to_all | solution.py:342
  46.5 50.0 %collective-permute-start.2 = (bf16[512,512]{1,0:T(8,128)(2,1)S(1)}, bf16[512,512]{1,0:T(8,128)(2,1)S(1)}, u32[]{:S(2)}, u32[]{:S(2)}) collective-permute-start(bf16[512,512]{1,0:T(8,128)(2,1)S(1)} %attention.1.refs_0_), channel_id=1, source_target_pairs={{0,4},{4,0},{8,12},{12,8},{1,5},{5,1},{9,13},{13,9},{2,6},{6,2},{1... | collective-permute-start | bytes 1572872 | tf_op jit(solution)/shard_map/ppermute | solution.py:31
  59.5 37.7 %collective-permute-start.4 = (bf16[512,512]{1,0:T(8,128)(2,1)S(1)}, bf16[512,512]{1,0:T(8,128)(2,1)S(1)}, u32[]{:S(2)}, u32[]{:S(2)}) collective-permute-start(bf16[512,512]{1,0:T(8,128)(2,1)S(1)} %collective-permute-done.3.refs_2_), channel_id=1, source_target_pairs={{0,4},{4,0},{8,12},{12,8},{1,5},{5,1},{9,13},{13,9},{2,6},{6,2},{1... | collective-permute-start | bytes 1572872 | tf_op jit(solution)/shard_map/ppermute | solution.py:31
  92.9 26.8 %all-to-all-start.1 = ((bf16[4,128,896]{2,1,0:T(8,128)(2,1)}), bf16[4,128,896]{2,1,0:T(8,128)(2,1)S(1)}, u32[]{:S(2)}, u32[]{:S(2)}) async-start(bf16[4,128,896]{2,1,0:T(8,128)(2,1)} %get-tuple-element.43), calls=%async_computation.1 | async-start | bytes 1835008 | tf_op jit(solution)/shard_map/all_to_all | solution.py:365
  119.7 26.4 %all-to-all-start.2 = ((bf16[4,128,896]{2,1,0:T(8,128)(2,1)}), bf16[4,128,896]{2,1,0:T(8,128)(2,1)S(1)}, u32[]{:S(2)}, u32[]{:S(2)}) async-start(bf16[4,128,896]{2,1,0:T(8,128)(2,1)} %get-tuple-element.47), calls=%async_computation.2 | async-start | bytes 1835008 | tf_op jit(solution)/shard_map/all_to_all | solution.py:375
  124.2 145.7 %all-gather.5.cloned.1.call-start = ((), (), s32[]{:S(2)}) async-start(), calls=%async_computation.8 | async-start | bytes 4718592 | tf_op jit(solution)/shard_map/all_gather | solution.py:389
  146.1 45.5 %all-to-all-start.3 = ((bf16[4,128,896]{2,1,0:T(8,128)(2,1)}), bf16[4,128,896]{2,1,0:T(8,128)(2,1)S(1)}, u32[]{:S(2)}, u32[]{:S(2)}) async-start(bf16[4,128,896]{2,1,0:T(8,128)(2,1)} %get-tuple-element.52), calls=%async_computation.3 | async-start | bytes 1835008 | tf_op jit(solution)/shard_map/all_to_all | solution.py:391
  149.6 23.4 %collective-permute-start.8 = (bf16[4,128,896]{2,1,0:T(8,128)(2,1)S(1)}, bf16[4,128,896]{2,1,0:T(8,128)(2,1)S(1)}, u32[]{:S(2)}, u32[]{:S(2)}) collective-permute-start(bf16[4,128,896]{2,1,0:T(8,128)(2,1)S(1)} %all-to-all-done.1), channel_id=1, source_target_pairs={{0,8},{4,12},{8,0},{12,4},{1,9},{5,13},{9,1},{13,5},{2,10},{6,14},... | collective-permute-start | bytes 2752520 | tf_op jit(solution)/shard_map/ppermute | solution.py:31
  151.3 39.3 %collective-permute-start.9 = (bf16[4,128,896]{2,1,0:T(8,128)(2,1)S(1)}, bf16[4,128,896]{2,1,0:T(8,128)(2,1)S(1)}, u32[]{:S(2)}, u32[]{:S(2)}) collective-permute-start(bf16[4,128,896]{2,1,0:T(8,128)(2,1)S(1)} %all-to-all-done.2), channel_id=1, source_target_pairs={{0,8},{4,12},{8,0},{12,4},{1,9},{5,13},{9,1},{13,5},{2,10},{6,14},... | collective-permute-start | bytes 2752520 | tf_op jit(solution)/shard_map/ppermute | solution.py:31
  191.6 51.6 %all-to-all-start.4 = ((bf16[4,128,896]{2,1,0:T(8,128)(2,1)}), bf16[4,128,896]{2,1,0:T(8,128)(2,1)}, u32[]{:S(2)}, u32[]{:S(2)}) async-start(bf16[4,128,896]{2,1,0:T(8,128)(2,1)} %get-tuple-element.55), calls=%async_computation.4 | async-start | bytes 1835008 | tf_op jit(solution)/shard_map/all_to_all | solution.py:392
  196.3 20.1 %collective-permute-start.10 = (bf16[4,128,896]{2,1,0:T(8,128)(2,1)S(1)}, bf16[4,128,896]{2,1,0:T(8,128)(2,1)}, u32[]{:S(2)}, u32[]{:S(2)}) collective-permute-start(bf16[4,128,896]{2,1,0:T(8,128)(2,1)S(1)} %all-to-all-done.3), channel_id=1, source_target_pairs={{0,8},{4,12},{8,0},{12,4},{1,9},{5,13},{9,1},{13,5},{2,10},{6,14},... | collective-permute-start | bytes 2752520 | tf_op jit(solution)/shard_map/ppermute | solution.py:31
  243.3 26.6 %all-to-all-start.5 = ((bf16[4,896,128]{2,1,0:T(8,128)(2,1)}), bf16[4,896,128]{2,1,0:T(8,128)(2,1)S(1)}, u32[]{:S(2)}, u32[]{:S(2)}) async-start(bf16[4,896,128]{2,1,0:T(8,128)(2,1)} %get-tuple-element.61), calls=%async_computation.5 | async-start | bytes 1835008 | tf_op jit(solution)/shard_map/all_to_all | solution.py:393
  247.0 20.1 %collective-permute-start.11 = (bf16[4,128,896]{2,1,0:T(8,128)(2,1)}, bf16[4,128,896]{2,1,0:T(8,128)(2,1)}, u32[]{:S(2)}, u32[]{:S(2)}) collective-permute-start(bf16[4,128,896]{2,1,0:T(8,128)(2,1)} %all-to-all-done.4), channel_id=1, source_target_pairs={{0,8},{4,12},{8,0},{12,4},{1,9},{5,13},{9,1},{13,5},{2,10},{6,14},... | collective-permute-start | bytes 2752520 | tf_op jit(solution)/shard_map/ppermute | solution.py:31
  286.4 30.9 %collective-permute-start.12 = (bf16[2,1024,896]{2,1,0:T(8,128)(2,1)}, bf16[2,1024,896]{2,1,0:T(8,128)(2,1)}, u32[]{:S(2)}, u32[]{:S(2)}) collective-permute-start(bf16[2,1024,896]{2,1,0:T(8,128)(2,1)} %gate_up.1.here_ref), channel_id=1, source_target_pairs={{0,4},{4,0},{8,12},{12,8},{1,5},{5,1},{9,13},{13,9},{2,6},{6,2},{1... | collective-permute-start | bytes 11010056 | tf_op jit(solution)/shard_map/ppermute | solution.py:31
  286.5 28.1 %all-to-all-start.6 = ((bf16[4,896,128]{2,1,0:T(8,128)(2,1)}), bf16[4,896,128]{2,1,0:T(8,128)(2,1)}, u32[]{:S(2)}, u32[]{:S(2)}) async-start(bf16[4,896,128]{2,1,0:T(8,128)(2,1)} %get-tuple-element.67), calls=%async_computation.6 | async-start | bytes 1835008 | tf_op jit(solution)/shard_map/all_to_all | solution.py:394
  290.8 22.8 %collective-permute-start.17 = (bf16[4,896,128]{2,1,0:T(8,128)(2,1)S(1)}, bf16[4,896,128]{2,1,0:T(8,128)(2,1)S(1)}, u32[]{:S(2)}, u32[]{:S(2)}) collective-permute-start(bf16[4,896,128]{2,1,0:T(8,128)(2,1)S(1)} %all-to-all-done.5.weights_ref), channel_id=1, source_target_pairs={{0,8},{4,12},{8,0},{12,4},{1,9},{5,13},{9,1},{13,5},{2,10},{6,14},... | collective-permute-start | bytes 2752520 | tf_op jit(solution)/shard_map/ppermute | solution.py:31
  314.7 24.1 %collective-permute-start.27 = (bf16[4,896,128]{2,1,0:T(8,128)(2,1)}, bf16[4,896,128]{2,1,0:T(8,128)(2,1)}, u32[]{:S(2)}, u32[]{:S(2)}) collective-permute-start(bf16[4,896,128]{2,1,0:T(8,128)(2,1)} %all-to-all-done.6.weights_ref), channel_id=1, source_target_pairs={{0,8},{4,12},{8,0},{12,4},{1,9},{5,13},{9,1},{13,5},{2,10},{6,14},... | collective-permute-start | bytes 2752520 | tf_op jit(solution)/shard_map/ppermute | solution.py:31
  341.2 23.1 %collective-permute-start.28 = (bf16[512,512]{1,0:T(8,128)(2,1)S(1)}, bf16[512,512]{1,0:T(8,128)(2,1)S(1)}, u32[]{:S(2)}, u32[]{:S(2)}) collective-permute-start(bf16[512,512]{1,0:T(8,128)(2,1)S(1)} %bitcast.113), channel_id=1, source_target_pairs={{0,16},{16,0},{1,17},{17,1},{2,18},{18,2},{3,19},{19,3},{4,20},{20... | collective-permute-start | bytes 1572872 | tf_op jit(solution)/shard_map/ppermute | solution.py:31
  344.5 29.5 %collective-permute-start.22 = (bf16[512,512]{1,0:T(8,128)(2,1)S(1)}, bf16[512,512]{1,0:T(8,128)(2,1)S(1)}, u32[]{:S(2)}, u32[]{:S(2)}) collective-permute-start(bf16[512,512]{1,0:T(8,128)(2,1)S(1)} %bitcast.112), channel_id=1, source_target_pairs={{0,16},{16,0},{1,17},{17,1},{2,18},{18,2},{3,19},{19,3},{4,20},{20... | collective-permute-start | bytes 1572872 | tf_op jit(solution)/shard_map/ppermute | solution.py:31
  346.4 31.4 %collective-permute-start.21 = (bf16[128,512]{1,0:T(8,128)(2,1)S(1)}, bf16[128,512]{1,0:T(8,128)(2,1)S(1)}, u32[]{:S(2)}, u32[]{:S(2)}) collective-permute-start(bf16[128,512]{1,0:T(8,128)(2,1)S(1)} %get-tuple-element.90), channel_id=1, source_target_pairs={{0,3},{1,2},{2,1},{3,0},{4,7},{5,6},{6,5},{7,4},{8,11},{9,10},{10,... | collective-permute-start | bytes 393224 | tf_op jit(solution)/shard_map/ppermute | solution.py:31
  349.7 29.5 %collective-permute-start.20 = (bf16[128,512]{1,0:T(8,128)(2,1)S(1)}, bf16[128,512]{1,0:T(8,128)(2,1)S(1)}, u32[]{:S(2)}, u32[]{:S(2)}) collective-permute-start(bf16[128,512]{1,0:T(8,128)(2,1)S(1)} %get-tuple-element.91), channel_id=1, source_target_pairs={{0,2},{1,3},{2,0},{3,1},{4,6},{5,7},{6,4},{7,5},{8,10},{9,11},{10,... | collective-permute-start | bytes 393224 | tf_op jit(solution)/shard_map/ppermute | solution.py:31
  353.1 27.1 %collective-permute-start.19 = (bf16[128,512]{1,0:T(8,128)(2,1)S(1)}, bf16[128,512]{1,0:T(8,128)(2,1)S(1)}, u32[]{:S(2)}, u32[]{:S(2)}) collective-permute-start(bf16[128,512]{1,0:T(8,128)(2,1)S(1)} %get-tuple-element.89), channel_id=1, source_target_pairs={{0,1},{1,0},{2,3},{3,2},{4,5},{5,4},{6,7},{7,6},{8,9},{9,8},{10,11... | collective-permute-start | bytes 393224 | tf_op jit(solution)/shard_map/ppermute | solution.py:31
  380.2 19.8 %collective-permute-start.30 = (bf16[128,512]{1,0:T(8,128)(2,1)}, bf16[128,512]{1,0:T(8,128)(2,1)}, u32[]{:S(2)}, u32[]{:S(2)}) collective-permute-start(bf16[128,512]{1,0:T(8,128)(2,1)} %get-tuple-element.85), channel_id=1, source_target_pairs={{0,2},{1,3},{2,0},{3,1},{4,6},{5,7},{6,4},{7,5},{8,10},{9,11},{10,... | collective-permute-start | bytes 393224 | tf_op jit(solution)/shard_map/ppermute | solution.py:31
  (37 other events, 347.9 us)
Sparse Core Ops, SparseCore 0:
  9.6 83.2 all-gather.2
  146.2 114.0 all-gather.4

commit v6 on v5

--- a/solution.py
+++ b/solution.py
@@ -24,11 +24,11 @@
 SMEM = pl.BlockSpec(memory_space=pltpu.SMEM)
 
 
-def swap(array, axis, distance):
+def swap(array, axis, distance, only=None):
     if distance == 0:
         return array
-    count = lax.axis_size(axis)
-    return lax.ppermute(array, axis, [(s, s ^ distance) for s in range(count)])
+    members = range(lax.axis_size(axis)) if only is None else only
+    return lax.ppermute(array, axis, [(s, s ^ distance) for s in members])
 
 
 def after(array, earlier):
@@ -117,41 +117,30 @@
     )(starts, packed, packed, halo)
 
 
-def cut_kernel(gain_ref, gate_up_ref, down_ref, *out_refs):
-    rows, cols = out_refs[0].shape[1], out_refs[-1].shape[2]
-    for part in range(PARTS):
-        at = slice(part * rows, (part + 1) * rows)
-        for which in range(2):
-            scaled = gate_up_ref[which, at].astype(jnp.float32) * gain_ref[at]
-            out_refs[2 * part + which][0] = scaled.astype(jnp.bfloat16)
-        out_refs[2 * PARTS + part][0] = down_ref[:, part * cols : (part + 1) * cols]
-
-
-def cut_weights(w_gate_up, w_down, gain, outer_count):
-    _, features, width = w_gate_up.shape
+def gain_kernel(gain_ref, weights_ref, out_ref):
+    for which in range(2):
+        out_ref[0, which] = (weights_ref[which].astype(jnp.float32) * gain_ref[...]).astype(jnp.bfloat16)
+
+
+def take_gain(w_gate_up, gain, outer_count):
+    _, rows, width = w_gate_up.shape
     cols = width // outer_count
-    rows = features // PARTS
     if cols % HEAD_WIDTH:
         wide = (w_gate_up.astype(jnp.float32) * gain[None]).astype(jnp.bfloat16)
-        wide = jnp.transpose(wide.reshape(2, PARTS, rows, outer_count, cols), (1, 0, 3, 2, 4))
-        tall = jnp.transpose(w_down.reshape(outer_count, cols, PARTS, rows), (2, 0, 1, 3))
-        return [wide[part, which] for part in range(PARTS) for which in range(2)] + [tall[part] for part in range(PARTS)]
-    return pl.pallas_call(
-        cut_kernel,
+        return jnp.transpose(wide.reshape(2, rows, outer_count, cols), (2, 0, 1, 3))
+    return pl.pallas_call(
+        gain_kernel,
         grid=(outer_count,),
         in_specs=[
-            pl.BlockSpec((features, 1), lambda p: (0, 0)),
-            pl.BlockSpec((2, features, cols), lambda p: (0, 0, p)),
-            pl.BlockSpec((cols, features), lambda p: (p, 0)),
+            pl.BlockSpec((rows, 1), lambda p: (0, 0)),
+            pl.BlockSpec((2, rows, cols), lambda p: (0, 0, p)),
         ],
-        out_specs=[pl.BlockSpec((1, rows, cols), lambda p: (p, 0, 0))] * (2 * PARTS)
-        + [pl.BlockSpec((1, cols, rows), lambda p: (p, 0, 0))] * PARTS,
-        out_shape=[jax.ShapeDtypeStruct((outer_count, rows, cols), jnp.bfloat16)] * (2 * PARTS)
-        + [jax.ShapeDtypeStruct((outer_count, cols, rows), jnp.bfloat16)] * PARTS,
-        compiler_params=pltpu.CompilerParams(vmem_limit_bytes=VMEM_LIMIT),
-        cost_estimate=pl.CostEstimate(flops=2 * features * width, bytes_accessed=12 * features * width, transcendentals=0),
-        name="cut_weights",
-    )(gain, w_gate_up, w_down)
+        out_specs=pl.BlockSpec((1, 2, rows, cols), lambda p: (p, 0, 0, 0)),
+        out_shape=jax.ShapeDtypeStruct((outer_count, 2, rows, cols), jnp.bfloat16),
+        compiler_params=pltpu.CompilerParams(vmem_limit_bytes=VMEM_LIMIT),
+        cost_estimate=pl.CostEstimate(flops=2 * rows * width, bytes_accessed=8 * rows * width, transcendentals=0),
+        name="take_gain",
+    )(gain, w_gate_up)
 
 
 def projection_kernel(block_count, place_ref, *refs):
@@ -196,18 +185,21 @@
     )(place, *blocks, weights)
 
 
-def gate_up_kernel(block_count, tokens, *refs):
-    weights = refs[: 2 * PARTS * block_count]
-    out_ref, held, near, sums, token_sems, weight_sems = refs[2 * PARTS * block_count :]
-    rows, depth = weights[0].shape[0], weights[0].shape[0] * PARTS
+def gate_up_kernel(place_ref, tokens, cut, far, cut_y, far_y, out_ref, held, near, sums, token_sems, weight_sems):
+    outer = place_ref[2]
+    sources, _, rows, _ = cut.shape
+    depth = sources * rows
     copies = []
-    for a in range(block_count):
+    for a, far_ref in enumerate((far, far_y)):
         cols = slice(a * depth, (a + 1) * depth)
         copies.append([pltpu.make_async_copy(tokens.at[:, cols], held.at[:, cols], token_sems.at[a])])
-        for j in range(2 * PARTS * a, 2 * PARTS * (a + 1)):
-            part, which = (j // 2) % PARTS, j % 2
-            target = near.at[which, pl.ds(a * depth + part * rows, rows)]
-            copies[a].append(pltpu.make_async_copy(weights[j], target, weight_sems.at[j]))
+        for which in range(2):
+            for d in range(sources):
+                own = cut.at[outer, which] if a == 0 else cut_y.at[which]
+                first = pl.multiple_of(a * depth + (outer ^ d) * rows, rows)
+                target = near.at[which, pl.ds(first, rows)]
+                source = far_ref.at[d - 1, which] if d else own
+                copies[a].append(pltpu.make_async_copy(source, target, weight_sems.at[a, which, d]))
     for group in copies:
         for copy in group:
             copy.start()
@@ -218,29 +210,26 @@
         for which in range(2):
             for tile in row_tiles(held.shape[0]):
                 product = jnp.dot(held[tile, at], near[which, at], preferred_element_type=jnp.float32)
-                total = product if a == 0 else sums[which, tile, :] + product
-                if a < block_count - 1:
-                    sums[which, tile, :] = total
+                if a == 0:
+                    sums[which, tile, :] = product
                 else:
-                    out_ref[which, tile, :] = total.astype(jnp.bfloat16)
-
-
-def gate_up(tokens, blocks):
-    rows = tokens.shape[0]
-    weights = [stream for block in blocks for stream in block]
-    depth, cols = weights[0].shape
-    depth = depth * PARTS * len(blocks)
-    return pl.pallas_call(
-        functools.partial(gate_up_kernel, len(blocks)),
-        in_specs=[ANY] * (1 + len(weights)),
+                    out_ref[which, tile, :] = (sums[which, tile, :] + product).astype(jnp.bfloat16)
+
+
+def gate_up(place, tokens, cut, far, cut_y, far_y):
+    rows, depth = tokens.shape
+    sources, _, _, cols = cut.shape
+    return pl.pallas_call(
+        gate_up_kernel,
+        in_specs=[SMEM] + [ANY] * 5,
         out_specs=VMEM,
         out_shape=jax.ShapeDtypeStruct((2, rows, cols), jnp.bfloat16),
         scratch_shapes=[
             pltpu.VMEM((rows, depth), jnp.bfloat16),
             pltpu.VMEM((2, depth, cols), jnp.bfloat16),
             pltpu.VMEM((2, rows, cols), jnp.float32),
-            pltpu.SemaphoreType.DMA((len(blocks),)),
-            pltpu.SemaphoreType.DMA((len(weights),)),
+            pltpu.SemaphoreType.DMA((2,)),
+            pltpu.SemaphoreType.DMA((2, 2, sources)),
         ],
         compiler_params=pltpu.CompilerParams(vmem_limit_bytes=VMEM_LIMIT),
         cost_estimate=pl.CostEstimate(
@@ -249,7 +238,7 @@
             transcendentals=0,
         ),
         name="gate_up",
-    )(tokens, *weights)
+    )(place, tokens, cut, far, cut_y, far_y)
 
 
 def activation_kernel(here_ref, there_ref, out_ref):
@@ -273,45 +262,52 @@
     )(here, there)
 
 
-def down_kernel(place_ref, activated_ref, weights_ref, kept_ref, sent_ref):
-    sources, _, cols = weights_ref.shape
+def down_kernel(part, place_ref, activated_ref, weights, kept_ref, sent_ref, near, sems):
+    sources = weights.shape[0]
+    cols = weights.shape[2]
+    head, outer = place_ref[1], place_ref[2]
+    count = near.shape[0]
+    copies = [
+        pltpu.make_async_copy(weights.at[outer ^ (part * count + s)], near.at[s], sems.at[s]) for s in range(count)
+    ]
+    for copy in copies:
+        copy.start()
     head_count = sent_ref.shape[0] + 1
-    head = place_ref[1]
     piece = kept_ref.shape[0] // sources
-    if cols % HEAD_WIDTH:
-        blocks = [weights_ref[s] for s in range(sources)]
-    else:
-        blocks = [jnp.concatenate([weights_ref[s] for s in range(sources)], axis=1)]
     for e in range(head_count):
         rows = []
         for o in range(sources):
             first = pl.multiple_of((o * head_count + (head ^ e)) * piece, piece)
             rows.append(activated_ref[pl.ds(first, piece), :])
         rows = jnp.concatenate(rows, axis=0)
-        for s, block in enumerate(blocks):
-            at = slice(s * block.shape[1], (s + 1) * block.shape[1])
-            product = jnp.dot(rows, block, preferred_element_type=jnp.float32)
+        for s in range(count):
+            if e == 0:
+                copies[s].wait()
+            at = slice(s * cols, (s + 1) * cols)
+            product = jnp.dot(rows, near[s], preferred_element_type=jnp.float32)
             if e == 0:
                 kept_ref[:, at] = product.astype(jnp.bfloat16)
             else:
                 sent_ref[e - 1, :, at] = product.astype(jnp.bfloat16)
 
 
-def down_product(activated, weights, place, head_count):
+def down_product(place, activated, weights, part, head_count):
     rows = activated.shape[0] // head_count
     sources, depth, cols = weights.shape
-    return pl.pallas_call(
-        down_kernel,
-        in_specs=[SMEM, VMEM, VMEM],
+    count = sources // PARTS
+    return pl.pallas_call(
+        functools.partial(down_kernel, part),
+        in_specs=[SMEM, VMEM, ANY],
         out_specs=[VMEM, VMEM],
         out_shape=[
-            jax.ShapeDtypeStruct((rows, sources * cols), jnp.bfloat16),
-            jax.ShapeDtypeStruct((head_count - 1, rows, sources * cols), jnp.bfloat16),
+            jax.ShapeDtypeStruct((rows, count * cols), jnp.bfloat16),
+            jax.ShapeDtypeStruct((head_count - 1, rows, count * cols), jnp.bfloat16),
         ],
+        scratch_shapes=[pltpu.VMEM((count, depth, cols), jnp.bfloat16), pltpu.SemaphoreType.DMA((count,))],
         compiler_params=pltpu.CompilerParams(vmem_limit_bytes=VMEM_LIMIT),
         cost_estimate=pl.CostEstimate(
-            flops=2 * activated.size * sources * cols,
-            bytes_accessed=2 * (activated.size + weights.size + head_count * rows * sources * cols),
+            flops=2 * activated.size * count * cols,
+            bytes_accessed=2 * (activated.size + weights.size // PARTS + head_count * rows * count * cols),
             transcendentals=0,
         ),
         name="down",
@@ -335,12 +331,15 @@
     packing = (rows, head_count, KEY_VALUE_HEADS // head_count, -1)
 
     weights_out = lax.all_gather(w_out, "outer", axis=1, tiled=True)
+    fence = lambda *arrays: lax.optimization_barrier(arrays)
+    own_gain = lax.dynamic_slice_in_dim(norm_gain, outer * feature_rows, feature_rows, 0)
+    cut = take_gain(w_gate_up, own_gain[:, None], outer_count)
     if packing[2] == inner_count and hops == 1:
         earlier = [lax.ppermute(part, "outer", [(s, s + 1) for s in range(outer_count - 1)]) for part in (key, value)]
         groups = jnp.concatenate([part.reshape(packing) for part in (query, key, value, *earlier)], axis=3)
         groups = jnp.transpose(groups, (2, 1, 0, 3)).reshape(inner_count * head_count, rows, -1)
         packed = lax.all_to_all(groups, ("inner", "head"), split_axis=0, concat_axis=0, tiled=True)
-        packed = packed.reshape(plane_rows, -1)
+        packed, cut = fence(packed.reshape(plane_rows, -1), cut)
         starts = document_starts(bounds, outer * plane_rows, plane_rows)
         own_context = attention(packed, packed, Q_COLS // KV_COLS + 1, starts, reach)
         blocks = blocks_over_inner(own_context)
@@ -355,24 +354,36 @@
         own_context = attention(packed, halo, 0, starts, reach)
         blocks = [lax.all_gather(own_context, "inner", axis=0, tiled=True)]
 
-    spread = functools.partial(lax.all_to_all, axis_name="outer", split_axis=0, concat_axis=0, tiled=True)
     over_y = functools.partial(swap, axis="inner", distance=2)
-    fence = lambda *arrays: lax.optimization_barrier(arrays)
-    own_gain = lax.dynamic_slice_in_dim(norm_gain, outer * feature_rows, feature_rows, 0)
-    cut = cut_weights(w_gate_up, w_down, own_gain[:, None], outer_count)
-
-    place = jnp.stack([inner, head]).astype(jnp.int32)
-    first = spread(after(cut[0], weights_out))
+    piece_for = lambda array, d: lax.dynamic_index_in_dim(array, outer ^ d, 0, False)
+    down_cut = w_down.reshape(outer_count, hidden_cols, feature_rows)
+    ends, middle = (0, outer_count - 1), (1, 2)
+    split_last = outer_count == 4
+    early = []
+    if split_last:
+        early = [swap(piece_for(array, 3), "outer", 3, middle) for array in (cut, down_cut)]
+    cut_y = over_y(after(piece_for(cut, 0), blocks[-1]))
+    weights_out, cut_y, *early = fence(weights_out, cut_y, *early)
+
+    def send(array):
+        moved = [swap(piece_for(array, d), "outer", d) for d in range(1, outer_count - split_last)]
+        return moved + ([swap(piece_for(array, 3), "outer", 3, ends)] if split_last else [])
+
+    def received(pieces, met):
+        return pieces[:-1] + [pieces[-1] + met] if split_last else pieces
+
+    place = jnp.stack([inner, head, outer]).astype(jnp.int32)
+    gates = send(after(cut[:, 0], weights_out))
     kept, sent, *whole = projection(blocks, weights_out, place, head_count, inner_count)
     context = whole[0] if whole else own_context
     projected = kept.astype(jnp.float32)
     for e in range(1, head_count):
         projected = projected + swap(sent[e - 1], "head", e).astype(jnp.float32)
-    projected, first = fence(projected, first)
+    projected, *gates = fence(projected, *gates)
     own_resid = lax.dynamic_slice_in_dim(resid, head * half, half, 0)
     hidden_part = (own_resid.astype(jnp.float32) + projected).astype(jnp.bfloat16)
 
-    second = spread(after(cut[1], first))
+    ups = send(after(cut[:, 1], gates[0]))
     upper = inner // 2
     own_rows = half // 2
     mine = lax.dynamic_slice_in_dim(hidden_part, upper * own_rows, own_rows, 0)
@@ -381,43 +392,36 @@
     squares = sum([jnp.sum(block * block, axis=1) for block in state])
     squares = squares + swap(squares, "inner", 1)
     inverse = lax.rsqrt(squares / D + 1e-05)[:, None]
-    part_rows = feature_rows // PARTS
-    normed = jnp.stack([block * inverse for block in state], axis=1).astype(jnp.bfloat16)
-    normed = normed.reshape(own_rows, 2, outer_count, PARTS, part_rows)
-    normed = jnp.transpose(normed, (0, 1, 3, 2, 4)).reshape(own_rows, 2 * feature_rows * outer_count)
-    normed, first, second = fence(normed, first, second)
+    normed = jnp.concatenate([block * inverse for block in state], axis=1).astype(jnp.bfloat16)
+    normed, *ups = fence(normed, *ups)
     tokens = lax.all_gather(normed, ("outer", "head"), axis=0, tiled=True)
 
-    third, first_y, second_y = fence(spread(after(cut[2], normed)), over_y(first), over_y(second))
-    fourth, third_y = fence(spread(after(cut[3], third)), over_y(third))
-    fifth, fourth_y = fence(spread(after(cut[4], fourth)), over_y(fourth))
-    sixth, fifth_y = fence(spread(after(cut[5], fifth)), over_y(fifth))
-    here = [first, second, third, fourth]
-    there = [first_y, second_y, third_y, fourth_y]
-    flat = [[stream.reshape(-1, hidden_cols) for stream in streams] for streams in (here, there)]
-    sums = gate_up(tokens, flat)
+    gates = received(gates, early[0][0] if early else None)
+    ups = received(ups, early[0][1] if early else None)
+    far = jnp.stack([jnp.stack(pair) for pair in zip(gates, ups)])
+    far_y, *downs = fence(over_y(far), *send(after(down_cut, normed)))
+    downs = jnp.stack([piece_for(down_cut, 0)] + received(downs, early[1] if early else None))
+    sums = gate_up(place, tokens, cut, far, cut_y, far_y)
     activated = activation(sums, swap(sums, "inner", 1))
 
-    downs = [[fifth, sixth], [fifth_y, over_y(sixth)]]
-    pieces = [[None] * PARTS, [None] * PARTS]
-    for part in range(PARTS):
-        for a in range(2):
-            kept, sent = down_product(activated, downs[a][part], place, head_count)
+    downs = [downs, over_y(downs)]
+    layer_out = jnp.zeros((half, outer_count * feature_rows), jnp.bfloat16)
+    for a in range(2):
+        for part in range(PARTS):
+            kept, sent = down_product(place, activated, downs[a], part, head_count)
+            if a == 0:
+                downs[1] = after(downs[1], kept)
             paired = kept.astype(jnp.float32)
             for e in range(1, head_count):
                 paired = paired + swap(sent[e - 1], "head", e).astype(jnp.float32)
             paired = paired.reshape(outer_count, own_rows, -1)
-            total = lax.dynamic_index_in_dim(paired, outer, 0, False)
+            total = piece_for(paired, 0)
             for d in range(1, outer_count):
-                sent = lax.dynamic_index_in_dim(paired, outer ^ d, 0, False).astype(jnp.bfloat16)
-                total = total + swap(sent, "outer", d).astype(jnp.float32)
-            near = state[a].reshape(own_rows, outer_count, PARTS, part_rows)[:, :, part]
-            total = (near.reshape(own_rows, -1) + total).astype(jnp.bfloat16)
-            pieces[a][part] = (over_y(total) if a else total).reshape(own_rows, outer_count, 1, part_rows)
-    halves = [jnp.concatenate(parts, axis=2).reshape(own_rows, -1) for parts in pieces]
-    layer_out = jnp.zeros((half, halves[0].shape[1]), jnp.bfloat16)
-    layer_out = lax.dynamic_update_slice(layer_out, halves[0], (upper * own_rows, 0))
-    layer_out = lax.dynamic_update_slice(layer_out, halves[1], ((1 - upper) * own_rows, 0))
+                total = total + swap(piece_for(paired, d).astype(jnp.bfloat16), "outer", d).astype(jnp.float32)
+            width = total.shape[1]
+            total = (state[a][:, part * width : (part + 1) * width] + total).astype(jnp.bfloat16)
+            first_row = ((1 - upper) if a else upper) * own_rows
+            layer_out = lax.dynamic_update_slice(layer_out, over_y(total) if a else total, (first_row, part * width))
     return (context, layer_out)
 
 

time: 421 us -> 466 us (1.11)
  waiting for transfers between devices: 237 us -> 285 us
  local copies, waits for them, and re-layouts: 35.5 us -> 20.6 us
  starting transfers between devices: 78.4 us -> 91.2 us
    ppermute x31 -> x39, waiting for transfers between devices: 159 us -> 222 us  [swap(): return lax.ppermute(array, axis, [(s, s ^ distance) for s in members])]
    ppermute x31 -> x39, starting transfers between devices: 42.1 us -> 79 us  [swap(): return lax.ppermute(array, axis, [(s, s ^ distance) for s in members])]
    all_to_all x6 -> x0, waiting for transfers between devices: 36.1 us -> none  [the longest x1 26.9 us: per_device(): fourth, third_y = fence(spread(after(cut[3], third)), over_y(third))]
    all_gather x1, waiting for transfers between devices: 0.01 us -> 34.9 us  [per_device(): tokens = lax.all_gather(normed, ('outer', 'head'), axis=0, tiled=True)]
    all_to_all x6 -> x0, starting transfers between devices: 24.2 us -> none  [the longest x1 4.71 us: per_device(): fourth, third_y = fence(spread(after(cut[3], third)), over_y(third))]
    all_gather x1, waiting for transfers between devices: 27 us -> 18.7 us  [per_device(): weights_out = lax.all_gather(w_out, 'outer', axis=1, tiled=True)]
    all_to_all x1, waiting for transfers between devices: 14.4 us -> 8.38 us  [per_device(): lax.all_to_all(groups, ('inner', 'head'), split_axis=0, concat_axis=0, ti...]
    squeeze x0 -> x5, local copies, waits for them, and re-layouts: none -> 5.82 us  [the longest x4 5.47 us: per_device(): lax.dynamic_index_in_dim(array, outer ^ d, 0, False)]
  transfers between devices with their start and end apart: 42 -> 44, of which waited for: 23 -> 23; matrix products, arithmetic and copies ran while one was open for 8% -> 5% of each run, Pallas kernels for 7% -> 5%
where the time goes in v6:
time: 466 us; the launch traced here: 465 us
  waiting for transfers between devices  285 us (61%)
  starting transfers between devices  91.2 us (20%)
  Pallas kernels  45 us (10%)
  local copies, waits for them, and re-layouts  20.6 us (4%)
  between operations  14.6 us (3%)
  other arithmetic  8.96 us (2%)
    ppermute x39, waiting for transfers between devices, swap(): return lax.ppermute(array, axis, [(s, s ^ distance) for s in members])  222 us
    ppermute x39, starting transfers between devices, swap(): return lax.ppermute(array, axis, [(s, s ^ distance) for s in members])  79 us
    all_gather x1, waiting for transfers between devices, per_device(): tokens = lax.all_gather(normed, ('outer', 'head'), axis=0, tiled=True)  34.9 us
    all_gather x1, waiting for transfers between devices, per_device(): weights_out = lax.all_gather(w_out, 'outer', axis=1, tiled=True)  18.7 us
    pallas_call x1, Pallas kernels, gate_up(): pl.pallas_call(gate_up_kernel, in_specs=[SMEM] + [ANY] * 5, out_specs=VME...  13.8 us
    pallas_call x4, Pallas kernels, down_product(): pl.pallas_call(functools.partial(down_kernel, part), in_specs=[SMEM, VMEM...  12.6 us
  transfers between devices with their start and end apart: 44, of which 23 were waited for; matrix products, arithmetic and copies ran while one was open for 5% of the time, Pallas kernels for 5%

profile of v6, /device:TPU:0, one launch (start us, length us, event | category | flops | bytes accessed | tf_op | source)
XLA Modules:
  0.0 465.0 jit_solution(10095643564233946046)
XLA Ops:
  31.6 8.4 %all-to-all-done = bf16[8,64,1024]{2,1,0:T(8,128)(2,1)S(1)} async-done(((bf16[8,64,1024]{2,1,0:T(8,128)(2,1)}), bf16[8,64,1024]{2,1,0:T(8,128)(2,1)S(1)}, u32[]{:S(2)}, u32[]{:S(2)}) %all-to-all-start) | async-done | bytes 1048608 | tf_op jit(solution)/shard_map/all_to_all | solution.py:341
  40.0 5.9 %attention.1.refs_0_ = bf16[512,512]{1,0:T(8,128)(2,1)S(1)} custom-call(s32[512,1]{1,0:T(8,128)S(1)} %copy.20.starts_ref, bf16[512,1024]{1,0:T(8,128)(2,1)S(1)} %bitcast.133, bf16[512,1024]{1,0:T(8,128)(2,1)S(1)} %bitcast.134, bf16[512,1024]{1,0:T(8,128)(2,1)S(1)} %bitcast.135), custom_call_target="tpu_custom_call" | custom-call | flops 671088640 | bytes 1048576 | tf_op jit(solution)/shard_map/attention/pallas_call | solution.py:95
  46.5 13.1 %collective-permute-done.3.refs_2_ = bf16[512,512]{1,0:T(8,128)(2,1)S(1)} collective-permute-done((bf16[512,512]{1,0:T(8,128)(2,1)S(1)}, bf16[512,512]{1,0:T(8,128)(2,1)S(1)}, u32[]{:S(2)}, u32[]{:S(2)}) %collective-permute-start.3) | collective-permute-done | bytes 524320 | tf_op jit(solution)/shard_map/ppermute | solution.py:31
  68.3 18.8 %collective-permute-done.5.cut_y = bf16[2,256,896]{2,1,0:T(8,128)(2,1)S(1)} collective-permute-done((bf16[2,256,896]{2,1,0:T(8,128)(2,1)}, bf16[2,256,896]{2,1,0:T(8,128)(2,1)S(1)}, u32[]{:S(2)}, u32[]{:S(2)}) %collective-permute-start.5) | collective-permute-done | bytes 917536 | tf_op jit(solution)/shard_map/ppermute | solution.py:31
  87.1 18.7 %all-gather.3.cloned.1.call-done.refs_4_ = bf16[2048,1024]{1,0:T(8,128)(2,1)} async-done(((bf16[2048,256]{1,0:T(8,128)(2,1)}), bf16[2048,1024]{1,0:T(8,128)(2,1)}) %all-gather.3.cloned.1.call-update) | async-done | bytes 4194320 | tf_op jit(solution)/shard_map/all_gather | solution.py:333
  107.6 5.6 %projection.1 = (bf16[256,1024]{1,0:T(8,128)(2,1)S(1)}, bf16[1,256,1024]{2,1,0:T(8,128)(2,1)}, bf16[128,2048]{1,0:T(8,128)(2,1)}) custom-call(s32[3]{0:T(128)S(1)} %pad_add_fusion.place_ref, bf16[512,512]{1,0:T(8,128)(2,1)S(1)} %attention.1.refs_0_, bf16[512,512]{1,0:T(8,128)(2,1)S(1)} %copy-done.6, bf16[512,512]{1,0:T(8,128)(2,1)S(1)} %collective-permute-done.3.refs_2_, ...), custom_call_target="tpu_custom_call" | custom-call | flops 2147483648 | bytes 6291456 | tf_op jit(solution)/shard_map/projection/pallas_call | solution.py:175
  117.9 25.9 %collective-permute-start.10 = (bf16[256,896]{1,0:T(8,128)(2,1)}, bf16[256,896]{1,0:T(8,128)(2,1)}, u32[]{:S(2)}, u32[]{:S(2)}) collective-permute-start(bf16[256,896]{1,0:T(8,128)(2,1)} %get-tuple-element.85), channel_id=1, source_target_pairs={{0,2},{1,3},{2,0},{3,1},{4,6},{5,7},{6,4},{7,5},{8,10},{9,11},{10,... | collective-permute-start | bytes 1376264 | tf_op jit(solution)/shard_map/ppermute | solution.py:31
  144.9 19.5 %collective-permute-done.10 = bf16[256,896]{1,0:T(8,128)(2,1)} collective-permute-done((bf16[256,896]{1,0:T(8,128)(2,1)}, bf16[256,896]{1,0:T(8,128)(2,1)}, u32[]{:S(2)}, u32[]{:S(2)}) %collective-permute-start.10) | collective-permute-done | bytes 458784 | tf_op jit(solution)/shard_map/ppermute | solution.py:31
  166.2 5.9 %collective-permute-done.12 = bf16[128,1024]{1,0:T(8,128)(2,1)S(1)} collective-permute-done((bf16[128,1024]{1,0:T(8,128)(2,1)S(1)}, bf16[128,1024]{1,0:T(8,128)(2,1)S(1)}, u32[]{:S(2)}, u32[]{:S(2)}) %collective-permute-start.12) | collective-permute-done | bytes 262176 | tf_op jit(solution)/shard_map/ppermute | solution.py:31
  180.9 10.0 %collective-permute-done.16 = bf16[256,896]{1,0:T(8,128)(2,1)S(1)} collective-permute-done((bf16[256,896]{1,0:T(8,128)(2,1)}, bf16[256,896]{1,0:T(8,128)(2,1)S(1)}, u32[]{:S(2)}, u32[]{:S(2)}) %collective-permute-start.16) | collective-permute-done | bytes 458784 | tf_op jit(solution)/shard_map/ppermute | solution.py:31
  191.0 19.3 %collective-permute-done.15 = bf16[256,896]{1,0:T(8,128)(2,1)S(1)} collective-permute-done((bf16[256,896]{1,0:T(8,128)(2,1)}, bf16[256,896]{1,0:T(8,128)(2,1)S(1)}, u32[]{:S(2)}, u32[]{:S(2)}) %collective-permute-start.15) | collective-permute-done | bytes 458784 | tf_op jit(solution)/shard_map/ppermute | solution.py:31
  221.7 19.5 %collective-permute-done.20 = bf16[896,256]{1,0:T(8,128)(2,1)} collective-permute-done((bf16[896,256]{1,0:T(8,128)(2,1)S(1)}, bf16[896,256]{1,0:T(8,128)(2,1)}, u32[]{:S(2)}, u32[]{:S(2)}) %collective-permute-start.20) | collective-permute-done | bytes 458784 | tf_op jit(solution)/shard_map/ppermute | solution.py:31
  241.2 26.5 %collective-permute-done.19 = bf16[896,256]{1,0:T(8,128)(2,1)} collective-permute-done((bf16[896,256]{1,0:T(8,128)(2,1)S(1)}, bf16[896,256]{1,0:T(8,128)(2,1)}, u32[]{:S(2)}, u32[]{:S(2)}) %collective-permute-start.19) | collective-permute-done | bytes 458784 | tf_op jit(solution)/shard_map/ppermute | solution.py:31
  267.8 7.5 %collective-permute-done.17.far_y = bf16[3,2,256,896]{3,2,1,0:T(8,128)(2,1)} collective-permute-done((bf16[3,2,256,896]{3,2,1,0:T(8,128)(2,1)S(1)}, bf16[3,2,256,896]{3,2,1,0:T(8,128)(2,1)}, u32[]{:S(2)}, u32[]{:S(2)}) %collective-permute-start.17) | collective-permute-done | bytes 2752544 | tf_op jit(solution)/shard_map/ppermute | solution.py:31
  275.3 34.9 %all-gather.5.cloned.1.call-done.tokens = bf16[1024,2048]{1,0:T(8,128)(2,1)} async-done(((bf16[128,2048]{1,0:T(8,128)(2,1)}), bf16[1024,2048]{1,0:T(8,128)(2,1)}) %all-gather.5.cloned.1.call-update) | async-done | bytes 4194320 | tf_op jit(solution)/shard_map/all_gather | solution.py:397
  311.4 13.8 %gate_up.1.here_ref = bf16[2,1024,896]{2,1,0:T(8,128)(2,1)} custom-call(s32[3]{0:T(128)S(1)} %pad_add_fusion.place_ref, bf16[1024,2048]{1,0:T(8,128)(2,1)} %all-gather.5.cloned.1.call-done.tokens, bf16[4,2,256,896]{3,2,1,0:T(8,128)(2,1)} %copy-done, bf16[3,2,256,896]{3,2,1,0:T(8,128)(2,1)S(1)} %pad_maximum_fusion.far, bf16[2,256,896]{2,1,0:T(8,128)(2,1)S(1)} %copy-done.4, ...), custom_call_target="tpu_custom_call" | custom-call | flops 7516192768 | bytes 15204352 | tf_op jit(solution)/shard_map/gate_up/pallas_call | solution.py:222
  343.8 26.7 %collective-permute-done.30.weights = bf16[4,896,256]{2,1,0:T(8,128)(2,1)S(1)} collective-permute-done((bf16[4,896,256]{2,1,0:T(8,128)(2,1)S(1)}, bf16[4,896,256]{2,1,0:T(8,128)(2,1)S(1)}, u32[]{:S(2)}, u32[]{:S(2)}) %collective-permute-start.30) | collective-permute-done | bytes 1835040 | tf_op jit(solution)/shard_map/ppermute | solution.py:31
  381.2 7.5 %collective-permute-done.36 = bf16[512,512]{1,0:T(8,128)(2,1)S(1)} collective-permute-done((bf16[512,512]{1,0:T(8,128)(2,1)S(1)}, bf16[512,512]{1,0:T(8,128)(2,1)S(1)}, u32[]{:S(2)}, u32[]{:S(2)}) %collective-permute-start.36) | collective-permute-done | bytes 524320 | tf_op jit(solution)/shard_map/ppermute | solution.py:31
  392.0 7.9 %collective-permute-done.31 = bf16[512,512]{1,0:T(8,128)(2,1)S(1)} collective-permute-done((bf16[512,512]{1,0:T(8,128)(2,1)S(1)}, bf16[512,512]{1,0:T(8,128)(2,1)S(1)}, u32[]{:S(2)}, u32[]{:S(2)}) %collective-permute-start.31) | collective-permute-done | bytes 524320 | tf_op jit(solution)/shard_map/ppermute | solution.py:31
  401.7 9.4 %collective-permute-done.22 = bf16[512,512]{1,0:T(8,128)(2,1)S(1)} collective-permute-done((bf16[512,512]{1,0:T(8,128)(2,1)S(1)}, bf16[512,512]{1,0:T(8,128)(2,1)S(1)}, u32[]{:S(2)}, u32[]{:S(2)}) %collective-permute-start.22) | collective-permute-done | bytes 524320 | tf_op jit(solution)/shard_map/ppermute | solution.py:31
  412.1 9.0 %collective-permute-done.26 = bf16[512,512]{1,0:T(8,128)(2,1)S(1)} collective-permute-done((bf16[512,512]{1,0:T(8,128)(2,1)S(1)}, bf16[512,512]{1,0:T(8,128)(2,1)S(1)}, u32[]{:S(2)}, u32[]{:S(2)}) %collective-permute-start.26) | collective-permute-done | bytes 524320 | tf_op jit(solution)/shard_map/ppermute | solution.py:31
  429.4 6.1 %collective-permute-start.27 = (bf16[128,512]{1,0:T(8,128)(2,1)S(1)}, bf16[128,512]{1,0:T(8,128)(2,1)S(1)}, u32[]{:S(2)}, u32[]{:S(2)}) collective-permute-start(bf16[128,512]{1,0:T(8,128)(2,1)S(1)} %get-tuple-element.93), channel_id=1, source_target_pairs={{0,1},{1,0},{2,3},{3,2},{4,5},{5,4},{6,7},{7,6},{8,9},{9,8},{10,11... | collective-permute-start | bytes 393224 | tf_op jit(solution)/shard_map/ppermute | solution.py:31
  435.4 6.4 %collective-permute-done.33 = bf16[128,512]{1,0:T(8,128)(2,1)S(1)} collective-permute-done((bf16[128,512]{1,0:T(8,128)(2,1)S(1)}, bf16[128,512]{1,0:T(8,128)(2,1)S(1)}, u32[]{:S(2)}, u32[]{:S(2)}) %collective-permute-start.33) | collective-permute-done | bytes 131104 | tf_op jit(solution)/shard_map/ppermute | solution.py:31
  444.7 7.6 %collective-permute-done.24 = bf16[128,512]{1,0:T(8,128)(2,1)S(1)} collective-permute-done((bf16[128,512]{1,0:T(8,128)(2,1)S(1)}, bf16[128,512]{1,0:T(8,128)(2,1)S(1)}, u32[]{:S(2)}, u32[]{:S(2)}) %collective-permute-start.24) | collective-permute-done | bytes 131104 | tf_op jit(solution)/shard_map/ppermute | solution.py:31
  (162 shorter events, 116.7 us)
Async XLA Ops:
  7.2 98.6 %all-gather.3.cloned.1.call-start = ((), (), s32[]{:S(2)}) async-start(), calls=%async_computation.1 | async-start | bytes 5242880 | tf_op jit(solution)/shard_map/all_gather | solution.py:333
  25.0 285.1 %all-gather.5.cloned.1.call-start = ((), (), s32[]{:S(2)}) async-start(), calls=%async_computation.2 | async-start | bytes 4718592 | tf_op jit(solution)/shard_map/all_gather | solution.py:397
  64.1 23.0 %collective-permute-start.5 = (bf16[2,256,896]{2,1,0:T(8,128)(2,1)}, bf16[2,256,896]{2,1,0:T(8,128)(2,1)S(1)}, u32[]{:S(2)}, u32[]{:S(2)}) collective-permute-start(bf16[2,256,896]{2,1,0:T(8,128)(2,1)} %get-tuple-element.39), channel_id=1, source_target_pairs={{0,8},{4,12},{8,0},{12,4},{1,9},{5,13},{9,1},{13,5},{2,10},{6,14},... | collective-permute-start | bytes 2752520 | tf_op jit(solution)/shard_map/ppermute | solution.py:31
  65.6 40.2 %collective-permute-start.2 = (bf16[512,512]{1,0:T(8,128)(2,1)S(1)}, bf16[512,512]{1,0:T(8,128)(2,1)S(1)}, u32[]{:S(2)}, u32[]{:S(2)}) collective-permute-start(bf16[512,512]{1,0:T(8,128)(2,1)S(1)} %attention.1.refs_0_), channel_id=1, source_target_pairs={{0,4},{4,0},{8,12},{12,8},{1,5},{5,1},{9,13},{13,9},{2,6},{6,2},{1... | collective-permute-start | bytes 1572872 | tf_op jit(solution)/shard_map/ppermute | solution.py:31
  113.3 31.5 %collective-permute-start.8 = (bf16[256,1024]{1,0:T(8,128)(2,1)}, bf16[256,1024]{1,0:T(8,128)(2,1)S(1)}, u32[]{:S(2)}, u32[]{:S(2)}) collective-permute-start(bf16[256,1024]{1,0:T(8,128)(2,1)} %bitcast.13), channel_id=1, source_target_pairs={{0,16},{16,0},{1,17},{17,1},{2,18},{18,2},{3,19},{19,3},{4,20},{20... | collective-permute-start | bytes 1572872 | tf_op jit(solution)/shard_map/ppermute | solution.py:31
  115.9 28.9 %collective-permute-start.11 = (bf16[256,896]{1,0:T(8,128)(2,1)}, bf16[256,896]{1,0:T(8,128)(2,1)}, u32[]{:S(2)}, u32[]{:S(2)}) collective-permute-start(bf16[256,896]{1,0:T(8,128)(2,1)} %get-tuple-element.84), channel_id=1, source_target_pairs={{0,3},{3,0},{4,7},{7,4},{8,11},{11,8},{12,15},{15,12},{16,19},{19,... | collective-permute-start | bytes 1376264 | tf_op jit(solution)/shard_map/ppermute | solution.py:31
  117.9 46.5 %collective-permute-start.10 = (bf16[256,896]{1,0:T(8,128)(2,1)}, bf16[256,896]{1,0:T(8,128)(2,1)}, u32[]{:S(2)}, u32[]{:S(2)}) collective-permute-start(bf16[256,896]{1,0:T(8,128)(2,1)} %get-tuple-element.85), channel_id=1, source_target_pairs={{0,2},{1,3},{2,0},{3,1},{4,6},{5,7},{6,4},{7,5},{8,10},{9,11},{10,... | collective-permute-start | bytes 1376264 | tf_op jit(solution)/shard_map/ppermute | solution.py:31
  143.7 20.6 %collective-permute-start.9 = (bf16[256,896]{1,0:T(8,128)(2,1)}, bf16[256,896]{1,0:T(8,128)(2,1)}, u32[]{:S(2)}, u32[]{:S(2)}) collective-permute-start(bf16[256,896]{1,0:T(8,128)(2,1)} %get-tuple-element.86), channel_id=1, source_target_pairs={{0,1},{1,0},{2,3},{3,2},{4,5},{5,4},{6,7},{7,6},{8,9},{9,8},{10,11... | collective-permute-start | bytes 1376264 | tf_op jit(solution)/shard_map/ppermute | solution.py:31
  179.1 31.1 %collective-permute-start.15 = (bf16[256,896]{1,0:T(8,128)(2,1)}, bf16[256,896]{1,0:T(8,128)(2,1)S(1)}, u32[]{:S(2)}, u32[]{:S(2)}) collective-permute-start(bf16[256,896]{1,0:T(8,128)(2,1)} %get-tuple-element.82), channel_id=1, source_target_pairs={{0,2},{1,3},{2,0},{3,1},{4,6},{5,7},{6,4},{7,5},{8,10},{9,11},{10,... | collective-permute-start | bytes 1376264 | tf_op jit(solution)/shard_map/ppermute | solution.py:31
  179.2 31.0 %collective-permute-start.14 = (bf16[256,896]{1,0:T(8,128)(2,1)}, bf16[256,896]{1,0:T(8,128)(2,1)S(1)}, u32[]{:S(2)}, u32[]{:S(2)}) collective-permute-start(bf16[256,896]{1,0:T(8,128)(2,1)} %get-tuple-element.83), channel_id=1, source_target_pairs={{0,1},{1,0},{2,3},{3,2},{4,5},{5,4},{6,7},{7,6},{8,9},{9,8},{10,11... | collective-permute-start | bytes 1376264 | tf_op jit(solution)/shard_map/ppermute | solution.py:31
  213.5 61.8 %collective-permute-start.17 = (bf16[3,2,256,896]{3,2,1,0:T(8,128)(2,1)S(1)}, bf16[3,2,256,896]{3,2,1,0:T(8,128)(2,1)}, u32[]{:S(2)}, u32[]{:S(2)}) collective-permute-start(bf16[3,2,256,896]{3,2,1,0:T(8,128)(2,1)S(1)} %pad_maximum_fusion.far), channel_id=1, source_target_pairs={{0,8},{4,12},{8,0},{12,4},{1,9},{5,13},{9,1},{13,5},{2,10},{6,14},... | collective-permute-start | bytes 8257544 | tf_op jit(solution)/shard_map/ppermute | solution.py:31
  215.2 26.1 %collective-permute-start.20 = (bf16[896,256]{1,0:T(8,128)(2,1)S(1)}, bf16[896,256]{1,0:T(8,128)(2,1)}, u32[]{:S(2)}, u32[]{:S(2)}) collective-permute-start(bf16[896,256]{1,0:T(8,128)(2,1)S(1)} %get-tuple-element.78), channel_id=1, source_target_pairs={{0,3},{3,0},{4,7},{7,4},{8,11},{11,8},{12,15},{15,12},{16,19},{19,... | collective-permute-start | bytes 1376264 | tf_op jit(solution)/shard_map/ppermute | solution.py:31
  220.0 47.8 %collective-permute-start.19 = (bf16[896,256]{1,0:T(8,128)(2,1)S(1)}, bf16[896,256]{1,0:T(8,128)(2,1)}, u32[]{:S(2)}, u32[]{:S(2)}) collective-permute-start(bf16[896,256]{1,0:T(8,128)(2,1)S(1)} %get-tuple-element.79), channel_id=1, source_target_pairs={{0,2},{1,3},{2,0},{3,1},{4,6},{5,7},{6,4},{7,5},{8,10},{9,11},{10,... | collective-permute-start | bytes 1376264 | tf_op jit(solution)/shard_map/ppermute | solution.py:31
  220.1 47.7 %collective-permute-start.18 = (bf16[896,256]{1,0:T(8,128)(2,1)S(1)}, bf16[896,256]{1,0:T(8,128)(2,1)}, u32[]{:S(2)}, u32[]{:S(2)}) collective-permute-start(bf16[896,256]{1,0:T(8,128)(2,1)S(1)} %get-tuple-element.80), channel_id=1, source_target_pairs={{0,1},{1,0},{2,3},{3,2},{4,5},{5,4},{6,7},{7,6},{8,9},{9,8},{10,11... | collective-permute-start | bytes 1376264 | tf_op jit(solution)/shard_map/ppermute | solution.py:31
  328.0 42.5 %collective-permute-start.30 = (bf16[4,896,256]{2,1,0:T(8,128)(2,1)S(1)}, bf16[4,896,256]{2,1,0:T(8,128)(2,1)S(1)}, u32[]{:S(2)}, u32[]{:S(2)}) collective-permute-start(bf16[4,896,256]{2,1,0:T(8,128)(2,1)S(1)} %pad_maximum_fusion.1.weights), channel_id=1, source_target_pairs={{0,8},{4,12},{8,0},{12,4},{1,9},{5,13},{9,1},{13,5},{2,10},{6,14},... | collective-permute-start | bytes 5505032 | tf_op jit(solution)/shard_map/ppermute | solution.py:31
  377.5 22.4 %collective-permute-start.31 = (bf16[512,512]{1,0:T(8,128)(2,1)S(1)}, bf16[512,512]{1,0:T(8,128)(2,1)S(1)}, u32[]{:S(2)}, u32[]{:S(2)}) collective-permute-start(bf16[512,512]{1,0:T(8,128)(2,1)S(1)} %bitcast.138), channel_id=1, source_target_pairs={{0,16},{16,0},{1,17},{17,1},{2,18},{18,2},{3,19},{19,3},{4,20},{20... | collective-permute-start | bytes 1572872 | tf_op jit(solution)/shard_map/ppermute | solution.py:31
  379.1 32.1 %collective-permute-start.22 = (bf16[512,512]{1,0:T(8,128)(2,1)S(1)}, bf16[512,512]{1,0:T(8,128)(2,1)S(1)}, u32[]{:S(2)}, u32[]{:S(2)}) collective-permute-start(bf16[512,512]{1,0:T(8,128)(2,1)S(1)} %bitcast.137), channel_id=1, source_target_pairs={{0,16},{16,0},{1,17},{17,1},{2,18},{18,2},{3,19},{19,3},{4,20},{20... | collective-permute-start | bytes 1572872 | tf_op jit(solution)/shard_map/ppermute | solution.py:31
  379.7 41.4 %collective-permute-start.26 = (bf16[512,512]{1,0:T(8,128)(2,1)S(1)}, bf16[512,512]{1,0:T(8,128)(2,1)S(1)}, u32[]{:S(2)}, u32[]{:S(2)}) collective-permute-start(bf16[512,512]{1,0:T(8,128)(2,1)S(1)} %bitcast.136), channel_id=1, source_target_pairs={{0,16},{16,0},{1,17},{17,1},{2,18},{18,2},{3,19},{19,3},{4,20},{20... | collective-permute-start | bytes 1572872 | tf_op jit(solution)/shard_map/ppermute | solution.py:31
  388.9 33.9 %collective-permute-start.37 = (bf16[128,512]{1,0:T(8,128)(2,1)S(1)}, bf16[128,512]{1,0:T(8,128)(2,1)S(1)}, u32[]{:S(2)}, u32[]{:S(2)}) collective-permute-start(bf16[128,512]{1,0:T(8,128)(2,1)S(1)} %get-tuple-element.87), channel_id=1, source_target_pairs={{0,1},{1,0},{2,3},{3,2},{4,5},{5,4},{6,7},{7,6},{8,9},{9,8},{10,11... | collective-permute-start | bytes 393224 | tf_op jit(solution)/shard_map/ppermute | solution.py:31
  389.8 34.0 %collective-permute-start.39 = (bf16[128,512]{1,0:T(8,128)(2,1)S(1)}, bf16[128,512]{1,0:T(8,128)(2,1)S(1)}, u32[]{:S(2)}, u32[]{:S(2)}) collective-permute-start(bf16[128,512]{1,0:T(8,128)(2,1)S(1)} %get-tuple-element.88), channel_id=1, source_target_pairs={{0,3},{1,2},{2,1},{3,0},{4,7},{5,6},{6,5},{7,4},{8,11},{9,10},{10,... | collective-permute-start | bytes 393224 | tf_op jit(solution)/shard_map/ppermute | solution.py:31
  399.9 26.0 %collective-permute-start.38 = (bf16[128,512]{1,0:T(8,128)(2,1)S(1)}, bf16[128,512]{1,0:T(8,128)(2,1)S(1)}, u32[]{:S(2)}, u32[]{:S(2)}) collective-permute-start(bf16[128,512]{1,0:T(8,128)(2,1)S(1)} %get-tuple-element.89), channel_id=1, source_target_pairs={{0,2},{1,3},{2,0},{3,1},{4,6},{5,7},{6,4},{7,5},{8,10},{9,11},{10,... | collective-permute-start | bytes 393224 | tf_op jit(solution)/shard_map/ppermute | solution.py:31
  423.7 19.4 %collective-permute-start.23 = (bf16[128,512]{1,0:T(8,128)(2,1)S(1)}, bf16[128,512]{1,0:T(8,128)(2,1)S(1)}, u32[]{:S(2)}, u32[]{:S(2)}) collective-permute-start(bf16[128,512]{1,0:T(8,128)(2,1)S(1)} %get-tuple-element.96), channel_id=1, source_target_pairs={{0,1},{1,0},{2,3},{3,2},{4,5},{5,4},{6,7},{7,6},{8,9},{9,8},{10,11... | collective-permute-start | bytes 393224 | tf_op jit(solution)/shard_map/ppermute | solution.py:31
  427.5 24.9 %collective-permute-start.24 = (bf16[128,512]{1,0:T(8,128)(2,1)S(1)}, bf16[128,512]{1,0:T(8,128)(2,1)S(1)}, u32[]{:S(2)}, u32[]{:S(2)}) collective-permute-start(bf16[128,512]{1,0:T(8,128)(2,1)S(1)} %get-tuple-element.98), channel_id=1, source_target_pairs={{0,2},{1,3},{2,0},{3,1},{4,6},{5,7},{6,4},{7,5},{8,10},{9,11},{10,... | collective-permute-start | bytes 393224 | tf_op jit(solution)/shard_map/ppermute | solution.py:31
  429.4 24.7 %collective-permute-start.27 = (bf16[128,512]{1,0:T(8,128)(2,1)S(1)}, bf16[128,512]{1,0:T(8,128)(2,1)S(1)}, u32[]{:S(2)}, u32[]{:S(2)}) collective-permute-start(bf16[128,512]{1,0:T(8,128)(2,1)S(1)} %get-tuple-element.93), channel_id=1, source_target_pairs={{0,1},{1,0},{2,3},{3,2},{4,5},{5,4},{6,7},{7,6},{8,9},{9,8},{10,11... | collective-permute-start | bytes 393224 | tf_op jit(solution)/shard_map/ppermute | solution.py:31
  (35 other events, 330.1 us)
Sparse Core Ops, SparseCore 0:
  9.6 96.1 all-gather.2
  210.4 99.7 all-gather.4

commit v7 on v5

--- a/solution.py
+++ b/solution.py
@@ -196,28 +196,32 @@
     )(place, *blocks, weights)
 
 
-def gate_up_kernel(block_count, tokens, *refs):
-    weights = refs[: 2 * PARTS * block_count]
-    out_ref, held, near, sums, token_sems, weight_sems = refs[2 * PARTS * block_count :]
-    rows, depth = weights[0].shape[0], weights[0].shape[0] * PARTS
+def gate_up_kernel(block_count, head_count, *refs):
+    tokens = refs[: block_count * head_count]
+    weights = refs[len(tokens) : len(tokens) + 2 * PARTS * block_count]
+    out_ref, held, near, sums, token_sems, weight_sems = refs[len(tokens) + len(weights) :]
+    rows, depth = tokens[0].shape
     copies = []
     for a in range(block_count):
-        cols = slice(a * depth, (a + 1) * depth)
-        copies.append([pltpu.make_async_copy(tokens.at[:, cols], held.at[:, cols], token_sems.at[a])])
+        group = []
+        for e in range(head_count):
+            j = a * head_count + e
+            target = held.at[pl.ds(e * rows, rows), pl.ds(a * depth, depth)]
+            group.append(pltpu.make_async_copy(tokens[j], target, token_sems.at[j]))
         for j in range(2 * PARTS * a, 2 * PARTS * (a + 1)):
-            part, which = (j // 2) % PARTS, j % 2
-            target = near.at[which, pl.ds(a * depth + part * rows, rows)]
-            copies[a].append(pltpu.make_async_copy(weights[j], target, weight_sems.at[j]))
+            target = near.at[j % 2, a, :, (j // 2) % PARTS]
+            group.append(pltpu.make_async_copy(weights[j], target, weight_sems.at[j]))
+        copies.append(group)
     for group in copies:
         for copy in group:
             copy.start()
     for a, group in enumerate(copies):
         for copy in group:
             copy.wait()
-        at = slice(a * depth, (a + 1) * depth)
         for which in range(2):
+            block = near[which, a].reshape(depth, -1)
             for tile in row_tiles(held.shape[0]):
-                product = jnp.dot(held[tile, at], near[which, at], preferred_element_type=jnp.float32)
+                product = jnp.dot(held[tile, a * depth : (a + 1) * depth], block, preferred_element_type=jnp.float32)
                 total = product if a == 0 else sums[which, tile, :] + product
                 if a < block_count - 1:
                     sums[which, tile, :] = total
@@ -226,30 +230,32 @@
 
 
 def gate_up(tokens, blocks):
-    rows = tokens.shape[0]
+    head_count = len(tokens[0])
+    rows, depth = tokens[0][0].shape
+    sources, stream_rows, cols = blocks[0][0].shape
+    tokens = [piece for block in tokens for piece in block]
     weights = [stream for block in blocks for stream in block]
-    depth, cols = weights[0].shape
-    depth = depth * PARTS * len(blocks)
-    return pl.pallas_call(
-        functools.partial(gate_up_kernel, len(blocks)),
-        in_specs=[ANY] * (1 + len(weights)),
+    rows, all_depth = rows * head_count, depth * len(blocks)
+    return pl.pallas_call(
+        functools.partial(gate_up_kernel, len(blocks), head_count),
+        in_specs=[ANY] * (len(tokens) + len(weights)),
         out_specs=VMEM,
         out_shape=jax.ShapeDtypeStruct((2, rows, cols), jnp.bfloat16),
         scratch_shapes=[
-            pltpu.VMEM((rows, depth), jnp.bfloat16),
-            pltpu.VMEM((2, depth, cols), jnp.bfloat16),
+            pltpu.VMEM((rows, all_depth), jnp.bfloat16),
+            pltpu.VMEM((2, len(blocks), sources, PARTS, stream_rows, cols), jnp.bfloat16),
             pltpu.VMEM((2, rows, cols), jnp.float32),
-            pltpu.SemaphoreType.DMA((len(blocks),)),
+            pltpu.SemaphoreType.DMA((len(tokens),)),
             pltpu.SemaphoreType.DMA((len(weights),)),
         ],
         compiler_params=pltpu.CompilerParams(vmem_limit_bytes=VMEM_LIMIT),
         cost_estimate=pl.CostEstimate(
-            flops=4 * rows * depth * cols,
-            bytes_accessed=2 * (rows * depth + 2 * depth * cols + 2 * rows * cols),
+            flops=4 * rows * all_depth * cols,
+            bytes_accessed=2 * (rows * all_depth + 2 * all_depth * cols + 2 * rows * cols),
             transcendentals=0,
         ),
         name="gate_up",
-    )(tokens, *weights)
+    )(*tokens, *weights)
 
 
 def activation_kernel(here_ref, there_ref, out_ref):
@@ -273,21 +279,15 @@
     )(here, there)
 
 
-def down_kernel(place_ref, activated_ref, weights_ref, kept_ref, sent_ref):
+def down_kernel(activated_ref, weights_ref, kept_ref, sent_ref):
     sources, _, cols = weights_ref.shape
-    head_count = sent_ref.shape[0] + 1
-    head = place_ref[1]
-    piece = kept_ref.shape[0] // sources
+    kept_rows = kept_ref.shape[0]
     if cols % HEAD_WIDTH:
         blocks = [weights_ref[s] for s in range(sources)]
     else:
         blocks = [jnp.concatenate([weights_ref[s] for s in range(sources)], axis=1)]
-    for e in range(head_count):
-        rows = []
-        for o in range(sources):
-            first = pl.multiple_of((o * head_count + (head ^ e)) * piece, piece)
-            rows.append(activated_ref[pl.ds(first, piece), :])
-        rows = jnp.concatenate(rows, axis=0)
+    for e in range(sent_ref.shape[0] + 1):
+        rows = activated_ref[e * kept_rows : (e + 1) * kept_rows, :]
         for s, block in enumerate(blocks):
             at = slice(s * block.shape[1], (s + 1) * block.shape[1])
             product = jnp.dot(rows, block, preferred_element_type=jnp.float32)
@@ -297,12 +297,12 @@
                 sent_ref[e - 1, :, at] = product.astype(jnp.bfloat16)
 
 
-def down_product(activated, weights, place, head_count):
+def down_product(activated, weights, head_count):
     rows = activated.shape[0] // head_count
     sources, depth, cols = weights.shape
     return pl.pallas_call(
         down_kernel,
-        in_specs=[SMEM, VMEM, VMEM],
+        in_specs=[VMEM, VMEM],
         out_specs=[VMEM, VMEM],
         out_shape=[
             jax.ShapeDtypeStruct((rows, sources * cols), jnp.bfloat16),
@@ -315,7 +315,7 @@
             transcendentals=0,
         ),
         name="down",
-    )(place, activated, weights)
+    )(activated, weights)
 
 
 def per_device(query, key, value, doc_lengths, resid, norm_gain, w_out, w_gate_up, w_down):
@@ -382,37 +382,44 @@
     squares = squares + swap(squares, "inner", 1)
     inverse = lax.rsqrt(squares / D + 1e-05)[:, None]
     part_rows = feature_rows // PARTS
-    normed = jnp.stack([block * inverse for block in state], axis=1).astype(jnp.bfloat16)
-    normed = normed.reshape(own_rows, 2, outer_count, PARTS, part_rows)
-    normed = jnp.transpose(normed, (0, 1, 3, 2, 4)).reshape(own_rows, 2 * feature_rows * outer_count)
-    normed, first, second = fence(normed, first, second)
-    tokens = lax.all_gather(normed, ("outer", "head"), axis=0, tiled=True)
-
-    third, first_y, second_y = fence(spread(after(cut[2], normed)), over_y(first), over_y(second))
-    fourth, third_y = fence(spread(after(cut[3], third)), over_y(third))
-    fifth, fourth_y = fence(spread(after(cut[4], fourth)), over_y(fourth))
-    sixth, fifth_y = fence(spread(after(cut[5], fifth)), over_y(fifth))
-    here = [first, second, third, fourth]
-    there = [first_y, second_y, third_y, fourth_y]
-    flat = [[stream.reshape(-1, hidden_cols) for stream in streams] for streams in (here, there)]
-    sums = gate_up(tokens, flat)
+    normed = [(block * inverse).astype(jnp.bfloat16) for block in state]
+    *normed, first, second = fence(*normed, first, second)
+    state = [block.reshape(own_rows, outer_count, PARTS, part_rows) for block in state]
+    state = [[block[:, :, part].reshape(own_rows, -1) for part in range(PARTS)] for block in state]
+
+    tokens = []
+    for block in normed:
+        block = lax.all_gather(block, "outer", axis=0, tiled=True)
+        tokens.append([swap(block, "head", e) if e else block for e in range(head_count)])
+
+    third, first_y, second_y = fence(spread(after(cut[2], normed[0])), over_y(first), over_y(second))
+    fourth, third_y, state = fence(spread(after(cut[3], third)), over_y(third), state)
+    fifth, fourth_y, tokens = fence(spread(after(cut[4], fourth)), over_y(fourth), tokens)
+    sums = gate_up(tokens, [[first, second, third, fourth], [first_y, second_y, third_y, fourth_y]])
     activated = activation(sums, swap(sums, "inner", 1))
 
-    downs = [[fifth, sixth], [fifth_y, over_y(sixth)]]
+    def over_heads(weights):
+        kept, sent = down_product(activated, weights, head_count)
+        paired = kept.astype(jnp.float32)
+        for e in range(1, head_count):
+            paired = paired + swap(sent[e - 1], "head", e).astype(jnp.float32)
+        return paired.reshape(outer_count, own_rows, -1)
+
+    paired = {(0, 0): over_heads(fifth)}
+    sixth, fifth_y, paired[0, 0] = fence(spread(after(cut[5], fifth)), over_y(fifth), paired[0, 0])
+    sixth_y = over_y(sixth)
+    paired[1, 0] = over_heads(fifth_y)
+    paired[0, 1] = over_heads(sixth)
+    paired[1, 1] = over_heads(after(sixth_y, paired[1, 0]))
+
     pieces = [[None] * PARTS, [None] * PARTS]
     for part in range(PARTS):
         for a in range(2):
-            kept, sent = down_product(activated, downs[a][part], place, head_count)
-            paired = kept.astype(jnp.float32)
-            for e in range(1, head_count):
-                paired = paired + swap(sent[e - 1], "head", e).astype(jnp.float32)
-            paired = paired.reshape(outer_count, own_rows, -1)
-            total = lax.dynamic_index_in_dim(paired, outer, 0, False)
+            total = state[a][part] + lax.dynamic_index_in_dim(paired[a, part], outer, 0, False)
             for d in range(1, outer_count):
-                sent = lax.dynamic_index_in_dim(paired, outer ^ d, 0, False).astype(jnp.bfloat16)
+                sent = lax.dynamic_index_in_dim(paired[a, part], outer ^ d, 0, False).astype(jnp.bfloat16)
                 total = total + swap(sent, "outer", d).astype(jnp.float32)
-            near = state[a].reshape(own_rows, outer_count, PARTS, part_rows)[:, :, part]
-            total = (near.reshape(own_rows, -1) + total).astype(jnp.bfloat16)
+            total = total.astype(jnp.bfloat16)
             pieces[a][part] = (over_y(total) if a else total).reshape(own_rows, outer_count, 1, part_rows)
     halves = [jnp.concatenate(parts, axis=2).reshape(own_rows, -1) for parts in pieces]
     layer_out = jnp.zeros((half, halves[0].shape[1]), jnp.bfloat16)

time: 421 us -> 401 us (0.952)
  waiting for transfers between devices: 237 us -> 226 us
  local copies, waits for them, and re-layouts: 35.5 us -> 27.7 us
    all_to_all x4, waiting for transfers between devices: 29.9 us -> 13.5 us  [the longest x1 13.4 us: per_device(): spread(after(cut[3], third))]
    ppermute x31 -> x33, waiting for transfers between devices: 159 us -> 153 us  [swap(): return lax.ppermute(array, axis, [(s, s ^ distance) for s in range(count)])]
    all_to_all x1, waiting for transfers between devices: 5.94 us -> 11.4 us  [per_device(): second = spread(after(cut[1], first))]
    unnamed x42 -> x36, local copies, waits for them, and re-layouts: 13.5 us -> 10.6 us
    ppermute x31 -> x33, starting transfers between devices: 42.1 us -> 42.4 us  [swap(): return lax.ppermute(array, axis, [(s, s ^ distance) for s in range(count)])]
  transfers between devices with their start and end apart: 42 -> 45, of which waited for: 23 -> 23; matrix products, arithmetic and copies ran while one was open for 8% -> 7% of each run, Pallas kernels for 7% -> 7%
where the time goes in v7:
time: 401 us; the launch traced here: 399 us
  waiting for transfers between devices  226 us (56%)
  starting transfers between devices  78.8 us (20%)
  Pallas kernels  42.6 us (11%)
  local copies, waits for them, and re-layouts  27.7 us (7%)
  between operations  14.3 us (4%)
  other arithmetic  10.2 us (3%)
    ppermute x33, waiting for transfers between devices, swap(): return lax.ppermute(array, axis, [(s, s ^ distance) for s in range(count)])  153 us
    ppermute x33, starting transfers between devices, swap(): return lax.ppermute(array, axis, [(s, s ^ distance) for s in range(count)])  42.4 us
    all_gather x1, waiting for transfers between devices, per_device(): weights_out = lax.all_gather(w_out, 'outer', axis=1, tiled=True)  27 us
    all_to_all x1, waiting for transfers between devices, per_device(): lax.all_to_all(groups, ('inner', 'head'), split_axis=0, concat_axis=0, ti...  14.4 us
    all_to_all x1, waiting for transfers between devices, per_device(): spread(after(cut[3], third))  13.4 us
    pallas_call x1, Pallas kernels, gate_up(): pl.pallas_call(functools.partial(gate_up_kernel, len(blocks), head_count)...  13.1 us
    all_to_all x1, waiting for transfers between devices, per_device(): second = spread(after(cut[1], first))  11.4 us
    unnamed x36, local copies, waits for them, and re-layouts  10.6 us
  transfers between devices with their start and end apart: 45, of which 23 were waited for; matrix products, arithmetic and copies ran while one was open for 7% of the time, Pallas kernels for 7%

profile of v7, /device:TPU:0, one launch (start us, length us, event | category | flops | bytes accessed | tf_op | source)
XLA Modules:
  0.0 399.2 jit_solution(8812978586704031033)
XLA Ops:
  7.9 4.9 %collective-permute-start = (bf16[64,1024]{1,0:T(8,128)(2,1)}, bf16[64,1024]{1,0:T(8,128)(2,1)S(1)}, u32[]{:S(2)}, u32[]{:S(2)}) collective-permute-start(bf16[64,1024]{1,0:T(8,128)(2,1)} %param.10), channel_id=1, source_target_pairs={{0,1},{1,2},{2,3},{4,5},{5,6},{6,7},{8,9},{9,10},{10,11},{12,13},{... | collective-permute-start | bytes 393224 | tf_op jit(solution)/shard_map/ppermute | solution.py:339
  25.6 14.4 %all-to-all-done = bf16[8,64,1024]{2,1,0:T(8,128)(2,1)S(1)} async-done(((bf16[8,64,1024]{2,1,0:T(8,128)(2,1)}), bf16[8,64,1024]{2,1,0:T(8,128)(2,1)S(1)}, u32[]{:S(2)}, u32[]{:S(2)}) %all-to-all-start) | async-done | bytes 1048608 | tf_op jit(solution)/shard_map/all_to_all | solution.py:342
  40.0 5.9 %attention.1.refs_0_ = bf16[512,512]{1,0:T(8,128)(2,1)S(1)} custom-call(s32[512,1]{1,0:T(8,128)S(1)} %copy.27.starts_ref, bf16[512,1024]{1,0:T(8,128)(2,1)S(1)} %bitcast.93, bf16[512,1024]{1,0:T(8,128)(2,1)S(1)} %bitcast.94, bf16[512,1024]{1,0:T(8,128)(2,1)S(1)} %bitcast.95), custom_call_target="tpu_custom_call" | custom-call | flops 671088640 | bytes 1048576 | tf_op jit(solution)/shard_map/attention/pallas_call | solution.py:95
  46.9 12.6 %collective-permute-done.3.refs_2_ = bf16[512,512]{1,0:T(8,128)(2,1)S(1)} collective-permute-done((bf16[512,512]{1,0:T(8,128)(2,1)S(1)}, bf16[512,512]{1,0:T(8,128)(2,1)S(1)}, u32[]{:S(2)}, u32[]{:S(2)}) %collective-permute-start.3) | collective-permute-done | bytes 524320 | tf_op jit(solution)/shard_map/ppermute | solution.py:31
  60.4 5.5 %cut_weights.1 = (bf16[4,128,896]{2,1,0:T(8,128)(2,1)}, bf16[4,128,896]{2,1,0:T(8,128)(2,1)}, bf16[4,128,896]{2,1,0:T(8,128)(2,1)}, bf16[4,128,896]{2,1,0:T(8,12...) custom-call(f32[256,1]{1,0:T(8,128)S(1)} %copy.28.gain_ref, bf16[2,256,3584]{2,1,0:T(8,128)(2,1)} %gate_up_ref.1, ...), custom_call_target="tpu_custom_call" | custom-call | flops 1835008 | bytes 11010048 | tf_op jit(solution)/shard_map/cut_weights/pallas_call | solution.py:139
  65.9 27.0 %all-gather.4.cloned.1.call-done.refs_4_ = bf16[2048,1024]{1,0:T(8,128)(2,1)} async-done(((bf16[2048,256]{1,0:T(8,128)(2,1)}), bf16[2048,1024]{1,0:T(8,128)(2,1)}) %all-gather.4.cloned.1.call-update) | async-done | bytes 4194320 | tf_op jit(solution)/shard_map/all_gather | solution.py:337
  96.5 5.3 %projection.1 = (bf16[256,1024]{1,0:T(8,128)(2,1)S(1)}, bf16[1,256,1024]{2,1,0:T(8,128)(2,1)S(1)}, bf16[128,2048]{1,0:T(8,128)(2,1)}) custom-call(s32[2]{0:T(128)S(1)} %pad_add_fusion.place_ref, bf16[512,512]{1,0:T(8,128)(2,1)S(1)} %attention.1.refs_0_, bf16[512,512]{1,0:T(8,128)(2,1)S(1)} %collective-permute-done.2.refs_1_, ...), custom_call_target="tpu_custom_call" | custom-call | flops 2147483648 | bytes 6291456 | tf_op jit(solution)/shard_map/projection/pallas_call | solution.py:186
  103.2 12.3 %collective-permute-done.5 = bf16[256,1024]{1,0:T(8,128)(2,1)S(1)} collective-permute-done((bf16[256,1024]{1,0:T(8,128)(2,1)S(1)}, bf16[256,1024]{1,0:T(8,128)(2,1)S(1)}, u32[]{:S(2)}, u32[]{:S(2)}) %collective-permute-start.5) | collective-permute-done | bytes 524320 | tf_op jit(solution)/shard_map/ppermute | solution.py:31
  126.3 5.7 %collective-permute-done.6 = bf16[128,1024]{1,0:T(8,128)(2,1)S(1)} collective-permute-done((bf16[128,1024]{1,0:T(8,128)(2,1)S(1)}, bf16[128,1024]{1,0:T(8,128)(2,1)S(1)}, u32[]{:S(2)}, u32[]{:S(2)}) %collective-permute-start.6) | collective-permute-done | bytes 262176 | tf_op jit(solution)/shard_map/ppermute | solution.py:31
  134.3 11.4 %all-to-all-done.2.refs_5_ = bf16[4,128,896]{2,1,0:T(8,128)(2,1)S(1)} async-done(((bf16[4,128,896]{2,1,0:T(8,128)(2,1)}), bf16[4,128,896]{2,1,0:T(8,128)(2,1)S(1)}, u32[]{:S(2)}, u32[]{:S(2)}) %all-to-all-start.2) | async-done | bytes 917536 | tf_op jit(solution)/shard_map/all_to_all | solution.py:375
  151.3 21.3 %collective-permute-done.8.refs_8_ = bf16[4,128,896]{2,1,0:T(8,128)(2,1)S(1)} collective-permute-done((bf16[4,128,896]{2,1,0:T(8,128)(2,1)S(1)}, bf16[4,128,896]{2,1,0:T(8,128)(2,1)S(1)}, u32[]{:S(2)}, u32[]{:S(2)}) %collective-permute-start.8) | collective-permute-done | bytes 917536 | tf_op jit(solution)/shard_map/ppermute | solution.py:31
  173.5 16.7 %collective-permute-done.9.refs_9_ = bf16[4,128,896]{2,1,0:T(8,128)(2,1)S(1)} collective-permute-done((bf16[4,128,896]{2,1,0:T(8,128)(2,1)S(1)}, bf16[4,128,896]{2,1,0:T(8,128)(2,1)S(1)}, u32[]{:S(2)}, u32[]{:S(2)}) %collective-permute-start.9) | collective-permute-done | bytes 917536 | tf_op jit(solution)/shard_map/ppermute | solution.py:31
  191.2 4.7 %all-to-all-start.4 = ((bf16[4,128,896]{2,1,0:T(8,128)(2,1)}), bf16[4,128,896]{2,1,0:T(8,128)(2,1)}, u32[]{:S(2)}, u32[]{:S(2)}) async-start(bf16[4,128,896]{2,1,0:T(8,128)(2,1)} %get-tuple-element.66), calls=%async_computation.4 | async-start | bytes 1835008 | tf_op jit(solution)/shard_map/all_to_all | solution.py:396
  206.0 10.7 %collective-permute-done.10.refs_10_ = bf16[4,128,896]{2,1,0:T(8,128)(2,1)} collective-permute-done((bf16[4,128,896]{2,1,0:T(8,128)(2,1)S(1)}, bf16[4,128,896]{2,1,0:T(8,128)(2,1)}, u32[]{:S(2)}, u32[]{:S(2)}) %collective-permute-start.10) | collective-permute-done | bytes 917536 | tf_op jit(solution)/shard_map/ppermute | solution.py:31
  216.7 13.4 %all-to-all-done.4.refs_7_ = bf16[4,128,896]{2,1,0:T(8,128)(2,1)} async-done(((bf16[4,128,896]{2,1,0:T(8,128)(2,1)}), bf16[4,128,896]{2,1,0:T(8,128)(2,1)}, u32[]{:S(2)}, u32[]{:S(2)}) %all-to-all-start.4) | async-done | bytes 917536 | tf_op jit(solution)/shard_map/all_to_all | solution.py:396
  230.1 4.2 %all-to-all-start.5 = ((bf16[4,896,128]{2,1,0:T(8,128)(2,1)}), bf16[4,896,128]{2,1,0:T(8,128)(2,1)}, u32[]{:S(2)}, u32[]{:S(2)}) async-start(bf16[4,896,128]{2,1,0:T(8,128)(2,1)} %get-tuple-element.71), calls=%async_computation.5 | async-start | bytes 1835008 | tf_op jit(solution)/shard_map/all_to_all | solution.py:397
  240.4 20.4 %collective-permute-done.12.refs_1_ = bf16[512,1024]{1,0:T(8,128)(2,1)} collective-permute-done((bf16[512,1024]{1,0:T(8,128)(2,1)}, bf16[512,1024]{1,0:T(8,128)(2,1)}, u32[]{:S(2)}, u32[]{:S(2)}) %collective-permute-start.12) | collective-permute-done | bytes 1048608 | tf_op jit(solution)/shard_map/ppermute | solution.py:31
  260.9 15.5 %collective-permute-done.13.refs_3_ = bf16[512,1024]{1,0:T(8,128)(2,1)} collective-permute-done((bf16[512,1024]{1,0:T(8,128)(2,1)}, bf16[512,1024]{1,0:T(8,128)(2,1)}, u32[]{:S(2)}, u32[]{:S(2)}) %collective-permute-start.13) | collective-permute-done | bytes 1048608 | tf_op jit(solution)/shard_map/ppermute | solution.py:31
  278.8 13.1 %gate_up.1.here_ref = bf16[2,1024,896]{2,1,0:T(8,128)(2,1)} custom-call(bf16[512,1024]{1,0:T(8,128)(2,1)} %all-gather.6.cloned.1.call-done.refs_0_, bf16[512,1024]{1,0:T(8,128)(2,1)} %collective-permute-done.12.refs_1_, bf16[512,1024]{1,0:T(8,128)(2,1)} %all-gather.8.cloned.1.call-done.refs_2_, bf16[512,1024]{1,0:T(8,128)(2,1)} %collective-permute-done.13.refs_3_, ...), custom_call_target="tpu_custom_call" | custom-call | flops 7516192768 | bytes 15204352 | tf_op jit(solution)/shard_map/gate_up/pallas_call | solution.py:239
  292.0 4.7 %all-to-all-start.6 = ((bf16[4,896,128]{2,1,0:T(8,128)(2,1)}), bf16[4,896,128]{2,1,0:T(8,128)(2,1)S(1)}, u32[]{:S(2)}, u32[]{:S(2)}) async-start(bf16[4,896,128]{2,1,0:T(8,128)(2,1)} %get-tuple-element.74), calls=%async_computation.6 | async-start | bytes 1835008 | tf_op jit(solution)/shard_map/all_to_all | solution.py:409
  308.9 12.3 %collective-permute-done.16 = bf16[512,512]{1,0:T(8,128)(2,1)S(1)} collective-permute-done((bf16[512,512]{1,0:T(8,128)(2,1)S(1)}, bf16[512,512]{1,0:T(8,128)(2,1)S(1)}, u32[]{:S(2)}, u32[]{:S(2)}) %collective-permute-start.16) | collective-permute-done | bytes 524320 | tf_op jit(solution)/shard_map/ppermute | solution.py:31
  339.4 5.9 %collective-permute-done.18 = bf16[128,512]{1,0:T(8,128)(2,1)} collective-permute-done((bf16[128,512]{1,0:T(8,128)(2,1)}, bf16[128,512]{1,0:T(8,128)(2,1)}, u32[]{:S(2)}, u32[]{:S(2)}) %collective-permute-start.18) | collective-permute-done | bytes 131104 | tf_op jit(solution)/shard_map/ppermute | solution.py:31
  369.1 4.1 %collective-permute-start.31 = (bf16[128,512]{1,0:T(8,128)(2,1)S(1)}, bf16[128,512]{1,0:T(8,128)(2,1)S(1)}, u32[]{:S(2)}, u32[]{:S(2)}) collective-permute-start(bf16[128,512]{1,0:T(8,128)(2,1)S(1)} %get-tuple-element.105), channel_id=1, source_target_pairs={{0,1},{1,0},{2,3},{3,2},{4,5},{5,4},{6,7},{7,6},{8,9},{9,8},{10,11... | collective-permute-start | bytes 393224 | tf_op jit(solution)/shard_map/ppermute | solution.py:31
  378.4 7.5 %collective-permute-done.32 = bf16[128,512]{1,0:T(8,128)(2,1)S(1)} collective-permute-done((bf16[128,512]{1,0:T(8,128)(2,1)S(1)}, bf16[128,512]{1,0:T(8,128)(2,1)S(1)}, u32[]{:S(2)}, u32[]{:S(2)}) %collective-permute-start.32) | collective-permute-done | bytes 131104 | tf_op jit(solution)/shard_map/ppermute | solution.py:31
  (168 shorter events, 125.4 us)
Async XLA Ops:
  7.2 85.7 %all-gather.4.cloned.1.call-start = ((), (), s32[]{:S(2)}) async-start(), calls=%async_computation.7 | async-start | bytes 5242880 | tf_op jit(solution)/shard_map/all_gather | solution.py:337
  21.3 18.7 %all-to-all-start = ((bf16[8,64,1024]{2,1,0:T(8,128)(2,1)}), bf16[8,64,1024]{2,1,0:T(8,128)(2,1)S(1)}, u32[]{:S(2)}, u32[]{:S(2)}) async-start(bf16[8,64,1024]{2,1,0:T(8,128)(2,1)} %bitcast.5), calls=%async_computation | async-start | bytes 2097152 | tf_op jit(solution)/shard_map/all_to_all | solution.py:342
  46.5 50.0 %collective-permute-start.2 = (bf16[512,512]{1,0:T(8,128)(2,1)S(1)}, bf16[512,512]{1,0:T(8,128)(2,1)S(1)}, u32[]{:S(2)}, u32[]{:S(2)}) collective-permute-start(bf16[512,512]{1,0:T(8,128)(2,1)S(1)} %attention.1.refs_0_), channel_id=1, source_target_pairs={{0,4},{4,0},{8,12},{12,8},{1,5},{5,1},{9,13},{13,9},{2,6},{6,2},{1... | collective-permute-start | bytes 1572872 | tf_op jit(solution)/shard_map/ppermute | solution.py:31
  59.5 36.9 %collective-permute-start.4 = (bf16[512,512]{1,0:T(8,128)(2,1)S(1)}, bf16[512,512]{1,0:T(8,128)(2,1)S(1)}, u32[]{:S(2)}, u32[]{:S(2)}) collective-permute-start(bf16[512,512]{1,0:T(8,128)(2,1)S(1)} %collective-permute-done.3.refs_2_), channel_id=1, source_target_pairs={{0,4},{4,0},{8,12},{12,8},{1,5},{5,1},{9,13},{13,9},{2,6},{6,2},{1... | collective-permute-start | bytes 1572872 | tf_op jit(solution)/shard_map/ppermute | solution.py:31
  92.9 26.8 %all-to-all-start.1 = ((bf16[4,128,896]{2,1,0:T(8,128)(2,1)}), bf16[4,128,896]{2,1,0:T(8,128)(2,1)S(1)}, u32[]{:S(2)}, u32[]{:S(2)}) async-start(bf16[4,128,896]{2,1,0:T(8,128)(2,1)} %get-tuple-element.56), calls=%async_computation.1 | async-start | bytes 1835008 | tf_op jit(solution)/shard_map/all_to_all | solution.py:365
  119.7 26.0 %all-to-all-start.2 = ((bf16[4,128,896]{2,1,0:T(8,128)(2,1)}), bf16[4,128,896]{2,1,0:T(8,128)(2,1)S(1)}, u32[]{:S(2)}, u32[]{:S(2)}) async-start(bf16[4,128,896]{2,1,0:T(8,128)(2,1)} %get-tuple-element.60), calls=%async_computation.2 | async-start | bytes 1835008 | tf_op jit(solution)/shard_map/all_to_all | solution.py:375
  123.2 111.2 %all-gather.6.cloned.1.call-start = ((), (), s32[]{:S(2)}) async-start(), calls=%async_computation.8 | async-start | bytes 1310720 | tf_op jit(solution)/shard_map/all_gather | solution.py:392
  145.7 45.5 %all-to-all-start.3 = ((bf16[4,128,896]{2,1,0:T(8,128)(2,1)}), bf16[4,128,896]{2,1,0:T(8,128)(2,1)S(1)}, u32[]{:S(2)}, u32[]{:S(2)}) async-start(bf16[4,128,896]{2,1,0:T(8,128)(2,1)} %get-tuple-element.62), calls=%async_computation.3 | async-start | bytes 1835008 | tf_op jit(solution)/shard_map/all_to_all | solution.py:395
  149.2 23.4 %collective-permute-start.8 = (bf16[4,128,896]{2,1,0:T(8,128)(2,1)S(1)}, bf16[4,128,896]{2,1,0:T(8,128)(2,1)S(1)}, u32[]{:S(2)}, u32[]{:S(2)}) collective-permute-start(bf16[4,128,896]{2,1,0:T(8,128)(2,1)S(1)} %all-to-all-done.1.refs_4_), channel_id=1, source_target_pairs={{0,8},{4,12},{8,0},{12,4},{1,9},{5,13},{9,1},{13,5},{2,10},{6,14},... | collective-permute-start | bytes 2752520 | tf_op jit(solution)/shard_map/ppermute | solution.py:31
  150.9 39.3 %collective-permute-start.9 = (bf16[4,128,896]{2,1,0:T(8,128)(2,1)S(1)}, bf16[4,128,896]{2,1,0:T(8,128)(2,1)S(1)}, u32[]{:S(2)}, u32[]{:S(2)}) collective-permute-start(bf16[4,128,896]{2,1,0:T(8,128)(2,1)S(1)} %all-to-all-done.2.refs_5_), channel_id=1, source_target_pairs={{0,8},{4,12},{8,0},{12,4},{1,9},{5,13},{9,1},{13,5},{2,10},{6,14},... | collective-permute-start | bytes 2752520 | tf_op jit(solution)/shard_map/ppermute | solution.py:31
  191.2 39.0 %all-to-all-start.4 = ((bf16[4,128,896]{2,1,0:T(8,128)(2,1)}), bf16[4,128,896]{2,1,0:T(8,128)(2,1)}, u32[]{:S(2)}, u32[]{:S(2)}) async-start(bf16[4,128,896]{2,1,0:T(8,128)(2,1)} %get-tuple-element.66), calls=%async_computation.4 | async-start | bytes 1835008 | tf_op jit(solution)/shard_map/all_to_all | solution.py:396
  195.9 41.4 %all-gather.8.cloned.1.call-start = ((), (), s32[]{:S(2)}) async-start(), calls=%async_computation.9 | async-start | bytes 1310720 | tf_op jit(solution)/shard_map/all_gather | solution.py:392
  196.6 20.1 %collective-permute-start.10 = (bf16[4,128,896]{2,1,0:T(8,128)(2,1)S(1)}, bf16[4,128,896]{2,1,0:T(8,128)(2,1)}, u32[]{:S(2)}, u32[]{:S(2)}) collective-permute-start(bf16[4,128,896]{2,1,0:T(8,128)(2,1)S(1)} %all-to-all-done.3.refs_6_), channel_id=1, source_target_pairs={{0,8},{4,12},{8,0},{12,4},{1,9},{5,13},{9,1},{13,5},{2,10},{6,14},... | collective-permute-start | bytes 2752520 | tf_op jit(solution)/shard_map/ppermute | solution.py:31
  230.1 46.3 %all-to-all-start.5 = ((bf16[4,896,128]{2,1,0:T(8,128)(2,1)}), bf16[4,896,128]{2,1,0:T(8,128)(2,1)}, u32[]{:S(2)}, u32[]{:S(2)}) async-start(bf16[4,896,128]{2,1,0:T(8,128)(2,1)} %get-tuple-element.71), calls=%async_computation.5 | async-start | bytes 1835008 | tf_op jit(solution)/shard_map/all_to_all | solution.py:397
  234.4 26.5 %collective-permute-start.12 = (bf16[512,1024]{1,0:T(8,128)(2,1)}, bf16[512,1024]{1,0:T(8,128)(2,1)}, u32[]{:S(2)}, u32[]{:S(2)}) collective-permute-start(bf16[512,1024]{1,0:T(8,128)(2,1)} %all-gather.6.cloned.1.call-done.refs_0_), channel_id=1, source_target_pairs={{0,16},{16,0},{1,17},{17,1},{2,18},{18,2},{3,19},{19,3},{4,20},{20... | collective-permute-start | bytes 3145736 | tf_op jit(solution)/shard_map/ppermute | solution.py:31
  237.3 39.1 %collective-permute-start.13 = (bf16[512,1024]{1,0:T(8,128)(2,1)}, bf16[512,1024]{1,0:T(8,128)(2,1)}, u32[]{:S(2)}, u32[]{:S(2)}) collective-permute-start(bf16[512,1024]{1,0:T(8,128)(2,1)} %all-gather.8.cloned.1.call-done.refs_2_), channel_id=1, source_target_pairs={{0,16},{16,0},{1,17},{17,1},{2,18},{18,2},{3,19},{19,3},{4,20},{20... | collective-permute-start | bytes 3145736 | tf_op jit(solution)/shard_map/ppermute | solution.py:31
  239.0 37.4 %collective-permute-start.11 = (bf16[4,128,896]{2,1,0:T(8,128)(2,1)}, bf16[4,128,896]{2,1,0:T(8,128)(2,1)}, u32[]{:S(2)}, u32[]{:S(2)}) collective-permute-start(bf16[4,128,896]{2,1,0:T(8,128)(2,1)} %all-to-all-done.4.refs_7_), channel_id=1, source_target_pairs={{0,8},{4,12},{8,0},{12,4},{1,9},{5,13},{9,1},{13,5},{2,10},{6,14},... | collective-permute-start | bytes 2752520 | tf_op jit(solution)/shard_map/ppermute | solution.py:31
  292.0 31.3 %all-to-all-start.6 = ((bf16[4,896,128]{2,1,0:T(8,128)(2,1)}), bf16[4,896,128]{2,1,0:T(8,128)(2,1)S(1)}, u32[]{:S(2)}, u32[]{:S(2)}) async-start(bf16[4,896,128]{2,1,0:T(8,128)(2,1)} %get-tuple-element.74), calls=%async_computation.6 | async-start | bytes 1835008 | tf_op jit(solution)/shard_map/all_to_all | solution.py:409
  296.7 25.7 %collective-permute-start.14 = (bf16[4,896,128]{2,1,0:T(8,128)(2,1)}, bf16[4,896,128]{2,1,0:T(8,128)(2,1)S(1)}, u32[]{:S(2)}, u32[]{:S(2)}) collective-permute-start(bf16[4,896,128]{2,1,0:T(8,128)(2,1)} %all-to-all-done.5.weights_ref), channel_id=1, source_target_pairs={{0,8},{4,12},{8,0},{12,4},{1,9},{5,13},{9,1},{13,5},{2,10},{6,14},... | collective-permute-start | bytes 2752520 | tf_op jit(solution)/shard_map/ppermute | solution.py:31
  326.6 22.0 %collective-permute-start.24 = (bf16[512,512]{1,0:T(8,128)(2,1)}, bf16[512,512]{1,0:T(8,128)(2,1)}, u32[]{:S(2)}, u32[]{:S(2)}) collective-permute-start(bf16[512,512]{1,0:T(8,128)(2,1)} %bitcast.21), channel_id=1, source_target_pairs={{0,16},{16,0},{1,17},{17,1},{2,18},{18,2},{3,19},{19,3},{4,20},{20... | collective-permute-start | bytes 1572872 | tf_op jit(solution)/shard_map/ppermute | solution.py:31
  328.2 26.2 %collective-permute-start.29 = (bf16[4,896,128]{2,1,0:T(8,128)(2,1)S(1)}, bf16[4,896,128]{2,1,0:T(8,128)(2,1)}, u32[]{:S(2)}, u32[]{:S(2)}) collective-permute-start(bf16[4,896,128]{2,1,0:T(8,128)(2,1)S(1)} %all-to-all-done.6.weights_ref), channel_id=1, source_target_pairs={{0,8},{4,12},{8,0},{12,4},{1,9},{5,13},{9,1},{13,5},{2,10},{6,14},... | collective-permute-start | bytes 2752520 | tf_op jit(solution)/shard_map/ppermute | solution.py:31
  338.8 18.6 %collective-permute-start.20 = (bf16[512,512]{1,0:T(8,128)(2,1)}, bf16[512,512]{1,0:T(8,128)(2,1)}, u32[]{:S(2)}, u32[]{:S(2)}) collective-permute-start(bf16[512,512]{1,0:T(8,128)(2,1)} %bitcast.15), channel_id=1, source_target_pairs={{0,16},{16,0},{1,17},{17,1},{2,18},{18,2},{3,19},{19,3},{4,20},{20... | collective-permute-start | bytes 1572872 | tf_op jit(solution)/shard_map/ppermute | solution.py:31
  359.9 16.2 %collective-permute-start.22 = (bf16[128,512]{1,0:T(8,128)(2,1)S(1)}, bf16[128,512]{1,0:T(8,128)(2,1)S(1)}, u32[]{:S(2)}, u32[]{:S(2)}) collective-permute-start(bf16[128,512]{1,0:T(8,128)(2,1)S(1)} %get-tuple-element.113), channel_id=1, source_target_pairs={{0,2},{1,3},{2,0},{3,1},{4,6},{5,7},{6,4},{7,5},{8,10},{9,11},{10,... | collective-permute-start | bytes 393224 | tf_op jit(solution)/shard_map/ppermute | solution.py:31
  366.9 20.6 %collective-permute-start.28 = (bf16[128,512]{1,0:T(8,128)(2,1)S(1)}, bf16[128,512]{1,0:T(8,128)(2,1)S(1)}, u32[]{:S(2)}, u32[]{:S(2)}) collective-permute-start(bf16[128,512]{1,0:T(8,128)(2,1)S(1)} %fusion.7), channel_id=1, source_target_pairs={{0,8},{4,12},{8,0},{12,4},{1,9},{5,13},{9,1},{13,5},{2,10},{6,14},... | collective-permute-start | bytes 393224 | tf_op jit(solution)/shard_map/ppermute | solution.py:31
  (37 other events, 342.6 us)
Sparse Core Ops, SparseCore 0:
  9.6 83.2 all-gather.3
  145.8 42.1 all-gather.5
  198.3 38.9 all-gather.7

commit v8 on v7

--- a/solution.py
+++ b/solution.py
@@ -19,6 +19,7 @@
 ROW_TILE = 256
 PARTS = 2
 VMEM_LIMIT = 48 * 1024 * 1024
+BRIEF = pl.CostEstimate(flops=1, bytes_accessed=1, transcendentals=0)
 ANY = pl.BlockSpec(memory_space=pl.ANY)
 VMEM = pl.BlockSpec(memory_space=pltpu.VMEM)
 SMEM = pl.BlockSpec(memory_space=pltpu.SMEM)
@@ -108,23 +109,19 @@
             pltpu.VMEM((halo_rows + rows, HEAD_WIDTH), jnp.bfloat16),
         ],
         compiler_params=pltpu.CompilerParams(vmem_limit_bytes=VMEM_LIMIT),
-        cost_estimate=pl.CostEstimate(
-            flops=4 * rows * (reach + QUERY_TILE) * Q_COLS,
-            bytes_accessed=rows * 4 * Q_COLS,
-            transcendentals=rows * (reach + QUERY_TILE) * GROUP,
-        ),
+        cost_estimate=BRIEF,
         name="attention",
     )(starts, packed, packed, halo)
 
 
-def cut_kernel(gain_ref, gate_up_ref, down_ref, *out_refs):
-    rows, cols = out_refs[0].shape[1], out_refs[-1].shape[2]
-    for part in range(PARTS):
-        at = slice(part * rows, (part + 1) * rows)
-        for which in range(2):
-            scaled = gate_up_ref[which, at].astype(jnp.float32) * gain_ref[at]
-            out_refs[2 * part + which][0] = scaled.astype(jnp.bfloat16)
-        out_refs[2 * PARTS + part][0] = down_ref[:, part * cols : (part + 1) * cols]
+def cut_kernel(gain_ref, gate_up_ref, down_ref, both_ref, gate_ref, up_ref, *down_refs):
+    rows, cols = gate_ref.shape[1], down_refs[0].shape[2]
+    for which, second_ref in enumerate((gate_ref, up_ref)):
+        scaled = (gate_up_ref[which].astype(jnp.float32) * gain_ref[...]).astype(jnp.bfloat16)
+        both_ref[0, which] = scaled[:rows]
+        second_ref[0] = scaled[rows:]
+    for part, out_ref in enumerate(down_refs):
+        out_ref[0] = down_ref[:, part * cols : (part + 1) * cols]
 
 
 def cut_weights(w_gate_up, w_down, gain, outer_count):
@@ -133,9 +130,9 @@
     rows = features // PARTS
     if cols % HEAD_WIDTH:
         wide = (w_gate_up.astype(jnp.float32) * gain[None]).astype(jnp.bfloat16)
-        wide = jnp.transpose(wide.reshape(2, PARTS, rows, outer_count, cols), (1, 0, 3, 2, 4))
+        wide = jnp.transpose(wide.reshape(2, PARTS, rows, outer_count, cols), (1, 3, 0, 2, 4))
         tall = jnp.transpose(w_down.reshape(outer_count, cols, PARTS, rows), (2, 0, 1, 3))
-        return [wide[part, which] for part in range(PARTS) for which in range(2)] + [tall[part] for part in range(PARTS)]
+        return [wide[0], wide[1, :, 0], wide[1, :, 1], *tall]
     return pl.pallas_call(
         cut_kernel,
         grid=(outer_count,),
@@ -144,12 +141,14 @@
             pl.BlockSpec((2, features, cols), lambda p: (0, 0, p)),
             pl.BlockSpec((cols, features), lambda p: (p, 0)),
         ],
-        out_specs=[pl.BlockSpec((1, rows, cols), lambda p: (p, 0, 0))] * (2 * PARTS)
+        out_specs=[pl.BlockSpec((1, 2, rows, cols), lambda p: (p, 0, 0, 0))]
+        + [pl.BlockSpec((1, rows, cols), lambda p: (p, 0, 0))] * 2
         + [pl.BlockSpec((1, cols, rows), lambda p: (p, 0, 0))] * PARTS,
-        out_shape=[jax.ShapeDtypeStruct((outer_count, rows, cols), jnp.bfloat16)] * (2 * PARTS)
+        out_shape=[jax.ShapeDtypeStruct((outer_count, 2, rows, cols), jnp.bfloat16)]
+        + [jax.ShapeDtypeStruct((outer_count, rows, cols), jnp.bfloat16)] * 2
         + [jax.ShapeDtypeStruct((outer_count, cols, rows), jnp.bfloat16)] * PARTS,
         compiler_params=pltpu.CompilerParams(vmem_limit_bytes=VMEM_LIMIT),
-        cost_estimate=pl.CostEstimate(flops=2 * features * width, bytes_accessed=12 * features * width, transcendentals=0),
+        cost_estimate=BRIEF,
         name="cut_weights",
     )(gain, w_gate_up, w_down)
 
@@ -189,73 +188,56 @@
         out_specs=[VMEM] * len(outs),
         out_shape=[jax.ShapeDtypeStruct(shape, jnp.bfloat16) for shape in outs],
         compiler_params=pltpu.CompilerParams(vmem_limit_bytes=VMEM_LIMIT),
-        cost_estimate=pl.CostEstimate(
-            flops=2 * rows * weights.size, bytes_accessed=2 * (weights.size + rows * 2 * width), transcendentals=0
-        ),
+        cost_estimate=BRIEF,
         name="projection",
     )(place, *blocks, weights)
 
 
-def gate_up_kernel(block_count, head_count, *refs):
-    tokens = refs[: block_count * head_count]
-    weights = refs[len(tokens) : len(tokens) + 2 * PARTS * block_count]
-    out_ref, held, near, sums, token_sems, weight_sems = refs[len(tokens) + len(weights) :]
+def gate_up_kernel(head_count, *refs):
+    tokens = refs[:head_count]
+    both, gate, up = refs[head_count : head_count + 3]
+    *earlier, out_ref, held, near, token_sems, weight_sems = refs[head_count + 3 :]
     rows, depth = tokens[0].shape
-    copies = []
-    for a in range(block_count):
-        group = []
-        for e in range(head_count):
-            j = a * head_count + e
-            target = held.at[pl.ds(e * rows, rows), pl.ds(a * depth, depth)]
-            group.append(pltpu.make_async_copy(tokens[j], target, token_sems.at[j]))
-        for j in range(2 * PARTS * a, 2 * PARTS * (a + 1)):
-            target = near.at[j % 2, a, :, (j // 2) % PARTS]
-            group.append(pltpu.make_async_copy(weights[j], target, weight_sems.at[j]))
-        copies.append(group)
+    copies = [
+        [pltpu.make_async_copy(both.at[:, which], near.at[which, :, 0], weight_sems.at[which, 0]),
+         pltpu.make_async_copy(second, near.at[which, :, 1], weight_sems.at[which, 1])]
+        for which, second in enumerate((gate, up))
+    ]
+    for e, token_ref in enumerate(tokens):
+        copies[0].append(pltpu.make_async_copy(token_ref, held.at[pl.ds(e * rows, rows)], token_sems.at[e]))
     for group in copies:
         for copy in group:
             copy.start()
-    for a, group in enumerate(copies):
+    for which, group in enumerate(copies):
         for copy in group:
             copy.wait()
-        for which in range(2):
-            block = near[which, a].reshape(depth, -1)
-            for tile in row_tiles(held.shape[0]):
-                product = jnp.dot(held[tile, a * depth : (a + 1) * depth], block, preferred_element_type=jnp.float32)
-                total = product if a == 0 else sums[which, tile, :] + product
-                if a < block_count - 1:
-                    sums[which, tile, :] = total
-                else:
-                    out_ref[which, tile, :] = total.astype(jnp.bfloat16)
-
-
-def gate_up(tokens, blocks):
-    head_count = len(tokens[0])
-    rows, depth = tokens[0][0].shape
-    sources, stream_rows, cols = blocks[0][0].shape
-    tokens = [piece for block in tokens for piece in block]
-    weights = [stream for block in blocks for stream in block]
-    rows, all_depth = rows * head_count, depth * len(blocks)
-    return pl.pallas_call(
-        functools.partial(gate_up_kernel, len(blocks), head_count),
-        in_specs=[ANY] * (len(tokens) + len(weights)),
+        block = near[which].reshape(depth, -1)
+        for tile in row_tiles(held.shape[0]):
+            product = jnp.dot(held[tile, :], block, preferred_element_type=jnp.float32)
+            if earlier:
+                product = earlier[0][which, tile, :].astype(jnp.float32) + product
+            out_ref[which, tile, :] = product.astype(jnp.bfloat16)
+
+
+def gate_up(tokens, streams, earlier=()):
+    rows, depth = tokens[0].shape
+    sources, stream_rows, cols = streams[1].shape
+    all_rows = rows * len(tokens)
+    return pl.pallas_call(
+        functools.partial(gate_up_kernel, len(tokens)),
+        in_specs=[ANY] * (len(tokens) + len(streams)) + [VMEM] * len(earlier),
         out_specs=VMEM,
-        out_shape=jax.ShapeDtypeStruct((2, rows, cols), jnp.bfloat16),
+        out_shape=jax.ShapeDtypeStruct((2, all_rows, cols), jnp.bfloat16),
         scratch_shapes=[
-            pltpu.VMEM((rows, all_depth), jnp.bfloat16),
-            pltpu.VMEM((2, len(blocks), sources, PARTS, stream_rows, cols), jnp.bfloat16),
-            pltpu.VMEM((2, rows, cols), jnp.float32),
+            pltpu.VMEM((all_rows, depth), jnp.bfloat16),
+            pltpu.VMEM((2, sources, PARTS, stream_rows, cols), jnp.bfloat16),
             pltpu.SemaphoreType.DMA((len(tokens),)),
-            pltpu.SemaphoreType.DMA((len(weights),)),
+            pltpu.SemaphoreType.DMA((2, PARTS)),
         ],
         compiler_params=pltpu.CompilerParams(vmem_limit_bytes=VMEM_LIMIT),
-        cost_estimate=pl.CostEstimate(
-            flops=4 * rows * all_depth * cols,
-            bytes_accessed=2 * (rows * all_depth + 2 * all_depth * cols + 2 * rows * cols),
-            transcendentals=0,
-        ),
+        cost_estimate=BRIEF,
         name="gate_up",
-    )(*tokens, *weights)
+    )(*tokens, *streams, *earlier)
 
 
 def activation_kernel(here_ref, there_ref, out_ref):
@@ -274,7 +256,7 @@
         out_specs=pl.BlockSpec((step, cols), lambda t: (t, 0)),
         out_shape=jax.ShapeDtypeStruct((rows, cols), jnp.bfloat16),
         compiler_params=pltpu.CompilerParams(vmem_limit_bytes=VMEM_LIMIT),
-        cost_estimate=pl.CostEstimate(flops=8 * rows * cols, bytes_accessed=10 * rows * cols, transcendentals=rows * cols),
+        cost_estimate=BRIEF,
         name="activation",
     )(here, there)
 
@@ -309,11 +291,7 @@
             jax.ShapeDtypeStruct((head_count - 1, rows, sources * cols), jnp.bfloat16),
         ],
         compiler_params=pltpu.CompilerParams(vmem_limit_bytes=VMEM_LIMIT),
-        cost_estimate=pl.CostEstimate(
-            flops=2 * activated.size * sources * cols,
-            bytes_accessed=2 * (activated.size + weights.size + head_count * rows * sources * cols),
-            transcendentals=0,
-        ),
+        cost_estimate=BRIEF,
         name="down",
     )(activated, weights)
 
@@ -368,34 +346,30 @@
     projected = kept.astype(jnp.float32)
     for e in range(1, head_count):
         projected = projected + swap(sent[e - 1], "head", e).astype(jnp.float32)
-    projected, first = fence(projected, first)
     own_resid = lax.dynamic_slice_in_dim(resid, head * half, half, 0)
     hidden_part = (own_resid.astype(jnp.float32) + projected).astype(jnp.bfloat16)
 
-    second = spread(after(cut[1], first))
     upper = inner // 2
     own_rows = half // 2
     mine = lax.dynamic_slice_in_dim(hidden_part, upper * own_rows, own_rows, 0)
     others = lax.dynamic_slice_in_dim(hidden_part, (1 - upper) * own_rows, own_rows, 0)
-    state = [mine.astype(jnp.float32), over_y(others).astype(jnp.float32)]
+    others, first = fence(over_y(others), first)
+    state = [mine.astype(jnp.float32), others.astype(jnp.float32)]
     squares = sum([jnp.sum(block * block, axis=1) for block in state])
     squares = squares + swap(squares, "inner", 1)
     inverse = lax.rsqrt(squares / D + 1e-05)[:, None]
     part_rows = feature_rows // PARTS
     normed = [(block * inverse).astype(jnp.bfloat16) for block in state]
-    *normed, first, second = fence(*normed, first, second)
     state = [block.reshape(own_rows, outer_count, PARTS, part_rows) for block in state]
     state = [[block[:, :, part].reshape(own_rows, -1) for part in range(PARTS)] for block in state]
 
-    tokens = []
-    for block in normed:
-        block = lax.all_gather(block, "outer", axis=0, tiled=True)
-        tokens.append([swap(block, "head", e) if e else block for e in range(head_count)])
-
-    third, first_y, second_y = fence(spread(after(cut[2], normed[0])), over_y(first), over_y(second))
-    fourth, third_y, state = fence(spread(after(cut[3], third)), over_y(third), state)
-    fifth, fourth_y, tokens = fence(spread(after(cut[4], fourth)), over_y(fourth), tokens)
-    sums = gate_up(tokens, [[first, second, third, fourth], [first_y, second_y, third_y, fourth_y]])
+    tokens = [lax.all_gather(block, "outer", axis=0, tiled=True) for block in normed]
+    second, first_y, tokens, state = fence(spread(after(cut[1], normed[0])), over_y(first), tokens, state)
+    tokens = [[swap(block, "head", e) if e else block for e in range(head_count)] for block in tokens]
+    third, second_y, tokens[0] = fence(spread(after(cut[2], second)), over_y(second), tokens[0])
+    own_sums = gate_up(tokens[0], [first, second, third])
+    fourth, third_y, own_sums = fence(spread(after(cut[3], third)), over_y(third), own_sums)
+    sums = gate_up(tokens[1], [first_y, second_y, third_y], [own_sums])
     activated = activation(sums, swap(sums, "inner", 1))
 
     def over_heads(weights):
@@ -405,12 +379,10 @@
             paired = paired + swap(sent[e - 1], "head", e).astype(jnp.float32)
         return paired.reshape(outer_count, own_rows, -1)
 
-    paired = {(0, 0): over_heads(fifth)}
-    sixth, fifth_y, paired[0, 0] = fence(spread(after(cut[5], fifth)), over_y(fifth), paired[0, 0])
-    sixth_y = over_y(sixth)
-    paired[1, 0] = over_heads(fifth_y)
-    paired[0, 1] = over_heads(sixth)
-    paired[1, 1] = over_heads(after(sixth_y, paired[1, 0]))
+    fifth, fourth_y, activated = fence(spread(after(cut[4], fourth)), over_y(fourth), activated)
+    fifth_y = over_y(fifth)
+    paired = {(0, 0): over_heads(fourth), (1, 0): over_heads(fourth_y), (0, 1): over_heads(fifth)}
+    paired[1, 1] = over_heads(after(fifth_y, paired[0, 0]))
 
     pieces = [[None] * PARTS, [None] * PARTS]
     for part in range(PARTS):

time: 401 us -> 424 us (1.057)
  local copies, waits for them, and re-layouts: 27.7 us -> 42.4 us
  waiting for transfers between devices: 226 us -> 233 us
    ppermute x33 -> x32, waiting for transfers between devices: 153 us -> 113 us  [swap(): return lax.ppermute(array, axis, [(s, s ^ distance) for s in range(count)])]
    all_gather x1, waiting for transfers between devices: 27 us -> 58.2 us  [per_device(): weights_out = lax.all_gather(w_out, 'outer', axis=1, tiled=True)]
    all_gather x2, waiting for transfers between devices: 1.23 us -> 28.4 us  [per_device(): lax.all_gather(block, 'outer', axis=0, tiled=True)]
    all_to_all x3 -> x2, waiting for transfers between devices: 11.4 us -> 32.2 us  [the longest x1 32.2 us: per_device(): spread(after(cut[1], normed[0]))]
    unnamed x36 -> x64, local copies, waits for them, and re-layouts: 10.6 us -> 25.7 us
    all_to_all x1, waiting for transfers between devices: 14.4 us -> 0.01 us  [per_device(): lax.all_to_all(groups, ('inner', 'head'), split_axis=0, concat_axis=0, ti...]
    all_to_all x1, waiting for transfers between devices: 13.4 us -> 0.01 us  [per_device(): spread(after(cut[3], third))]
    pallas_call x1 -> x2, Pallas kernels: 13.1 us -> 17.1 us  [gate_up(): pl.pallas_call(functools.partial(gate_up_kernel, len(tokens)), in_specs=[...]
  transfers between devices with their start and end apart: 45 -> 43, of which waited for: 23 -> 21; matrix products, arithmetic and copies ran while one was open for 7% -> 6% of each run, Pallas kernels for 7% -> 8%
where the time goes in v8:
time: 424 us; the launch traced here: 422 us
  waiting for transfers between devices  233 us (55%)
  starting transfers between devices  79.7 us (19%)
  Pallas kernels  44 us (10%)
  local copies, waits for them, and re-layouts  42.4 us (10%)
  between operations  14.3 us (3%)
  other arithmetic  9.26 us (2%)
    ppermute x32, waiting for transfers between devices, swap(): return lax.ppermute(array, axis, [(s, s ^ distance) for s in range(count)])  113 us
    all_gather x1, waiting for transfers between devices, per_device(): weights_out = lax.all_gather(w_out, 'outer', axis=1, tiled=True)  58.2 us
    ppermute x32, starting transfers between devices, swap(): return lax.ppermute(array, axis, [(s, s ^ distance) for s in range(count)])  45.5 us
    all_to_all x1, waiting for transfers between devices, per_device(): spread(after(cut[1], normed[0]))  32.2 us
    all_gather x2, waiting for transfers between devices, per_device(): lax.all_gather(block, 'outer', axis=0, tiled=True)  28.4 us
    unnamed x64, local copies, waits for them, and re-layouts  25.7 us
    pallas_call x2, Pallas kernels, gate_up(): pl.pallas_call(functools.partial(gate_up_kernel, len(tokens)), in_specs=[...  17.1 us
  transfers between devices with their start and end apart: 43, of which 21 were waited for; matrix products, arithmetic and copies ran while one was open for 6% of the time, Pallas kernels for 8%

profile of v8, /device:TPU:0, one launch (start us, length us, event | category | flops | bytes accessed | tf_op | source)
XLA Modules:
  0.0 422.2 jit_solution(11256960398063329315)
XLA Ops:
  7.9 4.9 %collective-permute-start = (bf16[64,1024]{1,0:T(8,128)(2,1)}, bf16[64,1024]{1,0:T(8,128)(2,1)S(1)}, u32[]{:S(2)}, u32[]{:S(2)}) collective-permute-start(bf16[64,1024]{1,0:T(8,128)(2,1)} %param.10), channel_id=1, source_target_pairs={{0,1},{1,2},{2,3},{4,5},{5,6},{6,7},{8,9},{9,10},{10,11},{12,13},{... | collective-permute-start | bytes 393224 | tf_op jit(solution)/shard_map/ppermute | solution.py:317
  34.6 58.2 %all-gather.4.cloned.1.call-done.refs_4_ = bf16[2048,1024]{1,0:T(8,128)(2,1)} async-done(((bf16[2048,256]{1,0:T(8,128)(2,1)}), bf16[2048,1024]{1,0:T(8,128)(2,1)}) %all-gather.4.cloned.1.call-update) | async-done | bytes 4194320 | tf_op jit(solution)/shard_map/all_gather | solution.py:315
  98.7 5.9 %attention.1.refs_0_ = bf16[512,512]{1,0:T(8,128)(2,1)S(1)} custom-call(s32[512,1]{1,0:T(8,128)S(1)} %copy-done.6, bf16[512,1024]{1,0:T(8,128)(2,1)S(1)} %bitcast.93, bf16[512,1024]{1,0:T(8,128)(2,1)S(1)} %bitcast.94, bf16[512,1024]{1,0:T(8,128)(2,1)S(1)} %bitcast.95), custom_call_target="tpu_custom_call" | custom-call | flops 1 | bytes 1 | tf_op jit(solution)/shard_map/attention/pallas_call | solution.py:96
  106.1 12.3 %collective-permute-done.3.refs_2_ = bf16[512,512]{1,0:T(8,128)(2,1)S(1)} collective-permute-done((bf16[512,512]{1,0:T(8,128)(2,1)S(1)}, bf16[512,512]{1,0:T(8,128)(2,1)S(1)}, u32[]{:S(2)}, u32[]{:S(2)}) %collective-permute-start.3) | collective-permute-done | bytes 524320 | tf_op jit(solution)/shard_map/ppermute | solution.py:32
  122.6 5.6 %projection.1 = (bf16[256,1024]{1,0:T(8,128)(2,1)S(1)}, bf16[1,256,1024]{2,1,0:T(8,128)(2,1)}, bf16[128,2048]{1,0:T(8,128)(2,1)}) custom-call(s32[2]{0:T(128)S(1)} %pad_add_fusion.place_ref, bf16[512,512]{1,0:T(8,128)(2,1)S(1)} %attention.1.refs_0_, bf16[512,512]{1,0:T(8,128)(2,1)S(1)} %copy-done.21, bf16[512,512]{1,0:T(8,128)(2,1)S(1)} %copy-done.19, ...), custom_call_target="tpu_custom_call" | custom-call | flops 1 | bytes 1 | tf_op jit(solution)/shard_map/projection/pallas_call | solution.py:185
  130.5 12.6 %collective-permute-done.5 = bf16[256,1024]{1,0:T(8,128)(2,1)S(1)} collective-permute-done((bf16[256,1024]{1,0:T(8,128)(2,1)}, bf16[256,1024]{1,0:T(8,128)(2,1)S(1)}, u32[]{:S(2)}, u32[]{:S(2)}) %collective-permute-start.5) | collective-permute-done | bytes 524320 | tf_op jit(solution)/shard_map/ppermute | solution.py:32
  146.5 5.8 %collective-permute-done.6 = bf16[128,1024]{1,0:T(8,128)(2,1)S(1)} collective-permute-done((bf16[128,1024]{1,0:T(8,128)(2,1)S(1)}, bf16[128,1024]{1,0:T(8,128)(2,1)S(1)}, u32[]{:S(2)}, u32[]{:S(2)}) %collective-permute-start.6) | collective-permute-done | bytes 262176 | tf_op jit(solution)/shard_map/ppermute | solution.py:32
  156.3 4.7 %all-to-all-start.2 = ((bf16[4,128,896]{2,1,0:T(8,128)(2,1)}), bf16[4,128,896]{2,1,0:T(8,128)(2,1)S(1)}, u32[]{:S(2)}, u32[]{:S(2)}) async-start(bf16[4,128,896]{2,1,0:T(8,128)(2,1)} %copy-done.14), calls=%async_computation.2 | async-start | bytes 1835008 | tf_op jit(solution)/shard_map/all_to_all | solution.py:367
  168.7 32.2 %all-to-all-done.2.refs_3_ = bf16[4,128,896]{2,1,0:T(8,128)(2,1)S(1)} async-done(((bf16[4,128,896]{2,1,0:T(8,128)(2,1)}), bf16[4,128,896]{2,1,0:T(8,128)(2,1)S(1)}, u32[]{:S(2)}, u32[]{:S(2)}) %all-to-all-start.2) | async-done | bytes 917536 | tf_op jit(solution)/shard_map/all_to_all | solution.py:367
  200.9 28.4 %all-gather.8.cloned.1.call-done.refs_0_ = bf16[512,1024]{1,0:T(8,128)(2,1)} async-done(((bf16[128,1024]{1,0:T(8,128)(2,1)}), bf16[512,1024]{1,0:T(8,128)(2,1)}) %all-gather.8.cloned.1.call-update) | async-done | bytes 1048592 | tf_op jit(solution)/shard_map/all_gather | solution.py:366
  229.3 4.4 %all-to-all-start.3 = ((bf16[4,128,896]{2,1,0:T(8,128)(2,1)}), bf16[4,128,896]{2,1,0:T(8,128)(2,1)}, u32[]{:S(2)}, u32[]{:S(2)}) async-start(bf16[4,128,896]{2,1,0:T(8,128)(2,1)} %copy-done.13), calls=%async_computation.3 | async-start | bytes 1835008 | tf_op jit(solution)/shard_map/all_to_all | solution.py:369
  236.7 20.2 %collective-permute-done.9.refs_3_ = bf16[4,128,896]{2,1,0:T(8,128)(2,1)S(1)} collective-permute-done((bf16[4,128,896]{2,1,0:T(8,128)(2,1)S(1)}, bf16[4,128,896]{2,1,0:T(8,128)(2,1)S(1)}, u32[]{:S(2)}, u32[]{:S(2)}) %collective-permute-start.9) | collective-permute-done | bytes 917536 | tf_op jit(solution)/shard_map/ppermute | solution.py:32
  259.7 4.5 %all-to-all-start.4 = ((bf16[4,896,128]{2,1,0:T(8,128)(2,1)}), bf16[4,896,128]{2,1,0:T(8,128)(2,1)}, u32[]{:S(2)}, u32[]{:S(2)}) async-start(bf16[4,896,128]{2,1,0:T(8,128)(2,1)} %copy-done.12), calls=%async_computation.4 | async-start | bytes 1835008 | tf_op jit(solution)/shard_map/all_to_all | solution.py:371
  269.6 7.0 %gate_up.2.refs_5_ = bf16[2,1024,896]{2,1,0:T(8,128)(2,1)} custom-call(bf16[512,1024]{1,0:T(8,128)(2,1)S(1)} %copy-done.3, bf16[512,1024]{1,0:T(8,128)(2,1)S(1)} %copy-done.5, bf16[4,2,128,896]{3,2,1,0:T(8,128)(2,1)S(1)} %all-to-all-done.1.refs_2_, bf16[4,128,896]{2,1,0:T(8,128)(2,1)S(1)} %all-to-all-done.2.refs_3_, bf16[4,128,896]{2,1,0:T(8,128)(2,1)} %all-to-all-done.3.refs_4_), custom_call_target="tpu_custom_call" | custom-call | flops 1 | bytes 1 | tf_op jit(solution)/shard_map/gate_up/pallas_call | solution.py:226
  276.6 9.8 %collective-permute-done.11.refs_4_ = bf16[4,128,896]{2,1,0:T(8,128)(2,1)S(1)} collective-permute-done((bf16[4,128,896]{2,1,0:T(8,128)(2,1)}, bf16[4,128,896]{2,1,0:T(8,128)(2,1)S(1)}, u32[]{:S(2)}, u32[]{:S(2)}) %collective-permute-start.11) | collective-permute-done | bytes 917536 | tf_op jit(solution)/shard_map/ppermute | solution.py:32
  291.8 10.1 %gate_up.3.here_ref = bf16[2,1024,896]{2,1,0:T(8,128)(2,1)} custom-call(bf16[512,1024]{1,0:T(8,128)(2,1)S(1)} %copy-done.2, bf16[512,1024]{1,0:T(8,128)(2,1)} %collective-permute-done.13.refs_1_, bf16[4,2,128,896]{3,2,1,0:T(8,128)(2,1)} %collective-permute-done.8.refs_2_, bf16[4,128,896]{2,1,0:T(8,128)(2,1)S(1)} %copy-done.8, ...), custom_call_target="tpu_custom_call" | custom-call | flops 1 | bytes 1 | tf_op jit(solution)/shard_map/gate_up/pallas_call | solution.py:226
  302.0 4.7 %all-to-all-start.5 = ((bf16[4,896,128]{2,1,0:T(8,128)(2,1)}), bf16[4,896,128]{2,1,0:T(8,128)(2,1)S(1)}, u32[]{:S(2)}, u32[]{:S(2)}) async-start(bf16[4,896,128]{2,1,0:T(8,128)(2,1)} %copy-done.11), calls=%async_computation.5 | async-start | bytes 1835008 | tf_op jit(solution)/shard_map/all_to_all | solution.py:382
  310.8 3.9 activation.1.activated_ref
  314.8 14.7 %collective-permute-done.12.weights_ref = bf16[4,896,128]{2,1,0:T(8,128)(2,1)S(1)} collective-permute-done((bf16[4,896,128]{2,1,0:T(8,128)(2,1)}, bf16[4,896,128]{2,1,0:T(8,128)(2,1)S(1)}, u32[]{:S(2)}, u32[]{:S(2)}) %collective-permute-start.12) | collective-permute-done | bytes 917536 | tf_op jit(solution)/shard_map/ppermute | solution.py:32
  344.0 5.7 %collective-permute-done.23 = bf16[512,512]{1,0:T(8,128)(2,1)} collective-permute-done((bf16[512,512]{1,0:T(8,128)(2,1)}, bf16[512,512]{1,0:T(8,128)(2,1)}, u32[]{:S(2)}, u32[]{:S(2)}) %collective-permute-start.23) | collective-permute-done | bytes 524320 | tf_op jit(solution)/shard_map/ppermute | solution.py:32
  355.2 5.6 %collective-permute-done.15 = bf16[512,512]{1,0:T(8,128)(2,1)} collective-permute-done((bf16[512,512]{1,0:T(8,128)(2,1)}, bf16[512,512]{1,0:T(8,128)(2,1)}, u32[]{:S(2)}, u32[]{:S(2)}) %collective-permute-start.15) | collective-permute-done | bytes 524320 | tf_op jit(solution)/shard_map/ppermute | solution.py:32
  365.7 4.7 %collective-permute-done.19 = bf16[512,512]{1,0:T(8,128)(2,1)S(1)} collective-permute-done((bf16[512,512]{1,0:T(8,128)(2,1)S(1)}, bf16[512,512]{1,0:T(8,128)(2,1)S(1)}, u32[]{:S(2)}, u32[]{:S(2)}) %collective-permute-start.19) | collective-permute-done | bytes 524320 | tf_op jit(solution)/shard_map/ppermute | solution.py:32
  383.0 8.0 %collective-permute-done.17 = bf16[128,512]{1,0:T(8,128)(2,1)S(1)} collective-permute-done((bf16[128,512]{1,0:T(8,128)(2,1)S(1)}, bf16[128,512]{1,0:T(8,128)(2,1)S(1)}, u32[]{:S(2)}, u32[]{:S(2)}) %collective-permute-start.17) | collective-permute-done | bytes 131104 | tf_op jit(solution)/shard_map/ppermute | solution.py:32
  400.9 8.0 %collective-permute-done.31 = bf16[128,512]{1,0:T(8,128)(2,1)S(1)} collective-permute-done((bf16[128,512]{1,0:T(8,128)(2,1)S(1)}, bf16[128,512]{1,0:T(8,128)(2,1)S(1)}, u32[]{:S(2)}, u32[]{:S(2)}) %collective-permute-start.31) | collective-permute-done | bytes 131104 | tf_op jit(solution)/shard_map/ppermute | solution.py:32
  (192 shorter events, 125.8 us)
Async XLA Ops:
  7.2 85.7 %all-gather.4.cloned.1.call-start = ((), (), s32[]{:S(2)}) async-start(), calls=%async_computation.6 | async-start | bytes 5242880 | tf_op jit(solution)/shard_map/all_gather | solution.py:315
  21.3 71.6 %all-to-all-start = ((bf16[8,64,1024]{2,1,0:T(8,128)(2,1)}), bf16[8,64,1024]{2,1,0:T(8,128)(2,1)S(1)}, u32[]{:S(2)}, u32[]{:S(2)}) async-start(bf16[8,64,1024]{2,1,0:T(8,128)(2,1)} %bitcast.5), calls=%async_computation | async-start | bytes 2097152 | tf_op jit(solution)/shard_map/all_to_all | solution.py:320
  92.9 59.4 %all-to-all-start.1 = ((bf16[4,2,128,896]{3,2,1,0:T(8,128)(2,1)}), bf16[4,2,128,896]{3,2,1,0:T(8,128)(2,1)S(1)}, u32[]{:S(2)}, u32[]{:S(2)}) async-start(bf16[4,2,128,896]{3,2,1,0:T(8,128)(2,1)} %copy-done.1), calls=%async_computation.1 | async-start | bytes 3670016 | tf_op jit(solution)/shard_map/all_to_all | solution.py:343
  96.5 104.4 %all-gather.6.cloned.1.call-start = ((), (), s32[]{:S(2)}) async-start(), calls=%async_computation.7 | async-start | bytes 1310720 | tf_op jit(solution)/shard_map/all_gather | solution.py:366
  154.6 74.7 %all-gather.8.cloned.1.call-start = ((), (), s32[]{:S(2)}) async-start(), calls=%async_computation.8 | async-start | bytes 1310720 | tf_op jit(solution)/shard_map/all_gather | solution.py:366
  154.7 74.6 %collective-permute-start.8 = (bf16[4,2,128,896]{3,2,1,0:T(8,128)(2,1)S(1)}, bf16[4,2,128,896]{3,2,1,0:T(8,128)(2,1)}, u32[]{:S(2)}, u32[]{:S(2)}) collective-permute-start(bf16[4,2,128,896]{3,2,1,0:T(8,128)(2,1)S(1)} %all-to-all-done.1.refs_2_), channel_id=1, source_target_pairs={{0,8},{4,12},{8,0},{12,4},{1,9},{5,13},{9,1},{13,5},{2,10},{6,14},... | collective-permute-start | bytes 5505032 | tf_op jit(solution)/shard_map/ppermute | solution.py:32
  156.3 44.6 %all-to-all-start.2 = ((bf16[4,128,896]{2,1,0:T(8,128)(2,1)}), bf16[4,128,896]{2,1,0:T(8,128)(2,1)S(1)}, u32[]{:S(2)}, u32[]{:S(2)}) async-start(bf16[4,128,896]{2,1,0:T(8,128)(2,1)} %copy-done.14), calls=%async_computation.2 | async-start | bytes 1835008 | tf_op jit(solution)/shard_map/all_to_all | solution.py:367
  229.3 30.4 %all-to-all-start.3 = ((bf16[4,128,896]{2,1,0:T(8,128)(2,1)}), bf16[4,128,896]{2,1,0:T(8,128)(2,1)}, u32[]{:S(2)}, u32[]{:S(2)}) async-start(bf16[4,128,896]{2,1,0:T(8,128)(2,1)} %copy-done.13), calls=%async_computation.3 | async-start | bytes 1835008 | tf_op jit(solution)/shard_map/all_to_all | solution.py:369
  233.7 25.0 %collective-permute-start.10 = (bf16[512,1024]{1,0:T(8,128)(2,1)}, bf16[512,1024]{1,0:T(8,128)(2,1)S(1)}, u32[]{:S(2)}, u32[]{:S(2)}) collective-permute-start(bf16[512,1024]{1,0:T(8,128)(2,1)} %all-gather.6.cloned.1.call-done.refs_0_), channel_id=1, source_target_pairs={{0,16},{16,0},{1,17},{17,1},{2,18},{18,2},{3,19},{19,3},{4,20},{20... | collective-permute-start | bytes 3145736 | tf_op jit(solution)/shard_map/ppermute | solution.py:32
  235.2 21.7 %collective-permute-start.9 = (bf16[4,128,896]{2,1,0:T(8,128)(2,1)S(1)}, bf16[4,128,896]{2,1,0:T(8,128)(2,1)S(1)}, u32[]{:S(2)}, u32[]{:S(2)}) collective-permute-start(bf16[4,128,896]{2,1,0:T(8,128)(2,1)S(1)} %all-to-all-done.2.refs_3_), channel_id=1, source_target_pairs={{0,8},{4,12},{8,0},{12,4},{1,9},{5,13},{9,1},{13,5},{2,10},{6,14},... | collective-permute-start | bytes 2752520 | tf_op jit(solution)/shard_map/ppermute | solution.py:32
  259.7 27.7 %all-to-all-start.4 = ((bf16[4,896,128]{2,1,0:T(8,128)(2,1)}), bf16[4,896,128]{2,1,0:T(8,128)(2,1)}, u32[]{:S(2)}, u32[]{:S(2)}) async-start(bf16[4,896,128]{2,1,0:T(8,128)(2,1)} %copy-done.12), calls=%async_computation.4 | async-start | bytes 1835008 | tf_op jit(solution)/shard_map/all_to_all | solution.py:371
  264.2 24.0 %collective-permute-start.13 = (bf16[512,1024]{1,0:T(8,128)(2,1)}, bf16[512,1024]{1,0:T(8,128)(2,1)}, u32[]{:S(2)}, u32[]{:S(2)}) collective-permute-start(bf16[512,1024]{1,0:T(8,128)(2,1)} %all-gather.8.cloned.1.call-done.refs_0_), channel_id=1, source_target_pairs={{0,16},{16,0},{1,17},{17,1},{2,18},{18,2},{3,19},{19,3},{4,20},{20... | collective-permute-start | bytes 3145736 | tf_op jit(solution)/shard_map/ppermute | solution.py:32
  265.7 20.8 %collective-permute-start.11 = (bf16[4,128,896]{2,1,0:T(8,128)(2,1)}, bf16[4,128,896]{2,1,0:T(8,128)(2,1)S(1)}, u32[]{:S(2)}, u32[]{:S(2)}) collective-permute-start(bf16[4,128,896]{2,1,0:T(8,128)(2,1)} %all-to-all-done.3.refs_4_), channel_id=1, source_target_pairs={{0,8},{4,12},{8,0},{12,4},{1,9},{5,13},{9,1},{13,5},{2,10},{6,14},... | collective-permute-start | bytes 2752520 | tf_op jit(solution)/shard_map/ppermute | solution.py:32
  302.0 28.4 %all-to-all-start.5 = ((bf16[4,896,128]{2,1,0:T(8,128)(2,1)}), bf16[4,896,128]{2,1,0:T(8,128)(2,1)S(1)}, u32[]{:S(2)}, u32[]{:S(2)}) async-start(bf16[4,896,128]{2,1,0:T(8,128)(2,1)} %copy-done.11), calls=%async_computation.5 | async-start | bytes 1835008 | tf_op jit(solution)/shard_map/all_to_all | solution.py:382
  306.7 22.7 %collective-permute-start.12 = (bf16[4,896,128]{2,1,0:T(8,128)(2,1)}, bf16[4,896,128]{2,1,0:T(8,128)(2,1)S(1)}, u32[]{:S(2)}, u32[]{:S(2)}) collective-permute-start(bf16[4,896,128]{2,1,0:T(8,128)(2,1)} %all-to-all-done.4.weights_ref), channel_id=1, source_target_pairs={{0,8},{4,12},{8,0},{12,4},{1,9},{5,13},{9,1},{13,5},{2,10},{6,14},... | collective-permute-start | bytes 2752520 | tf_op jit(solution)/shard_map/ppermute | solution.py:32
  339.2 21.7 %collective-permute-start.15 = (bf16[512,512]{1,0:T(8,128)(2,1)}, bf16[512,512]{1,0:T(8,128)(2,1)}, u32[]{:S(2)}, u32[]{:S(2)}) collective-permute-start(bf16[512,512]{1,0:T(8,128)(2,1)} %bitcast.9), channel_id=1, source_target_pairs={{0,16},{16,0},{1,17},{17,1},{2,18},{18,2},{3,19},{19,3},{4,20},{20... | collective-permute-start | bytes 1572872 | tf_op jit(solution)/shard_map/ppermute | solution.py:32
  339.7 32.2 %collective-permute-start.28 = (bf16[4,896,128]{2,1,0:T(8,128)(2,1)S(1)}, bf16[4,896,128]{2,1,0:T(8,128)(2,1)S(1)}, u32[]{:S(2)}, u32[]{:S(2)}) collective-permute-start(bf16[4,896,128]{2,1,0:T(8,128)(2,1)S(1)} %all-to-all-done.5.weights_ref), channel_id=1, source_target_pairs={{0,8},{4,12},{8,0},{12,4},{1,9},{5,13},{9,1},{13,5},{2,10},{6,14},... | collective-permute-start | bytes 2752520 | tf_op jit(solution)/shard_map/ppermute | solution.py:32
  342.4 27.9 %collective-permute-start.19 = (bf16[512,512]{1,0:T(8,128)(2,1)S(1)}, bf16[512,512]{1,0:T(8,128)(2,1)S(1)}, u32[]{:S(2)}, u32[]{:S(2)}) collective-permute-start(bf16[512,512]{1,0:T(8,128)(2,1)S(1)} %bitcast.97), channel_id=1, source_target_pairs={{0,16},{16,0},{1,17},{17,1},{2,18},{18,2},{3,19},{19,3},{4,20},{20... | collective-permute-start | bytes 1572872 | tf_op jit(solution)/shard_map/ppermute | solution.py:32
  351.1 24.5 %collective-permute-start.24 = (bf16[128,512]{1,0:T(8,128)(2,1)S(1)}, bf16[128,512]{1,0:T(8,128)(2,1)S(1)}, u32[]{:S(2)}, u32[]{:S(2)}) collective-permute-start(bf16[128,512]{1,0:T(8,128)(2,1)S(1)} %get-tuple-element.90), channel_id=1, source_target_pairs={{0,1},{1,0},{2,3},{3,2},{4,5},{5,4},{6,7},{7,6},{8,9},{9,8},{10,11... | collective-permute-start | bytes 393224 | tf_op jit(solution)/shard_map/ppermute | solution.py:32
  352.9 25.0 %collective-permute-start.25 = (bf16[128,512]{1,0:T(8,128)(2,1)S(1)}, bf16[128,512]{1,0:T(8,128)(2,1)S(1)}, u32[]{:S(2)}, u32[]{:S(2)}) collective-permute-start(bf16[128,512]{1,0:T(8,128)(2,1)S(1)} %get-tuple-element.92), channel_id=1, source_target_pairs={{0,2},{1,3},{2,0},{3,1},{4,6},{5,7},{6,4},{7,5},{8,10},{9,11},{10,... | collective-permute-start | bytes 393224 | tf_op jit(solution)/shard_map/ppermute | solution.py:32
  360.9 17.6 %collective-permute-start.26 = (bf16[128,512]{1,0:T(8,128)(2,1)S(1)}, bf16[128,512]{1,0:T(8,128)(2,1)S(1)}, u32[]{:S(2)}, u32[]{:S(2)}) collective-permute-start(bf16[128,512]{1,0:T(8,128)(2,1)S(1)} %get-tuple-element.91), channel_id=1, source_target_pairs={{0,3},{1,2},{2,1},{3,0},{4,7},{5,6},{6,5},{7,4},{8,11},{9,10},{10,... | collective-permute-start | bytes 393224 | tf_op jit(solution)/shard_map/ppermute | solution.py:32
  373.2 21.1 %collective-permute-start.29 = (bf16[512,512]{1,0:T(8,128)(2,1)S(1)}, bf16[512,512]{1,0:T(8,128)(2,1)S(1)}, u32[]{:S(2)}, u32[]{:S(2)}) collective-permute-start(bf16[512,512]{1,0:T(8,128)(2,1)S(1)} %bitcast.96), channel_id=1, source_target_pairs={{0,16},{16,0},{1,17},{17,1},{2,18},{18,2},{3,19},{19,3},{4,20},{20... | collective-permute-start | bytes 1572872 | tf_op jit(solution)/shard_map/ppermute | solution.py:32
  378.5 17.8 %collective-permute-start.20 = (bf16[128,512]{1,0:T(8,128)(2,1)}, bf16[128,512]{1,0:T(8,128)(2,1)}, u32[]{:S(2)}, u32[]{:S(2)}) collective-permute-start(bf16[128,512]{1,0:T(8,128)(2,1)} %get-tuple-element.99), channel_id=1, source_target_pairs={{0,1},{1,0},{2,3},{3,2},{4,5},{5,4},{6,7},{7,6},{8,9},{9,8},{10,11... | collective-permute-start | bytes 393224 | tf_op jit(solution)/shard_map/ppermute | solution.py:32
  392.7 18.7 %collective-permute-start.27 = (bf16[128,512]{1,0:T(8,128)(2,1)}, bf16[128,512]{1,0:T(8,128)(2,1)}, u32[]{:S(2)}, u32[]{:S(2)}) collective-permute-start(bf16[128,512]{1,0:T(8,128)(2,1)} %fusion.7), channel_id=1, source_target_pairs={{0,8},{4,12},{8,0},{12,4},{1,9},{5,13},{9,1},{13,5},{2,10},{6,14},... | collective-permute-start | bytes 393224 | tf_op jit(solution)/shard_map/ppermute | solution.py:32
  (49 other events, 372.3 us)
Sparse Core Ops, SparseCore 0:
  9.6 83.2 all-gather.3
  154.7 45.7 all-gather.5
  202.1 27.0 all-gather.7

commit v9 on v8

--- a/solution.py
+++ b/solution.py
@@ -340,6 +340,7 @@
     cut = cut_weights(w_gate_up, w_down, own_gain[:, None], outer_count)
 
     place = jnp.stack([inner, head]).astype(jnp.int32)
+    weights_out, *blocks = fence(weights_out, *blocks)
     first = spread(after(cut[0], weights_out))
     kept, sent, *whole = projection(blocks, weights_out, place, head_count, inner_count)
     context = whole[0] if whole else own_context
@@ -359,12 +360,13 @@
     squares = squares + swap(squares, "inner", 1)
     inverse = lax.rsqrt(squares / D + 1e-05)[:, None]
     part_rows = feature_rows // PARTS
-    normed = [(block * inverse).astype(jnp.bfloat16) for block in state]
+    normed = jnp.concatenate([block * inverse for block in state], axis=1).astype(jnp.bfloat16)
     state = [block.reshape(own_rows, outer_count, PARTS, part_rows) for block in state]
     state = [[block[:, :, part].reshape(own_rows, -1) for part in range(PARTS)] for block in state]
 
-    tokens = [lax.all_gather(block, "outer", axis=0, tiled=True) for block in normed]
-    second, first_y, tokens, state = fence(spread(after(cut[1], normed[0])), over_y(first), tokens, state)
+    tokens = lax.all_gather(normed, "outer", axis=0, tiled=True)
+    second, first_y, tokens, state = fence(spread(after(cut[1], normed)), over_y(first), tokens, state)
+    tokens = jnp.split(tokens, 2, axis=1)
     tokens = [[swap(block, "head", e) if e else block for e in range(head_count)] for block in tokens]
     third, second_y, tokens[0] = fence(spread(after(cut[2], second)), over_y(second), tokens[0])
     own_sums = gate_up(tokens[0], [first, second, third])
@@ -379,10 +381,12 @@
             paired = paired + swap(sent[e - 1], "head", e).astype(jnp.float32)
         return paired.reshape(outer_count, own_rows, -1)
 
-    fifth, fourth_y, activated = fence(spread(after(cut[4], fourth)), over_y(fourth), activated)
+    paired = {(0, 0): over_heads(fourth)}
+    fifth, fourth_y, paired[0, 0] = fence(spread(after(cut[4], fourth)), over_y(fourth), paired[0, 0])
     fifth_y = over_y(fifth)
-    paired = {(0, 0): over_heads(fourth), (1, 0): over_heads(fourth_y), (0, 1): over_heads(fifth)}
-    paired[1, 1] = over_heads(after(fifth_y, paired[0, 0]))
+    paired[1, 0] = over_heads(fourth_y)
+    paired[0, 1] = over_heads(fifth)
+    paired[1, 1] = over_heads(after(fifth_y, paired[1, 0]))
 
     pieces = [[None] * PARTS, [None] * PARTS]
     for part in range(PARTS):

time: 424 us -> 386 us (0.910)
  waiting for transfers between devices: 233 us -> 198 us
  starting transfers between devices: 79.7 us -> 73.5 us
    all_gather x1, waiting for transfers between devices: 58.2 us -> 22.9 us  [per_device(): weights_out = lax.all_gather(w_out, 'outer', axis=1, tiled=True)]
    all_gather x2 -> x1, waiting for transfers between devices: 28.4 us -> 10.2 us  [per_device(): tokens = lax.all_gather(normed, 'outer', axis=0, tiled=True)]
    ppermute x32, waiting for transfers between devices: 113 us -> 97.9 us  [swap(): return lax.ppermute(array, axis, [(s, s ^ distance) for s in range(count)])]
    all_to_all x1, waiting for transfers between devices: 0.01 us -> 14.4 us  [per_device(): lax.all_to_all(groups, ('inner', 'head'), split_axis=0, concat_axis=0, ti...]
    all_to_all x1, waiting for transfers between devices: 0.01 us -> 12.5 us  [per_device(): first = spread(after(cut[0], weights_out))]
    all_to_all x1, waiting for transfers between devices: 32.2 us -> 39.5 us  [per_device(): spread(after(cut[1], normed))]
    ppermute x32, starting transfers between devices: 45.5 us -> 40.5 us  [swap(): return lax.ppermute(array, axis, [(s, s ^ distance) for s in range(count)])]
    unnamed x64 -> x68, local copies, waits for them, and re-layouts: 25.7 us -> 24.2 us
  transfers between devices with their start and end apart: 43 -> 42, of which waited for: 21 -> 20; matrix products, arithmetic and copies ran while one was open for 6% -> 7% of each run, Pallas kernels for 8% -> 9%
where the time goes in v9:
time: 386 us; the launch traced here: 384 us
  waiting for transfers between devices  198 us (51%)
  starting transfers between devices  73.5 us (19%)
  Pallas kernels  45 us (12%)
  local copies, waits for them, and re-layouts  43.1 us (11%)
  between operations  14.6 us (4%)
  other arithmetic  10 us (3%)
    ppermute x32, waiting for transfers between devices, swap(): return lax.ppermute(array, axis, [(s, s ^ distance) for s in range(count)])  97.9 us
    ppermute x32, starting transfers between devices, swap(): return lax.ppermute(array, axis, [(s, s ^ distance) for s in range(count)])  40.5 us
    all_to_all x1, waiting for transfers between devices, per_device(): spread(after(cut[1], normed))  39.5 us
    unnamed x68, local copies, waits for them, and re-layouts  24.2 us
    all_gather x1, waiting for transfers between devices, per_device(): weights_out = lax.all_gather(w_out, 'outer', axis=1, tiled=True)  22.9 us
    pallas_call x2, Pallas kernels, gate_up(): pl.pallas_call(functools.partial(gate_up_kernel, len(tokens)), in_specs=[...  17.1 us
    all_to_all x1, waiting for transfers between devices, per_device(): lax.all_to_all(groups, ('inner', 'head'), split_axis=0, concat_axis=0, ti...  14.4 us
    all_to_all x1, waiting for transfers between devices, per_device(): first = spread(after(cut[0], weights_out))  12.5 us
  transfers between devices with their start and end apart: 42, of which 20 were waited for; matrix products, arithmetic and copies ran while one was open for 7% of the time, Pallas kernels for 9%

profile of v9, /device:TPU:0, one launch (start us, length us, event | category | flops | bytes accessed | tf_op | source)
XLA Modules:
  0.0 384.5 jit_solution(15574117601546749635)
XLA Ops:
  7.9 4.9 %collective-permute-start = (bf16[64,1024]{1,0:T(8,128)(2,1)}, bf16[64,1024]{1,0:T(8,128)(2,1)S(1)}, u32[]{:S(2)}, u32[]{:S(2)}) collective-permute-start(bf16[64,1024]{1,0:T(8,128)(2,1)} %param.10), channel_id=1, source_target_pairs={{0,1},{1,2},{2,3},{4,5},{5,6},{6,7},{8,9},{9,10},{10,11},{12,13},{... | collective-permute-start | bytes 393224 | tf_op jit(solution)/shard_map/ppermute | solution.py:317
  21.3 3.7 all-to-all-start
  25.6 14.4 %all-to-all-done = bf16[8,64,1024]{2,1,0:T(8,128)(2,1)S(1)} async-done(((bf16[8,64,1024]{2,1,0:T(8,128)(2,1)}), bf16[8,64,1024]{2,1,0:T(8,128)(2,1)S(1)}, u32[]{:S(2)}, u32[]{:S(2)}) %all-to-all-start) | async-done | bytes 1048608 | tf_op jit(solution)/shard_map/all_to_all | solution.py:320
  40.0 5.9 %attention.1.refs_0_ = bf16[512,512]{1,0:T(8,128)(2,1)S(1)} custom-call(s32[512,1]{1,0:T(8,128)S(1)} %copy.27.starts_ref, bf16[512,1024]{1,0:T(8,128)(2,1)S(1)} %bitcast.93, bf16[512,1024]{1,0:T(8,128)(2,1)S(1)} %bitcast.94, bf16[512,1024]{1,0:T(8,128)(2,1)S(1)} %bitcast.95), custom_call_target="tpu_custom_call" | custom-call | flops 1 | bytes 1 | tf_op jit(solution)/shard_map/attention/pallas_call | solution.py:96
  46.9 12.6 %collective-permute-done.3.refs_2_ = bf16[512,512]{1,0:T(8,128)(2,1)S(1)} collective-permute-done((bf16[512,512]{1,0:T(8,128)(2,1)S(1)}, bf16[512,512]{1,0:T(8,128)(2,1)S(1)}, u32[]{:S(2)}, u32[]{:S(2)}) %collective-permute-start.3) | collective-permute-done | bytes 524320 | tf_op jit(solution)/shard_map/ppermute | solution.py:32
  70.0 22.9 %all-gather.3.cloned.1.call-done.refs_4_ = bf16[2048,1024]{1,0:T(8,128)(2,1)} async-done(((bf16[2048,256]{1,0:T(8,128)(2,1)}), bf16[2048,1024]{1,0:T(8,128)(2,1)}) %all-gather.3.cloned.1.call-update) | async-done | bytes 4194320 | tf_op jit(solution)/shard_map/all_gather | solution.py:315
  98.7 5.5 %projection.1 = (bf16[256,1024]{1,0:T(8,128)(2,1)S(1)}, bf16[1,256,1024]{2,1,0:T(8,128)(2,1)}, bf16[128,2048]{1,0:T(8,128)(2,1)}) custom-call(s32[2]{0:T(128)S(1)} %pad_add_fusion.place_ref, bf16[512,512]{1,0:T(8,128)(2,1)S(1)} %attention.1.refs_0_, bf16[512,512]{1,0:T(8,128)(2,1)S(1)} %copy-done.20, bf16[512,512]{1,0:T(8,128)(2,1)S(1)} %collective-permute-done.3.refs_2_, ...), custom_call_target="tpu_custom_call" | custom-call | flops 1 | bytes 1 | tf_op jit(solution)/shard_map/projection/pallas_call | solution.py:185
  105.6 12.5 %collective-permute-done.5 = bf16[256,1024]{1,0:T(8,128)(2,1)S(1)} collective-permute-done((bf16[256,1024]{1,0:T(8,128)(2,1)}, bf16[256,1024]{1,0:T(8,128)(2,1)S(1)}, u32[]{:S(2)}, u32[]{:S(2)}) %collective-permute-start.5) | collective-permute-done | bytes 524320 | tf_op jit(solution)/shard_map/ppermute | solution.py:32
  121.3 5.6 %collective-permute-done.6 = bf16[128,1024]{1,0:T(8,128)(2,1)S(1)} collective-permute-done((bf16[128,1024]{1,0:T(8,128)(2,1)S(1)}, bf16[128,1024]{1,0:T(8,128)(2,1)S(1)}, u32[]{:S(2)}, u32[]{:S(2)}) %collective-permute-start.6) | collective-permute-done | bytes 262176 | tf_op jit(solution)/shard_map/ppermute | solution.py:32
  126.9 12.5 %all-to-all-done.1.refs_2_ = bf16[4,2,128,896]{3,2,1,0:T(8,128)(2,1)S(1)} async-done(((bf16[4,2,128,896]{3,2,1,0:T(8,128)(2,1)}), bf16[4,2,128,896]{3,2,1,0:T(8,128)(2,1)S(1)}, u32[]{:S(2)}, u32[]{:S(2)}) %all-to-all-start.1) | async-done | bytes 1835040 | tf_op jit(solution)/shard_map/all_to_all | solution.py:344
  154.6 39.5 %all-to-all-done.2.refs_3_ = bf16[4,128,896]{2,1,0:T(8,128)(2,1)S(1)} async-done(((bf16[4,128,896]{2,1,0:T(8,128)(2,1)}), bf16[4,128,896]{2,1,0:T(8,128)(2,1)S(1)}, u32[]{:S(2)}, u32[]{:S(2)}) %all-to-all-start.2) | async-done | bytes 917536 | tf_op jit(solution)/shard_map/all_to_all | solution.py:368
  194.2 10.2 %all-gather.5.cloned.1.call-done = bf16[512,2048]{1,0:T(8,128)(2,1)} async-done(((bf16[128,2048]{1,0:T(8,128)(2,1)}), bf16[512,2048]{1,0:T(8,128)(2,1)}) %all-gather.5.cloned.1.call-update) | async-done | bytes 2097168 | tf_op jit(solution)/shard_map/all_gather | solution.py:367
  204.4 4.4 %all-to-all-start.3 = ((bf16[4,128,896]{2,1,0:T(8,128)(2,1)}), bf16[4,128,896]{2,1,0:T(8,128)(2,1)}, u32[]{:S(2)}, u32[]{:S(2)}) async-start(bf16[4,128,896]{2,1,0:T(8,128)(2,1)} %copy-done.15), calls=%async_computation.3 | async-start | bytes 1835008 | tf_op jit(solution)/shard_map/all_to_all | solution.py:371
  213.7 21.4 %collective-permute-done.9.refs_3_ = bf16[4,128,896]{2,1,0:T(8,128)(2,1)S(1)} collective-permute-done((bf16[4,128,896]{2,1,0:T(8,128)(2,1)S(1)}, bf16[4,128,896]{2,1,0:T(8,128)(2,1)S(1)}, u32[]{:S(2)}, u32[]{:S(2)}) %collective-permute-start.9) | collective-permute-done | bytes 917536 | tf_op jit(solution)/shard_map/ppermute | solution.py:32
  237.1 4.6 %all-to-all-start.4 = ((bf16[4,896,128]{2,1,0:T(8,128)(2,1)}), bf16[4,896,128]{2,1,0:T(8,128)(2,1)}, u32[]{:S(2)}, u32[]{:S(2)}) async-start(bf16[4,896,128]{2,1,0:T(8,128)(2,1)} %copy-done.14), calls=%async_computation.4 | async-start | bytes 1835008 | tf_op jit(solution)/shard_map/all_to_all | solution.py:373
  247.0 7.0 %gate_up.2.refs_5_ = bf16[2,1024,896]{2,1,0:T(8,128)(2,1)} custom-call(bf16[512,1024]{1,0:T(8,128)(2,1)S(1)} %copy-done.2, bf16[512,1024]{1,0:T(8,128)(2,1)S(1)} %copy-done.8, bf16[4,2,128,896]{3,2,1,0:T(8,128)(2,1)S(1)} %all-to-all-done.1.refs_2_, bf16[4,128,896]{2,1,0:T(8,128)(2,1)S(1)} %copy-done.5, bf16[4,128,896]{2,1,0:T(8,128)(2,1)} %all-to-all-done.3.refs_4_), custom_call_target="tpu_custom_call" | custom-call | flops 1 | bytes 1 | tf_op jit(solution)/shard_map/gate_up/pallas_call | solution.py:226
  254.0 9.9 %collective-permute-done.11.refs_4_ = bf16[4,128,896]{2,1,0:T(8,128)(2,1)S(1)} collective-permute-done((bf16[4,128,896]{2,1,0:T(8,128)(2,1)}, bf16[4,128,896]{2,1,0:T(8,128)(2,1)S(1)}, u32[]{:S(2)}, u32[]{:S(2)}) %collective-permute-start.11) | collective-permute-done | bytes 917536 | tf_op jit(solution)/shard_map/ppermute | solution.py:32
  267.8 10.1 %gate_up.3.here_ref = bf16[2,1024,896]{2,1,0:T(8,128)(2,1)} custom-call(bf16[512,1024]{1,0:T(8,128)(2,1)S(1)} %get-tuple-element.99.refs_0_, bf16[512,1024]{1,0:T(8,128)(2,1)} %collective-permute-done.13.refs_1_, bf16[4,2,128,896]{3,2,1,0:T(8,128)(2,1)} %collective-permute-done.8.refs_2_, bf16[4,128,896]{2,1,0:T(8,128)(2,1)S(1)} %copy-done.10, ...), custom_call_target="tpu_custom_call" | custom-call | flops 1 | bytes 1 | tf_op jit(solution)/shard_map/gate_up/pallas_call | solution.py:226
  278.0 4.7 %all-to-all-start.5 = ((bf16[4,896,128]{2,1,0:T(8,128)(2,1)}), bf16[4,896,128]{2,1,0:T(8,128)(2,1)S(1)}, u32[]{:S(2)}, u32[]{:S(2)}) async-start(bf16[4,896,128]{2,1,0:T(8,128)(2,1)} %copy-done.13), calls=%async_computation.5 | async-start | bytes 1835008 | tf_op jit(solution)/shard_map/all_to_all | solution.py:385
  286.8 3.9 %activation.1.activated_ref = bf16[1024,896]{1,0:T(8,128)(2,1)S(1)} custom-call(bf16[2,1024,896]{2,1,0:T(8,128)(2,1)S(1)} %copy-done, bf16[2,1024,896]{2,1,0:T(8,128)(2,1)} %collective-permute-done.14.there_ref), custom_call_target="tpu_custom_call" | custom-call | flops 1 | bytes 1 | tf_op jit(solution)/shard_map/activation/pallas_call | solution.py:252
  294.7 12.5 %collective-permute-done.15 = bf16[512,512]{1,0:T(8,128)(2,1)S(1)} collective-permute-done((bf16[512,512]{1,0:T(8,128)(2,1)S(1)}, bf16[512,512]{1,0:T(8,128)(2,1)S(1)}, u32[]{:S(2)}, u32[]{:S(2)}) %collective-permute-start.15) | collective-permute-done | bytes 524320 | tf_op jit(solution)/shard_map/ppermute | solution.py:32
  324.3 5.9 %collective-permute-done.17 = bf16[128,512]{1,0:T(8,128)(2,1)} collective-permute-done((bf16[128,512]{1,0:T(8,128)(2,1)}, bf16[128,512]{1,0:T(8,128)(2,1)}, u32[]{:S(2)}, u32[]{:S(2)}) %collective-permute-start.17) | collective-permute-done | bytes 131104 | tf_op jit(solution)/shard_map/ppermute | solution.py:32
  354.0 4.4 %collective-permute-start.30 = (bf16[128,512]{1,0:T(8,128)(2,1)S(1)}, bf16[128,512]{1,0:T(8,128)(2,1)S(1)}, u32[]{:S(2)}, u32[]{:S(2)}) collective-permute-start(bf16[128,512]{1,0:T(8,128)(2,1)S(1)} %get-tuple-element.103), channel_id=1, source_target_pairs={{0,1},{1,0},{2,3},{3,2},{4,5},{5,4},{6,7},{7,6},{8,9},{9,8},{10,11... | collective-permute-start | bytes 393224 | tf_op jit(solution)/shard_map/ppermute | solution.py:32
  364.4 6.4 %collective-permute-done.31 = bf16[128,512]{1,0:T(8,128)(2,1)S(1)} collective-permute-done((bf16[128,512]{1,0:T(8,128)(2,1)S(1)}, bf16[128,512]{1,0:T(8,128)(2,1)S(1)}, u32[]{:S(2)}, u32[]{:S(2)}) %collective-permute-start.31) | collective-permute-done | bytes 131104 | tf_op jit(solution)/shard_map/ppermute | solution.py:32
  (195 shorter events, 124.1 us)
Async XLA Ops:
  7.2 85.7 %all-gather.3.cloned.1.call-start = ((), (), s32[]{:S(2)}) async-start(), calls=%async_computation.6 | async-start | bytes 5242880 | tf_op jit(solution)/shard_map/all_gather | solution.py:315
  21.3 18.7 %all-to-all-start = ((bf16[8,64,1024]{2,1,0:T(8,128)(2,1)}), bf16[8,64,1024]{2,1,0:T(8,128)(2,1)S(1)}, u32[]{:S(2)}, u32[]{:S(2)}) async-start(bf16[8,64,1024]{2,1,0:T(8,128)(2,1)} %bitcast.5), calls=%async_computation | async-start | bytes 2097152 | tf_op jit(solution)/shard_map/all_to_all | solution.py:320
  46.5 22.7 %collective-permute-start.2 = (bf16[512,512]{1,0:T(8,128)(2,1)S(1)}, bf16[512,512]{1,0:T(8,128)(2,1)S(1)}, u32[]{:S(2)}, u32[]{:S(2)}) collective-permute-start(bf16[512,512]{1,0:T(8,128)(2,1)S(1)} %attention.1.refs_0_), channel_id=1, source_target_pairs={{0,4},{4,0},{8,12},{12,8},{1,5},{5,1},{9,13},{13,9},{2,6},{6,2},{1... | collective-permute-start | bytes 1572872 | tf_op jit(solution)/shard_map/ppermute | solution.py:32
  92.9 46.6 %all-to-all-start.1 = ((bf16[4,2,128,896]{3,2,1,0:T(8,128)(2,1)}), bf16[4,2,128,896]{3,2,1,0:T(8,128)(2,1)S(1)}, u32[]{:S(2)}, u32[]{:S(2)}) async-start(bf16[4,2,128,896]{3,2,1,0:T(8,128)(2,1)} %copy-done.6), calls=%async_computation.1 | async-start | bytes 3670016 | tf_op jit(solution)/shard_map/all_to_all | solution.py:344
  96.5 107.9 %all-gather.5.cloned.1.call-start = ((), (), s32[]{:S(2)}) async-start(), calls=%async_computation.7 | async-start | bytes 2621440 | tf_op jit(solution)/shard_map/all_gather | solution.py:367
  104.1 14.0 %collective-permute-start.5 = (bf16[256,1024]{1,0:T(8,128)(2,1)}, bf16[256,1024]{1,0:T(8,128)(2,1)S(1)}, u32[]{:S(2)}, u32[]{:S(2)}) collective-permute-start(bf16[256,1024]{1,0:T(8,128)(2,1)} %bitcast.8), channel_id=1, source_target_pairs={{0,16},{16,0},{1,17},{17,1},{2,18},{18,2},{3,19},{19,3},{4,20},{20... | collective-permute-start | bytes 1572872 | tf_op jit(solution)/shard_map/ppermute | solution.py:32
  141.8 52.4 %collective-permute-start.8 = (bf16[4,2,128,896]{3,2,1,0:T(8,128)(2,1)S(1)}, bf16[4,2,128,896]{3,2,1,0:T(8,128)(2,1)}, u32[]{:S(2)}, u32[]{:S(2)}) collective-permute-start(bf16[4,2,128,896]{3,2,1,0:T(8,128)(2,1)S(1)} %all-to-all-done.1.refs_2_), channel_id=1, source_target_pairs={{0,8},{4,12},{8,0},{12,4},{1,9},{5,13},{9,1},{13,5},{2,10},{6,14},... | collective-permute-start | bytes 5505032 | tf_op jit(solution)/shard_map/ppermute | solution.py:32
  143.4 50.8 %all-to-all-start.2 = ((bf16[4,128,896]{2,1,0:T(8,128)(2,1)}), bf16[4,128,896]{2,1,0:T(8,128)(2,1)S(1)}, u32[]{:S(2)}, u32[]{:S(2)}) async-start(bf16[4,128,896]{2,1,0:T(8,128)(2,1)} %copy-done.16), calls=%async_computation.2 | async-start | bytes 1835008 | tf_op jit(solution)/shard_map/all_to_all | solution.py:368
  204.4 32.7 %all-to-all-start.3 = ((bf16[4,128,896]{2,1,0:T(8,128)(2,1)}), bf16[4,128,896]{2,1,0:T(8,128)(2,1)}, u32[]{:S(2)}, u32[]{:S(2)}) async-start(bf16[4,128,896]{2,1,0:T(8,128)(2,1)} %copy-done.15), calls=%async_computation.3 | async-start | bytes 1835008 | tf_op jit(solution)/shard_map/all_to_all | solution.py:371
  210.6 25.5 %collective-permute-start.10 = (bf16[512,1024]{1,0:T(8,128)(2,1)S(1)}, bf16[512,1024]{1,0:T(8,128)(2,1)S(1)}, u32[]{:S(2)}, u32[]{:S(2)}) collective-permute-start(bf16[512,1024]{1,0:T(8,128)(2,1)S(1)} %get-tuple-element.71.refs_0_), channel_id=1, source_target_pairs={{0,16},{16,0},{1,17},{17,1},{2,18},{18,2},{3,19},{19,3},{4,20},{20... | collective-permute-start | bytes 3145736 | tf_op jit(solution)/shard_map/ppermute | solution.py:32
  213.2 22.0 %collective-permute-start.9 = (bf16[4,128,896]{2,1,0:T(8,128)(2,1)S(1)}, bf16[4,128,896]{2,1,0:T(8,128)(2,1)S(1)}, u32[]{:S(2)}, u32[]{:S(2)}) collective-permute-start(bf16[4,128,896]{2,1,0:T(8,128)(2,1)S(1)} %copy-done.4), channel_id=1, source_target_pairs={{0,8},{4,12},{8,0},{12,4},{1,9},{5,13},{9,1},{13,5},{2,10},{6,14},... | collective-permute-start | bytes 2752520 | tf_op jit(solution)/shard_map/ppermute | solution.py:32
  237.1 27.8 %all-to-all-start.4 = ((bf16[4,896,128]{2,1,0:T(8,128)(2,1)}), bf16[4,896,128]{2,1,0:T(8,128)(2,1)}, u32[]{:S(2)}, u32[]{:S(2)}) async-start(bf16[4,896,128]{2,1,0:T(8,128)(2,1)} %copy-done.14), calls=%async_computation.4 | async-start | bytes 1835008 | tf_op jit(solution)/shard_map/all_to_all | solution.py:373
  241.7 23.7 %collective-permute-start.13 = (bf16[512,1024]{1,0:T(8,128)(2,1)S(1)}, bf16[512,1024]{1,0:T(8,128)(2,1)}, u32[]{:S(2)}, u32[]{:S(2)}) collective-permute-start(bf16[512,1024]{1,0:T(8,128)(2,1)S(1)} %get-tuple-element.99.refs_0_), channel_id=1, source_target_pairs={{0,16},{16,0},{1,17},{17,1},{2,18},{18,2},{3,19},{19,3},{4,20},{20... | collective-permute-start | bytes 3145736 | tf_op jit(solution)/shard_map/ppermute | solution.py:32
  242.8 21.1 %collective-permute-start.11 = (bf16[4,128,896]{2,1,0:T(8,128)(2,1)}, bf16[4,128,896]{2,1,0:T(8,128)(2,1)S(1)}, u32[]{:S(2)}, u32[]{:S(2)}) collective-permute-start(bf16[4,128,896]{2,1,0:T(8,128)(2,1)} %all-to-all-done.3.refs_4_), channel_id=1, source_target_pairs={{0,8},{4,12},{8,0},{12,4},{1,9},{5,13},{9,1},{13,5},{2,10},{6,14},... | collective-permute-start | bytes 2752520 | tf_op jit(solution)/shard_map/ppermute | solution.py:32
  278.0 31.3 %all-to-all-start.5 = ((bf16[4,896,128]{2,1,0:T(8,128)(2,1)}), bf16[4,896,128]{2,1,0:T(8,128)(2,1)S(1)}, u32[]{:S(2)}, u32[]{:S(2)}) async-start(bf16[4,896,128]{2,1,0:T(8,128)(2,1)} %copy-done.13), calls=%async_computation.5 | async-start | bytes 1835008 | tf_op jit(solution)/shard_map/all_to_all | solution.py:385
  282.7 25.7 %collective-permute-start.12 = (bf16[4,896,128]{2,1,0:T(8,128)(2,1)}, bf16[4,896,128]{2,1,0:T(8,128)(2,1)S(1)}, u32[]{:S(2)}, u32[]{:S(2)}) collective-permute-start(bf16[4,896,128]{2,1,0:T(8,128)(2,1)} %all-to-all-done.4.weights_ref), channel_id=1, source_target_pairs={{0,8},{4,12},{8,0},{12,4},{1,9},{5,13},{9,1},{13,5},{2,10},{6,14},... | collective-permute-start | bytes 2752520 | tf_op jit(solution)/shard_map/ppermute | solution.py:32
  293.2 14.0 %collective-permute-start.15 = (bf16[512,512]{1,0:T(8,128)(2,1)S(1)}, bf16[512,512]{1,0:T(8,128)(2,1)S(1)}, u32[]{:S(2)}, u32[]{:S(2)}) collective-permute-start(bf16[512,512]{1,0:T(8,128)(2,1)S(1)} %bitcast.97), channel_id=1, source_target_pairs={{0,16},{16,0},{1,17},{17,1},{2,18},{18,2},{3,19},{19,3},{4,20},{20... | collective-permute-start | bytes 1572872 | tf_op jit(solution)/shard_map/ppermute | solution.py:32
  312.6 20.9 %collective-permute-start.23 = (bf16[512,512]{1,0:T(8,128)(2,1)}, bf16[512,512]{1,0:T(8,128)(2,1)}, u32[]{:S(2)}, u32[]{:S(2)}) collective-permute-start(bf16[512,512]{1,0:T(8,128)(2,1)} %bitcast.21), channel_id=1, source_target_pairs={{0,16},{16,0},{1,17},{17,1},{2,18},{18,2},{3,19},{19,3},{4,20},{20... | collective-permute-start | bytes 1572872 | tf_op jit(solution)/shard_map/ppermute | solution.py:32
  314.0 25.3 %collective-permute-start.28 = (bf16[4,896,128]{2,1,0:T(8,128)(2,1)S(1)}, bf16[4,896,128]{2,1,0:T(8,128)(2,1)}, u32[]{:S(2)}, u32[]{:S(2)}) collective-permute-start(bf16[4,896,128]{2,1,0:T(8,128)(2,1)S(1)} %all-to-all-done.5.weights_ref), channel_id=1, source_target_pairs={{0,8},{4,12},{8,0},{12,4},{1,9},{5,13},{9,1},{13,5},{2,10},{6,14},... | collective-permute-start | bytes 2752520 | tf_op jit(solution)/shard_map/ppermute | solution.py:32
  323.8 18.6 %collective-permute-start.19 = (bf16[512,512]{1,0:T(8,128)(2,1)}, bf16[512,512]{1,0:T(8,128)(2,1)}, u32[]{:S(2)}, u32[]{:S(2)}) collective-permute-start(bf16[512,512]{1,0:T(8,128)(2,1)} %bitcast.15), channel_id=1, source_target_pairs={{0,16},{16,0},{1,17},{17,1},{2,18},{18,2},{3,19},{19,3},{4,20},{20... | collective-permute-start | bytes 1572872 | tf_op jit(solution)/shard_map/ppermute | solution.py:32
  343.7 14.8 %collective-permute-start.20 = (bf16[128,512]{1,0:T(8,128)(2,1)S(1)}, bf16[128,512]{1,0:T(8,128)(2,1)S(1)}, u32[]{:S(2)}, u32[]{:S(2)}) collective-permute-start(bf16[128,512]{1,0:T(8,128)(2,1)S(1)} %get-tuple-element.109), channel_id=1, source_target_pairs={{0,1},{1,0},{2,3},{3,2},{4,5},{5,4},{6,7},{7,6},{8,9},{9,8},{10,11... | collective-permute-start | bytes 393224 | tf_op jit(solution)/shard_map/ppermute | solution.py:32
  344.8 16.2 %collective-permute-start.21 = (bf16[128,512]{1,0:T(8,128)(2,1)S(1)}, bf16[128,512]{1,0:T(8,128)(2,1)S(1)}, u32[]{:S(2)}, u32[]{:S(2)}) collective-permute-start(bf16[128,512]{1,0:T(8,128)(2,1)S(1)} %get-tuple-element.111), channel_id=1, source_target_pairs={{0,2},{1,3},{2,0},{3,1},{4,6},{5,7},{6,4},{7,5},{8,10},{9,11},{10,... | collective-permute-start | bytes 393224 | tf_op jit(solution)/shard_map/ppermute | solution.py:32
  349.4 14.9 %collective-permute-start.22 = (bf16[128,512]{1,0:T(8,128)(2,1)S(1)}, bf16[128,512]{1,0:T(8,128)(2,1)S(1)}, u32[]{:S(2)}, u32[]{:S(2)}) collective-permute-start(bf16[128,512]{1,0:T(8,128)(2,1)S(1)} %get-tuple-element.110), channel_id=1, source_target_pairs={{0,3},{1,2},{2,1},{3,0},{4,7},{5,6},{6,5},{7,4},{8,11},{9,10},{10,... | collective-permute-start | bytes 393224 | tf_op jit(solution)/shard_map/ppermute | solution.py:32
  351.8 21.4 %collective-permute-start.27 = (bf16[128,512]{1,0:T(8,128)(2,1)S(1)}, bf16[128,512]{1,0:T(8,128)(2,1)S(1)}, u32[]{:S(2)}, u32[]{:S(2)}) collective-permute-start(bf16[128,512]{1,0:T(8,128)(2,1)S(1)} %fusion.7), channel_id=1, source_target_pairs={{0,8},{4,12},{8,0},{12,4},{1,9},{5,13},{9,1},{13,5},{2,10},{6,14},... | collective-permute-start | bytes 393224 | tf_op jit(solution)/shard_map/ppermute | solution.py:32
  (50 other events, 327.9 us)
Sparse Core Ops, SparseCore 0:
  9.6 83.2 all-gather.2
  141.9 62.4 all-gather.4

commit v10 on v9

--- a/solution.py
+++ b/solution.py
@@ -114,14 +114,14 @@
     )(starts, packed, packed, halo)
 
 
-def cut_kernel(gain_ref, gate_up_ref, down_ref, both_ref, gate_ref, up_ref, *down_refs):
-    rows, cols = gate_ref.shape[1], down_refs[0].shape[2]
+def cut_kernel(gain_ref, gate_up_ref, down_ref, both_ref, gate_ref, up_ref, out_ref):
+    rows, cols = gate_ref.shape[1], out_ref.shape[3]
     for which, second_ref in enumerate((gate_ref, up_ref)):
         scaled = (gate_up_ref[which].astype(jnp.float32) * gain_ref[...]).astype(jnp.bfloat16)
         both_ref[0, which] = scaled[:rows]
         second_ref[0] = scaled[rows:]
-    for part, out_ref in enumerate(down_refs):
-        out_ref[0] = down_ref[:, part * cols : (part + 1) * cols]
+    for part in range(PARTS):
+        out_ref[0, part] = down_ref[:, part * cols : (part + 1) * cols]
 
 
 def cut_weights(w_gate_up, w_down, gain, outer_count):
@@ -131,8 +131,8 @@
     if cols % HEAD_WIDTH:
         wide = (w_gate_up.astype(jnp.float32) * gain[None]).astype(jnp.bfloat16)
         wide = jnp.transpose(wide.reshape(2, PARTS, rows, outer_count, cols), (1, 3, 0, 2, 4))
-        tall = jnp.transpose(w_down.reshape(outer_count, cols, PARTS, rows), (2, 0, 1, 3))
-        return [wide[0], wide[1, :, 0], wide[1, :, 1], *tall]
+        tall = jnp.transpose(w_down.reshape(outer_count, cols, PARTS, rows), (0, 2, 1, 3))
+        return [wide[0], wide[1, :, 0], wide[1, :, 1], tall]
     return pl.pallas_call(
         cut_kernel,
         grid=(outer_count,),
@@ -143,10 +143,10 @@
         ],
         out_specs=[pl.BlockSpec((1, 2, rows, cols), lambda p: (p, 0, 0, 0))]
         + [pl.BlockSpec((1, rows, cols), lambda p: (p, 0, 0))] * 2
-        + [pl.BlockSpec((1, cols, rows), lambda p: (p, 0, 0))] * PARTS,
+        + [pl.BlockSpec((1, PARTS, cols, rows), lambda p: (p, 0, 0, 0))],
         out_shape=[jax.ShapeDtypeStruct((outer_count, 2, rows, cols), jnp.bfloat16)]
         + [jax.ShapeDtypeStruct((outer_count, rows, cols), jnp.bfloat16)] * 2
-        + [jax.ShapeDtypeStruct((outer_count, cols, rows), jnp.bfloat16)] * PARTS,
+        + [jax.ShapeDtypeStruct((outer_count, PARTS, cols, rows), jnp.bfloat16)],
         compiler_params=pltpu.CompilerParams(vmem_limit_bytes=VMEM_LIMIT),
         cost_estimate=BRIEF,
         name="cut_weights",
@@ -262,12 +262,12 @@
 
 
 def down_kernel(activated_ref, weights_ref, kept_ref, sent_ref):
-    sources, _, cols = weights_ref.shape
+    sources, _, _, cols = weights_ref.shape
     kept_rows = kept_ref.shape[0]
     if cols % HEAD_WIDTH:
-        blocks = [weights_ref[s] for s in range(sources)]
+        blocks = [weights_ref[s, 0] for s in range(sources)]
     else:
-        blocks = [jnp.concatenate([weights_ref[s] for s in range(sources)], axis=1)]
+        blocks = [jnp.concatenate([weights_ref[s, 0] for s in range(sources)], axis=1)]
     for e in range(sent_ref.shape[0] + 1):
         rows = activated_ref[e * kept_rows : (e + 1) * kept_rows, :]
         for s, block in enumerate(blocks):
@@ -279,13 +279,21 @@
                 sent_ref[e - 1, :, at] = product.astype(jnp.bfloat16)
 
 
-def down_product(activated, weights, head_count):
+def down_product(activated, weights, part, head_count):
     rows = activated.shape[0] // head_count
-    sources, depth, cols = weights.shape
+    sources, _, depth, cols = weights.shape
+    wide = sources * cols
     return pl.pallas_call(
         down_kernel,
-        in_specs=[VMEM, VMEM],
-        out_specs=[VMEM, VMEM],
+        grid=(1,),
+        in_specs=[
+            pl.BlockSpec(activated.shape, lambda t: (0, 0)),
+            pl.BlockSpec((sources, 1, depth, cols), lambda t: (0, part, 0, 0)),
+        ],
+        out_specs=[
+            pl.BlockSpec((rows, wide), lambda t: (0, 0)),
+            pl.BlockSpec((head_count - 1, rows, wide), lambda t: (0, 0, 0)),
+        ],
         out_shape=[
             jax.ShapeDtypeStruct((rows, sources * cols), jnp.bfloat16),
             jax.ShapeDtypeStruct((head_count - 1, rows, sources * cols), jnp.bfloat16),
@@ -354,8 +362,7 @@
     own_rows = half // 2
     mine = lax.dynamic_slice_in_dim(hidden_part, upper * own_rows, own_rows, 0)
     others = lax.dynamic_slice_in_dim(hidden_part, (1 - upper) * own_rows, own_rows, 0)
-    others, first = fence(over_y(others), first)
-    state = [mine.astype(jnp.float32), others.astype(jnp.float32)]
+    state = [mine.astype(jnp.float32), over_y(others).astype(jnp.float32)]
     squares = sum([jnp.sum(block * block, axis=1) for block in state])
     squares = squares + swap(squares, "inner", 1)
     inverse = lax.rsqrt(squares / D + 1e-05)[:, None]
@@ -365,28 +372,28 @@
     state = [[block[:, :, part].reshape(own_rows, -1) for part in range(PARTS)] for block in state]
 
     tokens = lax.all_gather(normed, "outer", axis=0, tiled=True)
-    second, first_y, tokens, state = fence(spread(after(cut[1], normed)), over_y(first), tokens, state)
+    first = after(first, normed)
+    second, first_y, state = fence(spread(after(cut[1], tokens)), over_y(first), state)
     tokens = jnp.split(tokens, 2, axis=1)
     tokens = [[swap(block, "head", e) if e else block for e in range(head_count)] for block in tokens]
     third, second_y, tokens[0] = fence(spread(after(cut[2], second)), over_y(second), tokens[0])
     own_sums = gate_up(tokens[0], [first, second, third])
-    fourth, third_y, own_sums = fence(spread(after(cut[3], third)), over_y(third), own_sums)
+    fourth = spread(after(cut[3], third))
+    third_y, own_sums = fence(over_y(third), own_sums)
     sums = gate_up(tokens[1], [first_y, second_y, third_y], [own_sums])
     activated = activation(sums, swap(sums, "inner", 1))
 
-    def over_heads(weights):
-        kept, sent = down_product(activated, weights, head_count)
-        paired = kept.astype(jnp.float32)
+    def over_heads(weights, part):
+        kept, sent = down_product(activated, weights, part, head_count)
+        moved = kept.astype(jnp.float32)
         for e in range(1, head_count):
-            paired = paired + swap(sent[e - 1], "head", e).astype(jnp.float32)
-        return paired.reshape(outer_count, own_rows, -1)
-
-    paired = {(0, 0): over_heads(fourth)}
-    fifth, fourth_y, paired[0, 0] = fence(spread(after(cut[4], fourth)), over_y(fourth), paired[0, 0])
-    fifth_y = over_y(fifth)
-    paired[1, 0] = over_heads(fourth_y)
-    paired[0, 1] = over_heads(fifth)
-    paired[1, 1] = over_heads(after(fifth_y, paired[1, 0]))
+            moved = moved + swap(sent[e - 1], "head", e).astype(jnp.float32)
+        return moved.reshape(outer_count, own_rows, -1)
+
+    fourth_y = [over_y(fourth[:, part : part + 1]) for part in range(PARTS)]
+    paired = {(0, part): over_heads(fourth, part) for part in range(PARTS)}
+    for part in range(PARTS):
+        paired[1, part] = over_heads(after(fourth_y[part], paired[0, part]), 0)
 
     pieces = [[None] * PARTS, [None] * PARTS]
     for part in range(PARTS):

time: 386 us -> 464 us (1.20)
  waiting for transfers between devices: 198 us -> 249 us
  blocking collectives: 0 us -> 47.6 us
  starting transfers between devices: 73.5 us -> 61.9 us
  local copies, waits for them, and re-layouts: 43.1 us -> 34.6 us
    all_to_all x1, waiting for transfers between devices: 12.5 us -> 76.1 us  [per_device(): first = spread(after(cut[0], weights_out))]
    all_to_all x0 -> x1, blocking collectives: none -> 47.6 us  [per_device(): fourth = spread(after(cut[3], third))]
    all_to_all x3 -> x1, waiting for transfers between devices: 39.5 us -> 0.01 us  [per_device(): spread(after(cut[1], tokens))]
    ppermute x32, waiting for transfers between devices: 97.9 us -> 126 us  [swap(): return lax.ppermute(array, axis, [(s, s ^ distance) for s in range(count)])]
    all_gather x1, waiting for transfers between devices: 10.2 us -> 0.01 us  [per_device(): tokens = lax.all_gather(normed, 'outer', axis=0, tiled=True)]
    all_to_all x3 -> x1, starting transfers between devices: 12.8 us -> 3.5 us  [per_device(): spread(after(cut[1], tokens))]
    all_gather x1, waiting for transfers between devices: 22.9 us -> 31.4 us  [per_device(): weights_out = lax.all_gather(w_out, 'outer', axis=1, tiled=True)]
    unnamed x68 -> x56, local copies, waits for them, and re-layouts: 24.2 us -> 16.8 us
  transfers between devices with their start and end apart: 42 -> 40, of which waited for: 20 -> 19; matrix products, arithmetic and copies ran while one was open for 7% -> 6% of each run, Pallas kernels for 9% -> 6%
where the time goes in v10:
time: 464 us; the launch traced here: 463 us
  waiting for transfers between devices  249 us (54%)
  starting transfers between devices  61.9 us (13%)
  blocking collectives  47.6 us (10%)
  Pallas kernels  45.4 us (10%)
  local copies, waits for them, and re-layouts  34.6 us (7%)
  between operations  14.6 us (3%)
  other arithmetic  10.4 us (2%)
    ppermute x32, waiting for transfers between devices, swap(): return lax.ppermute(array, axis, [(s, s ^ distance) for s in range(count)])  126 us
    all_to_all x1, waiting for transfers between devices, per_device(): first = spread(after(cut[0], weights_out))  76.1 us
    all_to_all x1, blocking collectives, per_device(): fourth = spread(after(cut[3], third))  47.6 us
    ppermute x32, starting transfers between devices, swap(): return lax.ppermute(array, axis, [(s, s ^ distance) for s in range(count)])  38.2 us
    all_gather x1, waiting for transfers between devices, per_device(): weights_out = lax.all_gather(w_out, 'outer', axis=1, tiled=True)  31.4 us
    pallas_call x2, Pallas kernels, gate_up(): pl.pallas_call(functools.partial(gate_up_kernel, len(tokens)), in_specs=[...  17.1 us
    unnamed x56, local copies, waits for them, and re-layouts  16.8 us
    all_to_all x1, waiting for transfers between devices, per_device(): lax.all_to_all(groups, ('inner', 'head'), split_axis=0, concat_axis=0, ti...  14.4 us
  transfers between devices with their start and end apart: 40, of which 19 were waited for; matrix products, arithmetic and copies ran while one was open for 6% of the time, Pallas kernels for 6%

profile of v10, /device:TPU:0, one launch (start us, length us, event | category | flops | bytes accessed | tf_op | source)
XLA Modules:
  0.0 463.1 jit_solution(8816029530301617172)
XLA Ops:
  7.9 4.9 %collective-permute-start = (bf16[64,1024]{1,0:T(8,128)(2,1)}, bf16[64,1024]{1,0:T(8,128)(2,1)S(1)}, u32[]{:S(2)}, u32[]{:S(2)}) collective-permute-start(bf16[64,1024]{1,0:T(8,128)(2,1)} %param.10), channel_id=1, source_target_pairs={{0,1},{1,2},{2,3},{4,5},{5,6},{6,7},{8,9},{9,10},{10,11},{12,13},{... | collective-permute-start | bytes 393224 | tf_op jit(solution)/shard_map/ppermute | solution.py:325
  21.3 3.7 all-to-all-start
  25.6 14.4 %all-to-all-done = bf16[8,64,1024]{2,1,0:T(8,128)(2,1)S(1)} async-done(((bf16[8,64,1024]{2,1,0:T(8,128)(2,1)}), bf16[8,64,1024]{2,1,0:T(8,128)(2,1)S(1)}, u32[]{:S(2)}, u32[]{:S(2)}) %all-to-all-start) | async-done | bytes 1048608 | tf_op jit(solution)/shard_map/all_to_all | solution.py:328
  40.0 5.9 %attention.1.refs_0_ = bf16[512,512]{1,0:T(8,128)(2,1)S(1)} custom-call(s32[512,1]{1,0:T(8,128)S(1)} %copy.27.starts_ref, bf16[512,1024]{1,0:T(8,128)(2,1)S(1)} %bitcast.93, bf16[512,1024]{1,0:T(8,128)(2,1)S(1)} %bitcast.94, bf16[512,1024]{1,0:T(8,128)(2,1)S(1)} %bitcast.95), custom_call_target="tpu_custom_call" | custom-call | flops 1 | bytes 1 | tf_op jit(solution)/shard_map/attention/pallas_call | solution.py:96
  46.9 12.6 %collective-permute-done.3.refs_2_ = bf16[512,512]{1,0:T(8,128)(2,1)S(1)} collective-permute-done((bf16[512,512]{1,0:T(8,128)(2,1)S(1)}, bf16[512,512]{1,0:T(8,128)(2,1)S(1)}, u32[]{:S(2)}, u32[]{:S(2)}) %collective-permute-start.3) | collective-permute-done | bytes 524320 | tf_op jit(solution)/shard_map/ppermute | solution.py:32
  61.4 31.4 %all-gather.3.cloned.1.call-done.refs_4_ = bf16[2048,1024]{1,0:T(8,128)(2,1)} async-done(((bf16[2048,256]{1,0:T(8,128)(2,1)}), bf16[2048,1024]{1,0:T(8,128)(2,1)}) %all-gather.3.cloned.1.call-update) | async-done | bytes 4194320 | tf_op jit(solution)/shard_map/all_gather | solution.py:323
  92.9 5.3 %projection.1 = (bf16[256,1024]{1,0:T(8,128)(2,1)S(1)}, bf16[1,256,1024]{2,1,0:T(8,128)(2,1)S(1)}, bf16[128,2048]{1,0:T(8,128)(2,1)}) custom-call(s32[2]{0:T(128)S(1)} %pad_add_fusion.place_ref, bf16[512,512]{1,0:T(8,128)(2,1)S(1)} %attention.1.refs_0_, bf16[512,512]{1,0:T(8,128)(2,1)S(1)} %collective-permute-done.2.refs_1_, ...), custom_call_target="tpu_custom_call" | custom-call | flops 1 | bytes 1 | tf_op jit(solution)/shard_map/projection/pallas_call | solution.py:185
  99.6 12.3 %collective-permute-done.5 = bf16[256,1024]{1,0:T(8,128)(2,1)S(1)} collective-permute-done((bf16[256,1024]{1,0:T(8,128)(2,1)S(1)}, bf16[256,1024]{1,0:T(8,128)(2,1)S(1)}, u32[]{:S(2)}, u32[]{:S(2)}) %collective-permute-start.5) | collective-permute-done | bytes 524320 | tf_op jit(solution)/shard_map/ppermute | solution.py:32
  115.9 4.9 %collective-permute-done.6 = bf16[128,1024]{1,0:T(8,128)(2,1)S(1)} collective-permute-done((bf16[128,1024]{1,0:T(8,128)(2,1)S(1)}, bf16[128,1024]{1,0:T(8,128)(2,1)S(1)}, u32[]{:S(2)}, u32[]{:S(2)}) %collective-permute-start.6) | collective-permute-done | bytes 262176 | tf_op jit(solution)/shard_map/ppermute | solution.py:32
  121.1 3.7 cut_weights.1
  129.2 3.6 all-to-all-start.2
  133.9 76.1 %all-to-all-done.2.refs_2_ = bf16[4,2,128,896]{3,2,1,0:T(8,128)(2,1)S(1)} async-done(((bf16[4,2,128,896]{3,2,1,0:T(8,128)(2,1)}), bf16[4,2,128,896]{3,2,1,0:T(8,128)(2,1)S(1)}, u32[]{:S(2)}, u32[]{:S(2)}) %all-to-all-start.2) | async-done | bytes 1835040 | tf_op jit(solution)/shard_map/all_to_all | solution.py:352
  222.8 29.0 %collective-permute-done.8.refs_2_ = bf16[4,2,128,896]{3,2,1,0:T(8,128)(2,1)} collective-permute-done((bf16[4,2,128,896]{3,2,1,0:T(8,128)(2,1)S(1)}, bf16[4,2,128,896]{3,2,1,0:T(8,128)(2,1)}, u32[]{:S(2)}, u32[]{:S(2)}) %collective-permute-start.8) | collective-permute-done | bytes 1835040 | tf_op jit(solution)/shard_map/ppermute | solution.py:32
  252.8 4.4 all-to-all-start.3
  263.7 21.5 %collective-permute-done.11.refs_1_ = bf16[512,1024]{1,0:T(8,128)(2,1)S(1)} collective-permute-done((bf16[512,1024]{1,0:T(8,128)(2,1)S(1)}, bf16[512,1024]{1,0:T(8,128)(2,1)S(1)}, u32[]{:S(2)}, u32[]{:S(2)}) %collective-permute-start.11) | collective-permute-done | bytes 1048608 | tf_op jit(solution)/shard_map/ppermute | solution.py:32
  292.3 7.0 %gate_up.2.refs_5_ = bf16[2,1024,896]{2,1,0:T(8,128)(2,1)} custom-call(bf16[512,1024]{1,0:T(8,128)(2,1)S(1)} %copy-done.2, bf16[512,1024]{1,0:T(8,128)(2,1)S(1)} %copy-done.10, bf16[4,2,128,896]{3,2,1,0:T(8,128)(2,1)S(1)} %all-to-all-done.2.refs_2_, bf16[4,128,896]{2,1,0:T(8,128)(2,1)S(1)} %copy-done.5, bf16[4,128,896]{2,1,0:T(8,128)(2,1)} %all-to-all-done.3.refs_4_), custom_call_target="tpu_custom_call" | custom-call | flops 1 | bytes 1 | tf_op jit(solution)/shard_map/gate_up/pallas_call | solution.py:226
  299.3 6.1 %collective-permute-done.12.refs_4_ = bf16[4,128,896]{2,1,0:T(8,128)(2,1)S(1)} collective-permute-done((bf16[4,128,896]{2,1,0:T(8,128)(2,1)}, bf16[4,128,896]{2,1,0:T(8,128)(2,1)S(1)}, u32[]{:S(2)}, u32[]{:S(2)}) %collective-permute-start.12) | collective-permute-done | bytes 917536 | tf_op jit(solution)/shard_map/ppermute | solution.py:32
  305.6 10.1 %gate_up.3.here_ref = bf16[2,1024,896]{2,1,0:T(8,128)(2,1)} custom-call(bf16[512,1024]{1,0:T(8,128)(2,1)S(1)} %get-tuple-element.85.refs_0_, bf16[512,1024]{1,0:T(8,128)(2,1)} %collective-permute-done.9.refs_1_, bf16[4,2,128,896]{3,2,1,0:T(8,128)(2,1)} %collective-permute-done.8.refs_2_, bf16[4,128,896]{2,1,0:T(8,128)(2,1)S(1)} %copy-done.12, ...), custom_call_target="tpu_custom_call" | custom-call | flops 1 | bytes 1 | tf_op jit(solution)/shard_map/gate_up/pallas_call | solution.py:226
  315.8 47.6 %all_to_all.25.weights_ref = bf16[4,2,896,128]{3,2,1,0:T(8,128)(2,1)S(1)} all-to-all(bf16[4,2,896,128]{3,2,1,0:T(8,128)(2,1)S(1)} %copy-done.7), channel_id=1, replica_groups=mesh['head'=2,'inner'=4,'outer'=4] {'outer'}, dimensions={0} | all-to-all | bytes 3670016 | tf_op jit(solution)/shard_map/all_to_all | solution.py:381
  368.2 3.9 activation.1.activated_ref
  379.7 9.7 %collective-permute-done.14 = bf16[512,512]{1,0:T(8,128)(2,1)} collective-permute-done((bf16[512,512]{1,0:T(8,128)(2,1)}, bf16[512,512]{1,0:T(8,128)(2,1)}, u32[]{:S(2)}, u32[]{:S(2)}) %collective-permute-start.14) | collective-permute-done | bytes 524320 | tf_op jit(solution)/shard_map/ppermute | solution.py:32
  416.1 6.5 %collective-permute-done.20 = bf16[128,512]{1,0:T(8,128)(2,1)S(1)} collective-permute-done((bf16[128,512]{1,0:T(8,128)(2,1)}, bf16[128,512]{1,0:T(8,128)(2,1)S(1)}, u32[]{:S(2)}, u32[]{:S(2)}) %collective-permute-start.20) | collective-permute-done | bytes 131104 | tf_op jit(solution)/shard_map/ppermute | solution.py:32
  435.4 4.8 %collective-permute-done.25 = bf16[128,512]{1,0:T(8,128)(2,1)S(1)} collective-permute-done((bf16[128,512]{1,0:T(8,128)(2,1)S(1)}, bf16[128,512]{1,0:T(8,128)(2,1)S(1)}, u32[]{:S(2)}, u32[]{:S(2)}) %collective-permute-start.25) | collective-permute-done | bytes 131104 | tf_op jit(solution)/shard_map/ppermute | solution.py:32
  441.8 7.6 %collective-permute-done.31 = bf16[128,512]{1,0:T(8,128)(2,1)S(1)} collective-permute-done((bf16[128,512]{1,0:T(8,128)(2,1)S(1)}, bf16[128,512]{1,0:T(8,128)(2,1)S(1)}, u32[]{:S(2)}, u32[]{:S(2)}) %collective-permute-start.31) | collective-permute-done | bytes 131104 | tf_op jit(solution)/shard_map/ppermute | solution.py:32
  (181 shorter events, 111.3 us)
Async XLA Ops:
  7.2 85.7 %all-gather.3.cloned.1.call-start = ((), (), s32[]{:S(2)}) async-start(), calls=%async_computation.5 | async-start | bytes 5242880 | tf_op jit(solution)/shard_map/all_gather | solution.py:323
  21.3 18.7 %all-to-all-start = ((bf16[8,64,1024]{2,1,0:T(8,128)(2,1)}), bf16[8,64,1024]{2,1,0:T(8,128)(2,1)S(1)}, u32[]{:S(2)}, u32[]{:S(2)}) async-start(bf16[8,64,1024]{2,1,0:T(8,128)(2,1)} %bitcast.5), calls=%async_computation | async-start | bytes 2097152 | tf_op jit(solution)/shard_map/all_to_all | solution.py:328
  45.8 13.7 %collective-permute-start.3 = (bf16[512,512]{1,0:T(8,128)(2,1)S(1)}, bf16[512,512]{1,0:T(8,128)(2,1)S(1)}, u32[]{:S(2)}, u32[]{:S(2)}) collective-permute-start(bf16[512,512]{1,0:T(8,128)(2,1)S(1)} %attention.1.refs_0_), channel_id=1, source_target_pairs={{0,8},{4,12},{8,0},{12,4},{1,9},{5,13},{9,1},{13,5},{2,10},{6,14},... | collective-permute-start | bytes 1572872 | tf_op jit(solution)/shard_map/ppermute | solution.py:32
  98.2 13.8 %collective-permute-start.5 = (bf16[256,1024]{1,0:T(8,128)(2,1)S(1)}, bf16[256,1024]{1,0:T(8,128)(2,1)S(1)}, u32[]{:S(2)}, u32[]{:S(2)}) collective-permute-start(bf16[256,1024]{1,0:T(8,128)(2,1)S(1)} %bitcast.96), channel_id=1, source_target_pairs={{0,16},{16,0},{1,17},{17,1},{2,18},{18,2},{3,19},{19,3},{4,20},{20... | collective-permute-start | bytes 1572872 | tf_op jit(solution)/shard_map/ppermute | solution.py:32
  129.2 80.8 %all-to-all-start.2 = ((bf16[4,2,128,896]{3,2,1,0:T(8,128)(2,1)}), bf16[4,2,128,896]{3,2,1,0:T(8,128)(2,1)S(1)}, u32[]{:S(2)}, u32[]{:S(2)}) async-start(bf16[4,2,128,896]{3,2,1,0:T(8,128)(2,1)} %copy-done.8), calls=%async_computation.2 | async-start | bytes 3670016 | tf_op jit(solution)/shard_map/all_to_all | solution.py:352
  132.8 78.9 %all-gather.5.cloned.1.call-start = ((), (), s32[]{:S(2)}) async-start(), calls=%async_computation.6 | async-start | bytes 2621440 | tf_op jit(solution)/shard_map/all_gather | solution.py:374
  210.0 41.8 %collective-permute-start.8 = (bf16[4,2,128,896]{3,2,1,0:T(8,128)(2,1)S(1)}, bf16[4,2,128,896]{3,2,1,0:T(8,128)(2,1)}, u32[]{:S(2)}, u32[]{:S(2)}) collective-permute-start(bf16[4,2,128,896]{3,2,1,0:T(8,128)(2,1)S(1)} %all-to-all-done.2.refs_2_), channel_id=1, source_target_pairs={{0,8},{4,12},{8,0},{12,4},{1,9},{5,13},{9,1},{13,5},{2,10},{6,14},... | collective-permute-start | bytes 5505032 | tf_op jit(solution)/shard_map/ppermute | solution.py:32
  211.7 40.2 %all-to-all-start.1 = ((bf16[4,128,896]{2,1,0:T(8,128)(2,1)}), bf16[4,128,896]{2,1,0:T(8,128)(2,1)S(1)}, u32[]{:S(2)}, u32[]{:S(2)}) async-start(bf16[4,128,896]{2,1,0:T(8,128)(2,1)} %copy-done.14), calls=%async_computation.1 | async-start | bytes 1835008 | tf_op jit(solution)/shard_map/all_to_all | solution.py:376
  252.8 34.4 %all-to-all-start.3 = ((bf16[4,128,896]{2,1,0:T(8,128)(2,1)}), bf16[4,128,896]{2,1,0:T(8,128)(2,1)}, u32[]{:S(2)}, u32[]{:S(2)}) async-start(bf16[4,128,896]{2,1,0:T(8,128)(2,1)} %copy-done.13), calls=%async_computation.3 | async-start | bytes 1835008 | tf_op jit(solution)/shard_map/all_to_all | solution.py:379
  259.0 26.2 %collective-permute-start.11 = (bf16[512,1024]{1,0:T(8,128)(2,1)S(1)}, bf16[512,1024]{1,0:T(8,128)(2,1)S(1)}, u32[]{:S(2)}, u32[]{:S(2)}) collective-permute-start(bf16[512,1024]{1,0:T(8,128)(2,1)S(1)} %get-tuple-element.61.refs_0_), channel_id=1, source_target_pairs={{0,16},{16,0},{1,17},{17,1},{2,18},{18,2},{3,19},{19,3},{4,20},{20... | collective-permute-start | bytes 3145736 | tf_op jit(solution)/shard_map/ppermute | solution.py:32
  261.7 24.5 %collective-permute-start.10 = (bf16[4,128,896]{2,1,0:T(8,128)(2,1)S(1)}, bf16[4,128,896]{2,1,0:T(8,128)(2,1)S(1)}, u32[]{:S(2)}, u32[]{:S(2)}) collective-permute-start(bf16[4,128,896]{2,1,0:T(8,128)(2,1)S(1)} %copy-done.4), channel_id=1, source_target_pairs={{0,8},{4,12},{8,0},{12,4},{1,9},{5,13},{9,1},{13,5},{2,10},{6,14},... | collective-permute-start | bytes 2752520 | tf_op jit(solution)/shard_map/ppermute | solution.py:32
  263.1 42.4 %collective-permute-start.9 = (bf16[512,1024]{1,0:T(8,128)(2,1)S(1)}, bf16[512,1024]{1,0:T(8,128)(2,1)}, u32[]{:S(2)}, u32[]{:S(2)}) collective-permute-start(bf16[512,1024]{1,0:T(8,128)(2,1)S(1)} %get-tuple-element.85.refs_0_), channel_id=1, source_target_pairs={{0,16},{16,0},{1,17},{17,1},{2,18},{18,2},{3,19},{19,3},{4,20},{20... | collective-permute-start | bytes 3145736 | tf_op jit(solution)/shard_map/ppermute | solution.py:32
  287.1 18.3 %collective-permute-start.12 = (bf16[4,128,896]{2,1,0:T(8,128)(2,1)}, bf16[4,128,896]{2,1,0:T(8,128)(2,1)S(1)}, u32[]{:S(2)}, u32[]{:S(2)}) collective-permute-start(bf16[4,128,896]{2,1,0:T(8,128)(2,1)} %all-to-all-done.3.refs_4_), channel_id=1, source_target_pairs={{0,8},{4,12},{8,0},{12,4},{1,9},{5,13},{9,1},{13,5},{2,10},{6,14},... | collective-permute-start | bytes 2752520 | tf_op jit(solution)/shard_map/ppermute | solution.py:32
  315.7 50.7 %collective-permute-start.13 = (bf16[2,1024,896]{2,1,0:T(8,128)(2,1)}, bf16[2,1024,896]{2,1,0:T(8,128)(2,1)S(1)}, u32[]{:S(2)}, u32[]{:S(2)}) collective-permute-start(bf16[2,1024,896]{2,1,0:T(8,128)(2,1)} %gate_up.3.here_ref), channel_id=1, source_target_pairs={{0,4},{4,0},{8,12},{12,8},{1,5},{5,1},{9,13},{13,9},{2,6},{6,2},{1... | collective-permute-start | bytes 11010056 | tf_op jit(solution)/shard_map/ppermute | solution.py:32
  364.8 25.8 %collective-permute-start.22 = (bf16[4,1,896,128]{3,2,1,0:T(8,128)(2,1)}, bf16[4,1,896,128]{3,2,1,0:T(8,128)(2,1)}, u32[]{:S(2)}, u32[]{:S(2)}) collective-permute-start(bf16[4,1,896,128]{3,2,1,0:T(8,128)(2,1)} %get-tuple-element.86), channel_id=1, source_target_pairs={{0,8},{4,12},{8,0},{12,4},{1,9},{5,13},{9,1},{13,5},{2,10},{6,14},... | collective-permute-start | bytes 2752520 | tf_op jit(solution)/shard_map/ppermute | solution.py:32
  374.2 15.2 %collective-permute-start.14 = (bf16[512,512]{1,0:T(8,128)(2,1)}, bf16[512,512]{1,0:T(8,128)(2,1)}, u32[]{:S(2)}, u32[]{:S(2)}) collective-permute-start(bf16[512,512]{1,0:T(8,128)(2,1)} %bitcast.9), channel_id=1, source_target_pairs={{0,16},{16,0},{1,17},{17,1},{2,18},{18,2},{3,19},{19,3},{4,20},{20... | collective-permute-start | bytes 1572872 | tf_op jit(solution)/shard_map/ppermute | solution.py:32
  378.6 22.0 %collective-permute-start.18 = (bf16[512,512]{1,0:T(8,128)(2,1)}, bf16[512,512]{1,0:T(8,128)(2,1)}, u32[]{:S(2)}, u32[]{:S(2)}) collective-permute-start(bf16[512,512]{1,0:T(8,128)(2,1)} %bitcast.15), channel_id=1, source_target_pairs={{0,16},{16,0},{1,17},{17,1},{2,18},{18,2},{3,19},{19,3},{4,20},{20... | collective-permute-start | bytes 1572872 | tf_op jit(solution)/shard_map/ppermute | solution.py:32
  379.2 27.2 %collective-permute-start.28 = (bf16[4,1,896,128]{3,2,1,0:T(8,128)(2,1)}, bf16[4,1,896,128]{3,2,1,0:T(8,128)(2,1)S(1)}, u32[]{:S(2)}, u32[]{:S(2)}) collective-permute-start(bf16[4,1,896,128]{3,2,1,0:T(8,128)(2,1)} %get-tuple-element.87), channel_id=1, source_target_pairs={{0,8},{4,12},{8,0},{12,4},{1,9},{5,13},{9,1},{13,5},{2,10},{6,14},... | collective-permute-start | bytes 2752520 | tf_op jit(solution)/shard_map/ppermute | solution.py:32
  393.9 29.9 %collective-permute-start.23 = (bf16[512,512]{1,0:T(8,128)(2,1)}, bf16[512,512]{1,0:T(8,128)(2,1)}, u32[]{:S(2)}, u32[]{:S(2)}) collective-permute-start(bf16[512,512]{1,0:T(8,128)(2,1)} %bitcast.21), channel_id=1, source_target_pairs={{0,16},{16,0},{1,17},{17,1},{2,18},{18,2},{3,19},{19,3},{4,20},{20... | collective-permute-start | bytes 1572872 | tf_op jit(solution)/shard_map/ppermute | solution.py:32
  395.4 15.3 %collective-permute-start.15 = (bf16[128,512]{1,0:T(8,128)(2,1)S(1)}, bf16[128,512]{1,0:T(8,128)(2,1)S(1)}, u32[]{:S(2)}, u32[]{:S(2)}) collective-permute-start(bf16[128,512]{1,0:T(8,128)(2,1)S(1)} %get-tuple-element.94), channel_id=1, source_target_pairs={{0,1},{1,0},{2,3},{3,2},{4,5},{5,4},{6,7},{7,6},{8,9},{9,8},{10,11... | collective-permute-start | bytes 393224 | tf_op jit(solution)/shard_map/ppermute | solution.py:32
  395.7 15.0 %collective-permute-start.16 = (bf16[128,512]{1,0:T(8,128)(2,1)S(1)}, bf16[128,512]{1,0:T(8,128)(2,1)S(1)}, u32[]{:S(2)}, u32[]{:S(2)}) collective-permute-start(bf16[128,512]{1,0:T(8,128)(2,1)S(1)} %get-tuple-element.96), channel_id=1, source_target_pairs={{0,2},{1,3},{2,0},{3,1},{4,6},{5,7},{6,4},{7,5},{8,10},{9,11},{10,... | collective-permute-start | bytes 393224 | tf_op jit(solution)/shard_map/ppermute | solution.py:32
  409.2 20.5 %collective-permute-start.29 = (bf16[512,512]{1,0:T(8,128)(2,1)}, bf16[512,512]{1,0:T(8,128)(2,1)}, u32[]{:S(2)}, u32[]{:S(2)}) collective-permute-start(bf16[512,512]{1,0:T(8,128)(2,1)} %bitcast.27), channel_id=1, source_target_pairs={{0,16},{16,0},{1,17},{17,1},{2,18},{18,2},{3,19},{19,3},{4,20},{20... | collective-permute-start | bytes 1572872 | tf_op jit(solution)/shard_map/ppermute | solution.py:32
  432.0 17.4 %collective-permute-start.31 = (bf16[128,512]{1,0:T(8,128)(2,1)S(1)}, bf16[128,512]{1,0:T(8,128)(2,1)S(1)}, u32[]{:S(2)}, u32[]{:S(2)}) collective-permute-start(bf16[128,512]{1,0:T(8,128)(2,1)S(1)} %get-tuple-element.93), channel_id=1, source_target_pairs={{0,2},{1,3},{2,0},{3,1},{4,6},{5,7},{6,4},{7,5},{8,10},{9,11},{10,... | collective-permute-start | bytes 393224 | tf_op jit(solution)/shard_map/ppermute | solution.py:32
  433.2 16.3 %collective-permute-start.32 = (bf16[128,512]{1,0:T(8,128)(2,1)S(1)}, bf16[128,512]{1,0:T(8,128)(2,1)S(1)}, u32[]{:S(2)}, u32[]{:S(2)}) collective-permute-start(bf16[128,512]{1,0:T(8,128)(2,1)S(1)} %get-tuple-element.92), channel_id=1, source_target_pairs={{0,3},{1,2},{2,1},{3,0},{4,7},{5,6},{6,5},{7,4},{8,11},{9,10},{10,... | collective-permute-start | bytes 393224 | tf_op jit(solution)/shard_map/ppermute | solution.py:32
  (42 other events, 275.1 us)
Sparse Core Ops, SparseCore 0:
  9.6 83.2 all-gather.2
  135.8 74.0 all-gather.4

commit v11 on v9

--- a/solution.py
+++ b/solution.py
@@ -193,18 +193,15 @@
     )(place, *blocks, weights)
 
 
-def gate_up_kernel(head_count, *refs):
-    tokens = refs[:head_count]
-    both, gate, up = refs[head_count : head_count + 3]
-    *earlier, out_ref, held, near, token_sems, weight_sems = refs[head_count + 3 :]
-    rows, depth = tokens[0].shape
+def gate_up_kernel(tokens, both, gate, up, *refs):
+    *earlier, out_ref, held, near, token_sem, weight_sems = refs
+    depth = held.shape[1]
     copies = [
         [pltpu.make_async_copy(both.at[:, which], near.at[which, :, 0], weight_sems.at[which, 0]),
          pltpu.make_async_copy(second, near.at[which, :, 1], weight_sems.at[which, 1])]
         for which, second in enumerate((gate, up))
     ]
-    for e, token_ref in enumerate(tokens):
-        copies[0].append(pltpu.make_async_copy(token_ref, held.at[pl.ds(e * rows, rows)], token_sems.at[e]))
+    copies[0].append(pltpu.make_async_copy(tokens, held, token_sem))
     for group in copies:
         for copy in group:
             copy.start()
@@ -220,24 +217,23 @@
 
 
 def gate_up(tokens, streams, earlier=()):
-    rows, depth = tokens[0].shape
+    rows, depth = tokens.shape
     sources, stream_rows, cols = streams[1].shape
-    all_rows = rows * len(tokens)
-    return pl.pallas_call(
-        functools.partial(gate_up_kernel, len(tokens)),
-        in_specs=[ANY] * (len(tokens) + len(streams)) + [VMEM] * len(earlier),
+    return pl.pallas_call(
+        gate_up_kernel,
+        in_specs=[ANY] * (1 + len(streams)) + [VMEM] * len(earlier),
         out_specs=VMEM,
-        out_shape=jax.ShapeDtypeStruct((2, all_rows, cols), jnp.bfloat16),
+        out_shape=jax.ShapeDtypeStruct((2, rows, cols), jnp.bfloat16),
         scratch_shapes=[
-            pltpu.VMEM((all_rows, depth), jnp.bfloat16),
+            pltpu.VMEM((rows, depth), jnp.bfloat16),
             pltpu.VMEM((2, sources, PARTS, stream_rows, cols), jnp.bfloat16),
-            pltpu.SemaphoreType.DMA((len(tokens),)),
+            pltpu.SemaphoreType.DMA,
             pltpu.SemaphoreType.DMA((2, PARTS)),
         ],
         compiler_params=pltpu.CompilerParams(vmem_limit_bytes=VMEM_LIMIT),
         cost_estimate=BRIEF,
         name="gate_up",
-    )(*tokens, *streams, *earlier)
+    )(tokens, *streams, *earlier)
 
 
 def activation_kernel(here_ref, there_ref, out_ref):
@@ -261,35 +257,24 @@
     )(here, there)
 
 
-def down_kernel(activated_ref, weights_ref, kept_ref, sent_ref):
+def down_kernel(activated_ref, weights_ref, out_ref):
     sources, _, cols = weights_ref.shape
-    kept_rows = kept_ref.shape[0]
     if cols % HEAD_WIDTH:
         blocks = [weights_ref[s] for s in range(sources)]
     else:
         blocks = [jnp.concatenate([weights_ref[s] for s in range(sources)], axis=1)]
-    for e in range(sent_ref.shape[0] + 1):
-        rows = activated_ref[e * kept_rows : (e + 1) * kept_rows, :]
-        for s, block in enumerate(blocks):
-            at = slice(s * block.shape[1], (s + 1) * block.shape[1])
-            product = jnp.dot(rows, block, preferred_element_type=jnp.float32)
-            if e == 0:
-                kept_ref[:, at] = product.astype(jnp.bfloat16)
-            else:
-                sent_ref[e - 1, :, at] = product.astype(jnp.bfloat16)
-
-
-def down_product(activated, weights, head_count):
-    rows = activated.shape[0] // head_count
-    sources, depth, cols = weights.shape
+    for s, block in enumerate(blocks):
+        product = jnp.dot(activated_ref[...], block, preferred_element_type=jnp.float32)
+        out_ref[:, s * block.shape[1] : (s + 1) * block.shape[1]] = product.astype(jnp.bfloat16)
+
+
+def down_product(activated, weights):
+    sources, _, cols = weights.shape
     return pl.pallas_call(
         down_kernel,
         in_specs=[VMEM, VMEM],
-        out_specs=[VMEM, VMEM],
-        out_shape=[
-            jax.ShapeDtypeStruct((rows, sources * cols), jnp.bfloat16),
-            jax.ShapeDtypeStruct((head_count - 1, rows, sources * cols), jnp.bfloat16),
-        ],
+        out_specs=VMEM,
+        out_shape=jax.ShapeDtypeStruct((activated.shape[0], sources * cols), jnp.bfloat16),
         compiler_params=pltpu.CompilerParams(vmem_limit_bytes=VMEM_LIMIT),
         cost_estimate=BRIEF,
         name="down",
@@ -369,17 +354,22 @@
     tokens = jnp.split(tokens, 2, axis=1)
     tokens = [[swap(block, "head", e) if e else block for e in range(head_count)] for block in tokens]
     third, second_y, tokens[0] = fence(spread(after(cut[2], second)), over_y(second), tokens[0])
-    own_sums = gate_up(tokens[0], [first, second, third])
+    own_sums = [gate_up(rows_of, [first, second, third]) for rows_of in tokens[0]]
     fourth, third_y, own_sums = fence(spread(after(cut[3], third)), over_y(third), own_sums)
-    sums = gate_up(tokens[1], [first_y, second_y, third_y], [own_sums])
-    activated = activation(sums, swap(sums, "inner", 1))
+    streams = [first_y, second_y, third_y]
+    activated, earlier = {}, first_y
+    for e in [*range(1, head_count), 0]:
+        sums = gate_up(tokens[1][e], streams, [after(own_sums[e], earlier)])
+        activated[e] = activation(sums, swap(sums, "inner", 1))
+        earlier = sums
 
     def over_heads(weights):
-        kept, sent = down_product(activated, weights, head_count)
-        paired = kept.astype(jnp.float32)
-        for e in range(1, head_count):
-            paired = paired + swap(sent[e - 1], "head", e).astype(jnp.float32)
-        return paired.reshape(outer_count, own_rows, -1)
+        sent = [down_product(activated[e], weights) for e in range(1, head_count)]
+        moved = [swap(rows_of, "head", e) for e, rows_of in enumerate(sent, 1)]
+        total = down_product(after(activated[0], sent[-1]), weights).astype(jnp.float32)
+        for rows_of in moved:
+            total = total + rows_of.astype(jnp.float32)
+        return total.reshape(outer_count, own_rows, -1)
 
     paired = {(0, 0): over_heads(fourth)}
     fifth, fourth_y, paired[0, 0] = fence(spread(after(cut[4], fourth)), over_y(fourth), paired[0, 0])

time: 386 us -> 387 us (level)
  Pallas kernels: 45 us -> 52.4 us
  local copies, waits for them, and re-layouts: 43.1 us -> 36.9 us
    unnamed x68 -> x56, local copies, waits for them, and re-layouts: 24.2 us -> 17 us
    ppermute x32 -> x33, waiting for transfers between devices: 97.9 us -> 92.2 us  [swap(): return lax.ppermute(array, axis, [(s, s ^ distance) for s in range(count)])]
    pallas_call x6 -> x12, Pallas kernels: 26.1 us -> 31.5 us  [the longest x4 19.6 us: gate_up(): pl.pallas_call(gate_up_kernel, in_specs=[ANY] * (1 + len(streams)) + [VME...]
    ppermute x32 -> x33, starting transfers between devices: 40.5 us -> 40.5 us  [swap(): return lax.ppermute(array, axis, [(s, s ^ distance) for s in range(count)])]
  transfers between devices with their start and end apart: 42 -> 43, of which waited for: 20 -> 20; matrix products, arithmetic and copies ran while one was open for 7% -> 7% of each run, Pallas kernels for 9% -> 12%
where the time goes in v11:
time: 387 us; the launch traced here: 386 us
  waiting for transfers between devices  198 us (51%)
  starting transfers between devices  73.7 us (19%)
  Pallas kernels  52.4 us (14%)
  local copies, waits for them, and re-layouts  36.9 us (10%)
  between operations  14.7 us (4%)
  other arithmetic  10.2 us (3%)
    ppermute x33, waiting for transfers between devices, swap(): return lax.ppermute(array, axis, [(s, s ^ distance) for s in range(count)])  92.2 us
    ppermute x33, starting transfers between devices, swap(): return lax.ppermute(array, axis, [(s, s ^ distance) for s in range(count)])  40.5 us
    all_to_all x1, waiting for transfers between devices, per_device(): spread(after(cut[1], normed))  39.5 us
    all_gather x1, waiting for transfers between devices, per_device(): weights_out = lax.all_gather(w_out, 'outer', axis=1, tiled=True)  26 us
    pallas_call x4, Pallas kernels, gate_up(): pl.pallas_call(gate_up_kernel, in_specs=[ANY] * (1 + len(streams)) + [VME...  19.6 us
    unnamed x56, local copies, waits for them, and re-layouts  17 us
    all_to_all x1, waiting for transfers between devices, per_device(): first = spread(after(cut[0], weights_out))  15 us
    all_to_all x1, waiting for transfers between devices, per_device(): lax.all_to_all(groups, ('inner', 'head'), split_axis=0, concat_axis=0, ti...  14.4 us
  transfers between devices with their start and end apart: 43, of which 20 were waited for; matrix products, arithmetic and copies ran while one was open for 7% of the time, Pallas kernels for 12%

profile of v11, /device:TPU:0, one launch (start us, length us, event | category | flops | bytes accessed | tf_op | source)
XLA Modules:
  0.0 385.9 jit_solution(5277671753914402961)
XLA Ops:
  7.9 4.9 %collective-permute-start = (bf16[64,1024]{1,0:T(8,128)(2,1)}, bf16[64,1024]{1,0:T(8,128)(2,1)S(1)}, u32[]{:S(2)}, u32[]{:S(2)}) collective-permute-start(bf16[64,1024]{1,0:T(8,128)(2,1)} %param.10), channel_id=1, source_target_pairs={{0,1},{1,2},{2,3},{4,5},{5,6},{6,7},{8,9},{9,10},{10,11},{12,13},{... | collective-permute-start | bytes 393224 | tf_op jit(solution)/shard_map/ppermute | solution.py:302
  25.6 14.4 %all-to-all-done = bf16[8,64,1024]{2,1,0:T(8,128)(2,1)S(1)} async-done(((bf16[8,64,1024]{2,1,0:T(8,128)(2,1)}), bf16[8,64,1024]{2,1,0:T(8,128)(2,1)S(1)}, u32[]{:S(2)}, u32[]{:S(2)}) %all-to-all-start) | async-done | bytes 1048608 | tf_op jit(solution)/shard_map/all_to_all | solution.py:305
  40.0 5.9 %attention.1.refs_0_ = bf16[512,512]{1,0:T(8,128)(2,1)S(1)} custom-call(s32[512,1]{1,0:T(8,128)S(1)} %copy.27.starts_ref, bf16[512,1024]{1,0:T(8,128)(2,1)S(1)} %bitcast.89, bf16[512,1024]{1,0:T(8,128)(2,1)S(1)} %bitcast.90, bf16[512,1024]{1,0:T(8,128)(2,1)S(1)} %bitcast.91), custom_call_target="tpu_custom_call" | custom-call | flops 1 | bytes 1 | tf_op jit(solution)/shard_map/attention/pallas_call | solution.py:96
  46.9 12.6 %collective-permute-done.3.refs_2_ = bf16[512,512]{1,0:T(8,128)(2,1)S(1)} collective-permute-done((bf16[512,512]{1,0:T(8,128)(2,1)S(1)}, bf16[512,512]{1,0:T(8,128)(2,1)S(1)}, u32[]{:S(2)}, u32[]{:S(2)}) %collective-permute-start.3) | collective-permute-done | bytes 524320 | tf_op jit(solution)/shard_map/ppermute | solution.py:32
  60.5 5.2 %cut_weights.1 = (bf16[4,2,128,896]{3,2,1,0:T(8,128)(2,1)}, bf16[4,128,896]{2,1,0:T(8,128)(2,1)}, bf16[4,128,896]{2,1,0:T(8,128)(2,1)}, bf16[4,896,128]{2,1,0:T(8,128)(2,1)S(1)}, bf16[4,896,128]{2,1,0:T(8,128)(2,1)S(1)}) custom-call(f32[256,1]{1,0:T(8,128)S(1)} %copy.28.gain_ref, bf16[2,256,3584]{2,1,0:T(8,128)(2,1)} %gate_up_ref.1, bf16[3584,256]{1,0:T(8,128)(2,1)} %down_ref.1), custom_call_target="tpu_custom_call" | custom-call | flops 1 | bytes 1 | tf_op jit(solution)/shard_map/cut_weights/pallas_call | solution.py:136
  66.9 26.0 %all-gather.3.cloned.1.call-done.refs_4_ = bf16[2048,1024]{1,0:T(8,128)(2,1)} async-done(((bf16[2048,256]{1,0:T(8,128)(2,1)}), bf16[2048,1024]{1,0:T(8,128)(2,1)}) %all-gather.3.cloned.1.call-update) | async-done | bytes 4194320 | tf_op jit(solution)/shard_map/all_gather | solution.py:300
  92.9 4.4 %all-to-all-start.1 = ((bf16[4,2,128,896]{3,2,1,0:T(8,128)(2,1)}), bf16[4,2,128,896]{3,2,1,0:T(8,128)(2,1)}, u32[]{:S(2)}, u32[]{:S(2)}) async-start(bf16[4,2,128,896]{3,2,1,0:T(8,128)(2,1)} %get-tuple-element.57), calls=%async_computation.1 | async-start | bytes 3670016 | tf_op jit(solution)/shard_map/all_to_all | solution.py:329
  97.4 5.3 %projection.1 = (bf16[256,1024]{1,0:T(8,128)(2,1)S(1)}, bf16[1,256,1024]{2,1,0:T(8,128)(2,1)S(1)}, bf16[128,2048]{1,0:T(8,128)(2,1)}) custom-call(s32[2]{0:T(128)S(1)} %pad_add_fusion.place_ref, bf16[512,512]{1,0:T(8,128)(2,1)S(1)} %attention.1.refs_0_, bf16[512,512]{1,0:T(8,128)(2,1)S(1)} %collective-permute-done.2.refs_1_, ...), custom_call_target="tpu_custom_call" | custom-call | flops 1 | bytes 1 | tf_op jit(solution)/shard_map/projection/pallas_call | solution.py:185
  104.2 12.3 %collective-permute-done.5 = bf16[256,1024]{1,0:T(8,128)(2,1)S(1)} collective-permute-done((bf16[256,1024]{1,0:T(8,128)(2,1)S(1)}, bf16[256,1024]{1,0:T(8,128)(2,1)S(1)}, u32[]{:S(2)}, u32[]{:S(2)}) %collective-permute-start.5) | collective-permute-done | bytes 524320 | tf_op jit(solution)/shard_map/ppermute | solution.py:32
  119.6 5.7 %collective-permute-done.6 = bf16[128,1024]{1,0:T(8,128)(2,1)S(1)} collective-permute-done((bf16[128,1024]{1,0:T(8,128)(2,1)S(1)}, bf16[128,1024]{1,0:T(8,128)(2,1)S(1)}, u32[]{:S(2)}, u32[]{:S(2)}) %collective-permute-start.6) | collective-permute-done | bytes 262176 | tf_op jit(solution)/shard_map/ppermute | solution.py:32
  125.4 15.0 %all-to-all-done.1.both = bf16[4,2,128,896]{3,2,1,0:T(8,128)(2,1)} async-done(((bf16[4,2,128,896]{3,2,1,0:T(8,128)(2,1)}), bf16[4,2,128,896]{3,2,1,0:T(8,128)(2,1)}, u32[]{:S(2)}, u32[]{:S(2)}) %all-to-all-start.1) | async-done | bytes 1835040 | tf_op jit(solution)/shard_map/all_to_all | solution.py:329
  155.6 39.5 %all-to-all-done.2.gate = bf16[4,128,896]{2,1,0:T(8,128)(2,1)S(1)} async-done(((bf16[4,128,896]{2,1,0:T(8,128)(2,1)}), bf16[4,128,896]{2,1,0:T(8,128)(2,1)S(1)}, u32[]{:S(2)}, u32[]{:S(2)}) %all-to-all-start.2) | async-done | bytes 917536 | tf_op jit(solution)/shard_map/all_to_all | solution.py:353
  195.1 10.2 %all-gather.5.cloned.1.call-done = bf16[512,2048]{1,0:T(8,128)(2,1)} async-done(((bf16[128,2048]{1,0:T(8,128)(2,1)}), bf16[512,2048]{1,0:T(8,128)(2,1)}) %all-gather.5.cloned.1.call-update) | async-done | bytes 2097168 | tf_op jit(solution)/shard_map/all_gather | solution.py:352
  213.8 21.4 %collective-permute-done.9.gate = bf16[4,128,896]{2,1,0:T(8,128)(2,1)S(1)} collective-permute-done((bf16[4,128,896]{2,1,0:T(8,128)(2,1)S(1)}, bf16[4,128,896]{2,1,0:T(8,128)(2,1)S(1)}, u32[]{:S(2)}, u32[]{:S(2)}) %collective-permute-start.9) | collective-permute-done | bytes 917536 | tf_op jit(solution)/shard_map/ppermute | solution.py:32
  237.9 4.6 %all-to-all-start.4 = ((bf16[4,896,128]{2,1,0:T(8,128)(2,1)}), bf16[4,896,128]{2,1,0:T(8,128)(2,1)}, u32[]{:S(2)}, u32[]{:S(2)}) async-start(bf16[4,896,128]{2,1,0:T(8,128)(2,1)} %copy-done.17), calls=%async_computation.4 | async-start | bytes 1835008 | tf_op jit(solution)/shard_map/all_to_all | solution.py:358
  245.8 3.7 gate_up.5.refs_0_
  255.8 8.9 %collective-permute-done.11.up = bf16[4,128,896]{2,1,0:T(8,128)(2,1)S(1)} collective-permute-done((bf16[4,128,896]{2,1,0:T(8,128)(2,1)S(1)}, bf16[4,128,896]{2,1,0:T(8,128)(2,1)S(1)}, u32[]{:S(2)}, u32[]{:S(2)}) %collective-permute-start.11) | collective-permute-done | bytes 917536 | tf_op jit(solution)/shard_map/ppermute | solution.py:32
  269.1 5.6 %gate_up.6.here_ref = bf16[2,512,896]{2,1,0:T(8,128)(2,1)S(1)} custom-call(bf16[512,1024]{1,0:T(8,128)(2,1)} %collective-permute-done.13.tokens, bf16[4,2,128,896]{3,2,1,0:T(8,128)(2,1)} %copy-done.18, bf16[4,128,896]{2,1,0:T(8,128)(2,1)S(1)} %copy-done.9, bf16[4,128,896]{2,1,0:T(8,128)(2,1)S(1)} %copy-done.12, bf16[2,512,896]{2,1,0:T(8,128)(2,1)} %copy-done.3), custom_call_target="tpu_custom_call" | custom-call | flops 1 | bytes 1 | tf_op jit(solution)/shard_map/gate_up/pallas_call | solution.py:222
  276.5 6.5 %gate_up.7.here_ref = bf16[2,512,896]{2,1,0:T(8,128)(2,1)} custom-call(bf16[512,1024]{1,0:T(8,128)(2,1)S(1)} %copy-done.4, bf16[4,2,128,896]{3,2,1,0:T(8,128)(2,1)} %copy-done.18, bf16[4,128,896]{2,1,0:T(8,128)(2,1)S(1)} %copy-done.10, bf16[4,128,896]{2,1,0:T(8,128)(2,1)S(1)} %copy-done.12, bf16[2,512,896]{2,1,0:T(8,128)(2,1)} %copy-done.2), custom_call_target="tpu_custom_call" | custom-call | flops 1 | bytes 1 | tf_op jit(solution)/shard_map/gate_up/pallas_call | solution.py:222
  283.1 4.7 %all-to-all-start.5 = ((bf16[4,896,128]{2,1,0:T(8,128)(2,1)}), bf16[4,896,128]{2,1,0:T(8,128)(2,1)S(1)}, u32[]{:S(2)}, u32[]{:S(2)}) async-start(bf16[4,896,128]{2,1,0:T(8,128)(2,1)} %copy-done.16), calls=%async_computation.5 | async-start | bytes 1835008 | tf_op jit(solution)/shard_map/all_to_all | solution.py:375
  299.9 7.9 %collective-permute-done.16 = bf16[512,512]{1,0:T(8,128)(2,1)S(1)} collective-permute-done((bf16[512,512]{1,0:T(8,128)(2,1)S(1)}, bf16[512,512]{1,0:T(8,128)(2,1)S(1)}, u32[]{:S(2)}, u32[]{:S(2)}) %collective-permute-start.16) | collective-permute-done | bytes 524320 | tf_op jit(solution)/shard_map/ppermute | solution.py:32
  326.0 5.5 %collective-permute-done.18 = bf16[128,512]{1,0:T(8,128)(2,1)} collective-permute-done((bf16[128,512]{1,0:T(8,128)(2,1)S(1)}, bf16[128,512]{1,0:T(8,128)(2,1)}, u32[]{:S(2)}, u32[]{:S(2)}) %collective-permute-start.18) | collective-permute-done | bytes 131104 | tf_op jit(solution)/shard_map/ppermute | solution.py:32
  356.9 5.6 %collective-permute-start.31 = (bf16[128,512]{1,0:T(8,128)(2,1)S(1)}, bf16[128,512]{1,0:T(8,128)(2,1)S(1)}, u32[]{:S(2)}, u32[]{:S(2)}) collective-permute-start(bf16[128,512]{1,0:T(8,128)(2,1)S(1)} %get-tuple-element.101), channel_id=1, source_target_pairs={{0,1},{1,0},{2,3},{3,2},{4,5},{5,4},{6,7},{7,6},{8,9},{9,8},{10,11... | collective-permute-start | bytes 393224 | tf_op jit(solution)/shard_map/ppermute | solution.py:32
  366.7 5.5 %collective-permute-done.32 = bf16[128,512]{1,0:T(8,128)(2,1)S(1)} collective-permute-done((bf16[128,512]{1,0:T(8,128)(2,1)S(1)}, bf16[128,512]{1,0:T(8,128)(2,1)S(1)}, u32[]{:S(2)}, u32[]{:S(2)}) %collective-permute-start.32) | collective-permute-done | bytes 131104 | tf_op jit(solution)/shard_map/ppermute | solution.py:32
  (192 shorter events, 129.8 us)
Async XLA Ops:
  7.2 85.7 %all-gather.3.cloned.1.call-start = ((), (), s32[]{:S(2)}) async-start(), calls=%async_computation.6 | async-start | bytes 5242880 | tf_op jit(solution)/shard_map/all_gather | solution.py:300
  21.3 18.7 %all-to-all-start = ((bf16[8,64,1024]{2,1,0:T(8,128)(2,1)}), bf16[8,64,1024]{2,1,0:T(8,128)(2,1)S(1)}, u32[]{:S(2)}, u32[]{:S(2)}) async-start(bf16[8,64,1024]{2,1,0:T(8,128)(2,1)} %bitcast.5), calls=%async_computation | async-start | bytes 2097152 | tf_op jit(solution)/shard_map/all_to_all | solution.py:305
  46.5 19.2 %collective-permute-start.2 = (bf16[512,512]{1,0:T(8,128)(2,1)S(1)}, bf16[512,512]{1,0:T(8,128)(2,1)S(1)}, u32[]{:S(2)}, u32[]{:S(2)}) collective-permute-start(bf16[512,512]{1,0:T(8,128)(2,1)S(1)} %attention.1.refs_0_), channel_id=1, source_target_pairs={{0,4},{4,0},{8,12},{12,8},{1,5},{5,1},{9,13},{13,9},{2,6},{6,2},{1... | collective-permute-start | bytes 1572872 | tf_op jit(solution)/shard_map/ppermute | solution.py:32
  92.9 47.5 %all-to-all-start.1 = ((bf16[4,2,128,896]{3,2,1,0:T(8,128)(2,1)}), bf16[4,2,128,896]{3,2,1,0:T(8,128)(2,1)}, u32[]{:S(2)}, u32[]{:S(2)}) async-start(bf16[4,2,128,896]{3,2,1,0:T(8,128)(2,1)} %get-tuple-element.57), calls=%async_computation.1 | async-start | bytes 3670016 | tf_op jit(solution)/shard_map/all_to_all | solution.py:329
  97.3 108.1 %all-gather.5.cloned.1.call-start = ((), (), s32[]{:S(2)}) async-start(), calls=%async_computation.7 | async-start | bytes 2621440 | tf_op jit(solution)/shard_map/all_gather | solution.py:352
  142.7 52.4 %collective-permute-start.8 = (bf16[4,2,128,896]{3,2,1,0:T(8,128)(2,1)}, bf16[4,2,128,896]{3,2,1,0:T(8,128)(2,1)S(1)}, u32[]{:S(2)}, u32[]{:S(2)}) collective-permute-start(bf16[4,2,128,896]{3,2,1,0:T(8,128)(2,1)} %all-to-all-done.1.both), channel_id=1, source_target_pairs={{0,8},{4,12},{8,0},{12,4},{1,9},{5,13},{9,1},{13,5},{2,10},{6,14},... | collective-permute-start | bytes 5505032 | tf_op jit(solution)/shard_map/ppermute | solution.py:32
  144.4 50.8 %all-to-all-start.2 = ((bf16[4,128,896]{2,1,0:T(8,128)(2,1)}), bf16[4,128,896]{2,1,0:T(8,128)(2,1)S(1)}, u32[]{:S(2)}, u32[]{:S(2)}) async-start(bf16[4,128,896]{2,1,0:T(8,128)(2,1)} %get-tuple-element.59), calls=%async_computation.2 | async-start | bytes 1835008 | tf_op jit(solution)/shard_map/all_to_all | solution.py:353
  205.3 32.5 %all-to-all-start.3 = ((bf16[4,128,896]{2,1,0:T(8,128)(2,1)}), bf16[4,128,896]{2,1,0:T(8,128)(2,1)S(1)}, u32[]{:S(2)}, u32[]{:S(2)}) async-start(bf16[4,128,896]{2,1,0:T(8,128)(2,1)} %get-tuple-element.66), calls=%async_computation.3 | async-start | bytes 1835008 | tf_op jit(solution)/shard_map/all_to_all | solution.py:356
  211.8 25.1 %collective-permute-start.10 = (bf16[512,1024]{1,0:T(8,128)(2,1)S(1)}, bf16[512,1024]{1,0:T(8,128)(2,1)S(1)}, u32[]{:S(2)}, u32[]{:S(2)}) collective-permute-start(bf16[512,1024]{1,0:T(8,128)(2,1)S(1)} %get-tuple-element.70.tokens), channel_id=1, source_target_pairs={{0,16},{16,0},{1,17},{17,1},{2,18},{18,2},{3,19},{19,3},{4,20},{20... | collective-permute-start | bytes 3145736 | tf_op jit(solution)/shard_map/ppermute | solution.py:32
  213.3 22.0 %collective-permute-start.9 = (bf16[4,128,896]{2,1,0:T(8,128)(2,1)S(1)}, bf16[4,128,896]{2,1,0:T(8,128)(2,1)S(1)}, u32[]{:S(2)}, u32[]{:S(2)}) collective-permute-start(bf16[4,128,896]{2,1,0:T(8,128)(2,1)S(1)} %all-to-all-done.2.gate), channel_id=1, source_target_pairs={{0,8},{4,12},{8,0},{12,4},{1,9},{5,13},{9,1},{13,5},{2,10},{6,14},... | collective-permute-start | bytes 2752520 | tf_op jit(solution)/shard_map/ppermute | solution.py:32
  237.9 27.9 %all-to-all-start.4 = ((bf16[4,896,128]{2,1,0:T(8,128)(2,1)}), bf16[4,896,128]{2,1,0:T(8,128)(2,1)}, u32[]{:S(2)}, u32[]{:S(2)}) async-start(bf16[4,896,128]{2,1,0:T(8,128)(2,1)} %copy-done.17), calls=%async_computation.4 | async-start | bytes 1835008 | tf_op jit(solution)/shard_map/all_to_all | solution.py:358
  242.5 24.3 %collective-permute-start.13 = (bf16[512,1024]{1,0:T(8,128)(2,1)}, bf16[512,1024]{1,0:T(8,128)(2,1)}, u32[]{:S(2)}, u32[]{:S(2)}) collective-permute-start(bf16[512,1024]{1,0:T(8,128)(2,1)} %get-tuple-element.97.tokens), channel_id=1, source_target_pairs={{0,16},{16,0},{1,17},{17,1},{2,18},{18,2},{3,19},{19,3},{4,20},{20... | collective-permute-start | bytes 3145736 | tf_op jit(solution)/shard_map/ppermute | solution.py:32
  243.9 20.9 %collective-permute-start.11 = (bf16[4,128,896]{2,1,0:T(8,128)(2,1)S(1)}, bf16[4,128,896]{2,1,0:T(8,128)(2,1)S(1)}, u32[]{:S(2)}, u32[]{:S(2)}) collective-permute-start(bf16[4,128,896]{2,1,0:T(8,128)(2,1)S(1)} %all-to-all-done.3.up), channel_id=1, source_target_pairs={{0,8},{4,12},{8,0},{12,4},{1,9},{5,13},{9,1},{13,5},{2,10},{6,14},... | collective-permute-start | bytes 2752520 | tf_op jit(solution)/shard_map/ppermute | solution.py:32
  283.1 28.3 %all-to-all-start.5 = ((bf16[4,896,128]{2,1,0:T(8,128)(2,1)}), bf16[4,896,128]{2,1,0:T(8,128)(2,1)S(1)}, u32[]{:S(2)}, u32[]{:S(2)}) async-start(bf16[4,896,128]{2,1,0:T(8,128)(2,1)} %copy-done.16), calls=%async_computation.5 | async-start | bytes 1835008 | tf_op jit(solution)/shard_map/all_to_all | solution.py:375
  287.9 22.7 %collective-permute-start.12 = (bf16[4,896,128]{2,1,0:T(8,128)(2,1)}, bf16[4,896,128]{2,1,0:T(8,128)(2,1)S(1)}, u32[]{:S(2)}, u32[]{:S(2)}) collective-permute-start(bf16[4,896,128]{2,1,0:T(8,128)(2,1)} %all-to-all-done.4.weights_ref), channel_id=1, source_target_pairs={{0,8},{4,12},{8,0},{12,4},{1,9},{5,13},{9,1},{13,5},{2,10},{6,14},... | collective-permute-start | bytes 2752520 | tf_op jit(solution)/shard_map/ppermute | solution.py:32
  314.2 20.5 %collective-permute-start.24 = (bf16[512,512]{1,0:T(8,128)(2,1)}, bf16[512,512]{1,0:T(8,128)(2,1)}, u32[]{:S(2)}, u32[]{:S(2)}) collective-permute-start(bf16[512,512]{1,0:T(8,128)(2,1)} %down.12), channel_id=1, source_target_pairs={{0,16},{16,0},{1,17},{17,1},{2,18},{18,2},{3,19},{19,3},{4,20},{20... | collective-permute-start | bytes 1572872 | tf_op jit(solution)/shard_map/ppermute | solution.py:32
  315.6 24.9 %collective-permute-start.29 = (bf16[4,896,128]{2,1,0:T(8,128)(2,1)S(1)}, bf16[4,896,128]{2,1,0:T(8,128)(2,1)}, u32[]{:S(2)}, u32[]{:S(2)}) collective-permute-start(bf16[4,896,128]{2,1,0:T(8,128)(2,1)S(1)} %all-to-all-done.5.weights_ref), channel_id=1, source_target_pairs={{0,8},{4,12},{8,0},{12,4},{1,9},{5,13},{9,1},{13,5},{2,10},{6,14},... | collective-permute-start | bytes 2752520 | tf_op jit(solution)/shard_map/ppermute | solution.py:32
  325.5 17.6 %collective-permute-start.20 = (bf16[512,512]{1,0:T(8,128)(2,1)}, bf16[512,512]{1,0:T(8,128)(2,1)}, u32[]{:S(2)}, u32[]{:S(2)}) collective-permute-start(bf16[512,512]{1,0:T(8,128)(2,1)} %down.10), channel_id=1, source_target_pairs={{0,16},{16,0},{1,17},{17,1},{2,18},{18,2},{3,19},{19,3},{4,20},{20... | collective-permute-start | bytes 1572872 | tf_op jit(solution)/shard_map/ppermute | solution.py:32
  339.1 14.2 %collective-permute-start.27 = (bf16[128,512]{1,0:T(8,128)(2,1)S(1)}, bf16[128,512]{1,0:T(8,128)(2,1)S(1)}, u32[]{:S(2)}, u32[]{:S(2)}) collective-permute-start(bf16[128,512]{1,0:T(8,128)(2,1)S(1)} %get-tuple-element.99), channel_id=1, source_target_pairs={{0,3},{1,2},{2,1},{3,0},{4,7},{5,6},{6,5},{7,4},{8,11},{9,10},{10,... | collective-permute-start | bytes 393224 | tf_op jit(solution)/shard_map/ppermute | solution.py:32
  342.5 14.2 %collective-permute-start.30 = (bf16[512,512]{1,0:T(8,128)(2,1)S(1)}, bf16[512,512]{1,0:T(8,128)(2,1)S(1)}, u32[]{:S(2)}, u32[]{:S(2)}) collective-permute-start(bf16[512,512]{1,0:T(8,128)(2,1)S(1)} %down.14), channel_id=1, source_target_pairs={{0,16},{16,0},{1,17},{17,1},{2,18},{18,2},{3,19},{19,3},{4,20},{20... | collective-permute-start | bytes 1572872 | tf_op jit(solution)/shard_map/ppermute | solution.py:32
  344.3 18.2 %collective-permute-start.21 = (bf16[128,512]{1,0:T(8,128)(2,1)S(1)}, bf16[128,512]{1,0:T(8,128)(2,1)S(1)}, u32[]{:S(2)}, u32[]{:S(2)}) collective-permute-start(bf16[128,512]{1,0:T(8,128)(2,1)S(1)} %get-tuple-element.107), channel_id=1, source_target_pairs={{0,1},{1,0},{2,3},{3,2},{4,5},{5,4},{6,7},{7,6},{8,9},{9,8},{10,11... | collective-permute-start | bytes 393224 | tf_op jit(solution)/shard_map/ppermute | solution.py:32
  345.4 17.0 %collective-permute-start.22 = (bf16[128,512]{1,0:T(8,128)(2,1)S(1)}, bf16[128,512]{1,0:T(8,128)(2,1)S(1)}, u32[]{:S(2)}, u32[]{:S(2)}) collective-permute-start(bf16[128,512]{1,0:T(8,128)(2,1)S(1)} %get-tuple-element.109), channel_id=1, source_target_pairs={{0,2},{1,3},{2,0},{3,1},{4,6},{5,7},{6,4},{7,5},{8,10},{9,11},{10,... | collective-permute-start | bytes 393224 | tf_op jit(solution)/shard_map/ppermute | solution.py:32
  350.9 14.1 %collective-permute-start.23 = (bf16[128,512]{1,0:T(8,128)(2,1)S(1)}, bf16[128,512]{1,0:T(8,128)(2,1)S(1)}, u32[]{:S(2)}, u32[]{:S(2)}) collective-permute-start(bf16[128,512]{1,0:T(8,128)(2,1)S(1)} %get-tuple-element.108), channel_id=1, source_target_pairs={{0,3},{1,2},{2,1},{3,0},{4,7},{5,6},{6,5},{7,4},{8,11},{9,10},{10,... | collective-permute-start | bytes 393224 | tf_op jit(solution)/shard_map/ppermute | solution.py:32
  353.4 21.3 %collective-permute-start.28 = (bf16[128,512]{1,0:T(8,128)(2,1)S(1)}, bf16[128,512]{1,0:T(8,128)(2,1)S(1)}, u32[]{:S(2)}, u32[]{:S(2)}) collective-permute-start(bf16[128,512]{1,0:T(8,128)(2,1)S(1)} %fusion.7), channel_id=1, source_target_pairs={{0,8},{4,12},{8,0},{12,4},{1,9},{5,13},{9,1},{13,5},{2,10},{6,14},... | collective-permute-start | bytes 393224 | tf_op jit(solution)/shard_map/ppermute | solution.py:32
  (45 other events, 303.0 us)
Sparse Core Ops, SparseCore 0:
  9.6 83.2 all-gather.2
  142.9 62.4 all-gather.4

commit v12 on v11

--- a/solution.py
+++ b/solution.py
@@ -350,28 +350,30 @@
     state = [[block[:, :, part].reshape(own_rows, -1) for part in range(PARTS)] for block in state]
 
     tokens = lax.all_gather(normed, "outer", axis=0, tiled=True)
-    second, first_y, tokens, state = fence(spread(after(cut[1], normed)), over_y(first), tokens, state)
+    second, first_y, state = fence(spread(after(cut[1], normed)), over_y(first), state)
     tokens = jnp.split(tokens, 2, axis=1)
     tokens = [[swap(block, "head", e) if e else block for e in range(head_count)] for block in tokens]
     third, second_y, tokens[0] = fence(spread(after(cut[2], second)), over_y(second), tokens[0])
     own_sums = [gate_up(rows_of, [first, second, third]) for rows_of in tokens[0]]
     fourth, third_y, own_sums = fence(spread(after(cut[3], third)), over_y(third), own_sums)
     streams = [first_y, second_y, third_y]
-    activated, earlier = {}, first_y
+    activated, first_sent = {}, []
     for e in [*range(1, head_count), 0]:
-        sums = gate_up(tokens[1][e], streams, [after(own_sums[e], earlier)])
+        sums = gate_up(tokens[1][e], streams, [own_sums[e] if e else after(own_sums[e], first_sent)])
         activated[e] = activation(sums, swap(sums, "inner", 1))
-        earlier = sums
-
-    def over_heads(weights):
-        sent = [down_product(activated[e], weights) for e in range(1, head_count)]
+        if e:
+            first_sent.append(down_product(activated[e], fourth))
+
+    def over_heads(weights, sent=None):
+        if sent is None:
+            sent = [down_product(activated[e], weights) for e in range(1, head_count)]
         moved = [swap(rows_of, "head", e) for e, rows_of in enumerate(sent, 1)]
         total = down_product(after(activated[0], sent[-1]), weights).astype(jnp.float32)
         for rows_of in moved:
             total = total + rows_of.astype(jnp.float32)
         return total.reshape(outer_count, own_rows, -1)
 
-    paired = {(0, 0): over_heads(fourth)}
+    paired = {(0, 0): over_heads(fourth, first_sent)}
     fifth, fourth_y, paired[0, 0] = fence(spread(after(cut[4], fourth)), over_y(fourth), paired[0, 0])
     fifth_y = over_y(fifth)
     paired[1, 0] = over_heads(fourth_y)

time: 387 us -> 402 us (1.039)
  waiting for transfers between devices: 198 us -> 217 us
  local copies, waits for them, and re-layouts: 36.9 us -> 32.3 us
    ppermute x33, waiting for transfers between devices: 92.2 us -> 102 us  [swap(): return lax.ppermute(array, axis, [(s, s ^ distance) for s in range(count)])]
    all_gather x1, waiting for transfers between devices: 10.2 us -> 19 us  [per_device(): tokens = lax.all_gather(normed, 'outer', axis=0, tiled=True)]
    unnamed x56 -> x46, local copies, waits for them, and re-layouts: 17 us -> 12.5 us
  transfers between devices with their start and end apart: 43 -> 43, of which waited for: 20 -> 21; matrix products, arithmetic and copies ran while one was open for 7% -> 7% of each run, Pallas kernels for 12% -> 9%
where the time goes in v12:
time: 402 us; the launch traced here: 400 us
  waiting for transfers between devices  217 us (54%)
  starting transfers between devices  73.2 us (18%)
  Pallas kernels  52.2 us (13%)
  local copies, waits for them, and re-layouts  32.3 us (8%)
  between operations  14.7 us (4%)
  other arithmetic  10.8 us (3%)
    ppermute x33, waiting for transfers between devices, swap(): return lax.ppermute(array, axis, [(s, s ^ distance) for s in range(count)])  102 us
    ppermute x33, starting transfers between devices, swap(): return lax.ppermute(array, axis, [(s, s ^ distance) for s in range(count)])  40.5 us
    all_to_all x1, waiting for transfers between devices, per_device(): spread(after(cut[1], normed))  39.5 us
    all_gather x1, waiting for transfers between devices, per_device(): weights_out = lax.all_gather(w_out, 'outer', axis=1, tiled=True)  26.1 us
    pallas_call x4, Pallas kernels, gate_up(): pl.pallas_call(gate_up_kernel, in_specs=[ANY] * (1 + len(streams)) + [VME...  19.9 us
    all_gather x1, waiting for transfers between devices, per_device(): tokens = lax.all_gather(normed, 'outer', axis=0, tiled=True)  19 us
    all_to_all x1, waiting for transfers between devices, per_device(): first = spread(after(cut[0], weights_out))  15 us
    all_to_all x1, waiting for transfers between devices, per_device(): lax.all_to_all(groups, ('inner', 'head'), split_axis=0, concat_axis=0, ti...  14.4 us
  transfers between devices with their start and end apart: 43, of which 21 were waited for; matrix products, arithmetic and copies ran while one was open for 7% of the time, Pallas kernels for 9%

profile of v12, /device:TPU:0, one launch (start us, length us, event | category | flops | bytes accessed | tf_op | source)
XLA Modules:
  0.0 400.2 jit_solution(12135158956877404708)
XLA Ops:
  7.9 4.9 %collective-permute-start = (bf16[64,1024]{1,0:T(8,128)(2,1)}, bf16[64,1024]{1,0:T(8,128)(2,1)S(1)}, u32[]{:S(2)}, u32[]{:S(2)}) collective-permute-start(bf16[64,1024]{1,0:T(8,128)(2,1)} %param.10), channel_id=1, source_target_pairs={{0,1},{1,2},{2,3},{4,5},{5,6},{6,7},{8,9},{9,10},{10,11},{12,13},{... | collective-permute-start | bytes 393224 | tf_op jit(solution)/shard_map/ppermute | solution.py:302
  25.6 14.4 %all-to-all-done = bf16[8,64,1024]{2,1,0:T(8,128)(2,1)S(1)} async-done(((bf16[8,64,1024]{2,1,0:T(8,128)(2,1)}), bf16[8,64,1024]{2,1,0:T(8,128)(2,1)S(1)}, u32[]{:S(2)}, u32[]{:S(2)}) %all-to-all-start) | async-done | bytes 1048608 | tf_op jit(solution)/shard_map/all_to_all | solution.py:305
  40.0 5.9 %attention.1.refs_0_ = bf16[512,512]{1,0:T(8,128)(2,1)S(1)} custom-call(s32[512,1]{1,0:T(8,128)S(1)} %copy.27.starts_ref, bf16[512,1024]{1,0:T(8,128)(2,1)S(1)} %bitcast.89, bf16[512,1024]{1,0:T(8,128)(2,1)S(1)} %bitcast.90, bf16[512,1024]{1,0:T(8,128)(2,1)S(1)} %bitcast.91), custom_call_target="tpu_custom_call" | custom-call | flops 1 | bytes 1 | tf_op jit(solution)/shard_map/attention/pallas_call | solution.py:96
  46.9 12.6 %collective-permute-done.3.refs_2_ = bf16[512,512]{1,0:T(8,128)(2,1)S(1)} collective-permute-done((bf16[512,512]{1,0:T(8,128)(2,1)S(1)}, bf16[512,512]{1,0:T(8,128)(2,1)S(1)}, u32[]{:S(2)}, u32[]{:S(2)}) %collective-permute-start.3) | collective-permute-done | bytes 524320 | tf_op jit(solution)/shard_map/ppermute | solution.py:32
  60.4 5.4 %cut_weights.1 = (bf16[4,2,128,896]{3,2,1,0:T(8,128)(2,1)}, bf16[4,128,896]{2,1,0:T(8,128)(2,1)}, bf16[4,128,896]{2,1,0:T(8,128)(2,1)}, bf16[4,896,128]{2,1,0:T(8,128)(2,1)S(1)}, bf16[4,896,128]{2,1,0:T(8,128)(2,1)}) custom-call(f32[256,1]{1,0:T(8,128)S(1)} %copy.28.gain_ref, bf16[2,256,3584]{2,1,0:T(8,128)(2,1)} %gate_up_ref.1, bf16[3584,256]{1,0:T(8,128)(2,1)} %down_ref.1), custom_call_target="tpu_custom_call" | custom-call | flops 1 | bytes 1 | tf_op jit(solution)/shard_map/cut_weights/pallas_call | solution.py:136
  66.8 26.1 %all-gather.3.cloned.1.call-done.refs_4_ = bf16[2048,1024]{1,0:T(8,128)(2,1)} async-done(((bf16[2048,256]{1,0:T(8,128)(2,1)}), bf16[2048,1024]{1,0:T(8,128)(2,1)}) %all-gather.3.cloned.1.call-update) | async-done | bytes 4194320 | tf_op jit(solution)/shard_map/all_gather | solution.py:300
  92.9 4.4 %all-to-all-start.1 = ((bf16[4,2,128,896]{3,2,1,0:T(8,128)(2,1)}), bf16[4,2,128,896]{3,2,1,0:T(8,128)(2,1)}, u32[]{:S(2)}, u32[]{:S(2)}) async-start(bf16[4,2,128,896]{3,2,1,0:T(8,128)(2,1)} %get-tuple-element.55), calls=%async_computation.1 | async-start | bytes 3670016 | tf_op jit(solution)/shard_map/all_to_all | solution.py:329
  97.4 5.3 %projection.1 = (bf16[256,1024]{1,0:T(8,128)(2,1)S(1)}, bf16[1,256,1024]{2,1,0:T(8,128)(2,1)S(1)}, bf16[128,2048]{1,0:T(8,128)(2,1)}) custom-call(s32[2]{0:T(128)S(1)} %pad_add_fusion.place_ref, bf16[512,512]{1,0:T(8,128)(2,1)S(1)} %attention.1.refs_0_, bf16[512,512]{1,0:T(8,128)(2,1)S(1)} %collective-permute-done.2.refs_1_, ...), custom_call_target="tpu_custom_call" | custom-call | flops 1 | bytes 1 | tf_op jit(solution)/shard_map/projection/pallas_call | solution.py:185
  104.1 12.3 %collective-permute-done.5 = bf16[256,1024]{1,0:T(8,128)(2,1)S(1)} collective-permute-done((bf16[256,1024]{1,0:T(8,128)(2,1)S(1)}, bf16[256,1024]{1,0:T(8,128)(2,1)S(1)}, u32[]{:S(2)}, u32[]{:S(2)}) %collective-permute-start.5) | collective-permute-done | bytes 524320 | tf_op jit(solution)/shard_map/ppermute | solution.py:32
  119.6 5.7 %collective-permute-done.6 = bf16[128,1024]{1,0:T(8,128)(2,1)S(1)} collective-permute-done((bf16[128,1024]{1,0:T(8,128)(2,1)S(1)}, bf16[128,1024]{1,0:T(8,128)(2,1)S(1)}, u32[]{:S(2)}, u32[]{:S(2)}) %collective-permute-start.6) | collective-permute-done | bytes 262176 | tf_op jit(solution)/shard_map/ppermute | solution.py:32
  125.4 15.0 %all-to-all-done.1.both = bf16[4,2,128,896]{3,2,1,0:T(8,128)(2,1)} async-done(((bf16[4,2,128,896]{3,2,1,0:T(8,128)(2,1)}), bf16[4,2,128,896]{3,2,1,0:T(8,128)(2,1)}, u32[]{:S(2)}, u32[]{:S(2)}) %all-to-all-start.1) | async-done | bytes 1835040 | tf_op jit(solution)/shard_map/all_to_all | solution.py:329
  155.6 39.5 %all-to-all-done.2.gate = bf16[4,128,896]{2,1,0:T(8,128)(2,1)S(1)} async-done(((bf16[4,128,896]{2,1,0:T(8,128)(2,1)}), bf16[4,128,896]{2,1,0:T(8,128)(2,1)S(1)}, u32[]{:S(2)}, u32[]{:S(2)}) %all-to-all-start.2) | async-done | bytes 917536 | tf_op jit(solution)/shard_map/all_to_all | solution.py:353
  200.0 19.0 %all-gather.5.cloned.1.call-done = bf16[512,2048]{1,0:T(8,128)(2,1)} async-done(((bf16[128,2048]{1,0:T(8,128)(2,1)}), bf16[512,2048]{1,0:T(8,128)(2,1)}) %all-gather.5.cloned.1.call-update) | async-done | bytes 2097168 | tf_op jit(solution)/shard_map/all_gather | solution.py:352
  223.9 21.4 %collective-permute-done.9.gate = bf16[4,128,896]{2,1,0:T(8,128)(2,1)S(1)} collective-permute-done((bf16[4,128,896]{2,1,0:T(8,128)(2,1)S(1)}, bf16[4,128,896]{2,1,0:T(8,128)(2,1)S(1)}, u32[]{:S(2)}, u32[]{:S(2)}) %collective-permute-start.9) | collective-permute-done | bytes 917536 | tf_op jit(solution)/shard_map/ppermute | solution.py:32
  247.0 4.2 %all-to-all-start.4 = ((bf16[4,896,128]{2,1,0:T(8,128)(2,1)}), bf16[4,896,128]{2,1,0:T(8,128)(2,1)}, u32[]{:S(2)}, u32[]{:S(2)}) async-start(bf16[4,896,128]{2,1,0:T(8,128)(2,1)} %copy-done.12), calls=%async_computation.4 | async-start | bytes 1835008 | tf_op jit(solution)/shard_map/all_to_all | solution.py:358
  263.8 10.1 %collective-permute-done.11.up = bf16[4,128,896]{2,1,0:T(8,128)(2,1)S(1)} collective-permute-done((bf16[4,128,896]{2,1,0:T(8,128)(2,1)S(1)}, bf16[4,128,896]{2,1,0:T(8,128)(2,1)S(1)}, u32[]{:S(2)}, u32[]{:S(2)}) %collective-permute-start.11) | collective-permute-done | bytes 917536 | tf_op jit(solution)/shard_map/ppermute | solution.py:32
  278.2 5.6 %gate_up.6.here_ref = bf16[2,512,896]{2,1,0:T(8,128)(2,1)S(1)} custom-call(bf16[512,1024]{1,0:T(8,128)(2,1)} %collective-permute-done.13.tokens, bf16[4,2,128,896]{3,2,1,0:T(8,128)(2,1)} %copy-done.13, bf16[4,128,896]{2,1,0:T(8,128)(2,1)S(1)} %copy-done.7, bf16[4,128,896]{2,1,0:T(8,128)(2,1)S(1)} %copy-done.10, bf16[2,512,896]{2,1,0:T(8,128)(2,1)} %copy-done.1), custom_call_target="tpu_custom_call" | custom-call | flops 1 | bytes 1 | tf_op jit(solution)/shard_map/gate_up/pallas_call | solution.py:222
  290.9 6.5 %gate_up.7.here_ref = bf16[2,512,896]{2,1,0:T(8,128)(2,1)} custom-call(bf16[512,1024]{1,0:T(8,128)(2,1)S(1)} %copy-done.2, bf16[4,2,128,896]{3,2,1,0:T(8,128)(2,1)} %copy-done.13, bf16[4,128,896]{2,1,0:T(8,128)(2,1)S(1)} %copy-done.8, bf16[4,128,896]{2,1,0:T(8,128)(2,1)S(1)} %copy-done.10, bf16[2,512,896]{2,1,0:T(8,128)(2,1)} %copy-done), custom_call_target="tpu_custom_call" | custom-call | flops 1 | bytes 1 | tf_op jit(solution)/shard_map/gate_up/pallas_call | solution.py:222
  297.7 4.7 %all-to-all-start.5 = ((bf16[4,896,128]{2,1,0:T(8,128)(2,1)}), bf16[4,896,128]{2,1,0:T(8,128)(2,1)S(1)}, u32[]{:S(2)}, u32[]{:S(2)}) async-start(bf16[4,896,128]{2,1,0:T(8,128)(2,1)} %get-tuple-element.70), calls=%async_computation.5 | async-start | bytes 1835008 | tf_op jit(solution)/shard_map/all_to_all | solution.py:377
  308.9 7.8 %collective-permute-done.16 = bf16[512,512]{1,0:T(8,128)(2,1)S(1)} collective-permute-done((bf16[512,512]{1,0:T(8,128)(2,1)S(1)}, bf16[512,512]{1,0:T(8,128)(2,1)S(1)}, u32[]{:S(2)}, u32[]{:S(2)}) %collective-permute-start.16) | collective-permute-done | bytes 524320 | tf_op jit(solution)/shard_map/ppermute | solution.py:32
  317.8 7.2 %collective-permute-done.12.weights_ref = bf16[4,896,128]{2,1,0:T(8,128)(2,1)S(1)} collective-permute-done((bf16[4,896,128]{2,1,0:T(8,128)(2,1)}, bf16[4,896,128]{2,1,0:T(8,128)(2,1)S(1)}, u32[]{:S(2)}, u32[]{:S(2)}) %collective-permute-start.12) | collective-permute-done | bytes 917536 | tf_op jit(solution)/shard_map/ppermute | solution.py:32
  340.5 5.3 %collective-permute-done.18 = bf16[128,512]{1,0:T(8,128)(2,1)} collective-permute-done((bf16[128,512]{1,0:T(8,128)(2,1)S(1)}, bf16[128,512]{1,0:T(8,128)(2,1)}, u32[]{:S(2)}, u32[]{:S(2)}) %collective-permute-start.18) | collective-permute-done | bytes 131104 | tf_op jit(solution)/shard_map/ppermute | solution.py:32
  371.6 5.6 %collective-permute-start.31 = (bf16[128,512]{1,0:T(8,128)(2,1)S(1)}, bf16[128,512]{1,0:T(8,128)(2,1)S(1)}, u32[]{:S(2)}, u32[]{:S(2)}) collective-permute-start(bf16[128,512]{1,0:T(8,128)(2,1)S(1)} %get-tuple-element.97), channel_id=1, source_target_pairs={{0,1},{1,0},{2,3},{3,2},{4,5},{5,4},{6,7},{7,6},{8,9},{9,8},{10,11... | collective-permute-start | bytes 393224 | tf_op jit(solution)/shard_map/ppermute | solution.py:32
  381.9 4.7 %collective-permute-done.32 = bf16[128,512]{1,0:T(8,128)(2,1)S(1)} collective-permute-done((bf16[128,512]{1,0:T(8,128)(2,1)S(1)}, bf16[128,512]{1,0:T(8,128)(2,1)S(1)}, u32[]{:S(2)}, u32[]{:S(2)}) %collective-permute-start.32) | collective-permute-done | bytes 131104 | tf_op jit(solution)/shard_map/ppermute | solution.py:32
  (182 shorter events, 131.9 us)
Async XLA Ops:
  7.2 85.7 %all-gather.3.cloned.1.call-start = ((), (), s32[]{:S(2)}) async-start(), calls=%async_computation.6 | async-start | bytes 5242880 | tf_op jit(solution)/shard_map/all_gather | solution.py:300
  21.3 18.7 %all-to-all-start = ((bf16[8,64,1024]{2,1,0:T(8,128)(2,1)}), bf16[8,64,1024]{2,1,0:T(8,128)(2,1)S(1)}, u32[]{:S(2)}, u32[]{:S(2)}) async-start(bf16[8,64,1024]{2,1,0:T(8,128)(2,1)} %bitcast.5), calls=%async_computation | async-start | bytes 2097152 | tf_op jit(solution)/shard_map/all_to_all | solution.py:305
  46.5 20.3 %collective-permute-start.2 = (bf16[512,512]{1,0:T(8,128)(2,1)S(1)}, bf16[512,512]{1,0:T(8,128)(2,1)S(1)}, u32[]{:S(2)}, u32[]{:S(2)}) collective-permute-start(bf16[512,512]{1,0:T(8,128)(2,1)S(1)} %attention.1.refs_0_), channel_id=1, source_target_pairs={{0,4},{4,0},{8,12},{12,8},{1,5},{5,1},{9,13},{13,9},{2,6},{6,2},{1... | collective-permute-start | bytes 1572872 | tf_op jit(solution)/shard_map/ppermute | solution.py:32
  92.9 47.4 %all-to-all-start.1 = ((bf16[4,2,128,896]{3,2,1,0:T(8,128)(2,1)}), bf16[4,2,128,896]{3,2,1,0:T(8,128)(2,1)}, u32[]{:S(2)}, u32[]{:S(2)}) async-start(bf16[4,2,128,896]{3,2,1,0:T(8,128)(2,1)} %get-tuple-element.55), calls=%async_computation.1 | async-start | bytes 3670016 | tf_op jit(solution)/shard_map/all_to_all | solution.py:329
  97.3 121.8 %all-gather.5.cloned.1.call-start = ((), (), s32[]{:S(2)}) async-start(), calls=%async_computation.7 | async-start | bytes 2621440 | tf_op jit(solution)/shard_map/all_gather | solution.py:352
  142.7 52.4 %collective-permute-start.8 = (bf16[4,2,128,896]{3,2,1,0:T(8,128)(2,1)}, bf16[4,2,128,896]{3,2,1,0:T(8,128)(2,1)S(1)}, u32[]{:S(2)}, u32[]{:S(2)}) collective-permute-start(bf16[4,2,128,896]{3,2,1,0:T(8,128)(2,1)} %all-to-all-done.1.both), channel_id=1, source_target_pairs={{0,8},{4,12},{8,0},{12,4},{1,9},{5,13},{9,1},{13,5},{2,10},{6,14},... | collective-permute-start | bytes 5505032 | tf_op jit(solution)/shard_map/ppermute | solution.py:32
  144.3 50.8 %all-to-all-start.2 = ((bf16[4,128,896]{2,1,0:T(8,128)(2,1)}), bf16[4,128,896]{2,1,0:T(8,128)(2,1)S(1)}, u32[]{:S(2)}, u32[]{:S(2)}) async-start(bf16[4,128,896]{2,1,0:T(8,128)(2,1)} %get-tuple-element.57), calls=%async_computation.2 | async-start | bytes 1835008 | tf_op jit(solution)/shard_map/all_to_all | solution.py:353
  196.4 49.8 %all-to-all-start.3 = ((bf16[4,128,896]{2,1,0:T(8,128)(2,1)}), bf16[4,128,896]{2,1,0:T(8,128)(2,1)S(1)}, u32[]{:S(2)}, u32[]{:S(2)}) async-start(bf16[4,128,896]{2,1,0:T(8,128)(2,1)} %get-tuple-element.64), calls=%async_computation.3 | async-start | bytes 1835008 | tf_op jit(solution)/shard_map/all_to_all | solution.py:356
  221.8 25.2 %collective-permute-start.10 = (bf16[512,1024]{1,0:T(8,128)(2,1)S(1)}, bf16[512,1024]{1,0:T(8,128)(2,1)}, u32[]{:S(2)}, u32[]{:S(2)}) collective-permute-start(bf16[512,1024]{1,0:T(8,128)(2,1)S(1)} %get-tuple-element.67.tokens), channel_id=1, source_target_pairs={{0,16},{16,0},{1,17},{17,1},{2,18},{18,2},{3,19},{19,3},{4,20},{20... | collective-permute-start | bytes 3145736 | tf_op jit(solution)/shard_map/ppermute | solution.py:32
  223.2 22.0 %collective-permute-start.9 = (bf16[4,128,896]{2,1,0:T(8,128)(2,1)S(1)}, bf16[4,128,896]{2,1,0:T(8,128)(2,1)S(1)}, u32[]{:S(2)}, u32[]{:S(2)}) collective-permute-start(bf16[4,128,896]{2,1,0:T(8,128)(2,1)S(1)} %all-to-all-done.2.gate), channel_id=1, source_target_pairs={{0,8},{4,12},{8,0},{12,4},{1,9},{5,13},{9,1},{13,5},{2,10},{6,14},... | collective-permute-start | bytes 2752520 | tf_op jit(solution)/shard_map/ppermute | solution.py:32
  247.0 27.8 %all-to-all-start.4 = ((bf16[4,896,128]{2,1,0:T(8,128)(2,1)}), bf16[4,896,128]{2,1,0:T(8,128)(2,1)}, u32[]{:S(2)}, u32[]{:S(2)}) async-start(bf16[4,896,128]{2,1,0:T(8,128)(2,1)} %copy-done.12), calls=%async_computation.4 | async-start | bytes 1835008 | tf_op jit(solution)/shard_map/all_to_all | solution.py:358
  251.2 24.6 %collective-permute-start.13 = (bf16[512,1024]{1,0:T(8,128)(2,1)}, bf16[512,1024]{1,0:T(8,128)(2,1)}, u32[]{:S(2)}, u32[]{:S(2)}) collective-permute-start(bf16[512,1024]{1,0:T(8,128)(2,1)} %get-tuple-element.93.tokens), channel_id=1, source_target_pairs={{0,16},{16,0},{1,17},{17,1},{2,18},{18,2},{3,19},{19,3},{4,20},{20... | collective-permute-start | bytes 3145736 | tf_op jit(solution)/shard_map/ppermute | solution.py:32
  252.7 21.2 %collective-permute-start.11 = (bf16[4,128,896]{2,1,0:T(8,128)(2,1)S(1)}, bf16[4,128,896]{2,1,0:T(8,128)(2,1)S(1)}, u32[]{:S(2)}, u32[]{:S(2)}) collective-permute-start(bf16[4,128,896]{2,1,0:T(8,128)(2,1)S(1)} %all-to-all-done.3.up), channel_id=1, source_target_pairs={{0,8},{4,12},{8,0},{12,4},{1,9},{5,13},{9,1},{13,5},{2,10},{6,14},... | collective-permute-start | bytes 2752520 | tf_op jit(solution)/shard_map/ppermute | solution.py:32
  297.7 28.2 %all-to-all-start.5 = ((bf16[4,896,128]{2,1,0:T(8,128)(2,1)}), bf16[4,896,128]{2,1,0:T(8,128)(2,1)S(1)}, u32[]{:S(2)}, u32[]{:S(2)}) async-start(bf16[4,896,128]{2,1,0:T(8,128)(2,1)} %get-tuple-element.70), calls=%async_computation.5 | async-start | bytes 1835008 | tf_op jit(solution)/shard_map/all_to_all | solution.py:377
  302.4 22.5 %collective-permute-start.12 = (bf16[4,896,128]{2,1,0:T(8,128)(2,1)}, bf16[4,896,128]{2,1,0:T(8,128)(2,1)S(1)}, u32[]{:S(2)}, u32[]{:S(2)}) collective-permute-start(bf16[4,896,128]{2,1,0:T(8,128)(2,1)} %all-to-all-done.4.weights_ref), channel_id=1, source_target_pairs={{0,8},{4,12},{8,0},{12,4},{1,9},{5,13},{9,1},{13,5},{2,10},{6,14},... | collective-permute-start | bytes 2752520 | tf_op jit(solution)/shard_map/ppermute | solution.py:32
  328.6 20.4 %collective-permute-start.24 = (bf16[512,512]{1,0:T(8,128)(2,1)}, bf16[512,512]{1,0:T(8,128)(2,1)}, u32[]{:S(2)}, u32[]{:S(2)}) collective-permute-start(bf16[512,512]{1,0:T(8,128)(2,1)} %down.12), channel_id=1, source_target_pairs={{0,16},{16,0},{1,17},{17,1},{2,18},{18,2},{3,19},{19,3},{4,20},{20... | collective-permute-start | bytes 1572872 | tf_op jit(solution)/shard_map/ppermute | solution.py:32
  330.0 24.9 %collective-permute-start.29 = (bf16[4,896,128]{2,1,0:T(8,128)(2,1)S(1)}, bf16[4,896,128]{2,1,0:T(8,128)(2,1)}, u32[]{:S(2)}, u32[]{:S(2)}) collective-permute-start(bf16[4,896,128]{2,1,0:T(8,128)(2,1)S(1)} %all-to-all-done.5.weights_ref), channel_id=1, source_target_pairs={{0,8},{4,12},{8,0},{12,4},{1,9},{5,13},{9,1},{13,5},{2,10},{6,14},... | collective-permute-start | bytes 2752520 | tf_op jit(solution)/shard_map/ppermute | solution.py:32
  339.9 17.4 %collective-permute-start.20 = (bf16[512,512]{1,0:T(8,128)(2,1)}, bf16[512,512]{1,0:T(8,128)(2,1)}, u32[]{:S(2)}, u32[]{:S(2)}) collective-permute-start(bf16[512,512]{1,0:T(8,128)(2,1)} %down.10), channel_id=1, source_target_pairs={{0,16},{16,0},{1,17},{17,1},{2,18},{18,2},{3,19},{19,3},{4,20},{20... | collective-permute-start | bytes 1572872 | tf_op jit(solution)/shard_map/ppermute | solution.py:32
  353.4 14.1 %collective-permute-start.27 = (bf16[128,512]{1,0:T(8,128)(2,1)S(1)}, bf16[128,512]{1,0:T(8,128)(2,1)S(1)}, u32[]{:S(2)}, u32[]{:S(2)}) collective-permute-start(bf16[128,512]{1,0:T(8,128)(2,1)S(1)} %get-tuple-element.95), channel_id=1, source_target_pairs={{0,3},{1,2},{2,1},{3,0},{4,7},{5,6},{6,5},{7,4},{8,11},{9,10},{10,... | collective-permute-start | bytes 393224 | tf_op jit(solution)/shard_map/ppermute | solution.py:32
  356.8 14.7 %collective-permute-start.30 = (bf16[512,512]{1,0:T(8,128)(2,1)S(1)}, bf16[512,512]{1,0:T(8,128)(2,1)S(1)}, u32[]{:S(2)}, u32[]{:S(2)}) collective-permute-start(bf16[512,512]{1,0:T(8,128)(2,1)S(1)} %down.14), channel_id=1, source_target_pairs={{0,16},{16,0},{1,17},{17,1},{2,18},{18,2},{3,19},{19,3},{4,20},{20... | collective-permute-start | bytes 1572872 | tf_op jit(solution)/shard_map/ppermute | solution.py:32
  358.6 18.7 %collective-permute-start.21 = (bf16[128,512]{1,0:T(8,128)(2,1)S(1)}, bf16[128,512]{1,0:T(8,128)(2,1)S(1)}, u32[]{:S(2)}, u32[]{:S(2)}) collective-permute-start(bf16[128,512]{1,0:T(8,128)(2,1)S(1)} %get-tuple-element.103), channel_id=1, source_target_pairs={{0,1},{1,0},{2,3},{3,2},{4,5},{5,4},{6,7},{7,6},{8,9},{9,8},{10,11... | collective-permute-start | bytes 393224 | tf_op jit(solution)/shard_map/ppermute | solution.py:32
  359.7 17.6 %collective-permute-start.22 = (bf16[128,512]{1,0:T(8,128)(2,1)S(1)}, bf16[128,512]{1,0:T(8,128)(2,1)S(1)}, u32[]{:S(2)}, u32[]{:S(2)}) collective-permute-start(bf16[128,512]{1,0:T(8,128)(2,1)S(1)} %get-tuple-element.105), channel_id=1, source_target_pairs={{0,2},{1,3},{2,0},{3,1},{4,6},{5,7},{6,4},{7,5},{8,10},{9,11},{10,... | collective-permute-start | bytes 393224 | tf_op jit(solution)/shard_map/ppermute | solution.py:32
  365.1 14.6 %collective-permute-start.23 = (bf16[128,512]{1,0:T(8,128)(2,1)S(1)}, bf16[128,512]{1,0:T(8,128)(2,1)S(1)}, u32[]{:S(2)}, u32[]{:S(2)}) collective-permute-start(bf16[128,512]{1,0:T(8,128)(2,1)S(1)} %get-tuple-element.104), channel_id=1, source_target_pairs={{0,3},{1,2},{2,1},{3,0},{4,7},{5,6},{6,5},{7,4},{8,11},{9,10},{10,... | collective-permute-start | bytes 393224 | tf_op jit(solution)/shard_map/ppermute | solution.py:32
  368.3 20.6 %collective-permute-start.28 = (bf16[128,512]{1,0:T(8,128)(2,1)}, bf16[128,512]{1,0:T(8,128)(2,1)S(1)}, u32[]{:S(2)}, u32[]{:S(2)}) collective-permute-start(bf16[128,512]{1,0:T(8,128)(2,1)} %fusion.7), channel_id=1, source_target_pairs={{0,8},{4,12},{8,0},{12,4},{1,9},{5,13},{9,1},{13,5},{2,10},{6,14},... | collective-permute-start | bytes 393224 | tf_op jit(solution)/shard_map/ppermute | solution.py:32
  (40 other events, 247.2 us)
Sparse Core Ops, SparseCore 0:
  9.6 83.2 all-gather.2
  142.8 76.1 all-gather.4

commit v13 on v9

--- a/solution.py
+++ b/solution.py
@@ -246,13 +246,15 @@
     out_ref[...] = (gate / (1.0 + jnp.exp(-gate)) * up).astype(jnp.bfloat16)
 
 
-def activation(here, there):
+def activation(here, there, part, parts):
     _, rows, cols = here.shape
+    rows = rows // parts
     step = min(rows, ROW_TILE)
+    first = part * rows // step
     return pl.pallas_call(
         activation_kernel,
         grid=(rows // step,),
-        in_specs=[pl.BlockSpec((2, step, cols), lambda t: (0, t, 0))] * 2,
+        in_specs=[pl.BlockSpec((2, step, cols), lambda t: (0, first + t, 0))] * 2,
         out_specs=pl.BlockSpec((step, cols), lambda t: (t, 0)),
         out_shape=jax.ShapeDtypeStruct((rows, cols), jnp.bfloat16),
         compiler_params=pltpu.CompilerParams(vmem_limit_bytes=VMEM_LIMIT),
@@ -261,35 +263,24 @@
     )(here, there)
 
 
-def down_kernel(activated_ref, weights_ref, kept_ref, sent_ref):
+def down_kernel(activated_ref, weights_ref, out_ref):
     sources, _, cols = weights_ref.shape
-    kept_rows = kept_ref.shape[0]
     if cols % HEAD_WIDTH:
         blocks = [weights_ref[s] for s in range(sources)]
     else:
         blocks = [jnp.concatenate([weights_ref[s] for s in range(sources)], axis=1)]
-    for e in range(sent_ref.shape[0] + 1):
-        rows = activated_ref[e * kept_rows : (e + 1) * kept_rows, :]
-        for s, block in enumerate(blocks):
-            at = slice(s * block.shape[1], (s + 1) * block.shape[1])
-            product = jnp.dot(rows, block, preferred_element_type=jnp.float32)
-            if e == 0:
-                kept_ref[:, at] = product.astype(jnp.bfloat16)
-            else:
-                sent_ref[e - 1, :, at] = product.astype(jnp.bfloat16)
-
-
-def down_product(activated, weights, head_count):
-    rows = activated.shape[0] // head_count
-    sources, depth, cols = weights.shape
+    for s, block in enumerate(blocks):
+        product = jnp.dot(activated_ref[...], block, preferred_element_type=jnp.float32)
+        out_ref[:, s * block.shape[1] : (s + 1) * block.shape[1]] = product.astype(jnp.bfloat16)
+
+
+def down_product(activated, weights):
+    sources, _, cols = weights.shape
     return pl.pallas_call(
         down_kernel,
         in_specs=[VMEM, VMEM],
-        out_specs=[VMEM, VMEM],
-        out_shape=[
-            jax.ShapeDtypeStruct((rows, sources * cols), jnp.bfloat16),
-            jax.ShapeDtypeStruct((head_count - 1, rows, sources * cols), jnp.bfloat16),
-        ],
+        out_specs=VMEM,
+        out_shape=jax.ShapeDtypeStruct((activated.shape[0], sources * cols), jnp.bfloat16),
         compiler_params=pltpu.CompilerParams(vmem_limit_bytes=VMEM_LIMIT),
         cost_estimate=BRIEF,
         name="down",
@@ -372,21 +363,27 @@
     own_sums = gate_up(tokens[0], [first, second, third])
     fourth, third_y, own_sums = fence(spread(after(cut[3], third)), over_y(third), own_sums)
     sums = gate_up(tokens[1], [first_y, second_y, third_y], [own_sums])
-    activated = activation(sums, swap(sums, "inner", 1))
-
-    def over_heads(weights):
-        kept, sent = down_product(activated, weights, head_count)
-        paired = kept.astype(jnp.float32)
-        for e in range(1, head_count):
-            paired = paired + swap(sent[e - 1], "head", e).astype(jnp.float32)
-        return paired.reshape(outer_count, own_rows, -1)
-
-    paired = {(0, 0): over_heads(fourth)}
-    fifth, fourth_y, paired[0, 0] = fence(spread(after(cut[4], fourth)), over_y(fourth), paired[0, 0])
+    other_sums = swap(sums, "inner", 1)
+    activated = [activation(sums, other_sums, e, head_count) for e in range(1, head_count)]
+    sent = [down_product(rows_of, fourth) for rows_of in activated]
+    activated = [activation(after(sums, sent[-1]), other_sums, 0, head_count), *activated]
+
+    def over_heads(weights, moved=None):
+        if moved is None:
+            sent = [down_product(rows_of, weights) for rows_of in activated[1:]]
+            moved = [swap(rows_of, "head", e) for e, rows_of in enumerate(sent, 1)]
+        total = down_product(activated[0], weights).astype(jnp.float32)
+        for rows_of in moved:
+            total = total + rows_of.astype(jnp.float32)
+        return total.reshape(outer_count, own_rows, -1)
+
+    moved = [[swap(piece, "head", e) for piece in jnp.split(rows_of, 2)] for e, rows_of in enumerate(sent, 1)]
+    fifth, fourth_y, moved[0][0] = fence(spread(after(cut[4], fourth)), over_y(fourth), moved[0][0])
     fifth_y = over_y(fifth)
+    paired = {(0, 0): over_heads(fourth, [jnp.concatenate(pieces) for pieces in moved])}
     paired[1, 0] = over_heads(fourth_y)
     paired[0, 1] = over_heads(fifth)
-    paired[1, 1] = over_heads(after(fifth_y, paired[1, 0]))
+    paired[1, 1] = over_heads(after(fifth_y, paired[0, 0]))
 
     pieces = [[None] * PARTS, [None] * PARTS]
     for part in range(PARTS):

time: 386 us -> 383 us (level)
  waiting for transfers between devices: 198 us -> 188 us
  Pallas kernels: 45 us -> 50.7 us
    ppermute x32 -> x33, waiting for transfers between devices: 97.9 us -> 87.3 us  [swap(): return lax.ppermute(array, axis, [(s, s ^ distance) for s in range(count)])]
    pallas_call x4 -> x8, Pallas kernels: 8.94 us -> 14.3 us  [down_product(): pl.pallas_call(down_kernel, in_specs=[VMEM, VMEM], out_specs=VMEM, out_sh...]
    ppermute x32 -> x33, starting transfers between devices: 40.5 us -> 40.8 us  [swap(): return lax.ppermute(array, axis, [(s, s ^ distance) for s in range(count)])]
    unnamed x68 -> x66, local copies, waits for them, and re-layouts: 24.2 us -> 24.3 us
  transfers between devices with their start and end apart: 42 -> 43, of which waited for: 20 -> 20; matrix products, arithmetic and copies ran while one was open for 7% -> 7% of each run, Pallas kernels for 9% -> 11%
where the time goes in v13:
time: 383 us; the launch traced here: 381 us
  waiting for transfers between devices  188 us (49%)
  starting transfers between devices  73.8 us (19%)
  Pallas kernels  50.7 us (13%)
  local copies, waits for them, and re-layouts  42.8 us (11%)
  between operations  14.7 us (4%)
  other arithmetic  10.8 us (3%)
    ppermute x33, waiting for transfers between devices, swap(): return lax.ppermute(array, axis, [(s, s ^ distance) for s in range(count)])  87.3 us
    ppermute x33, starting transfers between devices, swap(): return lax.ppermute(array, axis, [(s, s ^ distance) for s in range(count)])  40.8 us
    all_to_all x1, waiting for transfers between devices, per_device(): spread(after(cut[1], normed))  39.6 us
    unnamed x66, local copies, waits for them, and re-layouts  24.3 us
    all_gather x1, waiting for transfers between devices, per_device(): weights_out = lax.all_gather(w_out, 'outer', axis=1, tiled=True)  22.9 us
    pallas_call x2, Pallas kernels, gate_up(): pl.pallas_call(functools.partial(gate_up_kernel, len(tokens)), in_specs=[...  17.1 us
    all_to_all x1, waiting for transfers between devices, per_device(): lax.all_to_all(groups, ('inner', 'head'), split_axis=0, concat_axis=0, ti...  14.4 us
    pallas_call x8, Pallas kernels, down_product(): pl.pallas_call(down_kernel, in_specs=[VMEM, VMEM], out_specs=VMEM, out_sh...  14.3 us
  transfers between devices with their start and end apart: 43, of which 20 were waited for; matrix products, arithmetic and copies ran while one was open for 7% of the time, Pallas kernels for 11%

profile of v13, /device:TPU:0, one launch (start us, length us, event | category | flops | bytes accessed | tf_op | source)
XLA Modules:
  0.0 381.1 jit_solution(17576918764203427125)
XLA Ops:
  7.9 4.9 %collective-permute-start = (bf16[64,1024]{1,0:T(8,128)(2,1)}, bf16[64,1024]{1,0:T(8,128)(2,1)S(1)}, u32[]{:S(2)}, u32[]{:S(2)}) collective-permute-start(bf16[64,1024]{1,0:T(8,128)(2,1)} %param.10), channel_id=1, source_target_pairs={{0,1},{1,2},{2,3},{4,5},{5,6},{6,7},{8,9},{9,10},{10,11},{12,13},{... | collective-permute-start | bytes 393224 | tf_op jit(solution)/shard_map/ppermute | solution.py:308
  21.3 3.7 all-to-all-start
  25.6 14.4 %all-to-all-done = bf16[8,64,1024]{2,1,0:T(8,128)(2,1)S(1)} async-done(((bf16[8,64,1024]{2,1,0:T(8,128)(2,1)}), bf16[8,64,1024]{2,1,0:T(8,128)(2,1)S(1)}, u32[]{:S(2)}, u32[]{:S(2)}) %all-to-all-start) | async-done | bytes 1048608 | tf_op jit(solution)/shard_map/all_to_all | solution.py:311
  40.0 5.8 %attention.1.refs_0_ = bf16[512,512]{1,0:T(8,128)(2,1)S(1)} custom-call(s32[512,1]{1,0:T(8,128)S(1)} %copy.27.starts_ref, bf16[512,1024]{1,0:T(8,128)(2,1)S(1)} %bitcast.89, bf16[512,1024]{1,0:T(8,128)(2,1)S(1)} %bitcast.90, bf16[512,1024]{1,0:T(8,128)(2,1)S(1)} %bitcast.91), custom_call_target="tpu_custom_call" | custom-call | flops 1 | bytes 1 | tf_op jit(solution)/shard_map/attention/pallas_call | solution.py:96
  46.9 12.6 %collective-permute-done.3.refs_2_ = bf16[512,512]{1,0:T(8,128)(2,1)S(1)} collective-permute-done((bf16[512,512]{1,0:T(8,128)(2,1)S(1)}, bf16[512,512]{1,0:T(8,128)(2,1)S(1)}, u32[]{:S(2)}, u32[]{:S(2)}) %collective-permute-start.3) | collective-permute-done | bytes 524320 | tf_op jit(solution)/shard_map/ppermute | solution.py:32
  60.4 3.7 cut_weights.1
  70.0 22.9 %all-gather.3.cloned.1.call-done.refs_4_ = bf16[2048,1024]{1,0:T(8,128)(2,1)} async-done(((bf16[2048,256]{1,0:T(8,128)(2,1)}), bf16[2048,1024]{1,0:T(8,128)(2,1)}) %all-gather.3.cloned.1.call-update) | async-done | bytes 4194320 | tf_op jit(solution)/shard_map/all_gather | solution.py:306
  92.9 3.6 all-to-all-start.1
  98.7 5.5 %projection.1 = (bf16[256,1024]{1,0:T(8,128)(2,1)S(1)}, bf16[1,256,1024]{2,1,0:T(8,128)(2,1)}, bf16[128,2048]{1,0:T(8,128)(2,1)}) custom-call(s32[2]{0:T(128)S(1)} %pad_add_fusion.place_ref, bf16[512,512]{1,0:T(8,128)(2,1)S(1)} %attention.1.refs_0_, bf16[512,512]{1,0:T(8,128)(2,1)S(1)} %copy-done.20, bf16[512,512]{1,0:T(8,128)(2,1)S(1)} %collective-permute-done.3.refs_2_, ...), custom_call_target="tpu_custom_call" | custom-call | flops 1 | bytes 1 | tf_op jit(solution)/shard_map/projection/pallas_call | solution.py:185
  105.6 12.5 %collective-permute-done.5 = bf16[256,1024]{1,0:T(8,128)(2,1)S(1)} collective-permute-done((bf16[256,1024]{1,0:T(8,128)(2,1)}, bf16[256,1024]{1,0:T(8,128)(2,1)S(1)}, u32[]{:S(2)}, u32[]{:S(2)}) %collective-permute-start.5) | collective-permute-done | bytes 524320 | tf_op jit(solution)/shard_map/ppermute | solution.py:32
  121.3 5.6 %collective-permute-done.6 = bf16[128,1024]{1,0:T(8,128)(2,1)S(1)} collective-permute-done((bf16[128,1024]{1,0:T(8,128)(2,1)S(1)}, bf16[128,1024]{1,0:T(8,128)(2,1)S(1)}, u32[]{:S(2)}, u32[]{:S(2)}) %collective-permute-start.6) | collective-permute-done | bytes 262176 | tf_op jit(solution)/shard_map/ppermute | solution.py:32
  126.9 12.5 %all-to-all-done.1.refs_2_ = bf16[4,2,128,896]{3,2,1,0:T(8,128)(2,1)S(1)} async-done(((bf16[4,2,128,896]{3,2,1,0:T(8,128)(2,1)}), bf16[4,2,128,896]{3,2,1,0:T(8,128)(2,1)S(1)}, u32[]{:S(2)}, u32[]{:S(2)}) %all-to-all-start.1) | async-done | bytes 1835040 | tf_op jit(solution)/shard_map/all_to_all | solution.py:335
  154.6 39.6 %all-to-all-done.2.refs_3_ = bf16[4,128,896]{2,1,0:T(8,128)(2,1)S(1)} async-done(((bf16[4,128,896]{2,1,0:T(8,128)(2,1)}), bf16[4,128,896]{2,1,0:T(8,128)(2,1)S(1)}, u32[]{:S(2)}, u32[]{:S(2)}) %all-to-all-start.2) | async-done | bytes 917536 | tf_op jit(solution)/shard_map/all_to_all | solution.py:359
  194.2 10.2 %all-gather.5.cloned.1.call-done = bf16[512,2048]{1,0:T(8,128)(2,1)} async-done(((bf16[128,2048]{1,0:T(8,128)(2,1)}), bf16[512,2048]{1,0:T(8,128)(2,1)}) %all-gather.5.cloned.1.call-update) | async-done | bytes 2097168 | tf_op jit(solution)/shard_map/all_gather | solution.py:358
  204.4 4.4 %all-to-all-start.3 = ((bf16[4,128,896]{2,1,0:T(8,128)(2,1)}), bf16[4,128,896]{2,1,0:T(8,128)(2,1)}, u32[]{:S(2)}, u32[]{:S(2)}) async-start(bf16[4,128,896]{2,1,0:T(8,128)(2,1)} %copy-done.17), calls=%async_computation.3 | async-start | bytes 1835008 | tf_op jit(solution)/shard_map/all_to_all | solution.py:362
  213.7 21.4 %collective-permute-done.10.refs_3_ = bf16[4,128,896]{2,1,0:T(8,128)(2,1)S(1)} collective-permute-done((bf16[4,128,896]{2,1,0:T(8,128)(2,1)S(1)}, bf16[4,128,896]{2,1,0:T(8,128)(2,1)S(1)}, u32[]{:S(2)}, u32[]{:S(2)}) %collective-permute-start.10) | collective-permute-done | bytes 917536 | tf_op jit(solution)/shard_map/ppermute | solution.py:32
  237.1 4.6 %all-to-all-start.4 = ((bf16[4,896,128]{2,1,0:T(8,128)(2,1)}), bf16[4,896,128]{2,1,0:T(8,128)(2,1)}, u32[]{:S(2)}, u32[]{:S(2)}) async-start(bf16[4,896,128]{2,1,0:T(8,128)(2,1)} %copy-done.16), calls=%async_computation.4 | async-start | bytes 1835008 | tf_op jit(solution)/shard_map/all_to_all | solution.py:364
  247.0 7.0 %gate_up.2.refs_5_ = bf16[2,1024,896]{2,1,0:T(8,128)(2,1)} custom-call(bf16[512,1024]{1,0:T(8,128)(2,1)S(1)} %copy-done.3, bf16[512,1024]{1,0:T(8,128)(2,1)S(1)} %copy-done.10, bf16[4,2,128,896]{3,2,1,0:T(8,128)(2,1)S(1)} %all-to-all-done.1.refs_2_, bf16[4,128,896]{2,1,0:T(8,128)(2,1)S(1)} %copy-done.6, bf16[4,128,896]{2,1,0:T(8,128)(2,1)} %all-to-all-done.3.refs_4_), custom_call_target="tpu_custom_call" | custom-call | flops 1 | bytes 1 | tf_op jit(solution)/shard_map/gate_up/pallas_call | solution.py:226
  254.0 9.9 %collective-permute-done.12.refs_4_ = bf16[4,128,896]{2,1,0:T(8,128)(2,1)S(1)} collective-permute-done((bf16[4,128,896]{2,1,0:T(8,128)(2,1)}, bf16[4,128,896]{2,1,0:T(8,128)(2,1)S(1)}, u32[]{:S(2)}, u32[]{:S(2)}) %collective-permute-start.12) | collective-permute-done | bytes 917536 | tf_op jit(solution)/shard_map/ppermute | solution.py:32
  267.8 10.2 %gate_up.3.here_ref = bf16[2,1024,896]{2,1,0:T(8,128)(2,1)} custom-call(bf16[512,1024]{1,0:T(8,128)(2,1)S(1)} %get-tuple-element.85.refs_0_, bf16[512,1024]{1,0:T(8,128)(2,1)} %collective-permute-done.9.refs_1_, bf16[4,2,128,896]{3,2,1,0:T(8,128)(2,1)} %collective-permute-done.8.refs_2_, bf16[4,128,896]{2,1,0:T(8,128)(2,1)S(1)} %copy-done.12, ...), custom_call_target="tpu_custom_call" | custom-call | flops 1 | bytes 1 | tf_op jit(solution)/shard_map/gate_up/pallas_call | solution.py:226
  278.0 4.7 %all-to-all-start.5 = ((bf16[4,896,128]{2,1,0:T(8,128)(2,1)}), bf16[4,896,128]{2,1,0:T(8,128)(2,1)S(1)}, u32[]{:S(2)}, u32[]{:S(2)}) async-start(bf16[4,896,128]{2,1,0:T(8,128)(2,1)} %copy-done.15), calls=%async_computation.5 | async-start | bytes 1835008 | tf_op jit(solution)/shard_map/all_to_all | solution.py:381
  299.7 5.9 %collective-permute-done.14.weights_ref = bf16[4,896,128]{2,1,0:T(8,128)(2,1)} collective-permute-done((bf16[4,896,128]{2,1,0:T(8,128)(2,1)}, bf16[4,896,128]{2,1,0:T(8,128)(2,1)}, u32[]{:S(2)}, u32[]{:S(2)}) %collective-permute-start.14) | collective-permute-done | bytes 917536 | tf_op jit(solution)/shard_map/ppermute | solution.py:32
  352.6 5.6 %collective-permute-start.31 = (bf16[128,512]{1,0:T(8,128)(2,1)S(1)}, bf16[128,512]{1,0:T(8,128)(2,1)S(1)}, u32[]{:S(2)}, u32[]{:S(2)}) collective-permute-start(bf16[128,512]{1,0:T(8,128)(2,1)S(1)} %get-tuple-element.89), channel_id=1, source_target_pairs={{0,1},{1,0},{2,3},{3,2},{4,5},{5,4},{6,7},{7,6},{8,9},{9,8},{10,11... | collective-permute-start | bytes 393224 | tf_op jit(solution)/shard_map/ppermute | solution.py:32
  362.2 5.2 %collective-permute-done.32 = bf16[128,512]{1,0:T(8,128)(2,1)S(1)} collective-permute-done((bf16[128,512]{1,0:T(8,128)(2,1)S(1)}, bf16[128,512]{1,0:T(8,128)(2,1)S(1)}, u32[]{:S(2)}, u32[]{:S(2)}) %collective-permute-start.32) | collective-permute-done | bytes 131104 | tf_op jit(solution)/shard_map/ppermute | solution.py:32
  (201 shorter events, 130.0 us)
Async XLA Ops:
  7.2 85.7 %all-gather.3.cloned.1.call-start = ((), (), s32[]{:S(2)}) async-start(), calls=%async_computation.6 | async-start | bytes 5242880 | tf_op jit(solution)/shard_map/all_gather | solution.py:306
  21.3 18.7 %all-to-all-start = ((bf16[8,64,1024]{2,1,0:T(8,128)(2,1)}), bf16[8,64,1024]{2,1,0:T(8,128)(2,1)S(1)}, u32[]{:S(2)}, u32[]{:S(2)}) async-start(bf16[8,64,1024]{2,1,0:T(8,128)(2,1)} %bitcast.5), calls=%async_computation | async-start | bytes 2097152 | tf_op jit(solution)/shard_map/all_to_all | solution.py:311
  46.5 22.7 %collective-permute-start.2 = (bf16[512,512]{1,0:T(8,128)(2,1)S(1)}, bf16[512,512]{1,0:T(8,128)(2,1)S(1)}, u32[]{:S(2)}, u32[]{:S(2)}) collective-permute-start(bf16[512,512]{1,0:T(8,128)(2,1)S(1)} %attention.1.refs_0_), channel_id=1, source_target_pairs={{0,4},{4,0},{8,12},{12,8},{1,5},{5,1},{9,13},{13,9},{2,6},{6,2},{1... | collective-permute-start | bytes 1572872 | tf_op jit(solution)/shard_map/ppermute | solution.py:32
  92.9 46.6 %all-to-all-start.1 = ((bf16[4,2,128,896]{3,2,1,0:T(8,128)(2,1)}), bf16[4,2,128,896]{3,2,1,0:T(8,128)(2,1)S(1)}, u32[]{:S(2)}, u32[]{:S(2)}) async-start(bf16[4,2,128,896]{3,2,1,0:T(8,128)(2,1)} %copy-done.8), calls=%async_computation.1 | async-start | bytes 3670016 | tf_op jit(solution)/shard_map/all_to_all | solution.py:335
  96.5 107.9 %all-gather.5.cloned.1.call-start = ((), (), s32[]{:S(2)}) async-start(), calls=%async_computation.7 | async-start | bytes 2621440 | tf_op jit(solution)/shard_map/all_gather | solution.py:358
  141.8 52.4 %collective-permute-start.8 = (bf16[4,2,128,896]{3,2,1,0:T(8,128)(2,1)S(1)}, bf16[4,2,128,896]{3,2,1,0:T(8,128)(2,1)}, u32[]{:S(2)}, u32[]{:S(2)}) collective-permute-start(bf16[4,2,128,896]{3,2,1,0:T(8,128)(2,1)S(1)} %all-to-all-done.1.refs_2_), channel_id=1, source_target_pairs={{0,8},{4,12},{8,0},{12,4},{1,9},{5,13},{9,1},{13,5},{2,10},{6,14},... | collective-permute-start | bytes 5505032 | tf_op jit(solution)/shard_map/ppermute | solution.py:32
  143.4 50.8 %all-to-all-start.2 = ((bf16[4,128,896]{2,1,0:T(8,128)(2,1)}), bf16[4,128,896]{2,1,0:T(8,128)(2,1)S(1)}, u32[]{:S(2)}, u32[]{:S(2)}) async-start(bf16[4,128,896]{2,1,0:T(8,128)(2,1)} %copy-done.18), calls=%async_computation.2 | async-start | bytes 1835008 | tf_op jit(solution)/shard_map/all_to_all | solution.py:359
  204.4 32.7 %all-to-all-start.3 = ((bf16[4,128,896]{2,1,0:T(8,128)(2,1)}), bf16[4,128,896]{2,1,0:T(8,128)(2,1)}, u32[]{:S(2)}, u32[]{:S(2)}) async-start(bf16[4,128,896]{2,1,0:T(8,128)(2,1)} %copy-done.17), calls=%async_computation.3 | async-start | bytes 1835008 | tf_op jit(solution)/shard_map/all_to_all | solution.py:362
  210.6 25.5 %collective-permute-start.11 = (bf16[512,1024]{1,0:T(8,128)(2,1)S(1)}, bf16[512,1024]{1,0:T(8,128)(2,1)S(1)}, u32[]{:S(2)}, u32[]{:S(2)}) collective-permute-start(bf16[512,1024]{1,0:T(8,128)(2,1)S(1)} %get-tuple-element.65.refs_0_), channel_id=1, source_target_pairs={{0,16},{16,0},{1,17},{17,1},{2,18},{18,2},{3,19},{19,3},{4,20},{20... | collective-permute-start | bytes 3145736 | tf_op jit(solution)/shard_map/ppermute | solution.py:32
  213.2 22.0 %collective-permute-start.10 = (bf16[4,128,896]{2,1,0:T(8,128)(2,1)S(1)}, bf16[4,128,896]{2,1,0:T(8,128)(2,1)S(1)}, u32[]{:S(2)}, u32[]{:S(2)}) collective-permute-start(bf16[4,128,896]{2,1,0:T(8,128)(2,1)S(1)} %copy-done.5), channel_id=1, source_target_pairs={{0,8},{4,12},{8,0},{12,4},{1,9},{5,13},{9,1},{13,5},{2,10},{6,14},... | collective-permute-start | bytes 2752520 | tf_op jit(solution)/shard_map/ppermute | solution.py:32
  237.1 27.8 %all-to-all-start.4 = ((bf16[4,896,128]{2,1,0:T(8,128)(2,1)}), bf16[4,896,128]{2,1,0:T(8,128)(2,1)}, u32[]{:S(2)}, u32[]{:S(2)}) async-start(bf16[4,896,128]{2,1,0:T(8,128)(2,1)} %copy-done.16), calls=%async_computation.4 | async-start | bytes 1835008 | tf_op jit(solution)/shard_map/all_to_all | solution.py:364
  241.7 23.7 %collective-permute-start.9 = (bf16[512,1024]{1,0:T(8,128)(2,1)S(1)}, bf16[512,1024]{1,0:T(8,128)(2,1)}, u32[]{:S(2)}, u32[]{:S(2)}) collective-permute-start(bf16[512,1024]{1,0:T(8,128)(2,1)S(1)} %get-tuple-element.85.refs_0_), channel_id=1, source_target_pairs={{0,16},{16,0},{1,17},{17,1},{2,18},{18,2},{3,19},{19,3},{4,20},{20... | collective-permute-start | bytes 3145736 | tf_op jit(solution)/shard_map/ppermute | solution.py:32
  242.8 21.1 %collective-permute-start.12 = (bf16[4,128,896]{2,1,0:T(8,128)(2,1)}, bf16[4,128,896]{2,1,0:T(8,128)(2,1)S(1)}, u32[]{:S(2)}, u32[]{:S(2)}) collective-permute-start(bf16[4,128,896]{2,1,0:T(8,128)(2,1)} %all-to-all-done.3.refs_4_), channel_id=1, source_target_pairs={{0,8},{4,12},{8,0},{12,4},{1,9},{5,13},{9,1},{13,5},{2,10},{6,14},... | collective-permute-start | bytes 2752520 | tf_op jit(solution)/shard_map/ppermute | solution.py:32
  278.0 28.3 %all-to-all-start.5 = ((bf16[4,896,128]{2,1,0:T(8,128)(2,1)}), bf16[4,896,128]{2,1,0:T(8,128)(2,1)S(1)}, u32[]{:S(2)}, u32[]{:S(2)}) async-start(bf16[4,896,128]{2,1,0:T(8,128)(2,1)} %copy-done.15), calls=%async_computation.5 | async-start | bytes 1835008 | tf_op jit(solution)/shard_map/all_to_all | solution.py:381
  282.8 22.8 %collective-permute-start.14 = (bf16[4,896,128]{2,1,0:T(8,128)(2,1)}, bf16[4,896,128]{2,1,0:T(8,128)(2,1)}, u32[]{:S(2)}, u32[]{:S(2)}) collective-permute-start(bf16[4,896,128]{2,1,0:T(8,128)(2,1)} %all-to-all-done.4.weights_ref), channel_id=1, source_target_pairs={{0,8},{4,12},{8,0},{12,4},{1,9},{5,13},{9,1},{13,5},{2,10},{6,14},... | collective-permute-start | bytes 2752520 | tf_op jit(solution)/shard_map/ppermute | solution.py:32
  291.6 14.8 %collective-permute-start.15 = (bf16[256,512]{1,0:T(8,128)(2,1)}, bf16[256,512]{1,0:T(8,128)(2,1)}, u32[]{:S(2)}, u32[]{:S(2)}) collective-permute-start(bf16[256,512]{1,0:T(8,128)(2,1)} %get-tuple-element.99), channel_id=1, source_target_pairs={{0,16},{16,0},{1,17},{17,1},{2,18},{18,2},{3,19},{19,3},{4,20},{20... | collective-permute-start | bytes 786440 | tf_op jit(solution)/shard_map/ppermute | solution.py:32
  293.0 18.1 %collective-permute-start.16 = (bf16[256,512]{1,0:T(8,128)(2,1)S(1)}, bf16[256,512]{1,0:T(8,128)(2,1)}, u32[]{:S(2)}, u32[]{:S(2)}) collective-permute-start(bf16[256,512]{1,0:T(8,128)(2,1)S(1)} %get-tuple-element.98), channel_id=1, source_target_pairs={{0,16},{16,0},{1,17},{17,1},{2,18},{18,2},{3,19},{19,3},{4,20},{20... | collective-permute-start | bytes 786440 | tf_op jit(solution)/shard_map/ppermute | solution.py:32
  309.0 20.8 %collective-permute-start.24 = (bf16[512,512]{1,0:T(8,128)(2,1)}, bf16[512,512]{1,0:T(8,128)(2,1)}, u32[]{:S(2)}, u32[]{:S(2)}) collective-permute-start(bf16[512,512]{1,0:T(8,128)(2,1)} %down.13), channel_id=1, source_target_pairs={{0,16},{16,0},{1,17},{17,1},{2,18},{18,2},{3,19},{19,3},{4,20},{20... | collective-permute-start | bytes 1572872 | tf_op jit(solution)/shard_map/ppermute | solution.py:32
  310.4 25.3 %collective-permute-start.29 = (bf16[4,896,128]{2,1,0:T(8,128)(2,1)S(1)}, bf16[4,896,128]{2,1,0:T(8,128)(2,1)}, u32[]{:S(2)}, u32[]{:S(2)}) collective-permute-start(bf16[4,896,128]{2,1,0:T(8,128)(2,1)S(1)} %all-to-all-done.5.weights_ref), channel_id=1, source_target_pairs={{0,8},{4,12},{8,0},{12,4},{1,9},{5,13},{9,1},{13,5},{2,10},{6,14},... | collective-permute-start | bytes 2752520 | tf_op jit(solution)/shard_map/ppermute | solution.py:32
  322.5 15.8 %collective-permute-start.20 = (bf16[512,512]{1,0:T(8,128)(2,1)}, bf16[512,512]{1,0:T(8,128)(2,1)}, u32[]{:S(2)}, u32[]{:S(2)}) collective-permute-start(bf16[512,512]{1,0:T(8,128)(2,1)} %down.11), channel_id=1, source_target_pairs={{0,16},{16,0},{1,17},{17,1},{2,18},{18,2},{3,19},{19,3},{4,20},{20... | collective-permute-start | bytes 1572872 | tf_op jit(solution)/shard_map/ppermute | solution.py:32
  337.6 14.7 %collective-permute-start.30 = (bf16[512,512]{1,0:T(8,128)(2,1)S(1)}, bf16[512,512]{1,0:T(8,128)(2,1)S(1)}, u32[]{:S(2)}, u32[]{:S(2)}) collective-permute-start(bf16[512,512]{1,0:T(8,128)(2,1)S(1)} %down.15), channel_id=1, source_target_pairs={{0,16},{16,0},{1,17},{17,1},{2,18},{18,2},{3,19},{19,3},{4,20},{20... | collective-permute-start | bytes 1572872 | tf_op jit(solution)/shard_map/ppermute | solution.py:32
  339.6 18.6 %collective-permute-start.21 = (bf16[128,512]{1,0:T(8,128)(2,1)S(1)}, bf16[128,512]{1,0:T(8,128)(2,1)S(1)}, u32[]{:S(2)}, u32[]{:S(2)}) collective-permute-start(bf16[128,512]{1,0:T(8,128)(2,1)S(1)} %get-tuple-element.95), channel_id=1, source_target_pairs={{0,1},{1,0},{2,3},{3,2},{4,5},{5,4},{6,7},{7,6},{8,9},{9,8},{10,11... | collective-permute-start | bytes 393224 | tf_op jit(solution)/shard_map/ppermute | solution.py:32
  340.7 17.8 %collective-permute-start.22 = (bf16[128,512]{1,0:T(8,128)(2,1)S(1)}, bf16[128,512]{1,0:T(8,128)(2,1)S(1)}, u32[]{:S(2)}, u32[]{:S(2)}) collective-permute-start(bf16[128,512]{1,0:T(8,128)(2,1)S(1)} %get-tuple-element.97), channel_id=1, source_target_pairs={{0,2},{1,3},{2,0},{3,1},{4,6},{5,7},{6,4},{7,5},{8,10},{9,11},{10,... | collective-permute-start | bytes 393224 | tf_op jit(solution)/shard_map/ppermute | solution.py:32
  349.1 20.7 %collective-permute-start.28 = (bf16[128,512]{1,0:T(8,128)(2,1)}, bf16[128,512]{1,0:T(8,128)(2,1)S(1)}, u32[]{:S(2)}, u32[]{:S(2)}) collective-permute-start(bf16[128,512]{1,0:T(8,128)(2,1)} %fusion.7), channel_id=1, source_target_pairs={{0,8},{4,12},{8,0},{12,4},{1,9},{5,13},{9,1},{13,5},{2,10},{6,14},... | collective-permute-start | bytes 393224 | tf_op jit(solution)/shard_map/ppermute | solution.py:32
  (50 other events, 316.4 us)
Sparse Core Ops, SparseCore 0:
  9.6 83.2 all-gather.2
  141.9 62.4 all-gather.4

commit v14 on v13

--- a/solution.py
+++ b/solution.py
@@ -114,14 +114,14 @@
     )(starts, packed, packed, halo)
 
 
-def cut_kernel(gain_ref, gate_up_ref, down_ref, both_ref, gate_ref, up_ref, *down_refs):
-    rows, cols = gate_ref.shape[1], down_refs[0].shape[2]
+def cut_kernel(gain_ref, gate_up_ref, down_ref, both_ref, gate_ref, up_ref, out_ref):
+    rows, cols = gate_ref.shape[1], out_ref.shape[3]
     for which, second_ref in enumerate((gate_ref, up_ref)):
         scaled = (gate_up_ref[which].astype(jnp.float32) * gain_ref[...]).astype(jnp.bfloat16)
         both_ref[0, which] = scaled[:rows]
         second_ref[0] = scaled[rows:]
-    for part, out_ref in enumerate(down_refs):
-        out_ref[0] = down_ref[:, part * cols : (part + 1) * cols]
+    for part in range(PARTS):
+        out_ref[0, part] = down_ref[:, part * cols : (part + 1) * cols]
 
 
 def cut_weights(w_gate_up, w_down, gain, outer_count):
@@ -131,8 +131,8 @@
     if cols % HEAD_WIDTH:
         wide = (w_gate_up.astype(jnp.float32) * gain[None]).astype(jnp.bfloat16)
         wide = jnp.transpose(wide.reshape(2, PARTS, rows, outer_count, cols), (1, 3, 0, 2, 4))
-        tall = jnp.transpose(w_down.reshape(outer_count, cols, PARTS, rows), (2, 0, 1, 3))
-        return [wide[0], wide[1, :, 0], wide[1, :, 1], *tall]
+        tall = jnp.transpose(w_down.reshape(outer_count, cols, PARTS, rows), (0, 2, 1, 3))
+        return [wide[0], wide[1, :, 0], wide[1, :, 1], tall]
     return pl.pallas_call(
         cut_kernel,
         grid=(outer_count,),
@@ -143,10 +143,10 @@
         ],
         out_specs=[pl.BlockSpec((1, 2, rows, cols), lambda p: (p, 0, 0, 0))]
         + [pl.BlockSpec((1, rows, cols), lambda p: (p, 0, 0))] * 2
-        + [pl.BlockSpec((1, cols, rows), lambda p: (p, 0, 0))] * PARTS,
+        + [pl.BlockSpec((1, PARTS, cols, rows), lambda p: (p, 0, 0, 0))],
         out_shape=[jax.ShapeDtypeStruct((outer_count, 2, rows, cols), jnp.bfloat16)]
         + [jax.ShapeDtypeStruct((outer_count, rows, cols), jnp.bfloat16)] * 2
-        + [jax.ShapeDtypeStruct((outer_count, cols, rows), jnp.bfloat16)] * PARTS,
+        + [jax.ShapeDtypeStruct((outer_count, PARTS, cols, rows), jnp.bfloat16)],
         compiler_params=pltpu.CompilerParams(vmem_limit_bytes=VMEM_LIMIT),
         cost_estimate=BRIEF,
         name="cut_weights",
@@ -264,23 +264,28 @@
 
 
 def down_kernel(activated_ref, weights_ref, out_ref):
-    sources, _, cols = weights_ref.shape
+    sources, _, _, cols = weights_ref.shape
     if cols % HEAD_WIDTH:
-        blocks = [weights_ref[s] for s in range(sources)]
+        blocks = [weights_ref[s, 0] for s in range(sources)]
     else:
-        blocks = [jnp.concatenate([weights_ref[s] for s in range(sources)], axis=1)]
+        blocks = [jnp.concatenate([weights_ref[s, 0] for s in range(sources)], axis=1)]
     for s, block in enumerate(blocks):
         product = jnp.dot(activated_ref[...], block, preferred_element_type=jnp.float32)
         out_ref[:, s * block.shape[1] : (s + 1) * block.shape[1]] = product.astype(jnp.bfloat16)
 
 
-def down_product(activated, weights):
-    sources, _, cols = weights.shape
+def down_product(activated, weights, part):
+    sources, _, depth, cols = weights.shape
+    out = (activated.shape[0], sources * cols)
     return pl.pallas_call(
         down_kernel,
-        in_specs=[VMEM, VMEM],
-        out_specs=VMEM,
-        out_shape=jax.ShapeDtypeStruct((activated.shape[0], sources * cols), jnp.bfloat16),
+        grid=(1,),
+        in_specs=[
+            pl.BlockSpec(activated.shape, lambda t: (0, 0)),
+            pl.BlockSpec((sources, 1, depth, cols), lambda t: (0, part, 0, 0)),
+        ],
+        out_specs=pl.BlockSpec(out, lambda t: (0, 0)),
+        out_shape=jax.ShapeDtypeStruct(out, jnp.bfloat16),
         compiler_params=pltpu.CompilerParams(vmem_limit_bytes=VMEM_LIMIT),
         cost_estimate=BRIEF,
         name="down",
@@ -361,29 +366,28 @@
     tokens = [[swap(block, "head", e) if e else block for e in range(head_count)] for block in tokens]
     third, second_y, tokens[0] = fence(spread(after(cut[2], second)), over_y(second), tokens[0])
     own_sums = gate_up(tokens[0], [first, second, third])
-    fourth, third_y, own_sums = fence(spread(after(cut[3], third)), over_y(third), own_sums)
+    fourth = spread(after(cut[3], third))
+    third_y, own_sums = fence(over_y(third), own_sums)
     sums = gate_up(tokens[1], [first_y, second_y, third_y], [own_sums])
+    fourth, sums = fence(fourth, sums)
     other_sums = swap(sums, "inner", 1)
+    fourth_y = [over_y(fourth[:, part : part + 1]) for part in range(PARTS)]
     activated = [activation(sums, other_sums, e, head_count) for e in range(1, head_count)]
-    sent = [down_product(rows_of, fourth) for rows_of in activated]
-    activated = [activation(after(sums, sent[-1]), other_sums, 0, head_count), *activated]
-
-    def over_heads(weights, moved=None):
-        if moved is None:
-            sent = [down_product(rows_of, weights) for rows_of in activated[1:]]
-            moved = [swap(rows_of, "head", e) for e, rows_of in enumerate(sent, 1)]
-        total = down_product(activated[0], weights).astype(jnp.float32)
+    sent = [[down_product(rows_of, fourth, part) for rows_of in activated] for part in range(PARTS)]
+    activated = [activation(after(sums, sent[-1][-1]), other_sums, 0, head_count), *activated]
+
+    def over_heads(weights, part, sent=None):
+        if sent is None:
+            sent = [down_product(rows_of, weights, part) for rows_of in activated[1:]]
+        moved = [swap(rows_of, "head", e) for e, rows_of in enumerate(sent, 1)]
+        total = down_product(activated[0], weights, part).astype(jnp.float32)
         for rows_of in moved:
             total = total + rows_of.astype(jnp.float32)
         return total.reshape(outer_count, own_rows, -1)
 
-    moved = [[swap(piece, "head", e) for piece in jnp.split(rows_of, 2)] for e, rows_of in enumerate(sent, 1)]
-    fifth, fourth_y, moved[0][0] = fence(spread(after(cut[4], fourth)), over_y(fourth), moved[0][0])
-    fifth_y = over_y(fifth)
-    paired = {(0, 0): over_heads(fourth, [jnp.concatenate(pieces) for pieces in moved])}
-    paired[1, 0] = over_heads(fourth_y)
-    paired[0, 1] = over_heads(fifth)
-    paired[1, 1] = over_heads(after(fifth_y, paired[0, 0]))
+    paired = {(0, part): over_heads(fourth, part, sent[part]) for part in range(PARTS)}
+    for part in range(PARTS):
+        paired[1, part] = over_heads(after(fourth_y[part], paired[0, part]), 0)
 
     pieces = [[None] * PARTS, [None] * PARTS]
     for part in range(PARTS):

time: 383 us -> 387 us (1.010)
  waiting for transfers between devices: 188 us -> 210 us
  starting transfers between devices: 73.8 us -> 62 us
    ppermute x33 -> x32, waiting for transfers between devices: 87.3 us -> 100 us  [swap(): return lax.ppermute(array, axis, [(s, s ^ distance) for s in range(count)])]
    all_to_all x2 -> x1, waiting for transfers between devices: 0.79 us -> 8.19 us  [per_device(): fourth = spread(after(cut[3], third))]
    ppermute x33 -> x32, starting transfers between devices: 40.8 us -> 33.7 us  [swap(): return lax.ppermute(array, axis, [(s, s ^ distance) for s in range(count)])]
    all_to_all x2 -> x1, starting transfers between devices: 9.29 us -> 4.58 us  [per_device(): fourth = spread(after(cut[3], third))]
  transfers between devices with their start and end apart: 43 -> 41, of which waited for: 20 -> 22; matrix products, arithmetic and copies ran while one was open for 7% -> 7% of each run, Pallas kernels for 11% -> 12%
where the time goes in v14:
time: 387 us; the launch traced here: 385 us
  waiting for transfers between devices  210 us (54%)
  starting transfers between devices  62 us (16%)
  Pallas kernels  47.7 us (12%)
  local copies, waits for them, and re-layouts  41 us (11%)
  between operations  14.7 us (4%)
  other arithmetic  10.2 us (3%)
    ppermute x32, waiting for transfers between devices, swap(): return lax.ppermute(array, axis, [(s, s ^ distance) for s in range(count)])  100 us
    all_to_all x1, waiting for transfers between devices, per_device(): spread(after(cut[1], normed))  39.7 us
    ppermute x32, starting transfers between devices, swap(): return lax.ppermute(array, axis, [(s, s ^ distance) for s in range(count)])  33.7 us
    all_gather x1, waiting for transfers between devices, per_device(): weights_out = lax.all_gather(w_out, 'outer', axis=1, tiled=True)  24.1 us
    unnamed x66, local copies, waits for them, and re-layouts  23.2 us
    pallas_call x2, Pallas kernels, gate_up(): pl.pallas_call(functools.partial(gate_up_kernel, len(tokens)), in_specs=[...  16.7 us
    all_to_all x1, waiting for transfers between devices, per_device(): lax.all_to_all(groups, ('inner', 'head'), split_axis=0, concat_axis=0, ti...  14.4 us
    all_to_all x1, waiting for transfers between devices, per_device(): first = spread(after(cut[0], weights_out))  12.5 us
  transfers between devices with their start and end apart: 41, of which 22 were waited for; matrix products, arithmetic and copies ran while one was open for 7% of the time, Pallas kernels for 12%

profile of v14, /device:TPU:0, one launch (start us, length us, event | category | flops | bytes accessed | tf_op | source)
XLA Modules:
  0.0 385.4 jit_solution(10804811326912439125)
XLA Ops:
  7.9 4.9 %collective-permute-start = (bf16[64,1024]{1,0:T(8,128)(2,1)}, bf16[64,1024]{1,0:T(8,128)(2,1)S(1)}, u32[]{:S(2)}, u32[]{:S(2)}) collective-permute-start(bf16[64,1024]{1,0:T(8,128)(2,1)} %param.10), channel_id=1, source_target_pairs={{0,1},{1,2},{2,3},{4,5},{5,6},{6,7},{8,9},{9,10},{10,11},{12,13},{... | collective-permute-start | bytes 393224 | tf_op jit(solution)/shard_map/ppermute | solution.py:313
  21.3 3.7 all-to-all-start
  25.6 14.4 %all-to-all-done = bf16[8,64,1024]{2,1,0:T(8,128)(2,1)S(1)} async-done(((bf16[8,64,1024]{2,1,0:T(8,128)(2,1)}), bf16[8,64,1024]{2,1,0:T(8,128)(2,1)S(1)}, u32[]{:S(2)}, u32[]{:S(2)}) %all-to-all-start) | async-done | bytes 1048608 | tf_op jit(solution)/shard_map/all_to_all | solution.py:316
  40.0 5.9 %attention.1.refs_0_ = bf16[512,512]{1,0:T(8,128)(2,1)S(1)} custom-call(s32[512,1]{1,0:T(8,128)S(1)} %copy.27.starts_ref, bf16[512,1024]{1,0:T(8,128)(2,1)S(1)} %bitcast.89, bf16[512,1024]{1,0:T(8,128)(2,1)S(1)} %bitcast.90, bf16[512,1024]{1,0:T(8,128)(2,1)S(1)} %bitcast.91), custom_call_target="tpu_custom_call" | custom-call | flops 1 | bytes 1 | tf_op jit(solution)/shard_map/attention/pallas_call | solution.py:96
  46.9 12.6 %collective-permute-done.3.refs_2_ = bf16[512,512]{1,0:T(8,128)(2,1)S(1)} collective-permute-done((bf16[512,512]{1,0:T(8,128)(2,1)S(1)}, bf16[512,512]{1,0:T(8,128)(2,1)S(1)}, u32[]{:S(2)}, u32[]{:S(2)}) %collective-permute-start.3) | collective-permute-done | bytes 524320 | tf_op jit(solution)/shard_map/ppermute | solution.py:32
  68.7 24.1 %all-gather.3.cloned.1.call-done.refs_4_ = bf16[2048,1024]{1,0:T(8,128)(2,1)} async-done(((bf16[2048,256]{1,0:T(8,128)(2,1)}), bf16[2048,1024]{1,0:T(8,128)(2,1)}) %all-gather.3.cloned.1.call-update) | async-done | bytes 4194320 | tf_op jit(solution)/shard_map/all_gather | solution.py:311
  98.7 5.5 %projection.1 = (bf16[256,1024]{1,0:T(8,128)(2,1)S(1)}, bf16[1,256,1024]{2,1,0:T(8,128)(2,1)}, bf16[128,2048]{1,0:T(8,128)(2,1)}) custom-call(s32[2]{0:T(128)S(1)} %pad_add_fusion.place_ref, bf16[512,512]{1,0:T(8,128)(2,1)S(1)} %attention.1.refs_0_, bf16[512,512]{1,0:T(8,128)(2,1)S(1)} %copy-done.20, bf16[512,512]{1,0:T(8,128)(2,1)S(1)} %collective-permute-done.3.refs_2_, ...), custom_call_target="tpu_custom_call" | custom-call | flops 1 | bytes 1 | tf_op jit(solution)/shard_map/projection/pallas_call | solution.py:185
  105.6 12.5 %collective-permute-done.5 = bf16[256,1024]{1,0:T(8,128)(2,1)S(1)} collective-permute-done((bf16[256,1024]{1,0:T(8,128)(2,1)}, bf16[256,1024]{1,0:T(8,128)(2,1)S(1)}, u32[]{:S(2)}, u32[]{:S(2)}) %collective-permute-start.5) | collective-permute-done | bytes 524320 | tf_op jit(solution)/shard_map/ppermute | solution.py:32
  121.3 5.6 %collective-permute-done.6 = bf16[128,1024]{1,0:T(8,128)(2,1)S(1)} collective-permute-done((bf16[128,1024]{1,0:T(8,128)(2,1)S(1)}, bf16[128,1024]{1,0:T(8,128)(2,1)S(1)}, u32[]{:S(2)}, u32[]{:S(2)}) %collective-permute-start.6) | collective-permute-done | bytes 262176 | tf_op jit(solution)/shard_map/ppermute | solution.py:32
  126.9 12.5 %all-to-all-done.1.refs_2_ = bf16[4,2,128,896]{3,2,1,0:T(8,128)(2,1)S(1)} async-done(((bf16[4,2,128,896]{3,2,1,0:T(8,128)(2,1)}), bf16[4,2,128,896]{3,2,1,0:T(8,128)(2,1)S(1)}, u32[]{:S(2)}, u32[]{:S(2)}) %all-to-all-start.1) | async-done | bytes 1835040 | tf_op jit(solution)/shard_map/all_to_all | solution.py:340
  154.5 39.7 %all-to-all-done.2.refs_3_ = bf16[4,128,896]{2,1,0:T(8,128)(2,1)S(1)} async-done(((bf16[4,128,896]{2,1,0:T(8,128)(2,1)}), bf16[4,128,896]{2,1,0:T(8,128)(2,1)S(1)}, u32[]{:S(2)}, u32[]{:S(2)}) %all-to-all-start.2) | async-done | bytes 917536 | tf_op jit(solution)/shard_map/all_to_all | solution.py:364
  194.2 10.2 %all-gather.5.cloned.1.call-done = bf16[512,2048]{1,0:T(8,128)(2,1)} async-done(((bf16[128,2048]{1,0:T(8,128)(2,1)}), bf16[512,2048]{1,0:T(8,128)(2,1)}) %all-gather.5.cloned.1.call-update) | async-done | bytes 2097168 | tf_op jit(solution)/shard_map/all_gather | solution.py:363
  204.4 4.4 %all-to-all-start.3 = ((bf16[4,128,896]{2,1,0:T(8,128)(2,1)}), bf16[4,128,896]{2,1,0:T(8,128)(2,1)}, u32[]{:S(2)}, u32[]{:S(2)}) async-start(bf16[4,128,896]{2,1,0:T(8,128)(2,1)} %copy-done.17), calls=%async_computation.3 | async-start | bytes 1835008 | tf_op jit(solution)/shard_map/all_to_all | solution.py:367
  213.7 21.4 %collective-permute-done.9.refs_3_ = bf16[4,128,896]{2,1,0:T(8,128)(2,1)S(1)} collective-permute-done((bf16[4,128,896]{2,1,0:T(8,128)(2,1)S(1)}, bf16[4,128,896]{2,1,0:T(8,128)(2,1)S(1)}, u32[]{:S(2)}, u32[]{:S(2)}) %collective-permute-start.9) | collective-permute-done | bytes 917536 | tf_op jit(solution)/shard_map/ppermute | solution.py:32
  237.1 4.6 %all-to-all-start.4 = ((bf16[4,2,896,128]{3,2,1,0:T(8,128)(2,1)}), bf16[4,2,896,128]{3,2,1,0:T(8,128)(2,1)S(1)}, u32[]{:S(2)}, u32[]{:S(2)}) async-start(bf16[4,2,896,128]{3,2,1,0:T(8,128)(2,1)} %copy-done.11), calls=%async_computation.4 | async-start | bytes 3670016 | tf_op jit(solution)/shard_map/all_to_all | solution.py:369
  248.5 7.0 %gate_up.2.refs_5_ = bf16[2,1024,896]{2,1,0:T(8,128)(2,1)} custom-call(bf16[512,1024]{1,0:T(8,128)(2,1)S(1)} %copy-done.7, bf16[512,1024]{1,0:T(8,128)(2,1)S(1)} %copy-done.14, bf16[4,2,128,896]{3,2,1,0:T(8,128)(2,1)S(1)} %copy-done.5, bf16[4,128,896]{2,1,0:T(8,128)(2,1)S(1)} %copy-done.10, bf16[4,128,896]{2,1,0:T(8,128)(2,1)} %all-to-all-done.3.refs_4_), custom_call_target="tpu_custom_call" | custom-call | flops 1 | bytes 1 | tf_op jit(solution)/shard_map/gate_up/pallas_call | solution.py:226
  255.5 8.0 %collective-permute-done.12.refs_4_ = bf16[4,128,896]{2,1,0:T(8,128)(2,1)S(1)} collective-permute-done((bf16[4,128,896]{2,1,0:T(8,128)(2,1)}, bf16[4,128,896]{2,1,0:T(8,128)(2,1)S(1)}, u32[]{:S(2)}, u32[]{:S(2)}) %collective-permute-start.12) | collective-permute-done | bytes 917536 | tf_op jit(solution)/shard_map/ppermute | solution.py:32
  265.0 9.8 %gate_up.3.here_ref = bf16[2,1024,896]{2,1,0:T(8,128)(2,1)} custom-call(bf16[512,1024]{1,0:T(8,128)(2,1)S(1)} %get-tuple-element.78.refs_0_, bf16[512,1024]{1,0:T(8,128)(2,1)S(1)} %collective-permute-done.11.refs_1_, bf16[4,2,128,896]{3,2,1,0:T(8,128)(2,1)} %collective-permute-done.8.refs_2_, bf16[4,128,896]{2,1,0:T(8,128)(2,1)S(1)} %copy-done.16, ...), custom_call_target="tpu_custom_call" | custom-call | flops 1 | bytes 1 | tf_op jit(solution)/shard_map/gate_up/pallas_call | solution.py:226
  274.8 8.2 %all-to-all-done.4.weights_ref = bf16[4,2,896,128]{3,2,1,0:T(8,128)(2,1)S(1)} async-done(((bf16[4,2,896,128]{3,2,1,0:T(8,128)(2,1)}), bf16[4,2,896,128]{3,2,1,0:T(8,128)(2,1)S(1)}, u32[]{:S(2)}, u32[]{:S(2)}) %all-to-all-start.4) | async-done | bytes 1835040 | tf_op jit(solution)/shard_map/all_to_all | solution.py:369
  285.0 4.6 %collective-permute-done.13.there_ref = bf16[2,1024,896]{2,1,0:T(8,128)(2,1)S(1)} collective-permute-done((bf16[2,1024,896]{2,1,0:T(8,128)(2,1)}, bf16[2,1024,896]{2,1,0:T(8,128)(2,1)S(1)}, u32[]{:S(2)}, u32[]{:S(2)}) %collective-permute-start.13) | collective-permute-done | bytes 3670048 | tf_op jit(solution)/shard_map/ppermute | solution.py:32
  316.9 4.5 %collective-permute-done.18 = bf16[512,512]{1,0:T(8,128)(2,1)} collective-permute-done((bf16[512,512]{1,0:T(8,128)(2,1)S(1)}, bf16[512,512]{1,0:T(8,128)(2,1)}, u32[]{:S(2)}, u32[]{:S(2)}) %collective-permute-start.18) | collective-permute-done | bytes 524320 | tf_op jit(solution)/shard_map/ppermute | solution.py:32
  339.2 6.3 %collective-permute-done.20 = bf16[128,512]{1,0:T(8,128)(2,1)S(1)} collective-permute-done((bf16[128,512]{1,0:T(8,128)(2,1)}, bf16[128,512]{1,0:T(8,128)(2,1)S(1)}, u32[]{:S(2)}, u32[]{:S(2)}) %collective-permute-start.20) | collective-permute-done | bytes 131104 | tf_op jit(solution)/shard_map/ppermute | solution.py:32
  358.1 4.8 %collective-permute-done.25 = bf16[128,512]{1,0:T(8,128)(2,1)S(1)} collective-permute-done((bf16[128,512]{1,0:T(8,128)(2,1)S(1)}, bf16[128,512]{1,0:T(8,128)(2,1)S(1)}, u32[]{:S(2)}, u32[]{:S(2)}) %collective-permute-start.25) | collective-permute-done | bytes 131104 | tf_op jit(solution)/shard_map/ppermute | solution.py:32
  363.8 8.0 %collective-permute-done.31 = bf16[128,512]{1,0:T(8,128)(2,1)S(1)} collective-permute-done((bf16[128,512]{1,0:T(8,128)(2,1)S(1)}, bf16[128,512]{1,0:T(8,128)(2,1)S(1)}, u32[]{:S(2)}, u32[]{:S(2)}) %collective-permute-start.31) | collective-permute-done | bytes 131104 | tf_op jit(solution)/shard_map/ppermute | solution.py:32
  (197 shorter events, 127.4 us)
Async XLA Ops:
  7.2 85.7 %all-gather.3.cloned.1.call-start = ((), (), s32[]{:S(2)}) async-start(), calls=%async_computation.5 | async-start | bytes 5242880 | tf_op jit(solution)/shard_map/all_gather | solution.py:311
  21.3 18.7 %all-to-all-start = ((bf16[8,64,1024]{2,1,0:T(8,128)(2,1)}), bf16[8,64,1024]{2,1,0:T(8,128)(2,1)S(1)}, u32[]{:S(2)}, u32[]{:S(2)}) async-start(bf16[8,64,1024]{2,1,0:T(8,128)(2,1)} %bitcast.5), calls=%async_computation | async-start | bytes 2097152 | tf_op jit(solution)/shard_map/all_to_all | solution.py:316
  46.5 19.5 %collective-permute-start.2 = (bf16[512,512]{1,0:T(8,128)(2,1)S(1)}, bf16[512,512]{1,0:T(8,128)(2,1)S(1)}, u32[]{:S(2)}, u32[]{:S(2)}) collective-permute-start(bf16[512,512]{1,0:T(8,128)(2,1)S(1)} %attention.1.refs_0_), channel_id=1, source_target_pairs={{0,4},{4,0},{8,12},{12,8},{1,5},{5,1},{9,13},{13,9},{2,6},{6,2},{1... | collective-permute-start | bytes 1572872 | tf_op jit(solution)/shard_map/ppermute | solution.py:32
  92.9 46.6 %all-to-all-start.1 = ((bf16[4,2,128,896]{3,2,1,0:T(8,128)(2,1)}), bf16[4,2,128,896]{3,2,1,0:T(8,128)(2,1)S(1)}, u32[]{:S(2)}, u32[]{:S(2)}) async-start(bf16[4,2,128,896]{3,2,1,0:T(8,128)(2,1)} %copy-done.12), calls=%async_computation.1 | async-start | bytes 3670016 | tf_op jit(solution)/shard_map/all_to_all | solution.py:340
  96.5 107.9 %all-gather.5.cloned.1.call-start = ((), (), s32[]{:S(2)}) async-start(), calls=%async_computation.6 | async-start | bytes 2621440 | tf_op jit(solution)/shard_map/all_gather | solution.py:363
  141.8 52.4 %collective-permute-start.8 = (bf16[4,2,128,896]{3,2,1,0:T(8,128)(2,1)S(1)}, bf16[4,2,128,896]{3,2,1,0:T(8,128)(2,1)}, u32[]{:S(2)}, u32[]{:S(2)}) collective-permute-start(bf16[4,2,128,896]{3,2,1,0:T(8,128)(2,1)S(1)} %all-to-all-done.1.refs_2_), channel_id=1, source_target_pairs={{0,8},{4,12},{8,0},{12,4},{1,9},{5,13},{9,1},{13,5},{2,10},{6,14},... | collective-permute-start | bytes 5505032 | tf_op jit(solution)/shard_map/ppermute | solution.py:32
  143.4 50.8 %all-to-all-start.2 = ((bf16[4,128,896]{2,1,0:T(8,128)(2,1)}), bf16[4,128,896]{2,1,0:T(8,128)(2,1)S(1)}, u32[]{:S(2)}, u32[]{:S(2)}) async-start(bf16[4,128,896]{2,1,0:T(8,128)(2,1)} %copy-done.18), calls=%async_computation.2 | async-start | bytes 1835008 | tf_op jit(solution)/shard_map/all_to_all | solution.py:364
  204.4 32.7 %all-to-all-start.3 = ((bf16[4,128,896]{2,1,0:T(8,128)(2,1)}), bf16[4,128,896]{2,1,0:T(8,128)(2,1)}, u32[]{:S(2)}, u32[]{:S(2)}) async-start(bf16[4,128,896]{2,1,0:T(8,128)(2,1)} %copy-done.17), calls=%async_computation.3 | async-start | bytes 1835008 | tf_op jit(solution)/shard_map/all_to_all | solution.py:367
  210.6 25.5 %collective-permute-start.10 = (bf16[512,1024]{1,0:T(8,128)(2,1)S(1)}, bf16[512,1024]{1,0:T(8,128)(2,1)S(1)}, u32[]{:S(2)}, u32[]{:S(2)}) collective-permute-start(bf16[512,1024]{1,0:T(8,128)(2,1)S(1)} %get-tuple-element.62.refs_0_), channel_id=1, source_target_pairs={{0,16},{16,0},{1,17},{17,1},{2,18},{18,2},{3,19},{19,3},{4,20},{20... | collective-permute-start | bytes 3145736 | tf_op jit(solution)/shard_map/ppermute | solution.py:32
  213.1 22.0 %collective-permute-start.9 = (bf16[4,128,896]{2,1,0:T(8,128)(2,1)S(1)}, bf16[4,128,896]{2,1,0:T(8,128)(2,1)S(1)}, u32[]{:S(2)}, u32[]{:S(2)}) collective-permute-start(bf16[4,128,896]{2,1,0:T(8,128)(2,1)S(1)} %copy-done.9), channel_id=1, source_target_pairs={{0,8},{4,12},{8,0},{12,4},{1,9},{5,13},{9,1},{13,5},{2,10},{6,14},... | collective-permute-start | bytes 2752520 | tf_op jit(solution)/shard_map/ppermute | solution.py:32
  237.1 45.9 %all-to-all-start.4 = ((bf16[4,2,896,128]{3,2,1,0:T(8,128)(2,1)}), bf16[4,2,896,128]{3,2,1,0:T(8,128)(2,1)S(1)}, u32[]{:S(2)}, u32[]{:S(2)}) async-start(bf16[4,2,896,128]{3,2,1,0:T(8,128)(2,1)} %copy-done.11), calls=%async_computation.4 | async-start | bytes 3670016 | tf_op jit(solution)/shard_map/all_to_all | solution.py:369
  241.7 23.3 %collective-permute-start.11 = (bf16[512,1024]{1,0:T(8,128)(2,1)S(1)}, bf16[512,1024]{1,0:T(8,128)(2,1)S(1)}, u32[]{:S(2)}, u32[]{:S(2)}) collective-permute-start(bf16[512,1024]{1,0:T(8,128)(2,1)S(1)} %get-tuple-element.78.refs_0_), channel_id=1, source_target_pairs={{0,16},{16,0},{1,17},{17,1},{2,18},{18,2},{3,19},{19,3},{4,20},{20... | collective-permute-start | bytes 3145736 | tf_op jit(solution)/shard_map/ppermute | solution.py:32
  242.8 20.8 %collective-permute-start.12 = (bf16[4,128,896]{2,1,0:T(8,128)(2,1)}, bf16[4,128,896]{2,1,0:T(8,128)(2,1)S(1)}, u32[]{:S(2)}, u32[]{:S(2)}) collective-permute-start(bf16[4,128,896]{2,1,0:T(8,128)(2,1)} %all-to-all-done.3.refs_4_), channel_id=1, source_target_pairs={{0,8},{4,12},{8,0},{12,4},{1,9},{5,13},{9,1},{13,5},{2,10},{6,14},... | collective-permute-start | bytes 2752520 | tf_op jit(solution)/shard_map/ppermute | solution.py:32
  284.4 27.0 %collective-permute-start.22 = (bf16[4,1,896,128]{3,2,1,0:T(8,128)(2,1)}, bf16[4,1,896,128]{3,2,1,0:T(8,128)(2,1)}, u32[]{:S(2)}, u32[]{:S(2)}) collective-permute-start(bf16[4,1,896,128]{3,2,1,0:T(8,128)(2,1)} %get-tuple-element.80), channel_id=1, source_target_pairs={{0,8},{4,12},{8,0},{12,4},{1,9},{5,13},{9,1},{13,5},{2,10},{6,14},... | collective-permute-start | bytes 2752520 | tf_op jit(solution)/shard_map/ppermute | solution.py:32
  295.1 15.1 %collective-permute-start.14 = (bf16[512,512]{1,0:T(8,128)(2,1)}, bf16[512,512]{1,0:T(8,128)(2,1)}, u32[]{:S(2)}, u32[]{:S(2)}) collective-permute-start(bf16[512,512]{1,0:T(8,128)(2,1)} %down.10), channel_id=1, source_target_pairs={{0,16},{16,0},{1,17},{17,1},{2,18},{18,2},{3,19},{19,3},{4,20},{20... | collective-permute-start | bytes 1572872 | tf_op jit(solution)/shard_map/ppermute | solution.py:32
  297.3 24.1 %collective-permute-start.18 = (bf16[512,512]{1,0:T(8,128)(2,1)S(1)}, bf16[512,512]{1,0:T(8,128)(2,1)}, u32[]{:S(2)}, u32[]{:S(2)}) collective-permute-start(bf16[512,512]{1,0:T(8,128)(2,1)S(1)} %down.8), channel_id=1, source_target_pairs={{0,16},{16,0},{1,17},{17,1},{2,18},{18,2},{3,19},{19,3},{4,20},{20... | collective-permute-start | bytes 1572872 | tf_op jit(solution)/shard_map/ppermute | solution.py:32
  298.0 29.8 %collective-permute-start.28 = (bf16[4,1,896,128]{3,2,1,0:T(8,128)(2,1)}, bf16[4,1,896,128]{3,2,1,0:T(8,128)(2,1)}, u32[]{:S(2)}, u32[]{:S(2)}) collective-permute-start(bf16[4,1,896,128]{3,2,1,0:T(8,128)(2,1)} %get-tuple-element.81), channel_id=1, source_target_pairs={{0,8},{4,12},{8,0},{12,4},{1,9},{5,13},{9,1},{13,5},{2,10},{6,14},... | collective-permute-start | bytes 2752520 | tf_op jit(solution)/shard_map/ppermute | solution.py:32
  313.3 33.4 %collective-permute-start.23 = (bf16[512,512]{1,0:T(8,128)(2,1)S(1)}, bf16[512,512]{1,0:T(8,128)(2,1)}, u32[]{:S(2)}, u32[]{:S(2)}) collective-permute-start(bf16[512,512]{1,0:T(8,128)(2,1)S(1)} %down.13), channel_id=1, source_target_pairs={{0,16},{16,0},{1,17},{17,1},{2,18},{18,2},{3,19},{19,3},{4,20},{20... | collective-permute-start | bytes 1572872 | tf_op jit(solution)/shard_map/ppermute | solution.py:32
  314.8 18.3 %collective-permute-start.15 = (bf16[128,512]{1,0:T(8,128)(2,1)S(1)}, bf16[128,512]{1,0:T(8,128)(2,1)S(1)}, u32[]{:S(2)}, u32[]{:S(2)}) collective-permute-start(bf16[128,512]{1,0:T(8,128)(2,1)S(1)} %get-tuple-element.88), channel_id=1, source_target_pairs={{0,1},{1,0},{2,3},{3,2},{4,5},{5,4},{6,7},{7,6},{8,9},{9,8},{10,11... | collective-permute-start | bytes 393224 | tf_op jit(solution)/shard_map/ppermute | solution.py:32
  314.9 18.2 %collective-permute-start.16 = (bf16[128,512]{1,0:T(8,128)(2,1)S(1)}, bf16[128,512]{1,0:T(8,128)(2,1)S(1)}, u32[]{:S(2)}, u32[]{:S(2)}) collective-permute-start(bf16[128,512]{1,0:T(8,128)(2,1)S(1)} %get-tuple-element.90), channel_id=1, source_target_pairs={{0,2},{1,3},{2,0},{3,1},{4,6},{5,7},{6,4},{7,5},{8,10},{9,11},{10,... | collective-permute-start | bytes 393224 | tf_op jit(solution)/shard_map/ppermute | solution.py:32
  321.4 14.6 %collective-permute-start.17 = (bf16[128,512]{1,0:T(8,128)(2,1)S(1)}, bf16[128,512]{1,0:T(8,128)(2,1)S(1)}, u32[]{:S(2)}, u32[]{:S(2)}) collective-permute-start(bf16[128,512]{1,0:T(8,128)(2,1)S(1)} %get-tuple-element.89), channel_id=1, source_target_pairs={{0,3},{1,2},{2,1},{3,0},{4,7},{5,6},{6,5},{7,4},{8,11},{9,10},{10,... | collective-permute-start | bytes 393224 | tf_op jit(solution)/shard_map/ppermute | solution.py:32
  331.6 20.8 %collective-permute-start.29 = (bf16[512,512]{1,0:T(8,128)(2,1)S(1)}, bf16[512,512]{1,0:T(8,128)(2,1)}, u32[]{:S(2)}, u32[]{:S(2)}) collective-permute-start(bf16[512,512]{1,0:T(8,128)(2,1)S(1)} %down.15), channel_id=1, source_target_pairs={{0,16},{16,0},{1,17},{17,1},{2,18},{18,2},{3,19},{19,3},{4,20},{20... | collective-permute-start | bytes 1572872 | tf_op jit(solution)/shard_map/ppermute | solution.py:32
  354.8 17.0 %collective-permute-start.31 = (bf16[128,512]{1,0:T(8,128)(2,1)S(1)}, bf16[128,512]{1,0:T(8,128)(2,1)S(1)}, u32[]{:S(2)}, u32[]{:S(2)}) collective-permute-start(bf16[128,512]{1,0:T(8,128)(2,1)S(1)} %get-tuple-element.87), channel_id=1, source_target_pairs={{0,2},{1,3},{2,0},{3,1},{4,6},{5,7},{6,4},{7,5},{8,10},{9,11},{10,... | collective-permute-start | bytes 393224 | tf_op jit(solution)/shard_map/ppermute | solution.py:32
  356.4 15.4 %collective-permute-start.32 = (bf16[128,512]{1,0:T(8,128)(2,1)S(1)}, bf16[128,512]{1,0:T(8,128)(2,1)S(1)}, u32[]{:S(2)}, u32[]{:S(2)}) collective-permute-start(bf16[128,512]{1,0:T(8,128)(2,1)S(1)} %get-tuple-element.86), channel_id=1, source_target_pairs={{0,3},{1,2},{2,1},{3,0},{4,7},{5,6},{6,5},{7,4},{8,11},{9,10},{10,... | collective-permute-start | bytes 393224 | tf_op jit(solution)/shard_map/ppermute | solution.py:32
  (48 other events, 311.0 us)
Sparse Core Ops, SparseCore 0:
  9.6 83.2 all-gather.2
  141.9 62.4 all-gather.4

commit v15 on v14

--- a/solution.py
+++ b/solution.py
@@ -369,8 +369,7 @@
     fourth = spread(after(cut[3], third))
     third_y, own_sums = fence(over_y(third), own_sums)
     sums = gate_up(tokens[1], [first_y, second_y, third_y], [own_sums])
-    fourth, sums = fence(fourth, sums)
-    other_sums = swap(sums, "inner", 1)
+    fourth, other_sums = fence(fourth, swap(sums, "inner", 1))
     fourth_y = [over_y(fourth[:, part : part + 1]) for part in range(PARTS)]
     activated = [activation(sums, other_sums, e, head_count) for e in range(1, head_count)]
     sent = [[down_product(rows_of, fourth, part) for rows_of in activated] for part in range(PARTS)]
@@ -392,10 +391,7 @@
     pieces = [[None] * PARTS, [None] * PARTS]
     for part in range(PARTS):
         for a in range(2):
-            total = state[a][part] + lax.dynamic_index_in_dim(paired[a, part], outer, 0, False)
-            for d in range(1, outer_count):
-                sent = lax.dynamic_index_in_dim(paired[a, part], outer ^ d, 0, False).astype(jnp.bfloat16)
-                total = total + swap(sent, "outer", d).astype(jnp.float32)
+            total = state[a][part] + jnp.sum(spread(paired[a, part].astype(jnp.bfloat16)).astype(jnp.float32), axis=0)
             total = total.astype(jnp.bfloat16)
             pieces[a][part] = (over_y(total) if a else total).reshape(own_rows, outer_count, 1, part_rows)
     halves = [jnp.concatenate(parts, axis=2).reshape(own_rows, -1) for parts in pieces]

time: 387 us -> 416 us (1.075)
  blocking collectives: 0 us -> 47.5 us
  starting transfers between devices: 62 us -> 53.4 us
  local copies, waits for them, and re-layouts: 41 us -> 34.3 us
    all_to_all x0 -> x1, blocking collectives: none -> 47.5 us  [per_device(): fourth = spread(after(cut[3], third))]
    ppermute x32 -> x20, starting transfers between devices: 33.7 us -> 14.8 us  [swap(): return lax.ppermute(array, axis, [(s, s ^ distance) for s in range(count)])]
    ppermute x32 -> x20, waiting for transfers between devices: 100 us -> 88.9 us  [swap(): return lax.ppermute(array, axis, [(s, s ^ distance) for s in range(count)])]
    all_to_all x1 -> x4, starting transfers between devices: 4.58 us -> 14.9 us  [per_device(): spread(paired[a, part].astype(jnp.bfloat16)).astype(jnp.float32)]
    all_to_all x1 -> x4, waiting for transfers between devices: 8.19 us -> 16.4 us  [per_device(): spread(paired[a, part].astype(jnp.bfloat16)).astype(jnp.float32)]
    unnamed x66 -> x64, local copies, waits for them, and re-layouts: 23.2 us -> 17.2 us
  transfers between devices with their start and end apart: 41 -> 32, of which waited for: 22 -> 20; matrix products, arithmetic and copies ran while one was open for 7% -> 7% of each run, Pallas kernels for 12% -> 8%
where the time goes in v15:
time: 416 us; the launch traced here: 414 us
  waiting for transfers between devices  206 us (50%)
  starting transfers between devices  53.4 us (13%)
  blocking collectives  47.5 us (11%)
  Pallas kernels  47 us (11%)
  local copies, waits for them, and re-layouts  34.3 us (8%)
  between operations  14.7 us (4%)
  other arithmetic  11.4 us (3%)
    ppermute x20, waiting for transfers between devices, swap(): return lax.ppermute(array, axis, [(s, s ^ distance) for s in range(count)])  88.9 us
    all_to_all x1, blocking collectives, per_device(): fourth = spread(after(cut[3], third))  47.5 us
    all_to_all x1, waiting for transfers between devices, per_device(): spread(after(cut[1], normed))  39.6 us
    all_gather x1, waiting for transfers between devices, per_device(): weights_out = lax.all_gather(w_out, 'outer', axis=1, tiled=True)  23.4 us
    unnamed x64, local copies, waits for them, and re-layouts  17.2 us
    pallas_call x2, Pallas kernels, gate_up(): pl.pallas_call(functools.partial(gate_up_kernel, len(tokens)), in_specs=[...  17.1 us
    all_to_all x4, waiting for transfers between devices, per_device(): spread(paired[a, part].astype(jnp.bfloat16)).astype(jnp.float32)  16.4 us
    all_to_all x4, starting transfers between devices, per_device(): spread(paired[a, part].astype(jnp.bfloat16)).astype(jnp.float32)  14.9 us
  transfers between devices with their start and end apart: 32, of which 20 were waited for; matrix products, arithmetic and copies ran while one was open for 7% of the time, Pallas kernels for 8%

profile of v15, /device:TPU:0, one launch (start us, length us, event | category | flops | bytes accessed | tf_op | source)
XLA Modules:
  0.0 414.4 jit_solution(8073629605347851378)
XLA Ops:
  7.9 4.9 %collective-permute-start = (bf16[64,1024]{1,0:T(8,128)(2,1)}, bf16[64,1024]{1,0:T(8,128)(2,1)S(1)}, u32[]{:S(2)}, u32[]{:S(2)}) collective-permute-start(bf16[64,1024]{1,0:T(8,128)(2,1)} %param.10), channel_id=1, source_target_pairs={{0,1},{1,2},{2,3},{4,5},{5,6},{6,7},{8,9},{9,10},{10,11},{12,13},{... | collective-permute-start | bytes 393224 | tf_op jit(solution)/shard_map/ppermute | solution.py:313
  25.5 14.4 %all-to-all-done = bf16[8,64,1024]{2,1,0:T(8,128)(2,1)S(1)} async-done(((bf16[8,64,1024]{2,1,0:T(8,128)(2,1)}), bf16[8,64,1024]{2,1,0:T(8,128)(2,1)S(1)}, u32[]{:S(2)}, u32[]{:S(2)}) %all-to-all-start) | async-done | bytes 1048608 | tf_op jit(solution)/shard_map/all_to_all | solution.py:316
  40.0 5.9 %attention.1.refs_0_ = bf16[512,512]{1,0:T(8,128)(2,1)S(1)} custom-call(s32[512,1]{1,0:T(8,128)S(1)} %copy.47.starts_ref, bf16[512,1024]{1,0:T(8,128)(2,1)S(1)} %bitcast.31, bf16[512,1024]{1,0:T(8,128)(2,1)S(1)} %bitcast.32, bf16[512,1024]{1,0:T(8,128)(2,1)S(1)} %bitcast.33), custom_call_target="tpu_custom_call" | custom-call | flops 1 | bytes 1 | tf_op jit(solution)/shard_map/attention/pallas_call | solution.py:96
  46.9 12.7 %collective-permute-done.3.refs_2_ = bf16[512,512]{1,0:T(8,128)(2,1)S(1)} collective-permute-done((bf16[512,512]{1,0:T(8,128)(2,1)S(1)}, bf16[512,512]{1,0:T(8,128)(2,1)S(1)}, u32[]{:S(2)}, u32[]{:S(2)}) %collective-permute-start.3) | collective-permute-done | bytes 524320 | tf_op jit(solution)/shard_map/ppermute | solution.py:32
  69.5 23.4 %all-gather.3.cloned.1.call-done.refs_4_ = bf16[2048,1024]{1,0:T(8,128)(2,1)} async-done(((bf16[2048,256]{1,0:T(8,128)(2,1)}), bf16[2048,1024]{1,0:T(8,128)(2,1)}) %all-gather.3.cloned.1.call-update) | async-done | bytes 4194320 | tf_op jit(solution)/shard_map/all_gather | solution.py:311
  98.7 5.5 %projection.1 = (bf16[256,1024]{1,0:T(8,128)(2,1)S(1)}, bf16[1,256,1024]{2,1,0:T(8,128)(2,1)}, bf16[128,2048]{1,0:T(8,128)(2,1)}) custom-call(s32[2]{0:T(128)S(1)} %pad_add_fusion.place_ref, bf16[512,512]{1,0:T(8,128)(2,1)S(1)} %attention.1.refs_0_, bf16[512,512]{1,0:T(8,128)(2,1)S(1)} %copy-done.19, bf16[512,512]{1,0:T(8,128)(2,1)S(1)} %collective-permute-done.3.refs_2_, ...), custom_call_target="tpu_custom_call" | custom-call | flops 1 | bytes 1 | tf_op jit(solution)/shard_map/projection/pallas_call | solution.py:185
  105.6 12.5 %collective-permute-done.5 = bf16[256,1024]{1,0:T(8,128)(2,1)S(1)} collective-permute-done((bf16[256,1024]{1,0:T(8,128)(2,1)}, bf16[256,1024]{1,0:T(8,128)(2,1)S(1)}, u32[]{:S(2)}, u32[]{:S(2)}) %collective-permute-start.5) | collective-permute-done | bytes 524320 | tf_op jit(solution)/shard_map/ppermute | solution.py:32
  121.3 5.6 %collective-permute-done.6 = bf16[128,1024]{1,0:T(8,128)(2,1)S(1)} collective-permute-done((bf16[128,1024]{1,0:T(8,128)(2,1)S(1)}, bf16[128,1024]{1,0:T(8,128)(2,1)S(1)}, u32[]{:S(2)}, u32[]{:S(2)}) %collective-permute-start.6) | collective-permute-done | bytes 262176 | tf_op jit(solution)/shard_map/ppermute | solution.py:32
  126.9 12.5 %all-to-all-done.1.refs_2_ = bf16[4,2,128,896]{3,2,1,0:T(8,128)(2,1)S(1)} async-done(((bf16[4,2,128,896]{3,2,1,0:T(8,128)(2,1)}), bf16[4,2,128,896]{3,2,1,0:T(8,128)(2,1)S(1)}, u32[]{:S(2)}, u32[]{:S(2)}) %all-to-all-start.1) | async-done | bytes 1835040 | tf_op jit(solution)/shard_map/all_to_all | solution.py:340
  154.6 39.6 %all-to-all-done.2.refs_3_ = bf16[4,128,896]{2,1,0:T(8,128)(2,1)S(1)} async-done(((bf16[4,128,896]{2,1,0:T(8,128)(2,1)}), bf16[4,128,896]{2,1,0:T(8,128)(2,1)S(1)}, u32[]{:S(2)}, u32[]{:S(2)}) %all-to-all-start.2) | async-done | bytes 917536 | tf_op jit(solution)/shard_map/all_to_all | solution.py:364
  194.2 10.2 %all-gather.5.cloned.1.call-done = bf16[512,2048]{1,0:T(8,128)(2,1)} async-done(((bf16[128,2048]{1,0:T(8,128)(2,1)}), bf16[512,2048]{1,0:T(8,128)(2,1)}) %all-gather.5.cloned.1.call-update) | async-done | bytes 2097168 | tf_op jit(solution)/shard_map/all_gather | solution.py:363
  204.4 4.4 %all-to-all-start.3 = ((bf16[4,128,896]{2,1,0:T(8,128)(2,1)}), bf16[4,128,896]{2,1,0:T(8,128)(2,1)}, u32[]{:S(2)}, u32[]{:S(2)}) async-start(bf16[4,128,896]{2,1,0:T(8,128)(2,1)} %copy-done.16), calls=%async_computation.3 | async-start | bytes 1835008 | tf_op jit(solution)/shard_map/all_to_all | solution.py:367
  214.2 20.9 %collective-permute-done.10.refs_3_ = bf16[4,128,896]{2,1,0:T(8,128)(2,1)S(1)} collective-permute-done((bf16[4,128,896]{2,1,0:T(8,128)(2,1)S(1)}, bf16[4,128,896]{2,1,0:T(8,128)(2,1)S(1)}, u32[]{:S(2)}, u32[]{:S(2)}) %collective-permute-start.10) | collective-permute-done | bytes 917536 | tf_op jit(solution)/shard_map/ppermute | solution.py:32
  241.8 7.0 %gate_up.2.refs_5_ = bf16[2,1024,896]{2,1,0:T(8,128)(2,1)} custom-call(bf16[512,1024]{1,0:T(8,128)(2,1)S(1)} %copy-done.5, bf16[512,1024]{1,0:T(8,128)(2,1)S(1)} %copy-done.13, bf16[4,2,128,896]{3,2,1,0:T(8,128)(2,1)S(1)} %all-to-all-done.1.refs_2_, bf16[4,128,896]{2,1,0:T(8,128)(2,1)S(1)} %copy-done.8, bf16[4,128,896]{2,1,0:T(8,128)(2,1)} %all-to-all-done.3.refs_4_), custom_call_target="tpu_custom_call" | custom-call | flops 1 | bytes 1 | tf_op jit(solution)/shard_map/gate_up/pallas_call | solution.py:226
  248.8 9.6 %collective-permute-done.12.refs_4_ = bf16[4,128,896]{2,1,0:T(8,128)(2,1)S(1)} collective-permute-done((bf16[4,128,896]{2,1,0:T(8,128)(2,1)}, bf16[4,128,896]{2,1,0:T(8,128)(2,1)S(1)}, u32[]{:S(2)}, u32[]{:S(2)}) %collective-permute-start.12) | collective-permute-done | bytes 917536 | tf_op jit(solution)/shard_map/ppermute | solution.py:32
  258.4 10.1 %gate_up.3.here_ref = bf16[2,1024,896]{2,1,0:T(8,128)(2,1)} custom-call(bf16[512,1024]{1,0:T(8,128)(2,1)S(1)} %get-tuple-element.79.refs_0_, bf16[512,1024]{1,0:T(8,128)(2,1)} %collective-permute-done.9.refs_1_, bf16[4,2,128,896]{3,2,1,0:T(8,128)(2,1)} %collective-permute-done.8.refs_2_, bf16[4,128,896]{2,1,0:T(8,128)(2,1)S(1)} %copy-done.15, ...), custom_call_target="tpu_custom_call" | custom-call | flops 1 | bytes 1 | tf_op jit(solution)/shard_map/gate_up/pallas_call | solution.py:226
  268.7 47.5 %all_to_all.45.weights_ref = bf16[4,2,896,128]{3,2,1,0:T(8,128)(2,1)S(1)} all-to-all(bf16[4,2,896,128]{3,2,1,0:T(8,128)(2,1)S(1)} %copy-done.10), channel_id=1, replica_groups=mesh['head'=2,'inner'=4,'outer'=4] {'outer'}, dimensions={0} | all-to-all | bytes 3670016 | tf_op jit(solution)/shard_map/all_to_all | solution.py:369
  328.6 7.2 %collective-permute-done.14 = bf16[512,512]{1,0:T(8,128)(2,1)S(1)} collective-permute-done((bf16[512,512]{1,0:T(8,128)(2,1)S(1)}, bf16[512,512]{1,0:T(8,128)(2,1)S(1)}, u32[]{:S(2)}, u32[]{:S(2)}) %collective-permute-start.14) | collective-permute-done | bytes 524320 | tf_op jit(solution)/shard_map/ppermute | solution.py:32
  336.7 4.4 %all-to-all-start.5 = ((bf16[4,128,512]{2,1,0:T(8,128)(2,1)}), bf16[4,128,512]{2,1,0:T(8,128)(2,1)}, u32[]{:S(2)}, u32[]{:S(2)}) async-start(bf16[4,128,512]{2,1,0:T(8,128)(2,1)} %bitcast.35), calls=%async_computation.5 | async-start | bytes 1048576 | tf_op jit(solution)/shard_map/all_to_all | solution.py:394
  342.5 4.9 %collective-permute-done.16.weights_ref = bf16[4,1,896,128]{3,2,1,0:T(8,128)(2,1)} collective-permute-done((bf16[4,1,896,128]{3,2,1,0:T(8,128)(2,1)}, bf16[4,1,896,128]{3,2,1,0:T(8,128)(2,1)}, u32[]{:S(2)}, u32[]{:S(2)}) %collective-permute-start.16) | collective-permute-done | bytes 917536 | tf_op jit(solution)/shard_map/ppermute | solution.py:32
  357.9 7.0 %collective-permute-done.19.weights_ref = bf16[4,1,896,128]{3,2,1,0:T(8,128)(2,1)} collective-permute-done((bf16[4,1,896,128]{3,2,1,0:T(8,128)(2,1)}, bf16[4,1,896,128]{3,2,1,0:T(8,128)(2,1)}, u32[]{:S(2)}, u32[]{:S(2)}) %collective-permute-start.19) | collective-permute-done | bytes 917536 | tf_op jit(solution)/shard_map/ppermute | solution.py:32
  380.6 4.7 %all-to-all-done.7 = bf16[4,128,512]{2,1,0:T(8,128)(2,1)S(1)} async-done(((bf16[4,128,512]{2,1,0:T(8,128)(2,1)}), bf16[4,128,512]{2,1,0:T(8,128)(2,1)S(1)}, u32[]{:S(2)}, u32[]{:S(2)}) %all-to-all-start.7) | async-done | bytes 524320 | tf_op jit(solution)/shard_map/all_to_all | solution.py:394
  390.2 11.0 %all-to-all-done.8 = bf16[4,128,512]{2,1,0:T(8,128)(2,1)S(1)} async-done(((bf16[4,128,512]{2,1,0:T(8,128)(2,1)}), bf16[4,128,512]{2,1,0:T(8,128)(2,1)S(1)}, u32[]{:S(2)}, u32[]{:S(2)}) %all-to-all-start.8) | async-done | bytes 524320 | tf_op jit(solution)/shard_map/all_to_all | solution.py:394
  402.4 4.0 collective-permute-done.21
  (180 shorter events, 109.7 us)
Async XLA Ops:
  7.2 85.7 %all-gather.3.cloned.1.call-start = ((), (), s32[]{:S(2)}) async-start(), calls=%async_computation.9 | async-start | bytes 5242880 | tf_op jit(solution)/shard_map/all_gather | solution.py:311
  21.3 18.7 %all-to-all-start = ((bf16[8,64,1024]{2,1,0:T(8,128)(2,1)}), bf16[8,64,1024]{2,1,0:T(8,128)(2,1)S(1)}, u32[]{:S(2)}, u32[]{:S(2)}) async-start(bf16[8,64,1024]{2,1,0:T(8,128)(2,1)} %bitcast.5), calls=%async_computation | async-start | bytes 2097152 | tf_op jit(solution)/shard_map/all_to_all | solution.py:316
  45.8 13.7 %collective-permute-start.3 = (bf16[512,512]{1,0:T(8,128)(2,1)S(1)}, bf16[512,512]{1,0:T(8,128)(2,1)S(1)}, u32[]{:S(2)}, u32[]{:S(2)}) collective-permute-start(bf16[512,512]{1,0:T(8,128)(2,1)S(1)} %attention.1.refs_0_), channel_id=1, source_target_pairs={{0,8},{4,12},{8,0},{12,4},{1,9},{5,13},{9,1},{13,5},{2,10},{6,14},... | collective-permute-start | bytes 1572872 | tf_op jit(solution)/shard_map/ppermute | solution.py:32
  46.5 22.2 %collective-permute-start.2 = (bf16[512,512]{1,0:T(8,128)(2,1)S(1)}, bf16[512,512]{1,0:T(8,128)(2,1)S(1)}, u32[]{:S(2)}, u32[]{:S(2)}) collective-permute-start(bf16[512,512]{1,0:T(8,128)(2,1)S(1)} %attention.1.refs_0_), channel_id=1, source_target_pairs={{0,4},{4,0},{8,12},{12,8},{1,5},{5,1},{9,13},{13,9},{2,6},{6,2},{1... | collective-permute-start | bytes 1572872 | tf_op jit(solution)/shard_map/ppermute | solution.py:32
  92.9 46.6 %all-to-all-start.1 = ((bf16[4,2,128,896]{3,2,1,0:T(8,128)(2,1)}), bf16[4,2,128,896]{3,2,1,0:T(8,128)(2,1)S(1)}, u32[]{:S(2)}, u32[]{:S(2)}) async-start(bf16[4,2,128,896]{3,2,1,0:T(8,128)(2,1)} %copy-done.11), calls=%async_computation.1 | async-start | bytes 3670016 | tf_op jit(solution)/shard_map/all_to_all | solution.py:340
  96.5 107.9 %all-gather.5.cloned.1.call-start = ((), (), s32[]{:S(2)}) async-start(), calls=%async_computation.10 | async-start | bytes 2621440 | tf_op jit(solution)/shard_map/all_gather | solution.py:363
  104.1 14.0 %collective-permute-start.5 = (bf16[256,1024]{1,0:T(8,128)(2,1)}, bf16[256,1024]{1,0:T(8,128)(2,1)S(1)}, u32[]{:S(2)}, u32[]{:S(2)}) collective-permute-start(bf16[256,1024]{1,0:T(8,128)(2,1)} %bitcast.8), channel_id=1, source_target_pairs={{0,16},{16,0},{1,17},{17,1},{2,18},{18,2},{3,19},{19,3},{4,20},{20... | collective-permute-start | bytes 1572872 | tf_op jit(solution)/shard_map/ppermute | solution.py:32
  141.8 52.4 %collective-permute-start.8 = (bf16[4,2,128,896]{3,2,1,0:T(8,128)(2,1)S(1)}, bf16[4,2,128,896]{3,2,1,0:T(8,128)(2,1)}, u32[]{:S(2)}, u32[]{:S(2)}) collective-permute-start(bf16[4,2,128,896]{3,2,1,0:T(8,128)(2,1)S(1)} %all-to-all-done.1.refs_2_), channel_id=1, source_target_pairs={{0,8},{4,12},{8,0},{12,4},{1,9},{5,13},{9,1},{13,5},{2,10},{6,14},... | collective-permute-start | bytes 5505032 | tf_op jit(solution)/shard_map/ppermute | solution.py:32
  143.4 50.8 %all-to-all-start.2 = ((bf16[4,128,896]{2,1,0:T(8,128)(2,1)}), bf16[4,128,896]{2,1,0:T(8,128)(2,1)S(1)}, u32[]{:S(2)}, u32[]{:S(2)}) async-start(bf16[4,128,896]{2,1,0:T(8,128)(2,1)} %copy-done.17), calls=%async_computation.2 | async-start | bytes 1835008 | tf_op jit(solution)/shard_map/all_to_all | solution.py:364
  204.4 33.3 %all-to-all-start.3 = ((bf16[4,128,896]{2,1,0:T(8,128)(2,1)}), bf16[4,128,896]{2,1,0:T(8,128)(2,1)}, u32[]{:S(2)}, u32[]{:S(2)}) async-start(bf16[4,128,896]{2,1,0:T(8,128)(2,1)} %copy-done.16), calls=%async_computation.3 | async-start | bytes 1835008 | tf_op jit(solution)/shard_map/all_to_all | solution.py:367
  210.6 26.1 %collective-permute-start.11 = (bf16[512,1024]{1,0:T(8,128)(2,1)S(1)}, bf16[512,1024]{1,0:T(8,128)(2,1)S(1)}, u32[]{:S(2)}, u32[]{:S(2)}) collective-permute-start(bf16[512,1024]{1,0:T(8,128)(2,1)S(1)} %get-tuple-element.60.refs_0_), channel_id=1, source_target_pairs={{0,16},{16,0},{1,17},{17,1},{2,18},{18,2},{3,19},{19,3},{4,20},{20... | collective-permute-start | bytes 3145736 | tf_op jit(solution)/shard_map/ppermute | solution.py:32
  213.1 22.0 %collective-permute-start.10 = (bf16[4,128,896]{2,1,0:T(8,128)(2,1)S(1)}, bf16[4,128,896]{2,1,0:T(8,128)(2,1)S(1)}, u32[]{:S(2)}, u32[]{:S(2)}) collective-permute-start(bf16[4,128,896]{2,1,0:T(8,128)(2,1)S(1)} %copy-done.7), channel_id=1, source_target_pairs={{0,8},{4,12},{8,0},{12,4},{1,9},{5,13},{9,1},{13,5},{2,10},{6,14},... | collective-permute-start | bytes 2752520 | tf_op jit(solution)/shard_map/ppermute | solution.py:32
  213.7 44.7 %collective-permute-start.9 = (bf16[512,1024]{1,0:T(8,128)(2,1)S(1)}, bf16[512,1024]{1,0:T(8,128)(2,1)}, u32[]{:S(2)}, u32[]{:S(2)}) collective-permute-start(bf16[512,1024]{1,0:T(8,128)(2,1)S(1)} %get-tuple-element.79.refs_0_), channel_id=1, source_target_pairs={{0,16},{16,0},{1,17},{17,1},{2,18},{18,2},{3,19},{19,3},{4,20},{20... | collective-permute-start | bytes 3145736 | tf_op jit(solution)/shard_map/ppermute | solution.py:32
  237.7 20.8 %collective-permute-start.12 = (bf16[4,128,896]{2,1,0:T(8,128)(2,1)}, bf16[4,128,896]{2,1,0:T(8,128)(2,1)S(1)}, u32[]{:S(2)}, u32[]{:S(2)}) collective-permute-start(bf16[4,128,896]{2,1,0:T(8,128)(2,1)} %all-to-all-done.3.refs_4_), channel_id=1, source_target_pairs={{0,8},{4,12},{8,0},{12,4},{1,9},{5,13},{9,1},{13,5},{2,10},{6,14},... | collective-permute-start | bytes 2752520 | tf_op jit(solution)/shard_map/ppermute | solution.py:32
  268.6 47.6 %collective-permute-start.13 = (bf16[2,1024,896]{2,1,0:T(8,128)(2,1)}, bf16[2,1024,896]{2,1,0:T(8,128)(2,1)S(1)}, u32[]{:S(2)}, u32[]{:S(2)}) collective-permute-start(bf16[2,1024,896]{2,1,0:T(8,128)(2,1)} %gate_up.3.here_ref), channel_id=1, source_target_pairs={{0,4},{4,0},{8,12},{12,8},{1,5},{5,1},{9,13},{13,9},{2,6},{6,2},{1... | collective-permute-start | bytes 11010056 | tf_op jit(solution)/shard_map/ppermute | solution.py:32
  320.9 14.9 %collective-permute-start.14 = (bf16[512,512]{1,0:T(8,128)(2,1)S(1)}, bf16[512,512]{1,0:T(8,128)(2,1)S(1)}, u32[]{:S(2)}, u32[]{:S(2)}) collective-permute-start(bf16[512,512]{1,0:T(8,128)(2,1)S(1)} %down.10), channel_id=1, source_target_pairs={{0,16},{16,0},{1,17},{17,1},{2,18},{18,2},{3,19},{19,3},{4,20},{20... | collective-permute-start | bytes 1572872 | tf_op jit(solution)/shard_map/ppermute | solution.py:32
  323.8 23.6 %collective-permute-start.16 = (bf16[4,1,896,128]{3,2,1,0:T(8,128)(2,1)}, bf16[4,1,896,128]{3,2,1,0:T(8,128)(2,1)}, u32[]{:S(2)}, u32[]{:S(2)}) collective-permute-start(bf16[4,1,896,128]{3,2,1,0:T(8,128)(2,1)} %get-tuple-element.80), channel_id=1, source_target_pairs={{0,8},{4,12},{8,0},{12,4},{1,9},{5,13},{9,1},{13,5},{2,10},{6,14},... | collective-permute-start | bytes 2752520 | tf_op jit(solution)/shard_map/ppermute | solution.py:32
  327.3 22.6 %collective-permute-start.15 = (bf16[512,512]{1,0:T(8,128)(2,1)S(1)}, bf16[512,512]{1,0:T(8,128)(2,1)}, u32[]{:S(2)}, u32[]{:S(2)}) collective-permute-start(bf16[512,512]{1,0:T(8,128)(2,1)S(1)} %down.8), channel_id=1, source_target_pairs={{0,16},{16,0},{1,17},{17,1},{2,18},{18,2},{3,19},{19,3},{4,20},{20... | collective-permute-start | bytes 1572872 | tf_op jit(solution)/shard_map/ppermute | solution.py:32
  336.7 15.7 %all-to-all-start.5 = ((bf16[4,128,512]{2,1,0:T(8,128)(2,1)}), bf16[4,128,512]{2,1,0:T(8,128)(2,1)}, u32[]{:S(2)}, u32[]{:S(2)}) async-start(bf16[4,128,512]{2,1,0:T(8,128)(2,1)} %bitcast.35), calls=%async_computation.5 | async-start | bytes 1048576 | tf_op jit(solution)/shard_map/all_to_all | solution.py:394
  341.1 23.8 %collective-permute-start.19 = (bf16[4,1,896,128]{3,2,1,0:T(8,128)(2,1)}, bf16[4,1,896,128]{3,2,1,0:T(8,128)(2,1)}, u32[]{:S(2)}, u32[]{:S(2)}) collective-permute-start(bf16[4,1,896,128]{3,2,1,0:T(8,128)(2,1)} %get-tuple-element.81), channel_id=1, source_target_pairs={{0,8},{4,12},{8,0},{12,4},{1,9},{5,13},{9,1},{13,5},{2,10},{6,14},... | collective-permute-start | bytes 2752520 | tf_op jit(solution)/shard_map/ppermute | solution.py:32
  349.3 18.1 %collective-permute-start.17 = (bf16[512,512]{1,0:T(8,128)(2,1)S(1)}, bf16[512,512]{1,0:T(8,128)(2,1)}, u32[]{:S(2)}, u32[]{:S(2)}) collective-permute-start(bf16[512,512]{1,0:T(8,128)(2,1)S(1)} %down.13), channel_id=1, source_target_pairs={{0,16},{16,0},{1,17},{17,1},{2,18},{18,2},{3,19},{19,3},{4,20},{20... | collective-permute-start | bytes 1572872 | tf_op jit(solution)/shard_map/ppermute | solution.py:32
  352.5 16.9 %all-to-all-start.6 = ((bf16[4,128,512]{2,1,0:T(8,128)(2,1)}), bf16[4,128,512]{2,1,0:T(8,128)(2,1)S(1)}, u32[]{:S(2)}, u32[]{:S(2)}) async-start(bf16[4,128,512]{2,1,0:T(8,128)(2,1)} %bitcast.11), calls=%async_computation.6 | async-start | bytes 1048576 | tf_op jit(solution)/shard_map/all_to_all | solution.py:394
  369.4 16.0 %all-to-all-start.7 = ((bf16[4,128,512]{2,1,0:T(8,128)(2,1)}), bf16[4,128,512]{2,1,0:T(8,128)(2,1)S(1)}, u32[]{:S(2)}, u32[]{:S(2)}) async-start(bf16[4,128,512]{2,1,0:T(8,128)(2,1)} %bitcast.14), calls=%async_computation.7 | async-start | bytes 1048576 | tf_op jit(solution)/shard_map/all_to_all | solution.py:394
  385.4 15.8 %all-to-all-start.8 = ((bf16[4,128,512]{2,1,0:T(8,128)(2,1)}), bf16[4,128,512]{2,1,0:T(8,128)(2,1)S(1)}, u32[]{:S(2)}, u32[]{:S(2)}) async-start(bf16[4,128,512]{2,1,0:T(8,128)(2,1)} %bitcast.16), calls=%async_computation.8 | async-start | bytes 1048576 | tf_op jit(solution)/shard_map/all_to_all | solution.py:394
  (38 other events, 295.1 us)
Sparse Core Ops, SparseCore 0:
  9.6 83.2 all-gather.2
  141.9 62.4 all-gather.4

commit v16 on v13

--- a/solution.py
+++ b/solution.py
@@ -345,13 +345,13 @@
     own_rows = half // 2
     mine = lax.dynamic_slice_in_dim(hidden_part, upper * own_rows, own_rows, 0)
     others = lax.dynamic_slice_in_dim(hidden_part, (1 - upper) * own_rows, own_rows, 0)
-    others, first = fence(over_y(others), first)
-    state = [mine.astype(jnp.float32), others.astype(jnp.float32)]
+    state = [mine.astype(jnp.float32), over_y(others).astype(jnp.float32)]
     squares = sum([jnp.sum(block * block, axis=1) for block in state])
     squares = squares + swap(squares, "inner", 1)
     inverse = lax.rsqrt(squares / D + 1e-05)[:, None]
     part_rows = feature_rows // PARTS
     normed = jnp.concatenate([block * inverse for block in state], axis=1).astype(jnp.bfloat16)
+    normed, first = fence(normed, first)
     state = [block.reshape(own_rows, outer_count, PARTS, part_rows) for block in state]
     state = [[block[:, :, part].reshape(own_rows, -1) for part in range(PARTS)] for block in state]
 

time: 383 us -> 380 us (level)
  transfers between devices with their start and end apart: 43 -> 43, of which waited for: 20 -> 20; matrix products, arithmetic and copies ran while one was open for 7% -> 8% of each run, Pallas kernels for 11% -> 11%
where the time goes in v16:
time: 380 us; the launch traced here: 378 us
  waiting for transfers between devices  185 us (49%)
  starting transfers between devices  73.9 us (19%)
  Pallas kernels  50.7 us (13%)
  local copies, waits for them, and re-layouts  42.8 us (11%)
  between operations  14.7 us (4%)
  other arithmetic  10.8 us (3%)
    ppermute x33, waiting for transfers between devices, swap(): return lax.ppermute(array, axis, [(s, s ^ distance) for s in range(count)])  87.3 us
    ppermute x33, starting transfers between devices, swap(): return lax.ppermute(array, axis, [(s, s ^ distance) for s in range(count)])  40.8 us
    all_to_all x1, waiting for transfers between devices, per_device(): spread(after(cut[1], normed))  38.6 us
    unnamed x66, local copies, waits for them, and re-layouts  24.3 us
    all_gather x1, waiting for transfers between devices, per_device(): weights_out = lax.all_gather(w_out, 'outer', axis=1, tiled=True)  22.9 us
    pallas_call x2, Pallas kernels, gate_up(): pl.pallas_call(functools.partial(gate_up_kernel, len(tokens)), in_specs=[...  17.1 us
    all_to_all x1, waiting for transfers between devices, per_device(): lax.all_to_all(groups, ('inner', 'head'), split_axis=0, concat_axis=0, ti...  14.4 us
    pallas_call x8, Pallas kernels, down_product(): pl.pallas_call(down_kernel, in_specs=[VMEM, VMEM], out_specs=VMEM, out_sh...  14.3 us
  transfers between devices with their start and end apart: 43, of which 20 were waited for; matrix products, arithmetic and copies ran while one was open for 8% of the time, Pallas kernels for 11%

profile of v16, /device:TPU:0, one launch (start us, length us, event | category | flops | bytes accessed | tf_op | source)
XLA Modules:
  0.0 377.8 jit_solution(5054493253713626755)
XLA Ops:
  7.9 4.9 %collective-permute-start = (bf16[64,1024]{1,0:T(8,128)(2,1)}, bf16[64,1024]{1,0:T(8,128)(2,1)S(1)}, u32[]{:S(2)}, u32[]{:S(2)}) collective-permute-start(bf16[64,1024]{1,0:T(8,128)(2,1)} %param.10), channel_id=1, source_target_pairs={{0,1},{1,2},{2,3},{4,5},{5,6},{6,7},{8,9},{9,10},{10,11},{12,13},{... | collective-permute-start | bytes 393224 | tf_op jit(solution)/shard_map/ppermute | solution.py:308
  21.3 3.7 all-to-all-start
  25.6 14.4 %all-to-all-done = bf16[8,64,1024]{2,1,0:T(8,128)(2,1)S(1)} async-done(((bf16[8,64,1024]{2,1,0:T(8,128)(2,1)}), bf16[8,64,1024]{2,1,0:T(8,128)(2,1)S(1)}, u32[]{:S(2)}, u32[]{:S(2)}) %all-to-all-start) | async-done | bytes 1048608 | tf_op jit(solution)/shard_map/all_to_all | solution.py:311
  40.0 5.8 %attention.1.refs_0_ = bf16[512,512]{1,0:T(8,128)(2,1)S(1)} custom-call(s32[512,1]{1,0:T(8,128)S(1)} %copy.27.starts_ref, bf16[512,1024]{1,0:T(8,128)(2,1)S(1)} %bitcast.89, bf16[512,1024]{1,0:T(8,128)(2,1)S(1)} %bitcast.90, bf16[512,1024]{1,0:T(8,128)(2,1)S(1)} %bitcast.91), custom_call_target="tpu_custom_call" | custom-call | flops 1 | bytes 1 | tf_op jit(solution)/shard_map/attention/pallas_call | solution.py:96
  46.9 12.6 %collective-permute-done.3.refs_2_ = bf16[512,512]{1,0:T(8,128)(2,1)S(1)} collective-permute-done((bf16[512,512]{1,0:T(8,128)(2,1)S(1)}, bf16[512,512]{1,0:T(8,128)(2,1)S(1)}, u32[]{:S(2)}, u32[]{:S(2)}) %collective-permute-start.3) | collective-permute-done | bytes 524320 | tf_op jit(solution)/shard_map/ppermute | solution.py:32
  60.4 3.7 cut_weights.1
  70.0 22.9 %all-gather.3.cloned.1.call-done.refs_4_ = bf16[2048,1024]{1,0:T(8,128)(2,1)} async-done(((bf16[2048,256]{1,0:T(8,128)(2,1)}), bf16[2048,1024]{1,0:T(8,128)(2,1)}) %all-gather.3.cloned.1.call-update) | async-done | bytes 4194320 | tf_op jit(solution)/shard_map/all_gather | solution.py:306
  92.9 3.6 all-to-all-start.1
  98.7 5.5 %projection.1 = (bf16[256,1024]{1,0:T(8,128)(2,1)S(1)}, bf16[1,256,1024]{2,1,0:T(8,128)(2,1)}, bf16[128,2048]{1,0:T(8,128)(2,1)}) custom-call(s32[2]{0:T(128)S(1)} %pad_add_fusion.place_ref, bf16[512,512]{1,0:T(8,128)(2,1)S(1)} %attention.1.refs_0_, bf16[512,512]{1,0:T(8,128)(2,1)S(1)} %copy-done.20, bf16[512,512]{1,0:T(8,128)(2,1)S(1)} %collective-permute-done.3.refs_2_, ...), custom_call_target="tpu_custom_call" | custom-call | flops 1 | bytes 1 | tf_op jit(solution)/shard_map/projection/pallas_call | solution.py:185
  105.6 12.5 %collective-permute-done.5 = bf16[256,1024]{1,0:T(8,128)(2,1)S(1)} collective-permute-done((bf16[256,1024]{1,0:T(8,128)(2,1)}, bf16[256,1024]{1,0:T(8,128)(2,1)S(1)}, u32[]{:S(2)}, u32[]{:S(2)}) %collective-permute-start.5) | collective-permute-done | bytes 524320 | tf_op jit(solution)/shard_map/ppermute | solution.py:32
  121.3 5.6 %collective-permute-done.6 = bf16[128,1024]{1,0:T(8,128)(2,1)S(1)} collective-permute-done((bf16[128,1024]{1,0:T(8,128)(2,1)S(1)}, bf16[128,1024]{1,0:T(8,128)(2,1)S(1)}, u32[]{:S(2)}, u32[]{:S(2)}) %collective-permute-start.6) | collective-permute-done | bytes 262176 | tf_op jit(solution)/shard_map/ppermute | solution.py:32
  129.3 10.2 %all-to-all-done.1.refs_2_ = bf16[4,2,128,896]{3,2,1,0:T(8,128)(2,1)S(1)} async-done(((bf16[4,2,128,896]{3,2,1,0:T(8,128)(2,1)}), bf16[4,2,128,896]{3,2,1,0:T(8,128)(2,1)S(1)}, u32[]{:S(2)}, u32[]{:S(2)}) %all-to-all-start.1) | async-done | bytes 1835040 | tf_op jit(solution)/shard_map/all_to_all | solution.py:335
  152.3 38.6 %all-to-all-done.2.refs_3_ = bf16[4,128,896]{2,1,0:T(8,128)(2,1)S(1)} async-done(((bf16[4,128,896]{2,1,0:T(8,128)(2,1)}), bf16[4,128,896]{2,1,0:T(8,128)(2,1)S(1)}, u32[]{:S(2)}, u32[]{:S(2)}) %all-to-all-start.2) | async-done | bytes 917536 | tf_op jit(solution)/shard_map/all_to_all | solution.py:359
  190.8 10.2 %all-gather.5.cloned.1.call-done = bf16[512,2048]{1,0:T(8,128)(2,1)} async-done(((bf16[128,2048]{1,0:T(8,128)(2,1)}), bf16[512,2048]{1,0:T(8,128)(2,1)}) %all-gather.5.cloned.1.call-update) | async-done | bytes 2097168 | tf_op jit(solution)/shard_map/all_gather | solution.py:358
  201.1 4.4 %all-to-all-start.3 = ((bf16[4,128,896]{2,1,0:T(8,128)(2,1)}), bf16[4,128,896]{2,1,0:T(8,128)(2,1)}, u32[]{:S(2)}, u32[]{:S(2)}) async-start(bf16[4,128,896]{2,1,0:T(8,128)(2,1)} %copy-done.17), calls=%async_computation.3 | async-start | bytes 1835008 | tf_op jit(solution)/shard_map/all_to_all | solution.py:362
  210.5 21.4 %collective-permute-done.10.refs_3_ = bf16[4,128,896]{2,1,0:T(8,128)(2,1)S(1)} collective-permute-done((bf16[4,128,896]{2,1,0:T(8,128)(2,1)S(1)}, bf16[4,128,896]{2,1,0:T(8,128)(2,1)S(1)}, u32[]{:S(2)}, u32[]{:S(2)}) %collective-permute-start.10) | collective-permute-done | bytes 917536 | tf_op jit(solution)/shard_map/ppermute | solution.py:32
  233.8 4.6 %all-to-all-start.4 = ((bf16[4,896,128]{2,1,0:T(8,128)(2,1)}), bf16[4,896,128]{2,1,0:T(8,128)(2,1)}, u32[]{:S(2)}, u32[]{:S(2)}) async-start(bf16[4,896,128]{2,1,0:T(8,128)(2,1)} %copy-done.16), calls=%async_computation.4 | async-start | bytes 1835008 | tf_op jit(solution)/shard_map/all_to_all | solution.py:364
  243.7 7.0 %gate_up.2.refs_5_ = bf16[2,1024,896]{2,1,0:T(8,128)(2,1)} custom-call(bf16[512,1024]{1,0:T(8,128)(2,1)S(1)} %copy-done.3, bf16[512,1024]{1,0:T(8,128)(2,1)S(1)} %copy-done.10, bf16[4,2,128,896]{3,2,1,0:T(8,128)(2,1)S(1)} %all-to-all-done.1.refs_2_, bf16[4,128,896]{2,1,0:T(8,128)(2,1)S(1)} %copy-done.6, bf16[4,128,896]{2,1,0:T(8,128)(2,1)} %all-to-all-done.3.refs_4_), custom_call_target="tpu_custom_call" | custom-call | flops 1 | bytes 1 | tf_op jit(solution)/shard_map/gate_up/pallas_call | solution.py:226
  250.7 9.8 %collective-permute-done.12.refs_4_ = bf16[4,128,896]{2,1,0:T(8,128)(2,1)S(1)} collective-permute-done((bf16[4,128,896]{2,1,0:T(8,128)(2,1)}, bf16[4,128,896]{2,1,0:T(8,128)(2,1)S(1)}, u32[]{:S(2)}, u32[]{:S(2)}) %collective-permute-start.12) | collective-permute-done | bytes 917536 | tf_op jit(solution)/shard_map/ppermute | solution.py:32
  264.5 10.2 %gate_up.3.here_ref = bf16[2,1024,896]{2,1,0:T(8,128)(2,1)} custom-call(bf16[512,1024]{1,0:T(8,128)(2,1)S(1)} %get-tuple-element.85.refs_0_, bf16[512,1024]{1,0:T(8,128)(2,1)} %collective-permute-done.9.refs_1_, bf16[4,2,128,896]{3,2,1,0:T(8,128)(2,1)} %collective-permute-done.8.refs_2_, bf16[4,128,896]{2,1,0:T(8,128)(2,1)S(1)} %copy-done.12, ...), custom_call_target="tpu_custom_call" | custom-call | flops 1 | bytes 1 | tf_op jit(solution)/shard_map/gate_up/pallas_call | solution.py:226
  274.7 4.7 %all-to-all-start.5 = ((bf16[4,896,128]{2,1,0:T(8,128)(2,1)}), bf16[4,896,128]{2,1,0:T(8,128)(2,1)S(1)}, u32[]{:S(2)}, u32[]{:S(2)}) async-start(bf16[4,896,128]{2,1,0:T(8,128)(2,1)} %copy-done.15), calls=%async_computation.5 | async-start | bytes 1835008 | tf_op jit(solution)/shard_map/all_to_all | solution.py:381
  296.3 5.9 %collective-permute-done.14.weights_ref = bf16[4,896,128]{2,1,0:T(8,128)(2,1)} collective-permute-done((bf16[4,896,128]{2,1,0:T(8,128)(2,1)}, bf16[4,896,128]{2,1,0:T(8,128)(2,1)}, u32[]{:S(2)}, u32[]{:S(2)}) %collective-permute-start.14) | collective-permute-done | bytes 917536 | tf_op jit(solution)/shard_map/ppermute | solution.py:32
  349.3 5.6 %collective-permute-start.31 = (bf16[128,512]{1,0:T(8,128)(2,1)S(1)}, bf16[128,512]{1,0:T(8,128)(2,1)S(1)}, u32[]{:S(2)}, u32[]{:S(2)}) collective-permute-start(bf16[128,512]{1,0:T(8,128)(2,1)S(1)} %get-tuple-element.89), channel_id=1, source_target_pairs={{0,1},{1,0},{2,3},{3,2},{4,5},{5,4},{6,7},{7,6},{8,9},{9,8},{10,11... | collective-permute-start | bytes 393224 | tf_op jit(solution)/shard_map/ppermute | solution.py:32
  358.9 5.2 %collective-permute-done.32 = bf16[128,512]{1,0:T(8,128)(2,1)S(1)} collective-permute-done((bf16[128,512]{1,0:T(8,128)(2,1)S(1)}, bf16[128,512]{1,0:T(8,128)(2,1)S(1)}, u32[]{:S(2)}, u32[]{:S(2)}) %collective-permute-start.32) | collective-permute-done | bytes 131104 | tf_op jit(solution)/shard_map/ppermute | solution.py:32
  (201 shorter events, 130.1 us)
Async XLA Ops:
  7.2 85.7 %all-gather.3.cloned.1.call-start = ((), (), s32[]{:S(2)}) async-start(), calls=%async_computation.6 | async-start | bytes 5242880 | tf_op jit(solution)/shard_map/all_gather | solution.py:306
  21.3 18.7 %all-to-all-start = ((bf16[8,64,1024]{2,1,0:T(8,128)(2,1)}), bf16[8,64,1024]{2,1,0:T(8,128)(2,1)S(1)}, u32[]{:S(2)}, u32[]{:S(2)}) async-start(bf16[8,64,1024]{2,1,0:T(8,128)(2,1)} %bitcast.5), calls=%async_computation | async-start | bytes 2097152 | tf_op jit(solution)/shard_map/all_to_all | solution.py:311
  46.5 22.7 %collective-permute-start.2 = (bf16[512,512]{1,0:T(8,128)(2,1)S(1)}, bf16[512,512]{1,0:T(8,128)(2,1)S(1)}, u32[]{:S(2)}, u32[]{:S(2)}) collective-permute-start(bf16[512,512]{1,0:T(8,128)(2,1)S(1)} %attention.1.refs_0_), channel_id=1, source_target_pairs={{0,4},{4,0},{8,12},{12,8},{1,5},{5,1},{9,13},{13,9},{2,6},{6,2},{1... | collective-permute-start | bytes 1572872 | tf_op jit(solution)/shard_map/ppermute | solution.py:32
  92.9 46.6 %all-to-all-start.1 = ((bf16[4,2,128,896]{3,2,1,0:T(8,128)(2,1)}), bf16[4,2,128,896]{3,2,1,0:T(8,128)(2,1)S(1)}, u32[]{:S(2)}, u32[]{:S(2)}) async-start(bf16[4,2,128,896]{3,2,1,0:T(8,128)(2,1)} %copy-done.8), calls=%async_computation.1 | async-start | bytes 3670016 | tf_op jit(solution)/shard_map/all_to_all | solution.py:335
  96.5 104.6 %all-gather.5.cloned.1.call-start = ((), (), s32[]{:S(2)}) async-start(), calls=%async_computation.7 | async-start | bytes 2621440 | tf_op jit(solution)/shard_map/all_gather | solution.py:358
  139.4 51.4 %collective-permute-start.8 = (bf16[4,2,128,896]{3,2,1,0:T(8,128)(2,1)S(1)}, bf16[4,2,128,896]{3,2,1,0:T(8,128)(2,1)}, u32[]{:S(2)}, u32[]{:S(2)}) collective-permute-start(bf16[4,2,128,896]{3,2,1,0:T(8,128)(2,1)S(1)} %all-to-all-done.1.refs_2_), channel_id=1, source_target_pairs={{0,8},{4,12},{8,0},{12,4},{1,9},{5,13},{9,1},{13,5},{2,10},{6,14},... | collective-permute-start | bytes 5505032 | tf_op jit(solution)/shard_map/ppermute | solution.py:32
  141.1 49.8 %all-to-all-start.2 = ((bf16[4,128,896]{2,1,0:T(8,128)(2,1)}), bf16[4,128,896]{2,1,0:T(8,128)(2,1)S(1)}, u32[]{:S(2)}, u32[]{:S(2)}) async-start(bf16[4,128,896]{2,1,0:T(8,128)(2,1)} %copy-done.18), calls=%async_computation.2 | async-start | bytes 1835008 | tf_op jit(solution)/shard_map/all_to_all | solution.py:359
  201.1 32.7 %all-to-all-start.3 = ((bf16[4,128,896]{2,1,0:T(8,128)(2,1)}), bf16[4,128,896]{2,1,0:T(8,128)(2,1)}, u32[]{:S(2)}, u32[]{:S(2)}) async-start(bf16[4,128,896]{2,1,0:T(8,128)(2,1)} %copy-done.17), calls=%async_computation.3 | async-start | bytes 1835008 | tf_op jit(solution)/shard_map/all_to_all | solution.py:362
  207.3 25.5 %collective-permute-start.11 = (bf16[512,1024]{1,0:T(8,128)(2,1)S(1)}, bf16[512,1024]{1,0:T(8,128)(2,1)S(1)}, u32[]{:S(2)}, u32[]{:S(2)}) collective-permute-start(bf16[512,1024]{1,0:T(8,128)(2,1)S(1)} %get-tuple-element.65.refs_0_), channel_id=1, source_target_pairs={{0,16},{16,0},{1,17},{17,1},{2,18},{18,2},{3,19},{19,3},{4,20},{20... | collective-permute-start | bytes 3145736 | tf_op jit(solution)/shard_map/ppermute | solution.py:32
  209.9 22.0 %collective-permute-start.10 = (bf16[4,128,896]{2,1,0:T(8,128)(2,1)S(1)}, bf16[4,128,896]{2,1,0:T(8,128)(2,1)S(1)}, u32[]{:S(2)}, u32[]{:S(2)}) collective-permute-start(bf16[4,128,896]{2,1,0:T(8,128)(2,1)S(1)} %copy-done.5), channel_id=1, source_target_pairs={{0,8},{4,12},{8,0},{12,4},{1,9},{5,13},{9,1},{13,5},{2,10},{6,14},... | collective-permute-start | bytes 2752520 | tf_op jit(solution)/shard_map/ppermute | solution.py:32
  233.8 27.8 %all-to-all-start.4 = ((bf16[4,896,128]{2,1,0:T(8,128)(2,1)}), bf16[4,896,128]{2,1,0:T(8,128)(2,1)}, u32[]{:S(2)}, u32[]{:S(2)}) async-start(bf16[4,896,128]{2,1,0:T(8,128)(2,1)} %copy-done.16), calls=%async_computation.4 | async-start | bytes 1835008 | tf_op jit(solution)/shard_map/all_to_all | solution.py:364
  238.4 23.7 %collective-permute-start.9 = (bf16[512,1024]{1,0:T(8,128)(2,1)S(1)}, bf16[512,1024]{1,0:T(8,128)(2,1)}, u32[]{:S(2)}, u32[]{:S(2)}) collective-permute-start(bf16[512,1024]{1,0:T(8,128)(2,1)S(1)} %get-tuple-element.85.refs_0_), channel_id=1, source_target_pairs={{0,16},{16,0},{1,17},{17,1},{2,18},{18,2},{3,19},{19,3},{4,20},{20... | collective-permute-start | bytes 3145736 | tf_op jit(solution)/shard_map/ppermute | solution.py:32
  239.5 21.1 %collective-permute-start.12 = (bf16[4,128,896]{2,1,0:T(8,128)(2,1)}, bf16[4,128,896]{2,1,0:T(8,128)(2,1)S(1)}, u32[]{:S(2)}, u32[]{:S(2)}) collective-permute-start(bf16[4,128,896]{2,1,0:T(8,128)(2,1)} %all-to-all-done.3.refs_4_), channel_id=1, source_target_pairs={{0,8},{4,12},{8,0},{12,4},{1,9},{5,13},{9,1},{13,5},{2,10},{6,14},... | collective-permute-start | bytes 2752520 | tf_op jit(solution)/shard_map/ppermute | solution.py:32
  274.7 28.3 %all-to-all-start.5 = ((bf16[4,896,128]{2,1,0:T(8,128)(2,1)}), bf16[4,896,128]{2,1,0:T(8,128)(2,1)S(1)}, u32[]{:S(2)}, u32[]{:S(2)}) async-start(bf16[4,896,128]{2,1,0:T(8,128)(2,1)} %copy-done.15), calls=%async_computation.5 | async-start | bytes 1835008 | tf_op jit(solution)/shard_map/all_to_all | solution.py:381
  279.4 22.8 %collective-permute-start.14 = (bf16[4,896,128]{2,1,0:T(8,128)(2,1)}, bf16[4,896,128]{2,1,0:T(8,128)(2,1)}, u32[]{:S(2)}, u32[]{:S(2)}) collective-permute-start(bf16[4,896,128]{2,1,0:T(8,128)(2,1)} %all-to-all-done.4.weights_ref), channel_id=1, source_target_pairs={{0,8},{4,12},{8,0},{12,4},{1,9},{5,13},{9,1},{13,5},{2,10},{6,14},... | collective-permute-start | bytes 2752520 | tf_op jit(solution)/shard_map/ppermute | solution.py:32
  288.3 14.8 %collective-permute-start.15 = (bf16[256,512]{1,0:T(8,128)(2,1)}, bf16[256,512]{1,0:T(8,128)(2,1)}, u32[]{:S(2)}, u32[]{:S(2)}) collective-permute-start(bf16[256,512]{1,0:T(8,128)(2,1)} %get-tuple-element.99), channel_id=1, source_target_pairs={{0,16},{16,0},{1,17},{17,1},{2,18},{18,2},{3,19},{19,3},{4,20},{20... | collective-permute-start | bytes 786440 | tf_op jit(solution)/shard_map/ppermute | solution.py:32
  289.7 18.1 %collective-permute-start.16 = (bf16[256,512]{1,0:T(8,128)(2,1)S(1)}, bf16[256,512]{1,0:T(8,128)(2,1)}, u32[]{:S(2)}, u32[]{:S(2)}) collective-permute-start(bf16[256,512]{1,0:T(8,128)(2,1)S(1)} %get-tuple-element.98), channel_id=1, source_target_pairs={{0,16},{16,0},{1,17},{17,1},{2,18},{18,2},{3,19},{19,3},{4,20},{20... | collective-permute-start | bytes 786440 | tf_op jit(solution)/shard_map/ppermute | solution.py:32
  305.7 20.9 %collective-permute-start.24 = (bf16[512,512]{1,0:T(8,128)(2,1)}, bf16[512,512]{1,0:T(8,128)(2,1)}, u32[]{:S(2)}, u32[]{:S(2)}) collective-permute-start(bf16[512,512]{1,0:T(8,128)(2,1)} %down.13), channel_id=1, source_target_pairs={{0,16},{16,0},{1,17},{17,1},{2,18},{18,2},{3,19},{19,3},{4,20},{20... | collective-permute-start | bytes 1572872 | tf_op jit(solution)/shard_map/ppermute | solution.py:32
  307.1 25.3 %collective-permute-start.29 = (bf16[4,896,128]{2,1,0:T(8,128)(2,1)S(1)}, bf16[4,896,128]{2,1,0:T(8,128)(2,1)}, u32[]{:S(2)}, u32[]{:S(2)}) collective-permute-start(bf16[4,896,128]{2,1,0:T(8,128)(2,1)S(1)} %all-to-all-done.5.weights_ref), channel_id=1, source_target_pairs={{0,8},{4,12},{8,0},{12,4},{1,9},{5,13},{9,1},{13,5},{2,10},{6,14},... | collective-permute-start | bytes 2752520 | tf_op jit(solution)/shard_map/ppermute | solution.py:32
  319.2 15.8 %collective-permute-start.20 = (bf16[512,512]{1,0:T(8,128)(2,1)}, bf16[512,512]{1,0:T(8,128)(2,1)}, u32[]{:S(2)}, u32[]{:S(2)}) collective-permute-start(bf16[512,512]{1,0:T(8,128)(2,1)} %down.11), channel_id=1, source_target_pairs={{0,16},{16,0},{1,17},{17,1},{2,18},{18,2},{3,19},{19,3},{4,20},{20... | collective-permute-start | bytes 1572872 | tf_op jit(solution)/shard_map/ppermute | solution.py:32
  334.4 14.7 %collective-permute-start.30 = (bf16[512,512]{1,0:T(8,128)(2,1)S(1)}, bf16[512,512]{1,0:T(8,128)(2,1)S(1)}, u32[]{:S(2)}, u32[]{:S(2)}) collective-permute-start(bf16[512,512]{1,0:T(8,128)(2,1)S(1)} %down.15), channel_id=1, source_target_pairs={{0,16},{16,0},{1,17},{17,1},{2,18},{18,2},{3,19},{19,3},{4,20},{20... | collective-permute-start | bytes 1572872 | tf_op jit(solution)/shard_map/ppermute | solution.py:32
  336.3 18.6 %collective-permute-start.21 = (bf16[128,512]{1,0:T(8,128)(2,1)S(1)}, bf16[128,512]{1,0:T(8,128)(2,1)S(1)}, u32[]{:S(2)}, u32[]{:S(2)}) collective-permute-start(bf16[128,512]{1,0:T(8,128)(2,1)S(1)} %get-tuple-element.95), channel_id=1, source_target_pairs={{0,1},{1,0},{2,3},{3,2},{4,5},{5,4},{6,7},{7,6},{8,9},{9,8},{10,11... | collective-permute-start | bytes 393224 | tf_op jit(solution)/shard_map/ppermute | solution.py:32
  337.4 17.8 %collective-permute-start.22 = (bf16[128,512]{1,0:T(8,128)(2,1)S(1)}, bf16[128,512]{1,0:T(8,128)(2,1)S(1)}, u32[]{:S(2)}, u32[]{:S(2)}) collective-permute-start(bf16[128,512]{1,0:T(8,128)(2,1)S(1)} %get-tuple-element.97), channel_id=1, source_target_pairs={{0,2},{1,3},{2,0},{3,1},{4,6},{5,7},{6,4},{7,5},{8,10},{9,11},{10,... | collective-permute-start | bytes 393224 | tf_op jit(solution)/shard_map/ppermute | solution.py:32
  345.8 20.7 %collective-permute-start.28 = (bf16[128,512]{1,0:T(8,128)(2,1)}, bf16[128,512]{1,0:T(8,128)(2,1)S(1)}, u32[]{:S(2)}, u32[]{:S(2)}) collective-permute-start(bf16[128,512]{1,0:T(8,128)(2,1)} %fusion.7), channel_id=1, source_target_pairs={{0,8},{4,12},{8,0},{12,4},{1,9},{5,13},{9,1},{13,5},{2,10},{6,14},... | collective-permute-start | bytes 393224 | tf_op jit(solution)/shard_map/ppermute | solution.py:32
  (50 other events, 316.4 us)
Sparse Core Ops, SparseCore 0:
  9.6 83.2 all-gather.2
  139.6 61.4 all-gather.4
